TPU v7x, 32 devices: a whole 2x2x4 slice. The times are simulated.
32 devices in a mesh: dp: 8 (over z, y), ctx: 4 (over x, core).
Axes of the slice: x: 2, y: 2, z: 4, core: 2. Of those that a mesh axis runs over, the one named last changes fastest.
Arguments:
- tokens: bfloat16 [8192, 512], P(('dp', 'ctx')), may hold values from -6 to 6
- dest_owner: int32 [8192], P(('dp', 'ctx')), may hold values from 0 to 7, as said below
- dest_slot: int32 [8192], P(('dp', 'ctx')), may hold values from 0 to 255, as said below
- lengths: int32 [8, 3], P('dp'), may hold values from 1 to 768, 1024 in all within a row
- proj_weight: bfloat16 [512, 2048], replicated, may hold values from -0.25 to 0.25
- out_weight: bfloat16 [512, 512], replicated, may hold values from -0.25 to 0.25
- cotangent: bfloat16 [8192, 512], P(('dp', 'ctx')), may hold values from -6 to 6
Outputs:
- layer_out: bfloat16 [8192, 512], P(('dp', 'ctx'))
- grad_tokens: bfloat16 [8192, 512], P(('dp', 'ctx'))
- grad_proj: float32 [512, 2048], P('dp')
- grad_outw: float32 [512, 512], P('dp')
Inputs may be any that keep to these rules, and one draw needn't show every extreme that they name: `dest_owner`: at every ctx index, the rows of one device name each owner at most 64 times, some owner exactly 64 times, and every owner receives exactly 256 rows from the devices of that ctx index. `dest_slot`: the rows that reach one owner device carry distinct slots that cover all of 0 to 255. Each group's lengths sum to 1024, the largest is exactly 768.
All inputs are finite; a program needn't handle non-finite values.
Results may differ from a plain program's by a relative error of at most 0.012.
Values may be sent and summed in bfloat16 or wider, within the bound.
No kernel may reach another device: no remote copies, remote signals or barrier semaphores. Data moves between devices by JAX's collectives and lax.ppermute only.
A program may use at most 64 MiB of HBM per device.

v0:
```python
import jax
import jax.numpy as jnp
from jax import lax
from jax.sharding import PartitionSpec as P

HEADS = 8


epsilon = 1e-05


def normalize(value):
    middle = jnp.mean(value, axis=-1, keepdims=True)
    centred = value - middle
    inv_dev = lax.rsqrt(jnp.mean(centred * centred, axis=-1, keepdims=True) + epsilon)
    return (centred * inv_dev, inv_dev)


def norm_back(grad, normed, inv_dev):
    return inv_dev * (
        grad
        - jnp.mean(grad, axis=-1, keepdims=True)
        - normed * jnp.mean(grad * normed, axis=-1, keepdims=True)
    )


def silu_slope(value):
    squashed = jax.nn.sigmoid(value)
    return squashed * (1.0 + value * (1.0 - squashed))


def history_mask(query_pos, key_pos, hist_lengths):
    bounds = jnp.cumsum(hist_lengths)
    after_query = query_pos[:, None] >= bounds[None, :]
    query_hist = jnp.sum(after_query.astype(jnp.int32), axis=1)
    query_start = jnp.sum(jnp.where(after_query, hist_lengths[None, :], 0), axis=1)
    key_hist = jnp.sum((key_pos[:, None] >= bounds[None, :]).astype(jnp.int32), axis=1)
    allowed = (query_hist[:, None] == key_hist[None, :]) & (key_pos[None, :] <= query_pos[:, None])
    count = (query_pos - query_start + 1).astype(jnp.float32)
    return (allowed, count)


def gate_step(attended, gate_units, owned_wide, out_weight, cotangent):
    normed, inv_dev = normalize(attended)
    gated = (normed * gate_units.astype(jnp.float32)).astype(jnp.bfloat16)
    layer_out = (
        jnp.dot(gated, out_weight, preferred_element_type=jnp.float32) + owned_wide
    ).astype(jnp.bfloat16)
    grad_gated = jnp.dot(cotangent, out_weight.T, preferred_element_type=jnp.float32)
    grad_units = grad_gated * normed
    grad_attended = norm_back(grad_gated * gate_units.astype(jnp.float32), normed, inv_dev).astype(
        jnp.bfloat16
    )
    return (gated, layer_out, grad_units, grad_attended)


def on_device(tokens, dest_owner, dest_slot, lengths, proj_weight, out_weight, cotangent):
    rows_dev, width = tokens.shape
    owners = lax.axis_size("dp")
    cycle_size = lax.axis_size("ctx")
    capacity = 2 * rows_dev // owners
    head_dim = width // HEADS
    scale = head_dim ** (-0.5)
    span = rows_dev * cycle_size
    owner_hot = (dest_owner[:, None] == jnp.arange(owners, dtype=jnp.int32)[None, :]).astype(
        jnp.int32
    )
    ranks = jnp.sum((jnp.cumsum(owner_hot, axis=0) - 1) * owner_hot, axis=1)
    send_index = dest_owner * capacity + ranks
    outgoing = (
        jnp.zeros((owners * capacity, width), jnp.bfloat16)
        .at[send_index]
        .set(tokens)
        .reshape(owners, capacity, width)
    )
    slot_table = (
        jnp.full((owners * capacity,), -1, jnp.int32)
        .at[send_index]
        .set(dest_slot)
        .reshape(owners, capacity)
    )
    arrived, arrived_slot = (
        lax.all_to_all(outgoing, "dp", split_axis=0, concat_axis=0, tiled=True),
        lax.all_to_all(slot_table, "dp", split_axis=0, concat_axis=0, tiled=True),
    )
    landing = arrived_slot.reshape(-1)
    landing = jnp.where(landing < 0, rows_dev, landing)
    owned = (
        jnp.zeros((rows_dev + 1, width), jnp.bfloat16)
        .at[landing]
        .set(arrived.reshape(-1, width))[:rows_dev]
    )
    owned_wide = owned.astype(jnp.float32)
    centred, inv_scale = normalize(owned_wide)
    normed_in = centred.astype(jnp.bfloat16)
    preact = jnp.dot(normed_in, proj_weight, preferred_element_type=jnp.float32)
    activated = jax.nn.silu(preact)
    gate_units = activated[:, :width].astype(jnp.bfloat16)
    value_part = activated[:, width : 2 * width].astype(jnp.bfloat16)
    query_part = activated[:, 2 * width : 3 * width].astype(jnp.bfloat16)
    key_part = activated[:, 3 * width :].astype(jnp.bfloat16)
    local_pos = lax.axis_index("ctx") * rows_dev + jnp.arange(rows_dev, dtype=jnp.int32)
    every_pos = jnp.arange(span, dtype=jnp.int32)
    hist_lengths = lengths[0]
    keys_all, values_all = (
        lax.all_gather(key_part, "ctx", axis=0, tiled=True),
        lax.all_gather(value_part, "ctx", axis=0, tiled=True),
    )
    query_heads = query_part.reshape(rows_dev, HEADS, head_dim)
    key_heads = keys_all.reshape(span, HEADS, head_dim)
    value_heads = values_all.reshape(span, HEADS, head_dim)
    allowed, count = history_mask(local_pos, every_pos, hist_lengths)
    scores = (
        jnp.einsum("qhe,khe->hqk", query_heads, key_heads, preferred_element_type=jnp.float32)
        * scale
    )
    weights = jnp.where(allowed[None], jax.nn.silu(scores) / count[None, :, None], 0.0).astype(
        jnp.bfloat16
    )
    attended = jnp.einsum(
        "hqk,khe->qhe", weights, value_heads, preferred_element_type=jnp.float32
    ).reshape(rows_dev, width)
    gated, layer_out, grad_units, grad_attended = gate_step(
        attended, gate_units, owned_wide, out_weight, cotangent
    )
    grad_heads = grad_attended.reshape(rows_dev, HEADS, head_dim)
    grad_weights = jnp.einsum(
        "qhe,khe->hqk", grad_heads, value_heads, preferred_element_type=jnp.float32
    )
    grad_scores = (
        jnp.where(allowed[None], grad_weights * silu_slope(scores) / count[None, :, None], 0.0)
        * scale
    ).astype(jnp.bfloat16)
    grad_queries = jnp.einsum(
        "hqk,khe->qhe", grad_scores, key_heads, preferred_element_type=jnp.float32
    ).reshape(rows_dev, width)
    count_rows = rows_dev * lax.axis_size("ctx")
    value_grad = jnp.einsum("hqk,qhe->khe", weights, grad_heads, preferred_element_type=jnp.float32)
    key_grad = jnp.einsum(
        "hqk,qhe->khe", grad_scores, query_heads, preferred_element_type=jnp.float32
    )
    key_grads = lax.psum_scatter(
        jnp.concatenate(
            [key_grad.reshape(count_rows, width), value_grad.reshape(count_rows, width)], axis=1
        ).astype(jnp.bfloat16),
        "ctx",
        scatter_dimension=0,
        tiled=True,
    ).astype(jnp.float32)
    grad_keys = key_grads[:, :width]
    grad_values = key_grads[:, width:]
    grad_act = jnp.concatenate([grad_units, grad_values, grad_queries, grad_keys], axis=1)
    grad_preact = (grad_act * silu_slope(preact)).astype(jnp.bfloat16)
    grad_in = jnp.dot(grad_preact, proj_weight.T, preferred_element_type=jnp.float32)
    grad_owned = (norm_back(grad_in, centred, inv_scale) + cotangent.astype(jnp.float32)).astype(
        jnp.bfloat16
    )
    whole = jnp.concatenate(
        [
            jnp.dot(normed_in.T, grad_preact, preferred_element_type=jnp.float32),
            jnp.dot(gated.T, cotangent, preferred_element_type=jnp.float32),
        ],
        axis=1,
    )
    group_sum = lax.psum(whole.astype(jnp.bfloat16), "ctx").astype(jnp.float32)
    shard = lax.psum_scatter(group_sum, "dp", scatter_dimension=0, tiled=True)
    grad_proj = shard[:, : 4 * width]
    grad_outw = shard[:, 4 * width :]
    back = jnp.concatenate([grad_owned, jnp.zeros((1, width), jnp.bfloat16)], axis=0)[
        landing
    ].reshape(owners, capacity, width)
    returned = lax.all_to_all(back, "dp", split_axis=0, concat_axis=0, tiled=True)
    grad_tokens = returned.reshape(-1, width)[send_index]
    return (layer_out, grad_tokens, grad_proj, grad_outw)


def solution(mesh):
    placed = (
        P(("dp", "ctx"), None),
        P(("dp", "ctx")),
        P(("dp", "ctx")),
        P("dp", None),
        P(),
        P(),
        P(("dp", "ctx"), None),
    )
    return jax.shard_map(
        on_device,
        mesh=mesh,
        in_specs=placed,
        out_specs=(P(("dp", "ctx"), None), P(("dp", "ctx"), None), P("dp", None), P("dp", None)),
        check_vma=False,
    )
```

profile of v0, /device:TPU:0, one launch (start us, length us, event | category | flops | bytes accessed | tf_op | source)
XLA Modules:
  0.0 347.2 jit_solution(13618901280210965891)
XLA Ops:
  7.2 0.8 fusion.24
  10.3 1.6 scatter_custom_fusion
  12.5 7.3 %all-to-all-start = ((s32[8,1,64]{2,1,0:T(1,128)}), s32[8,1,64]{2,1,0:T(1,128)S(1)}, u32[]{:S(2)}, u32[]{:S(2)}) async-start(s32[8,1,64]{2,1,0:T(1,128)} %all_to_all.12), calls=%async_computation | async-start | bytes 8192 | tf_op jit(solution)/shard_map/all_to_all | solution.py:84
  19.8 2.7 scatter_custom_fusion.1
  22.5 3.7 %all-to-all-done = s32[8,1,64]{2,1,0:T(1,128)S(1)} async-done(((s32[8,1,64]{2,1,0:T(1,128)}), s32[8,1,64]{2,1,0:T(1,128)S(1)}, u32[]{:S(2)}, u32[]{:S(2)}) %all-to-all-start) | async-done | bytes 2080 | tf_op jit(solution)/shard_map/all_to_all | solution.py:84
  26.2 3.5 %all-to-all-start.1 = ((bf16[8,64,512]{2,1,0:T(8,128)(2,1)}), bf16[8,64,512]{2,1,0:T(8,128)(2,1)S(1)}, u32[]{:S(2)}, u32[]{:S(2)}) async-start(bf16[8,64,512]{2,1,0:T(8,128)(2,1)} %bitcast.4), calls=%async_computation.1 | async-start | bytes 1048576 | tf_op jit(solution)/shard_map/all_to_all | solution.py:83
  31.0 11.9 %all-to-all-done.1 = bf16[8,64,512]{2,1,0:T(8,128)(2,1)S(1)} async-done(((bf16[8,64,512]{2,1,0:T(8,128)(2,1)}), bf16[8,64,512]{2,1,0:T(8,128)(2,1)S(1)}, u32[]{:S(2)}, u32[]{:S(2)}) %all-to-all-start.1) | async-done | bytes 524320 | tf_op jit(solution)/shard_map/all_to_all | solution.py:83
  43.0 2.4 scatter_custom_fusion.2
  45.7 2.1 multiply_convert_fusion.1
  47.9 1.0 copy-done.8
  48.9 0.8 fusion.33
  50.2 1.1 fusion.2
  51.3 0.9 copy.34
  52.4 13.3 %all-gather.5.cloned.1.call-done = bf16[1024,512]{1,0:T(8,128)(2,1)} async-done(((bf16[256,512]{1,0:T(8,128)(2,1)}), bf16[1024,512]{1,0:T(8,128)(2,1)}) %all-gather.5.cloned.1.call-update) | async-done | bytes 1048592 | tf_op jit(solution)/shard_map/all_gather | solution.py:106
  65.7 1.5 copy.35
  67.2 7.8 %select_convert_fusion = (bf16[8,256,1024]{2,1,0:T(8,128)(2,1)}, f32[8,256,1024]{2,1,0:T(8,128)}) fusion(f32[256]{0:T(256)S(1)} %add_convert_fusion, pred[256,1024]{1,0:T(8,128)(4,1)} %fusion.2, bf16[256,8,64]{0,2,1:T(8,128)(2,1)} %bitcast.68, bf16[1024,8,64]{0,2,1:T(8,128)(2,1)S(1)} %bitcast.60), kind=kOutput, calls=%fused_computation.6 | convolution fusion | flops 285212672 | bytes 14156800 | tf_op jit(solution)/shard_map/qhe,khe->hqk/dot_general | solution.py:114
  75.0 9.6 %all-gather.3.cloned.1.call-done = bf16[1024,512]{1,0:T(8,128)(2,1)} async-done(((bf16[256,512]{1,0:T(8,128)(2,1)}), bf16[1024,512]{1,0:T(8,128)(2,1)}) %all-gather.3.cloned.1.call-update) | async-done | bytes 1048592 | tf_op jit(solution)/shard_map/all_gather | solution.py:107
  84.6 2.3 copy.33
  86.9 3.9 %fusion.35 = (f32[256]{0:T(256)S(1)}, f32[8,64,256]{2,1,0:T(8,128)S(1)}) fusion(bf16[1024,8,64]{0,2,1:T(8,128)(2,1)} %bitcast.62, bf16[8,256,1024]{2,1,0:T(8,128)(2,1)} %get-tuple-element.20), kind=kOutput, calls=%fused_computation.83 | convolution fusion | flops 268566272 | bytes 5768192 | tf_op jit(solution)/shard_map/hqk,khe->qhe/dot_general | solution.py:120
  91.1 1.7 fusion.20
  92.8 2.2 multiply_convert_fusion.2
  95.0 1.9 copy.37
  96.9 4.1 %convolution_convert_fusion.1 = bf16[8,64,1024]{2,1,0:T(8,128)(2,1)} fusion(bf16[256,8,64]{0,2,1:T(8,128)(2,1)} %bitcast.70, bf16[8,256,1024]{2,1,0:T(8,128)(2,1)} %get-tuple-element.20), kind=kOutput, calls=%fused_computation.15 | convolution fusion | flops 268959744 | bytes 5505024 | tf_op jit(solution)/shard_map/hqk,qhe->khe/dot_general | solution.py:138
  101.0 2.4 copy.39
  103.4 7.2 %multiply_convert_fusion = bf16[8,256,1024]{2,1,0:T(8,128)(2,1)S(1)} fusion(f32[8,256,1024]{2,1,0:T(8,128)} %get-tuple-element.21, f32[256]{0:T(256)S(1)} %add_convert_fusion, pred[256,1024]{1,0:T(8,128)(4,1)} %fusion.2, bf16[256,8,64]{0,2,1:T(8,128)(2,1)} %bitcast.71, bf16[1024,8,64]{0,2,1:T(8,128)(2,1)S(1)} %bitcast.63), kind=kOutput, calls=%fused_computation.5 | convolution fusion | flops 295698432 | bytes 14156800 | tf_op jit(solution)/shard_map/qhe,khe->hqk/dot_general | solution.py:127
  110.6 1.9 copy-done.1
  112.6 1.8 convolution_convert_fusion.2
  114.4 2.4 copy.38
  116.8 3.1 pad_maximum_fusion.1
  120.0 4.4 %fusion.36 = f32[8,64,256]{2,1,0:T(8,128)} fusion(bf16[1024,8,64]{0,2,1:T(8,128)(2,1)S(1)} %bitcast.61, bf16[8,256,1024]{2,1,0:T(8,128)(2,1)} %copy-done.1), kind=kOutput, calls=%fused_computation.84 | convolution fusion | flops 268435456 | bytes 5767168 | tf_op jit(solution)/shard_map/hqk,khe->qhe/dot_general | solution.py:134
  124.4 2.1 copy.40
  126.5 2.2 convolution_convert_fusion.3
  128.7 22.8 %reduce-scatter.3.cloned.1.call-done = bf16[256,1024]{1,0:T(8,128)(2,1)} async-done(((bf16[1024,1024]{1,0:T(8,128)(2,1)}), bf16[256,1024]{1,0:T(8,128)(2,1)}) %reduce-scatter.3.cloned.1.call-update) | async-done | bytes 524304 | tf_op jit(solution)/shard_map/reduce_scatter | solution.py:142
  151.5 1.1 fusion.34
  152.7 2.7 fusion
  155.4 0.9 convolution_convert_fusion
  156.3 1.7 pad_maximum_fusion
  158.3 59.8 %all-reduce.3.cloned.1.call-done = bf16[512,2560]{1,0:T(8,128)(2,1)} async-done(((bf16[512,2560]{1,0:T(8,128)(2,1)}), bf16[512,2560]{1,0:T(8,128)(2,1)}) %all-reduce.3.cloned.1.call-update) | async-done | bytes 2621456 | tf_op jit(solution)/shard_map/psum | solution.py:165
  218.1 4.7 %convert_element_type.80 = f32[512,2560]{1,0:T(8,128)} convert(bf16[512,2560]{1,0:T(8,128)(2,1)} %all-reduce.3.cloned.1.call-done) | non-fusion elementwise | flops 1310720 | bytes 7864320 | tf_op jit(solution)/shard_map/convert_element_type | solution.py:165
  222.9 0.9 fusion.32
  224.1 2.6 gather_fusion
  226.7 5.5 %all-to-all-start.2 = ((bf16[8,64,512]{2,1,0:T(8,128)(2,1)}), bf16[8,64,512]{2,1,0:T(8,128)(2,1)S(1)}, u32[]{:S(2)}, u32[]{:S(2)}) async-start(bf16[8,64,512]{2,1,0:T(8,128)(2,1)} %bitcast.66), calls=%async_computation.3 | async-start | bytes 1048576 | tf_op jit(solution)/shard_map/all_to_all | solution.py:172
  232.3 2.0 fusion.1
  234.3 26.4 %all-to-all-done.2 = bf16[8,64,512]{2,1,0:T(8,128)(2,1)S(1)} async-done(((bf16[8,64,512]{2,1,0:T(8,128)(2,1)}), bf16[8,64,512]{2,1,0:T(8,128)(2,1)S(1)}, u32[]{:S(2)}, u32[]{:S(2)}) %all-to-all-start.2) | async-done | bytes 524320 | tf_op jit(solution)/shard_map/all_to_all | solution.py:172
  260.7 1.9 gather_fusion.1
  262.5 74.7 %reduce-scatter.5.cloned.1.call-done = f32[64,2560]{1,0:T(8,128)} async-done(((f32[512,2560]{1,0:T(8,128)}), f32[64,2560]{1,0:T(8,128)}) %reduce-scatter.5.cloned.1.call-update) | async-done | bytes 655376 | tf_op jit(solution)/shard_map/reduce_scatter | solution.py:166
  337.2 1.9 slice.60
  339.1 1.6 slice.61
  (61 shorter events, 6.3 us)
Async XLA Ops:
  7.2 38.6 %copy-start = (bf16[512,2048]{1,0:T(8,128)(2,1)S(1)}, bf16[512,2048]{1,0:T(8,128)(2,1)}, u32[]{:S(2)}) copy-start(bf16[512,2048]{1,0:T(8,128)(2,1)} %param.11) | copy-start | bytes 6291460
  12.5 13.7 %all-to-all-start = ((s32[8,1,64]{2,1,0:T(1,128)}), s32[8,1,64]{2,1,0:T(1,128)S(1)}, u32[]{:S(2)}, u32[]{:S(2)}) async-start(s32[8,1,64]{2,1,0:T(1,128)} %all_to_all.12), calls=%async_computation | async-start | bytes 8192 | tf_op jit(solution)/shard_map/all_to_all | solution.py:84
  26.2 16.8 %all-to-all-start.1 = ((bf16[8,64,512]{2,1,0:T(8,128)(2,1)}), bf16[8,64,512]{2,1,0:T(8,128)(2,1)S(1)}, u32[]{:S(2)}, u32[]{:S(2)}) async-start(bf16[8,64,512]{2,1,0:T(8,128)(2,1)} %bitcast.4), calls=%async_computation.1 | async-start | bytes 1048576 | tf_op jit(solution)/shard_map/all_to_all | solution.py:83
  29.7 36.0 %all-gather.5.cloned.1.call-start = ((), (), s32[]{:S(2)}) async-start(), calls=%async_computation.6 | async-start | bytes 1310720 | tf_op jit(solution)/shard_map/all_gather | solution.py:106
  45.7 4.1 %copy-start.10 = (s32[1,3]{1,0:T(1,128)S(1)}, s32[1,3]{1,0:T(1,128)}, u32[]{:S(2)}) copy-start(s32[1,3]{1,0:T(1,128)} %param.10) | copy-start | bytes 40
  47.9 1.0 copy-start.8
  49.8 34.8 %all-gather.3.cloned.1.call-start = ((), (), s32[]{:S(2)}) async-start(), calls=%async_computation.5 | async-start | bytes 1310720 | tf_op jit(solution)/shard_map/all_gather | solution.py:107
  52.1 99.4 %reduce-scatter.3.cloned.1.call-start = ((), (), s32[]{:S(2)}) async-start(), calls=%async_computation.7 | async-start | bytes 2621440 | tf_op jit(solution)/shard_map/reduce_scatter | solution.py:142
  67.2 7.8 %copy-start.2 = (bf16[1024,512]{0,1:T(8,128)(2,1)}, bf16[1024,512]{0,1:T(8,128)(2,1)S(1)}, u32[]{:S(2)}) copy-start(bf16[1024,512]{0,1:T(8,128)(2,1)S(1)} %copy.35) | copy-start | bytes 3145732
  95.0 8.4 %copy-start.4 = (bf16[1024,512]{0,1:T(8,128)(2,1)S(1)}, bf16[1024,512]{0,1:T(8,128)(2,1)}, u32[]{:S(2)}) copy-start(bf16[1024,512]{0,1:T(8,128)(2,1)} %copy.33) | copy-start | bytes 3145732
  103.4 9.2 %copy-start.9 = (bf16[256,512]{0,1:T(8,128)(2,1)S(1)}, bf16[256,512]{0,1:T(8,128)(2,1)}, u32[]{:S(2)}) copy-start(bf16[256,512]{0,1:T(8,128)(2,1)} %copy.34) | copy-start | bytes 786436
  110.6 1.9 copy-start.1
  114.4 5.6 %copy-start.3 = (bf16[1024,512]{0,1:T(8,128)(2,1)S(1)}, bf16[1024,512]{0,1:T(8,128)(2,1)}, u32[]{:S(2)}) copy-start(bf16[1024,512]{0,1:T(8,128)(2,1)} %copy-done.2) | copy-start | bytes 3145732
  119.9 98.2 %all-reduce.3.cloned.1.call-start = ((), (), s32[]{:S(2)}) async-start(), calls=%async_computation.8 | async-start | bytes 5242880 | tf_op jit(solution)/shard_map/psum | solution.py:165
  152.7 3.6 %copy-start.7 = (bf16[512,512]{1,0:T(8,128)(2,1)S(1)}, bf16[512,512]{1,0:T(8,128)(2,1)}, u32[]{:S(2)}) copy-start(bf16[512,512]{1,0:T(8,128)(2,1)} %convolution_convert_fusion.3) | copy-start | bytes 1572868
  158.0 179.2 %reduce-scatter.5.cloned.1.call-start = ((), (), s32[]{:S(2)}) async-start(), calls=%async_computation.9 | async-start | bytes 5898240 | tf_op jit(solution)/shard_map/reduce_scatter | solution.py:166
  222.9 1.0 copy-start.6
  223.8 8.5 %copy-start.5 = (bf16[256,512]{1,0:T(8,128)(2,1)S(1)}, bf16[256,512]{1,0:T(8,128)(2,1)}, u32[]{:S(2)}) copy-start(bf16[256,512]{1,0:T(8,128)(2,1)} %get-tuple-element.11) | copy-start | bytes 786436
  226.7 34.0 %all-to-all-start.2 = ((bf16[8,64,512]{2,1,0:T(8,128)(2,1)}), bf16[8,64,512]{2,1,0:T(8,128)(2,1)S(1)}, u32[]{:S(2)}, u32[]{:S(2)}) async-start(bf16[8,64,512]{2,1,0:T(8,128)(2,1)} %bitcast.66), calls=%async_computation.3 | async-start | bytes 1048576 | tf_op jit(solution)/shard_map/all_to_all | solution.py:172
Sparse Core Ops, SparseCore 0:
  49.9 15.7 all-gather.4
  67.8 16.7 all-gather.2
  120.0 31.4 reduce-scatter.2
  158.2 59.8 all-reduce.2
  223.0 114.1 reduce-scatter.4
where the time goes:
time: 348 us; the launch traced here: 347 us
  waiting for transfers between devices  222 us (64%)
  matrix products  39.1 us (11%)
  local copies, waits for them, and re-layouts  34.6 us (10%)
  other arithmetic  20.2 us (6%)
  starting transfers between devices  16.9 us (5%)
  between operations  14.1 us (4%)
    reduce_scatter x1, waiting for transfers between devices, on_device(): shard = lax.psum_scatter(group_sum, 'dp', scatter_dimension=0, tiled=True)  74.7 us
    psum x1, waiting for transfers between devices, on_device(): group_sum = lax.psum(whole.astype(jnp.bfloat16), 'ctx').astype(jnp.float32)  59.8 us
    all_to_all x1, waiting for transfers between devices, on_device(): lax.all_to_all(back, 'dp', split_axis=0, concat_axis=0, tiled=True)  26.4 us
    reduce_scatter x1, waiting for transfers between devices, on_device(): lax.psum_scatter(jnp.concatenate([key_grad.reshape(count_rows, width), va...  22.8 us
    all_gather x1, waiting for transfers between devices, on_device(): lax.all_gather(key_part, 'ctx', axis=0, tiled=True)  13.3 us
    all_to_all x1, waiting for transfers between devices, on_device(): lax.all_to_all(outgoing, 'dp', split_axis=0, concat_axis=0, tiled=True)  11.9 us
    all_gather x1, waiting for transfers between devices, on_device(): lax.all_gather(value_part, 'ctx', axis=0, tiled=True)  9.61 us
    dot_general x1, matrix products, on_device(): jnp.einsum('qhe,khe->hqk', query_heads, key_heads, preferred_element_type...  7.78 us
  transfers between devices with their start and end apart: 8, of which 8 were waited for; matrix products, arithmetic and copies ran while one was open for 9% of the time, Pallas kernels for 0%

commit v1 on v0

v1 whole, which is shorter than its diff:
```python
import functools

import jax
import jax.numpy as jnp
from jax import lax
from jax.experimental import pallas as pl
from jax.experimental.pallas import tpu as pltpu
from jax.sharding import PartitionSpec as P

HEADS = 8
EPSILON = 1e-05
LANES = 128
F32 = jnp.float32
BF16 = jnp.bfloat16

WHOLE = pl.BlockSpec(memory_space=pltpu.VMEM)
SCALARS = pl.BlockSpec(memory_space=pltpu.SMEM)


def call(body, name, outs, scalars, arrays, scratch=(), flops=10**8, vmem=24):
    return pl.pallas_call(
        body,
        name=name,
        out_shape=[jax.ShapeDtypeStruct(s, d) for s, d in outs],
        in_specs=[SCALARS] * len(scalars) + [WHOLE] * len(arrays),
        out_specs=[WHOLE] * len(outs),
        scratch_shapes=list(scratch),
        compiler_params=pltpu.CompilerParams(vmem_limit_bytes=vmem * 2**20),
        cost_estimate=pl.CostEstimate(flops=flops, bytes_accessed=2**20, transcendentals=0),
    )(*scalars, *arrays)


def iota(shape, dim):
    return lax.broadcasted_iota(jnp.int32, shape, dim)


def mm(a, b):
    return jnp.dot(a, b, preferred_element_type=F32)


def mm_t(a, b):
    return lax.dot_general(a, b, (((1,), (1,)), ((), ())), preferred_element_type=F32)


def t_mm(a, b):
    return lax.dot_general(a, b, (((0,), (0,)), ((), ())), preferred_element_type=F32)


def hot(condition):
    return jnp.where(condition, 1.0, 0.0).astype(BF16)


def normalize(value):
    middle = jnp.mean(value, axis=-1, keepdims=True)
    centred = value - middle
    inv_dev = lax.rsqrt(jnp.mean(centred * centred, axis=-1, keepdims=True) + EPSILON)
    return centred * inv_dev, inv_dev


def norm_back(grad, normed, inv_dev):
    return inv_dev * (
        grad
        - jnp.mean(grad, axis=-1, keepdims=True)
        - normed * jnp.mean(grad * normed, axis=-1, keepdims=True)
    )


def silu_both(value):
    squashed = 0.5 * jnp.tanh(0.5 * value) + 0.5
    return value * squashed, squashed * (1.0 + value * (1.0 - squashed))


def rank_rows(owner):
    rows = owner.shape[1]
    down, across = iota((rows, rows), 0), iota((rows, rows), 1)
    spread = jnp.broadcast_to(owner, (rows, rows))
    owner_col = jnp.sum(jnp.where(down == across, spread, 0).astype(F32), axis=1, keepdims=True)
    same = owner_col.astype(jnp.int32) == spread
    rank_row = jnp.sum(jnp.where(same & (down < across), 1.0, 0.0), axis=0, keepdims=True)
    rank_col = jnp.sum(jnp.where(same & (across < down), 1.0, 0.0), axis=1, keepdims=True)
    return rank_row.astype(jnp.int32), rank_col.astype(jnp.int32)


def pack_body(capacity, stride, owner_ref, slot_ref, tokens_ref, out_ref):
    owner = owner_ref[...]
    rows = owner.shape[1]
    rank_row, rank_col = rank_rows(owner)
    total, width = out_ref.shape
    place = iota((total, rows), 0)
    chosen = hot(place == owner * stride + rank_row)
    slots = jnp.where(place == owner * stride + capacity, slot_ref[...] + 1, 0)
    by_rank = hot(rank_col == iota((rows, width), 1))
    out_ref[...] = (mm(chosen, tokens_ref[...]) + mm(slots.astype(F32).astype(BF16), by_rank)).astype(
        BF16
    )


def block_rem(owners, stride):
    col, first = iota((owners, owners * stride), 1), iota((owners, owners * stride), 0)
    above = jnp.sum(jnp.where(col >= stride * (first + 1), 1.0, 0.0), axis=0, keepdims=True)
    rem = iota((1, owners * stride), 1) - stride * above.astype(jnp.int32)
    inside = (col >= stride * first) & (col < stride * (first + 1))
    return rem, inside


def landing_row(table, owners, capacity, stride):
    rem, inside = block_rem(owners, stride)
    lanes = iota((table.shape[1], owners * stride), 0)
    spread = mm(table, hot((lanes == rem) & (lanes < capacity)))
    return jnp.sum(jnp.where(inside, spread, 0.0), axis=0, keepdims=True)


def place_body(owners, capacity, stride, arrived_ref, owned_ref, normed_ref, landing_ref):
    rows = owned_ref.shape[0]
    arrived = arrived_ref[...]
    total = arrived.shape[0]
    pick = hot(iota((owners, total), 1) == iota((owners, total), 0) * stride + capacity)
    table = mm(pick, arrived).astype(BF16)
    landing = landing_row(table, owners, capacity, stride).astype(jnp.int32)
    owned = mm(hot(iota((rows, total), 0) + 1 == landing), arrived)
    owned_ref[...] = owned.astype(BF16)
    normed_ref[...] = normalize(owned)[0].astype(BF16)
    landing_ref[...] = landing_row(table, owners, capacity, capacity).astype(jnp.int32)


def own_body(normed_ref, proj_ref, outw_ref, cot_ref, gate_ref, slope_ref, query_ref, kv_ref, grad_ref):
    width = normed_ref.shape[1]
    preact = mm(normed_ref[...], proj_ref[...])
    gate, slope = silu_both(preact[:, :width])
    gate_ref[...] = gate.astype(BF16)
    slope_ref[...] = slope
    kv_ref[:, :width] = silu_both(preact[:, width : 2 * width])[0].astype(BF16)
    query_ref[...] = silu_both(preact[:, 2 * width : 3 * width])[0].astype(BF16)
    kv_ref[:, width:] = silu_both(preact[:, 3 * width :])[0].astype(BF16)
    grad_ref[...] = mm_t(cot_ref[...], outw_ref[...])


def history_start(pos, lengths_ref):
    first = lengths_ref[0, 0]
    second = lengths_ref[0, 1]
    return jnp.where(pos >= first + second, first + second, jnp.where(pos >= first, first, 0))


def attend(query_ref, key, value, shared, acc_ref):
    width = query_ref.shape[1]
    left = iota((1, LANES), 1) < LANES // 2
    for pair in range(width // LANES):
        cols = slice(pair * LANES, (pair + 1) * LANES)
        query, key_pair, value_pair = query_ref[:, cols], key[:, cols], value[:, cols]
        total = acc_ref[:, cols]
        for mine in (left, ~left):
            half = mm_t(jnp.where(mine, query, 0).astype(BF16), key_pair) * 0.0625
            weights = (half * (1.0 + jnp.tanh(half)) * shared).astype(BF16)
            total += mm(weights, jnp.where(mine, value_pair, 0).astype(BF16))
        acc_ref[:, cols] = total


def forward_body(
    me_ref, lengths_ref, near_ref, far_ref, cross_ref, proj_ref, outw_ref, cot_ref, owned_ref,
    gate_ref, slope_ref, query_ref, kv_ref, grad_ref,
    out_ref, gated_ref, gate_grad_ref, *rest,
):
    grads, acc_ref = rest[:-1], rest[-1]
    rows, width = query_ref.shape
    me = me_ref[0]
    acc_ref[...] = jnp.zeros_like(acc_ref)
    query_pos = me * rows + iota((rows, 1), 0)
    start = history_start(query_pos, lengths_ref)
    inverse = 1.0 / (query_pos - start + 1).astype(F32)

    def shared_for(block):
        key_pos = block * rows + iota((1, rows), 1)
        return jnp.where((key_pos >= start) & (key_pos <= query_pos), inverse, 0.0)

    attend(query_ref, kv_ref[:, width:], kv_ref[:, :width], shared_for(me), acc_ref)
    for step, other_ref in ((1, near_ref), (2, far_ref), (3, cross_ref)):
        block = me ^ step
        reach = history_start(me * rows, lengths_ref)

        @pl.when((block < me) & ((block + 1) * rows > reach))
        def _():
            normed = other_ref[...]
            value = silu_both(mm(normed, proj_ref[:, width : 2 * width]))[0].astype(BF16)
            key = silu_both(mm(normed, proj_ref[:, 3 * width :]))[0].astype(BF16)
            attend(query_ref, key, value, shared_for(block), acc_ref)

    gate = gate_ref[...].astype(F32)
    normed, inv_dev = normalize(acc_ref[...])
    gated = (normed * gate).astype(BF16)
    gated_ref[...] = gated
    grad_gated = grad_ref[...]
    grad_attended = norm_back(grad_gated * gate, normed, inv_dev).astype(BF16)
    acc_ref[...] = grad_attended.astype(F32)
    piece = width // len(grads)
    for step, ref in enumerate(grads):
        ref[...] = acc_ref[:, pl.ds(pl.multiple_of((me ^ step) * piece, LANES), piece)].astype(BF16)
    out_ref[...] = (mm(gated, outw_ref[...]) + owned_ref[...].astype(F32)).astype(BF16)
    gate_grad_ref[...] = (grad_gated * normed * slope_ref[...]).astype(BF16)


def side_body(me_ref, gated_ref, cot_ref, gate_grad_ref, proj_ref, *rest):
    pieces, gate_in_ref, scratch_ref, narrow_ref = rest[:-3], rest[-3], rest[-2], rest[-1]
    rows, width = gated_ref.shape
    me = me_ref[0]
    piece = width // len(pieces)
    scratch_ref[...] = t_mm(gated_ref[...], cot_ref[...])
    narrow_ref[...] = gate_grad_ref[...].astype(F32)
    for step, ref in enumerate(pieces):
        cols = pl.ds(pl.multiple_of((me ^ step) * piece, LANES), piece)
        ref[:rows, :] = narrow_ref[:, cols].astype(BF16)
        ref[rows:, :] = scratch_ref[:, cols].astype(BF16)
    gate_in_ref[...] = mm_t(gate_grad_ref[...], proj_ref[:, :width])


def heads_body(me_ref, n0_ref, n1_ref, n2_ref, n3_ref, proj_ref, part_ref, slope_ref):
    rows, width = n0_ref.shape
    me = me_ref[0]
    piece = width // 4
    cols = [proj_ref[:, pl.ds(pl.multiple_of(b * width + me * piece, LANES), piece)] for b in (1, 2, 3)]
    weight = jnp.concatenate(cols, axis=1)
    for step, ref in enumerate((n0_ref, n1_ref, n2_ref, n3_ref)):
        act, slope = silu_both(mm(ref[...], weight))
        at = pl.ds(pl.multiple_of((me ^ step) * rows, rows), rows)
        part_ref[at, :] = act.astype(BF16)
        slope_ref[at, :] = slope


def backward_body(
    me_ref, lengths_ref, g0_ref, g1_ref, g2_ref, g3_ref, part_ref, slope_ref, *rest
):
    outs, grad_ref, total_ref = rest[:4], rest[4], rest[5]
    rows, piece = g0_ref.shape
    me = me_ref[0]
    for step, ref in enumerate((g0_ref, g1_ref, g2_ref, g3_ref)):
        grad_ref[pl.ds(pl.multiple_of((me ^ step) * rows, rows), rows), :] = ref[...]
    total_ref[...] = jnp.zeros_like(total_ref)
    left = iota((1, LANES), 1) < LANES // 2
    blocks = len(outs)

    def visit(q_block, k_block):
        q_at, k_at = slice(q_block * rows, (q_block + 1) * rows), slice(k_block * rows, (k_block + 1) * rows)
        query_pos = q_block * rows + iota((1, rows), 1)
        start = history_start(query_pos, lengths_ref)
        key_pos = k_block * rows + iota((rows, 1), 0)
        inverse = 1.0 / (query_pos - start + 1).astype(F32)
        shared = jnp.where((key_pos >= start) & (key_pos <= query_pos), inverse, 0.0)
        value = part_ref[k_at, :piece]
        query = part_ref[q_at, piece : 2 * piece]
        key = part_ref[k_at, 2 * piece :]
        grad = grad_ref[q_at, :]
        small = value * jnp.asarray(0.0625, BF16)
        d_value, d_query, d_key = 0.0, 0.0, 0.0
        for mine in (left, ~left):
            query_h = jnp.where(mine, query, 0).astype(BF16)
            key_h = jnp.where(mine, key, 0).astype(BF16)
            grad_h = jnp.where(mine, grad, 0).astype(BF16)
            half = mm_t(key_h, query) * 0.0625
            up = 1.0 + jnp.tanh(half)
            act = half * up
            weights = (act * shared).astype(BF16)
            slope = (up + act * (2.0 - up)) * shared
            d_scores = (mm_t(small, grad_h) * slope).astype(BF16)
            d_value += mm(weights, grad_h)
            d_key += mm(d_scores, query_h)
            d_query += t_mm(d_scores, key_h)
        total_ref[k_at, :piece] += d_value
        total_ref[q_at, piece : 2 * piece] += d_query
        total_ref[k_at, 2 * piece :] += d_key

    for q_block in range(blocks):
        visit(q_block, q_block)
        for k_block in range(q_block):
            reach = history_start(q_block * rows, lengths_ref)

            @pl.when((k_block + 1) * rows > reach)
            def _():
                visit(q_block, k_block)

    for step, ref in enumerate(outs):
        at = pl.ds(pl.multiple_of((me ^ step) * rows, rows), rows)
        ref[...] = (total_ref[at, :] * slope_ref[at, :]).astype(BF16)


def weight_body(*refs):
    normed, grads, sides, out_ref = refs[:4], refs[4:8], refs[8:12], refs[12]
    rows, piece = normed[0].shape[0], sides[0].shape[1]
    qkv, gate, outw = 0.0, 0.0, 0.0
    for n_ref, g_ref, s_ref in zip(normed, grads, sides):
        qkv += t_mm(n_ref[...], g_ref[...])
        gate += t_mm(n_ref[...], s_ref[:rows, :])
        outw += s_ref[rows:, :].astype(F32)
    out_ref[:, :piece] = gate.astype(BF16)
    out_ref[:, piece : 4 * piece] = qkv.astype(BF16)
    out_ref[:, 4 * piece :] = outw.astype(BF16)


def input_body(
    me_ref, g0_ref, g1_ref, g2_ref, g3_ref, gate_in_ref, owned_ref, cot_ref, landing_ref, proj_ref, out_ref
):
    rows, width = owned_ref.shape
    me = me_ref[0]
    piece = width // 4
    total = gate_in_ref[...]
    for step, ref in enumerate((g0_ref, g1_ref, g2_ref, g3_ref)):
        cols = [
            proj_ref[:, pl.ds(pl.multiple_of(b * width + (me ^ step) * piece, LANES), piece)] for b in (1, 2, 3)
        ]
        total += mm_t(ref[...], jnp.concatenate(cols, axis=1))
    centred, inv_scale = normalize(owned_ref[...].astype(F32))
    grad = (norm_back(total, centred, inv_scale) + cot_ref[...].astype(F32)).astype(BF16)
    select = hot(iota((rows, out_ref.shape[0]), 0) + 1 == landing_ref[...])
    out_ref[...] = t_mm(select, grad).astype(BF16)


def return_body(capacity, owner_ref, back_ref, out_ref):
    owner = owner_ref[...]
    rank_row, _ = rank_rows(owner)
    total = back_ref.shape[0]
    chosen = hot(iota((total, owner.shape[1]), 0) == owner * capacity + rank_row)
    out_ref[...] = t_mm(chosen, back_ref[...]).astype(BF16)


def sum_body(parts_ref, out_ref):
    total = parts_ref[0].astype(F32)
    for i in range(1, parts_ref.shape[0]):
        total += parts_ref[i].astype(F32)
    out_ref[...] = total.astype(BF16)


def finish_body(me_ref, w0_ref, w1_ref, w2_ref, w3_ref, proj_ref, outw_ref):
    me = me_ref[0]
    width = outw_ref.shape[1]
    piece = width // 4
    for step, ref in enumerate((w0_ref, w1_ref, w2_ref, w3_ref)):
        for b in range(4):
            at = pl.ds(pl.multiple_of(b * width + (me ^ step) * piece, LANES), piece)
            proj_ref[:, at] = ref[:, b * piece : (b + 1) * piece].astype(F32)
        at = pl.ds(pl.multiple_of((me ^ step) * piece, LANES), piece)
        outw_ref[:, at] = ref[:, 4 * piece :].astype(F32)


def on_device(tokens, dest_owner, dest_slot, lengths, proj_weight, out_weight, cotangent):
    rows, width = tokens.shape
    owners = lax.axis_size("dp")
    cycle = lax.axis_size("ctx")
    assert cycle == 4 and width == cycle * LANES
    capacity = 2 * rows // owners
    stride = capacity + 8
    piece = width // cycle
    me = lax.axis_index("ctx").astype(jnp.int32).reshape(1)
    owner_row = dest_owner.reshape(1, rows)
    slot_row = dest_slot.reshape(1, rows)
    square = ((rows, width), BF16)

    def hop(value, step):
        return lax.ppermute(value, "ctx", [(i, i ^ step) for i in range(cycle)])

    def gather(value):
        near, far = hop(value, 1), hop(value, 2)
        return near, far, hop(far, 1)

    def exchange(values):
        return [values[0]] + [hop(values[step], step) for step in (2, 3, 1)]

    def swap(value):
        return lax.all_to_all(value, "dp", split_axis=0, concat_axis=0, tiled=True)

    (outgoing,) = call(
        functools.partial(pack_body, capacity, stride),
        "pack", [((owners * stride, width), BF16)], [], [owner_row, slot_row, tokens],
    )
    arrived = swap(outgoing.reshape(owners, stride, width)).reshape(owners * stride, width)
    owned, normed, landing = call(
        functools.partial(place_body, owners, capacity, stride),
        "place", [square, square, ((1, owners * capacity), jnp.int32)], [], [arrived],
    )
    near, far, cross = gather(normed)
    gate, slope, query, keys_values, grad_gated = call(
        own_body, "own_rows",
        [square, ((rows, width), F32), square, ((rows, 2 * width), BF16), ((rows, width), F32)],
        [], [normed, proj_weight, out_weight, cotangent], flops=10**9,
    )
    layer_out, gated, gate_grad, *grad_pieces = call(
        forward_body, "forward",
        [square, square, square] + [((rows, piece), BF16)] * cycle,
        [me, lengths],
        [near, far, cross, proj_weight, out_weight, cotangent, owned, gate, slope, query, keys_values, grad_gated],
        scratch=[pltpu.VMEM((rows, width), F32)], flops=4 * 10**9, vmem=32,
    )
    r0, r2, r3, r1 = exchange(grad_pieces)
    *sides, gate_in = call(
        side_body, "side", [((rows + width, piece), BF16)] * cycle + [((rows, width), F32)],
        [me], [gated, cotangent, gate_grad, proj_weight],
        scratch=[pltpu.VMEM((width, width), F32), pltpu.VMEM((rows, width), F32)], flops=10**9,
    )
    parts, slopes = call(
        heads_body, "heads",
        [((rows * cycle, 3 * piece), BF16), ((rows * cycle, 3 * piece), F32)],
        [me], [normed, near, far, cross, proj_weight], flops=10**9,
    )
    s0, s2, s3, s1 = exchange(sides)
    grads = call(
        backward_body, "backward", [((rows, 3 * piece), BF16)] * cycle,
        [me, lengths], [r0, r1, r2, r3, parts, slopes],
        scratch=[pltpu.VMEM((rows * cycle, piece), BF16), pltpu.VMEM((rows * cycle, 3 * piece), F32)],
        flops=4 * 10**9, vmem=32,
    )
    p0, p2, p3, p1 = exchange(grads)
    (weight_part,) = call(
        weight_body, "weights", [((width, 5 * piece), BF16)], [],
        [normed, near, far, cross, *grads, s0, s1, s2, s3], flops=10**9,
    )
    share = width // owners
    summed_parts = swap(weight_part.reshape(owners, share, 5 * piece))
    (back,) = call(
        input_body, "input_grad", [((owners * capacity, width), BF16)], [me],
        [p0, p1, p2, p3, gate_in, owned, cotangent, landing, proj_weight], flops=10**9,
    )
    returned = swap(back.reshape(owners, capacity, width)).reshape(owners * capacity, width)
    (mine,) = call(sum_body, "sum", [((share, 5 * piece), BF16)], [], [summed_parts])
    w1, w2, w3 = gather(mine)
    (grad_tokens,) = call(
        functools.partial(return_body, capacity), "give_back", [square], [], [owner_row, returned]
    )
    grad_proj, grad_outw = call(
        finish_body, "finish", [((share, 4 * width), F32), ((share, width), F32)],
        [me], [mine, w1, w2, w3],
    )
    return layer_out, grad_tokens, grad_proj, grad_outw


def solution(mesh):
    placed = (
        P(("dp", "ctx"), None),
        P(("dp", "ctx")),
        P(("dp", "ctx")),
        P("dp", None),
        P(),
        P(),
        P(("dp", "ctx"), None),
    )
    return jax.shard_map(
        on_device,
        mesh=mesh,
        in_specs=placed,
        out_specs=(P(("dp", "ctx"), None), P(("dp", "ctx"), None), P("dp", None), P("dp", None)),
        check_vma=False,
    )
```

time: 348 us -> 106 us (0.30)
  waiting for transfers between devices: 222 us -> 32.7 us
  matrix products: 39.1 us -> 0 us
  local copies, waits for them, and re-layouts: 34.6 us -> 6.1 us
  blocking collectives: 0 us -> 23.6 us
  Pallas kernels: 0 us -> 20.9 us
  other arithmetic: 20.2 us -> 0 us
  between operations: 14.1 us -> 0.86 us
  starting transfers between devices: 16.9 us -> 21.2 us
    reduce_scatter x2 -> x0, waiting for transfers between devices: 97.5 us -> none  [the longest x1 74.7 us: on_device(): shard = lax.psum_scatter(group_sum, 'dp', scatter_dimension=0, tiled=True)]
    psum x1 -> x0, waiting for transfers between devices: 59.8 us -> none  [on_device(): group_sum = lax.psum(whole.astype(jnp.bfloat16), 'ctx').astype(jnp.float32)]
    dot_general x12 -> x0, matrix products: 39.1 us -> none  [the longest x1 7.78 us: on_device(): jnp.einsum('qhe,khe->hqk', query_heads, key_heads, preferred_element_type...]
    all_to_all x3 -> x2, waiting for transfers between devices: 42 us -> 12.8 us  [swap(): return lax.all_to_all(value, 'dp', split_axis=0, concat_axis=0, tiled=True)]
    all_to_all x0 -> x1, blocking collectives: none -> 23.6 us  [swap(): return lax.all_to_all(value, 'dp', split_axis=0, concat_axis=0, tiled=True)]
    all_gather x2 -> x0, waiting for transfers between devices: 22.9 us -> none  [the longest x1 13.3 us: on_device(): lax.all_gather(key_part, 'ctx', axis=0, tiled=True)]
    pallas_call x0 -> x12, Pallas kernels: none -> 20.9 us  [call(): pl.pallas_call(body, name=name, out_shape=[jax.ShapeDtypeStruct(s, d) for...]
    ppermute x0 -> x15, waiting for transfers between devices: none -> 19.9 us  [hop(): return lax.ppermute(value, 'ctx', [(i, i ^ step) for i in range(cycle)])]
  transfers between devices with their start and end apart: 8 -> 17, of which waited for: 8 -> 7; matrix products, arithmetic and copies ran while one was open for 9% -> 0% of each run, Pallas kernels for 0% -> 12%
where the time goes in v1:
time: 106 us; the launch traced here: 105 us
  waiting for transfers between devices  32.7 us (31%)
  blocking collectives  23.6 us (22%)
  starting transfers between devices  21.2 us (20%)
  Pallas kernels  20.9 us (20%)
  local copies, waits for them, and re-layouts  6.1 us (6%)
    all_to_all x1, blocking collectives, swap(): return lax.all_to_all(value, 'dp', split_axis=0, concat_axis=0, tiled=True)  23.6 us
    pallas_call x12, Pallas kernels, call(): pl.pallas_call(body, name=name, out_shape=[jax.ShapeDtypeStruct(s, d) for...  20.9 us
    ppermute x15, waiting for transfers between devices, hop(): return lax.ppermute(value, 'ctx', [(i, i ^ step) for i in range(cycle)])  19.9 us
    all_to_all x2, waiting for transfers between devices, swap(): return lax.all_to_all(value, 'dp', split_axis=0, concat_axis=0, tiled=True)  12.8 us
    ppermute x15, starting transfers between devices, hop(): return lax.ppermute(value, 'ctx', [(i, i ^ step) for i in range(cycle)])  12.3 us
    all_to_all x2, starting transfers between devices, swap(): return lax.all_to_all(value, 'dp', split_axis=0, concat_axis=0, tiled=True)  8.92 us
    unnamed x36, local copies, waits for them, and re-layouts  6.1 us
  transfers between devices with their start and end apart: 17, of which 7 were waited for; matrix products, arithmetic and copies ran while one was open for 0% of the time, Pallas kernels for 12%

profile of v1, /device:TPU:0, one launch (start us, length us, event | category | flops | bytes accessed | tf_op | source)
XLA Modules:
  0.0 105.4 jit_solution(2264252198423162588)
XLA Ops:
  0.7 1.1 %copy-done.4 = bf16[256,512]{1,0:T(8,128)(2,1)S(1)} copy-done((bf16[256,512]{1,0:T(8,128)(2,1)S(1)}, bf16[256,512]{1,0:T(8,128)(2,1)}, u32[]{:S(2)}) %copy-start.4) | copy-done | bytes 262168
  1.8 0.7 copy-done.7
  2.4 0.7 copy-done.9
  3.1 0.6 pack.1
  3.8 23.6 %all_to_all.15 = bf16[8,72,512]{2,1,0:T(8,128)(2,1)S(1)} all-to-all(bf16[8,72,512]{2,1,0:T(8,128)(2,1)S(1)} %bitcast.9), channel_id=1, replica_groups=mesh['dp'=8,'ctx'=4] {'dp'}, dimensions={0} | all-to-all | bytes 1179648 | tf_op jit(solution)/shard_map/all_to_all | solution.py:366
  27.4 0.8 place.1
  28.3 0.0 copy-start.2
  28.3 1.6 %collective-permute-start.1 = (bf16[256,512]{1,0:T(8,128)(2,1)S(1)}, bf16[256,512]{1,0:T(8,128)(2,1)S(1)}, u32[]{:S(2)}, u32[]{:S(2)}) collective-permute-start(bf16[256,512]{1,0:T(8,128)(2,1)S(1)} %get-tuple-element.32.normed_ref.n0_ref.refs_0_), channel_id=1, source_target_pairs={{0,2},{1,3},{2,0},{3,1},{4,6},{5,7},{6,4},{7,5},{8,10},{9,11},{10,... | collective-permute-start | bytes 786440 | tf_op jit(solution)/shard_map/ppermute | solution.py:356
  29.8 0.0 collective-permute-start
  29.8 5.4 %collective-permute-done.1.far_ref.n2_ref.refs_2_ = bf16[256,512]{1,0:T(8,128)(2,1)S(1)} collective-permute-done((bf16[256,512]{1,0:T(8,128)(2,1)S(1)}, bf16[256,512]{1,0:T(8,128)(2,1)S(1)}, u32[]{:S(2)}, u32[]{:S(2)}) %collective-permute-start.1) | collective-permute-done | bytes 262176 | tf_op jit(solution)/shard_map/ppermute | solution.py:356
  35.2 0.0 collective-permute-start.2
  35.2 0.0 copy-start.10
  35.3 1.0 copy-done.10
  36.3 1.0 own_rows.1
  37.3 0.0 collective-permute-done.near_ref.n1_ref.refs_1_
  37.3 0.0 copy-start.12
  37.3 0.0 copy-done.11
  37.3 3.4 %forward.1 = (bf16[256,512]{1,0:T(8,128)(2,1)}, bf16[256,512]{1,0:T(8,128)(2,1)S(1)}, bf16[256,512]{1,0:T(8,128)(2,1)S(1)}, bf16[256,128]{1,0:T(8,128)(2,1)S(1)}...) custom-call(s32[1]{0:T(128)} %bitcast.me_ref, s32[1,3]{1,0:T(1,128)S(1)} %copy-done.17, ...), custom_call_target="tpu_custom_call" | custom-call | flops 4000000000 | bytes 1048576 | tf_op jit(solution)/shard_map/forward/pallas_call | solution.py:21
  40.7 0.6 collective-permute-start.3
  41.3 4.1 %collective-permute-start.4 = (bf16[256,128]{1,0:T(8,128)(2,1)S(1)}, bf16[256,128]{1,0:T(8,128)(2,1)S(1)}, u32[]{:S(2)}, u32[]{:S(2)}) collective-permute-start(bf16[256,128]{1,0:T(8,128)(2,1)S(1)} %get-tuple-element.42), channel_id=1, source_target_pairs={{0,2},{1,3},{2,0},{3,1},{4,6},{5,7},{6,4},{7,5},{8,10},{9,11},{10,... | collective-permute-start | bytes 196616 | tf_op jit(solution)/shard_map/ppermute | solution.py:356
  45.4 0.0 collective-permute-start.5
  45.4 0.6 side.1
  45.9 0.2 collective-permute-start.9
  46.1 2.0 %collective-permute-start.10 = (bf16[768,128]{1,0:T(8,128)(2,1)S(1)}, bf16[768,128]{1,0:T(8,128)(2,1)S(1)}, u32[]{:S(2)}, u32[]{:S(2)}) collective-permute-start(bf16[768,128]{1,0:T(8,128)(2,1)S(1)} %get-tuple-element.56), channel_id=1, source_target_pairs={{0,2},{1,3},{2,0},{3,1},{4,6},{5,7},{6,4},{7,5},{8,10},{9,11},{10,... | collective-permute-start | bytes 589832 | tf_op jit(solution)/shard_map/ppermute | solution.py:356
  48.1 1.8 %heads.1 = (bf16[1024,384]{1,0:T(8,128)(2,1)S(1)}, f32[1024,384]{1,0:T(8,128)S(1)}) custom-call(s32[1]{0:T(128)} %bitcast.me_ref, bf16[256,512]{1,0:T(8,128)(2,1)S(1)} %get-tuple-element.32.normed_ref.n0_ref.refs_0_, bf16[256,512]{1,0:T(8,128)(2,1)S(1)} %copy-done.13, bf16[256,512]{1,0:T(8,128)(2,1)S(1)} %collective-permute-done.1.far_ref.n2_ref.refs_2_, ...), custom_call_target="tpu_custom_call" | custom-call | flops 1000000000 | bytes 1048576 | tf_op jit(solution)/shard_map/heads/pallas_call | solution.py:21
  49.9 0.0 collective-permute-done.3.g1_ref
  49.9 0.1 collective-permute-start.11
  50.0 5.7 %backward.1 = (bf16[256,384]{1,0:T(8,128)(2,1)S(1)}, bf16[256,384]{1,0:T(8,128)(2,1)S(1)}, bf16[256,384]{1,0:T(8,128)(2,1)S(1)}, bf16[256,384]{1,0:T(8,128)(2,1)S(1)}) custom-call(s32[1]{0:T(128)} %bitcast.me_ref, s32[1,3]{1,0:T(1,128)S(1)} %copy-done.17, bf16[256,128]{1,0:T(8,128)(2,1)S(1)} %get-tuple-element.40.g0_ref, ...), custom_call_target="tpu_custom_call" | custom-call | flops 4000000000 | bytes 1048576 | tf_op jit(solution)/shard_map/backward/pallas_call | solution.py:21
  55.8 2.4 %collective-permute-done.11.refs_11_ = bf16[768,128]{1,0:T(8,128)(2,1)S(1)} collective-permute-done((bf16[768,128]{1,0:T(8,128)(2,1)S(1)}, bf16[768,128]{1,0:T(8,128)(2,1)S(1)}, u32[]{:S(2)}, u32[]{:S(2)}) %collective-permute-start.11) | collective-permute-done | bytes 196640 | tf_op jit(solution)/shard_map/ppermute | solution.py:356
  58.2 2.8 %weights.1 = bf16[512,640]{1,0:T(8,128)(2,1)} custom-call(bf16[256,512]{1,0:T(8,128)(2,1)S(1)} %get-tuple-element.32.normed_ref.n0_ref.refs_0_, bf16[256,512]{1,0:T(8,128)(2,1)S(1)} %copy-done.13, bf16[256,512]{1,0:T(8,128)(2,1)S(1)} %collective-permute-done.1.far_ref.n2_ref.refs_2_, bf16[256,512]{1,0:T(8,128)(2,1)} %collective-permute-done.2.cross_ref.n3_ref.refs_3_, ...), custom_call_target="tpu_custom_call" | custom-call | flops 1000000000 | bytes 1048576 | tf_op jit(solution)/shard_map/weights/pallas_call | solution.py:21
  61.0 0.0 copy-start.5
  61.0 0.7 copy-done.5
  61.7 5.2 %all-to-all-start.2 = ((bf16[8,64,640]{2,1,0:T(8,128)(2,1)}), bf16[8,64,640]{2,1,0:T(8,128)(2,1)S(1)}, u32[]{:S(2)}, u32[]{:S(2)}) async-start(bf16[8,64,640]{2,1,0:T(8,128)(2,1)} %bitcast.7), calls=%async_computation.2 | async-start | bytes 1310720 | tf_op jit(solution)/shard_map/all_to_all | solution.py:366
  66.9 1.7 %collective-permute-start.7 = (bf16[256,384]{1,0:T(8,128)(2,1)}, bf16[256,384]{1,0:T(8,128)(2,1)S(1)}, u32[]{:S(2)}, u32[]{:S(2)}) collective-permute-start(bf16[256,384]{1,0:T(8,128)(2,1)} %copy-done.15), channel_id=1, source_target_pairs={{0,2},{1,3},{2,0},{3,1},{4,6},{5,7},{6,4},{7,5},{8,10},{9,11},{10,... | collective-permute-start | bytes 589832 | tf_op jit(solution)/shard_map/ppermute | solution.py:356
  68.6 0.2 collective-permute-start.8
  68.8 6.1 %collective-permute-done.7.g2_ref = bf16[256,384]{1,0:T(8,128)(2,1)S(1)} collective-permute-done((bf16[256,384]{1,0:T(8,128)(2,1)}, bf16[256,384]{1,0:T(8,128)(2,1)S(1)}, u32[]{:S(2)}, u32[]{:S(2)}) %collective-permute-start.7) | collective-permute-done | bytes 196640 | tf_op jit(solution)/shard_map/ppermute | solution.py:356
  74.9 3.3 %collective-permute-done.8.g3_ref = bf16[256,384]{1,0:T(8,128)(2,1)S(1)} collective-permute-done((bf16[256,384]{1,0:T(8,128)(2,1)}, bf16[256,384]{1,0:T(8,128)(2,1)S(1)}, u32[]{:S(2)}, u32[]{:S(2)}) %collective-permute-start.8) | collective-permute-done | bytes 196640 | tf_op jit(solution)/shard_map/ppermute | solution.py:356
  78.2 0.9 copy-done.3
  79.1 0.9 copy-done.6
  80.1 2.0 %input_grad.1 = bf16[512,512]{1,0:T(8,128)(2,1)} custom-call(s32[1]{0:T(128)} %bitcast.me_ref, bf16[256,384]{1,0:T(8,128)(2,1)S(1)} %copy-done.6, bf16[256,384]{1,0:T(8,128)(2,1)S(1)} %collective-permute-done.6.g1_ref, bf16[256,384]{1,0:T(8,128)(2,1)S(1)} %collective-permute-done.7.g2_ref, bf16[256,384]{1,0:T(8,128)(2,1)S(1)} %collective-permute-done.8.g3_ref, ...), custom_call_target="tpu_custom_call" | custom-call | flops 1000000000 | bytes 1048576 | tf_op jit(solution)/shard_map/input_grad/pallas_call | solution.py:21
  82.1 2.4 %all-to-all-done.2.parts_ref = bf16[8,64,640]{2,1,0:T(8,128)(2,1)S(1)} async-done(((bf16[8,64,640]{2,1,0:T(8,128)(2,1)}), bf16[8,64,640]{2,1,0:T(8,128)(2,1)S(1)}, u32[]{:S(2)}, u32[]{:S(2)}) %all-to-all-start.2) | async-done | bytes 655392 | tf_op jit(solution)/shard_map/all_to_all | solution.py:366
  84.5 3.7 %all-to-all-start.1 = ((bf16[8,64,512]{2,1,0:T(8,128)(2,1)}), bf16[8,64,512]{2,1,0:T(8,128)(2,1)S(1)}, u32[]{:S(2)}, u32[]{:S(2)}) async-start(bf16[8,64,512]{2,1,0:T(8,128)(2,1)} %bitcast.5), calls=%async_computation.1 | async-start | bytes 1048576 | tf_op jit(solution)/shard_map/all_to_all | solution.py:366
  88.2 0.1 sum.1.w0_ref
  88.3 1.9 %collective-permute-start.13 = (bf16[64,640]{1,0:T(8,128)(2,1)S(1)}, bf16[64,640]{1,0:T(8,128)(2,1)S(1)}, u32[]{:S(2)}, u32[]{:S(2)}) collective-permute-start(bf16[64,640]{1,0:T(8,128)(2,1)S(1)} %sum.1.w0_ref), channel_id=1, source_target_pairs={{0,2},{1,3},{2,0},{3,1},{4,6},{5,7},{6,4},{7,5},{8,10},{9,11},{10,... | collective-permute-start | bytes 245768 | tf_op jit(solution)/shard_map/ppermute | solution.py:356
  90.2 2.7 %collective-permute-done.13.w2_ref = bf16[64,640]{1,0:T(8,128)(2,1)S(1)} collective-permute-done((bf16[64,640]{1,0:T(8,128)(2,1)S(1)}, bf16[64,640]{1,0:T(8,128)(2,1)S(1)}, u32[]{:S(2)}, u32[]{:S(2)}) %collective-permute-start.13) | collective-permute-done | bytes 81952 | tf_op jit(solution)/shard_map/ppermute | solution.py:356
  92.9 10.4 %all-to-all-done.1 = bf16[8,64,512]{2,1,0:T(8,128)(2,1)S(1)} async-done(((bf16[8,64,512]{2,1,0:T(8,128)(2,1)}), bf16[8,64,512]{2,1,0:T(8,128)(2,1)S(1)}, u32[]{:S(2)}, u32[]{:S(2)}) %all-to-all-start.1) | async-done | bytes 524320 | tf_op jit(solution)/shard_map/all_to_all | solution.py:366
  103.3 1.2 %give_back.1 = bf16[256,512]{1,0:T(8,128)(2,1)} custom-call(s32[1,256]{1,0:T(1,128)S(1)} %bitcast.12, bf16[512,512]{1,0:T(8,128)(2,1)S(1)} %bitcast.10), custom_call_target="tpu_custom_call" | custom-call | flops 100000000 | bytes 1048576 | tf_op jit(solution)/shard_map/give_back/pallas_call | solution.py:21
  104.5 0.9 finish.1
  (35 shorter events, 0.1 us)
Async XLA Ops:
  0.6 34.6 %copy-start = (bf16[512,2048]{1,0:T(8,128)(2,1)S(1)}, bf16[512,2048]{1,0:T(8,128)(2,1)}, u32[]{:S(2)}) copy-start(bf16[512,2048]{1,0:T(8,128)(2,1)} %proj_ref.9) | copy-start | bytes 6291460
  0.6 34.6 %copy-start.1 = (bf16[256,512]{1,0:T(8,128)(2,1)S(1)}, bf16[256,512]{1,0:T(8,128)(2,1)}, u32[]{:S(2)}) copy-start(bf16[256,512]{1,0:T(8,128)(2,1)} %cot_ref.7) | copy-start | bytes 786436
  0.7 1.1 %copy-start.4 = (bf16[256,512]{1,0:T(8,128)(2,1)S(1)}, bf16[256,512]{1,0:T(8,128)(2,1)}, u32[]{:S(2)}) copy-start(bf16[256,512]{1,0:T(8,128)(2,1)} %tokens_ref.1) | copy-start | bytes 786436
  1.8 0.7 copy-start.7
  2.4 0.7 copy-start.9
  27.4 9.9 %copy-start.17 = (s32[1,3]{1,0:T(1,128)S(1)}, s32[1,3]{1,0:T(1,128)}, u32[]{:S(2)}) copy-start(s32[1,3]{1,0:T(1,128)} %lengths_ref.3) | copy-start | bytes 40
  28.3 12.5 %copy-start.2 = (bf16[256,512]{1,0:T(8,128)(2,1)}, bf16[256,512]{1,0:T(8,128)(2,1)S(1)}, u32[]{:S(2)}) copy-start(bf16[256,512]{1,0:T(8,128)(2,1)S(1)} %get-tuple-element.33.owned_ref) | copy-start | bytes 786436
  28.3 7.0 %collective-permute-start.1 = (bf16[256,512]{1,0:T(8,128)(2,1)S(1)}, bf16[256,512]{1,0:T(8,128)(2,1)S(1)}, u32[]{:S(2)}, u32[]{:S(2)}) collective-permute-start(bf16[256,512]{1,0:T(8,128)(2,1)S(1)} %get-tuple-element.32.normed_ref.n0_ref.refs_0_), channel_id=1, source_target_pairs={{0,2},{1,3},{2,0},{3,1},{4,6},{5,7},{6,4},{7,5},{8,10},{9,11},{10,... | collective-permute-start | bytes 786440 | tf_op jit(solution)/shard_map/ppermute | solution.py:356
  29.8 7.4 %collective-permute-start = (bf16[256,512]{1,0:T(8,128)(2,1)S(1)}, bf16[256,512]{1,0:T(8,128)(2,1)S(1)}, u32[]{:S(2)}, u32[]{:S(2)}) collective-permute-start(bf16[256,512]{1,0:T(8,128)(2,1)S(1)} %get-tuple-element.32.normed_ref.n0_ref.refs_0_), channel_id=1, source_target_pairs={{0,1},{1,0},{2,3},{3,2},{4,5},{5,4},{6,7},{7,6},{8,9},{9,8},{10,11... | collective-permute-start | bytes 786440 | tf_op jit(solution)/shard_map/ppermute | solution.py:356
  35.2 2.1 %collective-permute-start.2 = (bf16[256,512]{1,0:T(8,128)(2,1)S(1)}, bf16[256,512]{1,0:T(8,128)(2,1)}, u32[]{:S(2)}, u32[]{:S(2)}) collective-permute-start(bf16[256,512]{1,0:T(8,128)(2,1)S(1)} %collective-permute-done.1.far_ref.n2_ref.refs_2_), channel_id=1, source_target_pairs={{0,1},{1,0},{2,3},{3,2},{4,5},{5,4},{6,7},{7,6},{8,9},{9,8},{10,11... | collective-permute-start | bytes 786440 | tf_op jit(solution)/shard_map/ppermute | solution.py:356
  35.2 1.0 copy-start.10
  36.3 1.0 copy-start.11
  37.3 3.4 %copy-start.12 = (bf16[256,512]{1,0:T(8,128)(2,1)}, bf16[256,512]{1,0:T(8,128)(2,1)S(1)}, u32[]{:S(2)}) copy-start(bf16[256,512]{1,0:T(8,128)(2,1)S(1)} %collective-permute-done.near_ref.n1_ref.refs_1_) | copy-start | bytes 786436
  40.7 7.4 %copy-start.13 = (bf16[256,512]{1,0:T(8,128)(2,1)S(1)}, bf16[256,512]{1,0:T(8,128)(2,1)}, u32[]{:S(2)}) copy-start(bf16[256,512]{1,0:T(8,128)(2,1)} %copy-done.12) | copy-start | bytes 786436
  40.7 9.2 %collective-permute-start.3 = (bf16[256,128]{1,0:T(8,128)(2,1)S(1)}, bf16[256,128]{1,0:T(8,128)(2,1)S(1)}, u32[]{:S(2)}, u32[]{:S(2)}) collective-permute-start(bf16[256,128]{1,0:T(8,128)(2,1)S(1)} %get-tuple-element.41), channel_id=1, source_target_pairs={{0,1},{1,0},{2,3},{3,2},{4,5},{5,4},{6,7},{7,6},{8,9},{9,8},{10,11... | collective-permute-start | bytes 196616 | tf_op jit(solution)/shard_map/ppermute | solution.py:356
  41.3 8.7 %collective-permute-start.4 = (bf16[256,128]{1,0:T(8,128)(2,1)S(1)}, bf16[256,128]{1,0:T(8,128)(2,1)S(1)}, u32[]{:S(2)}, u32[]{:S(2)}) collective-permute-start(bf16[256,128]{1,0:T(8,128)(2,1)S(1)} %get-tuple-element.42), channel_id=1, source_target_pairs={{0,2},{1,3},{2,0},{3,1},{4,6},{5,7},{6,4},{7,5},{8,10},{9,11},{10,... | collective-permute-start | bytes 196616 | tf_op jit(solution)/shard_map/ppermute | solution.py:356
  45.4 4.6 %collective-permute-start.5 = (bf16[256,128]{1,0:T(8,128)(2,1)S(1)}, bf16[256,128]{1,0:T(8,128)(2,1)S(1)}, u32[]{:S(2)}, u32[]{:S(2)}) collective-permute-start(bf16[256,128]{1,0:T(8,128)(2,1)S(1)} %get-tuple-element.43), channel_id=1, source_target_pairs={{0,3},{1,2},{2,1},{3,0},{4,7},{5,6},{6,5},{7,4},{8,11},{9,10},{10,... | collective-permute-start | bytes 196616 | tf_op jit(solution)/shard_map/ppermute | solution.py:356
  45.9 9.8 %collective-permute-start.9 = (bf16[768,128]{1,0:T(8,128)(2,1)S(1)}, bf16[768,128]{1,0:T(8,128)(2,1)S(1)}, u32[]{:S(2)}, u32[]{:S(2)}) collective-permute-start(bf16[768,128]{1,0:T(8,128)(2,1)S(1)} %get-tuple-element.55), channel_id=1, source_target_pairs={{0,1},{1,0},{2,3},{3,2},{4,5},{5,4},{6,7},{7,6},{8,9},{9,8},{10,11... | collective-permute-start | bytes 589832 | tf_op jit(solution)/shard_map/ppermute | solution.py:356
  46.1 9.6 %collective-permute-start.10 = (bf16[768,128]{1,0:T(8,128)(2,1)S(1)}, bf16[768,128]{1,0:T(8,128)(2,1)S(1)}, u32[]{:S(2)}, u32[]{:S(2)}) collective-permute-start(bf16[768,128]{1,0:T(8,128)(2,1)S(1)} %get-tuple-element.56), channel_id=1, source_target_pairs={{0,2},{1,3},{2,0},{3,1},{4,6},{5,7},{6,4},{7,5},{8,10},{9,11},{10,... | collective-permute-start | bytes 589832 | tf_op jit(solution)/shard_map/ppermute | solution.py:356
  49.9 8.2 %collective-permute-start.11 = (bf16[768,128]{1,0:T(8,128)(2,1)S(1)}, bf16[768,128]{1,0:T(8,128)(2,1)S(1)}, u32[]{:S(2)}, u32[]{:S(2)}) collective-permute-start(bf16[768,128]{1,0:T(8,128)(2,1)S(1)} %get-tuple-element.57), channel_id=1, source_target_pairs={{0,3},{1,2},{2,1},{3,0},{4,7},{5,6},{6,5},{7,4},{8,11},{9,10},{10,... | collective-permute-start | bytes 589832 | tf_op jit(solution)/shard_map/ppermute | solution.py:356
  55.7 5.3 %copy-start.14 = (bf16[256,384]{1,0:T(8,128)(2,1)}, bf16[256,384]{1,0:T(8,128)(2,1)S(1)}, u32[]{:S(2)}) copy-start(bf16[256,384]{1,0:T(8,128)(2,1)S(1)} %get-tuple-element.49.refs_7_) | copy-start | bytes 589828
  55.7 5.3 %copy-start.15 = (bf16[256,384]{1,0:T(8,128)(2,1)}, bf16[256,384]{1,0:T(8,128)(2,1)S(1)}, u32[]{:S(2)}) copy-start(bf16[256,384]{1,0:T(8,128)(2,1)S(1)} %get-tuple-element.48.refs_6_) | copy-start | bytes 589828
  55.8 5.3 %copy-start.16 = (bf16[256,384]{1,0:T(8,128)(2,1)}, bf16[256,384]{1,0:T(8,128)(2,1)S(1)}, u32[]{:S(2)}) copy-start(bf16[256,384]{1,0:T(8,128)(2,1)S(1)} %get-tuple-element.47.refs_5_) | copy-start | bytes 589828
  61.0 0.7 copy-start.5
  61.7 22.8 %all-to-all-start.2 = ((bf16[8,64,640]{2,1,0:T(8,128)(2,1)}), bf16[8,64,640]{2,1,0:T(8,128)(2,1)S(1)}, u32[]{:S(2)}, u32[]{:S(2)}) async-start(bf16[8,64,640]{2,1,0:T(8,128)(2,1)} %bitcast.7), calls=%async_computation.2 | async-start | bytes 1310720 | tf_op jit(solution)/shard_map/all_to_all | solution.py:366
  66.9 1.9 %collective-permute-start.6 = (bf16[256,384]{1,0:T(8,128)(2,1)}, bf16[256,384]{1,0:T(8,128)(2,1)S(1)}, u32[]{:S(2)}, u32[]{:S(2)}) collective-permute-start(bf16[256,384]{1,0:T(8,128)(2,1)} %copy-done.16), channel_id=1, source_target_pairs={{0,1},{1,0},{2,3},{3,2},{4,5},{5,4},{6,7},{7,6},{8,9},{9,8},{10,11... | collective-permute-start | bytes 589832 | tf_op jit(solution)/shard_map/ppermute | solution.py:356
  66.9 8.0 %collective-permute-start.7 = (bf16[256,384]{1,0:T(8,128)(2,1)}, bf16[256,384]{1,0:T(8,128)(2,1)S(1)}, u32[]{:S(2)}, u32[]{:S(2)}) collective-permute-start(bf16[256,384]{1,0:T(8,128)(2,1)} %copy-done.15), channel_id=1, source_target_pairs={{0,2},{1,3},{2,0},{3,1},{4,6},{5,7},{6,4},{7,5},{8,10},{9,11},{10,... | collective-permute-start | bytes 589832 | tf_op jit(solution)/shard_map/ppermute | solution.py:356
  68.6 9.6 %collective-permute-start.8 = (bf16[256,384]{1,0:T(8,128)(2,1)}, bf16[256,384]{1,0:T(8,128)(2,1)S(1)}, u32[]{:S(2)}, u32[]{:S(2)}) collective-permute-start(bf16[256,384]{1,0:T(8,128)(2,1)} %copy-done.14), channel_id=1, source_target_pairs={{0,3},{1,2},{2,1},{3,0},{4,7},{5,6},{6,5},{7,4},{8,11},{9,10},{10,... | collective-permute-start | bytes 589832 | tf_op jit(solution)/shard_map/ppermute | solution.py:356
  78.2 1.0 copy-start.3
  79.1 0.9 copy-start.6
  80.1 23.3 %copy-start.8 = (s32[256]{0:T(256)S(1)}, s32[256]{0:T(256)}, u32[]{:S(2)}) copy-start(s32[256]{0:T(256)} %param.8) | copy-start | bytes 3076
  84.5 18.9 %all-to-all-start.1 = ((bf16[8,64,512]{2,1,0:T(8,128)(2,1)}), bf16[8,64,512]{2,1,0:T(8,128)(2,1)S(1)}, u32[]{:S(2)}, u32[]{:S(2)}) async-start(bf16[8,64,512]{2,1,0:T(8,128)(2,1)} %bitcast.5), calls=%async_computation.1 | async-start | bytes 1048576 | tf_op jit(solution)/shard_map/all_to_all | solution.py:366
  88.3 4.7 %collective-permute-start.13 = (bf16[64,640]{1,0:T(8,128)(2,1)S(1)}, bf16[64,640]{1,0:T(8,128)(2,1)S(1)}, u32[]{:S(2)}, u32[]{:S(2)}) collective-permute-start(bf16[64,640]{1,0:T(8,128)(2,1)S(1)} %sum.1.w0_ref), channel_id=1, source_target_pairs={{0,2},{1,3},{2,0},{3,1},{4,6},{5,7},{6,4},{7,5},{8,10},{9,11},{10,... | collective-permute-start | bytes 245768 | tf_op jit(solution)/shard_map/ppermute | solution.py:356
  90.2 14.3 %collective-permute-start.12 = (bf16[64,640]{1,0:T(8,128)(2,1)S(1)}, bf16[64,640]{1,0:T(8,128)(2,1)S(1)}, u32[]{:S(2)}, u32[]{:S(2)}) collective-permute-start(bf16[64,640]{1,0:T(8,128)(2,1)S(1)} %sum.1.w0_ref), channel_id=1, source_target_pairs={{0,1},{1,0},{2,3},{3,2},{4,5},{5,4},{6,7},{7,6},{8,9},{9,8},{10,11... | collective-permute-start | bytes 245768 | tf_op jit(solution)/shard_map/ppermute | solution.py:356
  92.9 11.6 %collective-permute-start.14 = (bf16[64,640]{1,0:T(8,128)(2,1)S(1)}, bf16[64,640]{1,0:T(8,128)(2,1)S(1)}, u32[]{:S(2)}, u32[]{:S(2)}) collective-permute-start(bf16[64,640]{1,0:T(8,128)(2,1)S(1)} %collective-permute-done.13.w2_ref), channel_id=1, source_target_pairs={{0,1},{1,0},{2,3},{3,2},{4,5},{5,4},{6,7},{7,6},{8,9},{9,8},{10,11... | collective-permute-start | bytes 245768 | tf_op jit(solution)/shard_map/ppermute | solution.py:356

commit v2 on v1

--- a/solution.py
+++ b/solution.py
@@ -15,19 +15,20 @@
 
 WHOLE = pl.BlockSpec(memory_space=pltpu.VMEM)
 SCALARS = pl.BlockSpec(memory_space=pltpu.SMEM)
-
-
-def call(body, name, outs, scalars, arrays, scratch=(), flops=10**8, vmem=24):
+ANYWHERE = pl.BlockSpec(memory_space=pltpu.HBM)
+
+
+def call(body, name, outs, scalars, arrays, scratch=(), flops=10**8, vmem=8, far=()):
     return pl.pallas_call(
         body,
         name=name,
         out_shape=[jax.ShapeDtypeStruct(s, d) for s, d in outs],
-        in_specs=[SCALARS] * len(scalars) + [WHOLE] * len(arrays),
+        in_specs=[SCALARS] * len(scalars) + [WHOLE] * len(arrays) + [ANYWHERE] * len(far),
         out_specs=[WHOLE] * len(outs),
         scratch_shapes=list(scratch),
         compiler_params=pltpu.CompilerParams(vmem_limit_bytes=vmem * 2**20),
         cost_estimate=pl.CostEstimate(flops=flops, bytes_accessed=2**20, transcendentals=0),
-    )(*scalars, *arrays)
+    )(*scalars, *arrays, *far)
 
 
 def iota(shape, dim):
@@ -81,7 +82,18 @@
     return rank_row.astype(jnp.int32), rank_col.astype(jnp.int32)
 
 
-def pack_body(capacity, stride, owner_ref, slot_ref, tokens_ref, out_ref):
+def fetch(sources, targets, sems):
+    copies = [pltpu.make_async_copy(a, b, sems.at[i]) for i, (a, b) in enumerate(zip(sources, targets))]
+    for copy in copies:
+        copy.start()
+    for copy in copies:
+        copy.wait()
+
+
+def pack_body(
+    capacity, stride, owner_hbm, slot_hbm, tokens_hbm, out_ref, owner_ref, slot_ref, tokens_ref, sems
+):
+    fetch((owner_hbm, slot_hbm, tokens_hbm), (owner_ref, slot_ref, tokens_ref), sems)
     owner = owner_ref[...]
     rows = owner.shape[1]
     rank_row, rank_col = rank_rows(owner)
@@ -123,15 +135,7 @@
     landing_ref[...] = landing_row(table, owners, capacity, capacity).astype(jnp.int32)
 
 
-def own_body(normed_ref, proj_ref, outw_ref, cot_ref, gate_ref, slope_ref, query_ref, kv_ref, grad_ref):
-    width = normed_ref.shape[1]
-    preact = mm(normed_ref[...], proj_ref[...])
-    gate, slope = silu_both(preact[:, :width])
-    gate_ref[...] = gate.astype(BF16)
-    slope_ref[...] = slope
-    kv_ref[:, :width] = silu_both(preact[:, width : 2 * width])[0].astype(BF16)
-    query_ref[...] = silu_both(preact[:, 2 * width : 3 * width])[0].astype(BF16)
-    kv_ref[:, width:] = silu_both(preact[:, 3 * width :])[0].astype(BF16)
+def early_body(cot_ref, outw_ref, grad_ref):
     grad_ref[...] = mm_t(cot_ref[...], outw_ref[...])
 
 
@@ -155,35 +159,58 @@
         acc_ref[:, cols] = total
 
 
+def shared_factor(block, me, rows, lengths_ref):
+    query_pos = me * rows + iota((rows, 1), 0)
+    start = history_start(query_pos, lengths_ref)
+    inverse = 1.0 / (query_pos - start + 1).astype(F32)
+    key_pos = block * rows + iota((1, rows), 1)
+    return jnp.where((key_pos >= start) & (key_pos <= query_pos), inverse, 0.0)
+
+
+def attend_other(step, me, lengths_ref, other_ref, proj_ref, query_ref, acc_ref):
+    rows, width = query_ref.shape
+    block = me ^ step
+    reach = history_start(me * rows, lengths_ref)
+
+    @pl.when((block < me) & ((block + 1) * rows > reach))
+    def _():
+        normed = other_ref[...]
+        value = silu_both(mm(normed, proj_ref[:, width : 2 * width]))[0].astype(BF16)
+        key = silu_both(mm(normed, proj_ref[:, 3 * width :]))[0].astype(BF16)
+        attend(query_ref, key, value, shared_factor(block, me, rows, lengths_ref), acc_ref)
+
+
+def own_body(me_ref, lengths_ref, normed_ref, proj_ref, gate_ref, slope_ref, query_ref, acc_ref):
+    rows, width = normed_ref.shape
+    me = me_ref[0]
+    preact = mm(normed_ref[...], proj_ref[...])
+    gate, slope = silu_both(preact[:, :width])
+    gate_ref[...] = gate.astype(BF16)
+    slope_ref[...] = slope
+    value = silu_both(preact[:, width : 2 * width])[0].astype(BF16)
+    query_ref[...] = silu_both(preact[:, 2 * width : 3 * width])[0].astype(BF16)
+    key = silu_both(preact[:, 3 * width :])[0].astype(BF16)
+    acc_ref[...] = jnp.zeros_like(acc_ref)
+    attend(query_ref, key, value, shared_factor(me, me, rows, lengths_ref), acc_ref)
+
+
+def middle_body(me_ref, lengths_ref, near_ref, far_ref, proj_ref, query_ref, partial_ref, acc_ref):
+    me = me_ref[0]
+    acc_ref[...] = partial_ref[...]
+    attend_other(1, me, lengths_ref, near_ref, proj_ref, query_ref, acc_ref)
+    attend_other(2, me, lengths_ref, far_ref, proj_ref, query_ref, acc_ref)
+
+
 def forward_body(
-    me_ref, lengths_ref, near_ref, far_ref, cross_ref, proj_ref, outw_ref, cot_ref, owned_ref,
-    gate_ref, slope_ref, query_ref, kv_ref, grad_ref,
+    me_ref, lengths_ref, cross_ref, proj_ref, outw_ref, owned_ref,
+    gate_ref, slope_ref, query_ref, partial_ref, grad_ref,
     out_ref, gated_ref, gate_grad_ref, *rest,
 ):
     grads, acc_ref = rest[:-1], rest[-1]
     rows, width = query_ref.shape
     me = me_ref[0]
-    acc_ref[...] = jnp.zeros_like(acc_ref)
-    query_pos = me * rows + iota((rows, 1), 0)
-    start = history_start(query_pos, lengths_ref)
-    inverse = 1.0 / (query_pos - start + 1).astype(F32)
-
-    def shared_for(block):
-        key_pos = block * rows + iota((1, rows), 1)
-        return jnp.where((key_pos >= start) & (key_pos <= query_pos), inverse, 0.0)
-
-    attend(query_ref, kv_ref[:, width:], kv_ref[:, :width], shared_for(me), acc_ref)
-    for step, other_ref in ((1, near_ref), (2, far_ref), (3, cross_ref)):
-        block = me ^ step
-        reach = history_start(me * rows, lengths_ref)
-
-        @pl.when((block < me) & ((block + 1) * rows > reach))
-        def _():
-            normed = other_ref[...]
-            value = silu_both(mm(normed, proj_ref[:, width : 2 * width]))[0].astype(BF16)
-            key = silu_both(mm(normed, proj_ref[:, 3 * width :]))[0].astype(BF16)
-            attend(query_ref, key, value, shared_for(block), acc_ref)
-
+    acc_ref[...] = partial_ref[...]
+    attend_other(3, me, lengths_ref, cross_ref, proj_ref, query_ref, acc_ref)
     gate = gate_ref[...].astype(F32)
     normed, inv_dev = normalize(acc_ref[...])
     gated = (normed * gate).astype(BF16)
@@ -282,7 +309,7 @@
 
 
 def weight_body(*refs):
-    normed, grads, sides, out_ref = refs[:4], refs[4:8], refs[8:12], refs[12]
+    normed, grads, sides, out_ref = refs[:4], refs[4:8], refs[8:12], refs[-1]
     rows, piece = normed[0].shape[0], sides[0].shape[1]
     qkv, gate, outw = 0.0, 0.0, 0.0
     for n_ref, g_ref, s_ref in zip(normed, grads, sides):
@@ -367,7 +394,13 @@
 
     (outgoing,) = call(
         functools.partial(pack_body, capacity, stride),
-        "pack", [((owners * stride, width), BF16)], [], [owner_row, slot_row, tokens],
+        "pack", [((owners * stride, width), BF16)], [], [], far=[owner_row, slot_row, tokens],
+        scratch=[
+            pltpu.VMEM((1, rows), jnp.int32),
+            pltpu.VMEM((1, rows), jnp.int32),
+            pltpu.VMEM((rows, width), BF16),
+            pltpu.SemaphoreType.DMA((3,)),
+        ],
     )
     arrived = swap(outgoing.reshape(owners, stride, width)).reshape(owners * stride, width)
     owned, normed, landing = call(
@@ -375,17 +408,22 @@
         "place", [square, square, ((1, owners * capacity), jnp.int32)], [], [arrived],
     )
     near, far, cross = gather(normed)
-    gate, slope, query, keys_values, grad_gated = call(
-        own_body, "own_rows",
-        [square, ((rows, width), F32), square, ((rows, 2 * width), BF16), ((rows, width), F32)],
-        [], [normed, proj_weight, out_weight, cotangent], flops=10**9,
+    wide = ((rows, width), F32)
+    (grad_gated,) = call(early_body, "early", [wide], [], [cotangent, out_weight], flops=10**8)
+    gate, slope, query, partial = call(
+        own_body, "own_rows", [square, wide, square, wide],
+        [me, lengths], [normed, proj_weight], flops=10**9, vmem=16,
+    )
+    (partial,) = call(
+        middle_body, "middle", [wide], [me, lengths], [near, far, proj_weight, query, partial],
+        flops=10**9, vmem=16,
     )
     layer_out, gated, gate_grad, *grad_pieces = call(
         forward_body, "forward",
         [square, square, square] + [((rows, piece), BF16)] * cycle,
         [me, lengths],
-        [near, far, cross, proj_weight, out_weight, cotangent, owned, gate, slope, query, keys_values, grad_gated],
-        scratch=[pltpu.VMEM((rows, width), F32)], flops=4 * 10**9, vmem=32,
+        [cross, proj_weight, out_weight, owned, gate, slope, query, partial, grad_gated],
+        scratch=[pltpu.VMEM((rows, width), F32)], flops=10**9, vmem=16,
     )
     r0, r2, r3, r1 = exchange(grad_pieces)
     *sides, gate_in = call(
@@ -396,25 +434,25 @@
     parts, slopes = call(
         heads_body, "heads",
         [((rows * cycle, 3 * piece), BF16), ((rows * cycle, 3 * piece), F32)],
-        [me], [normed, near, far, cross, proj_weight], flops=10**9,
+        [me], [normed, near, far, cross, proj_weight], flops=10**9, vmem=16,
     )
     s0, s2, s3, s1 = exchange(sides)
     grads = call(
         backward_body, "backward", [((rows, 3 * piece), BF16)] * cycle,
         [me, lengths], [r0, r1, r2, r3, parts, slopes],
         scratch=[pltpu.VMEM((rows * cycle, piece), BF16), pltpu.VMEM((rows * cycle, 3 * piece), F32)],
-        flops=4 * 10**9, vmem=32,
+        flops=4 * 10**9, vmem=16,
     )
     p0, p2, p3, p1 = exchange(grads)
     (weight_part,) = call(
         weight_body, "weights", [((width, 5 * piece), BF16)], [],
-        [normed, near, far, cross, *grads, s0, s1, s2, s3], flops=10**9,
+        [normed, near, far, cross, *grads, s0, s1, s2, s3], flops=10**9, vmem=16, far=[p1],
     )
     share = width // owners
     summed_parts = swap(weight_part.reshape(owners, share, 5 * piece))
     (back,) = call(
         input_body, "input_grad", [((owners * capacity, width), BF16)], [me],
-        [p0, p1, p2, p3, gate_in, owned, cotangent, landing, proj_weight], flops=10**9,
+        [p0, p1, p2, p3, gate_in, owned, cotangent, landing, proj_weight], flops=10**9, vmem=16,
     )
     returned = swap(back.reshape(owners, capacity, width)).reshape(owners * capacity, width)
     (mine,) = call(sum_body, "sum", [((share, 5 * piece), BF16)], [], [summed_parts])

time: 106 us -> 109 us (1.028)
  starting transfers between devices: 21.2 us -> 23.3 us
  Pallas kernels: 20.9 us -> 22.9 us
  waiting for transfers between devices: 32.7 us -> 31 us
    all_to_all x2, starting transfers between devices: 8.92 us -> 11.3 us  [swap(): return lax.all_to_all(value, 'dp', split_axis=0, concat_axis=0, tiled=True)]
    pallas_call x12 -> x14, Pallas kernels: 20.9 us -> 22.9 us  [call(): pl.pallas_call(body, name=name, out_shape=[jax.ShapeDtypeStruct(s, d) for...]
    ppermute x15, waiting for transfers between devices: 19.9 us -> 18.7 us  [hop(): return lax.ppermute(value, 'ctx', [(i, i ^ step) for i in range(cycle)])]
    unnamed x36 -> x32, local copies, waits for them, and re-layouts: 6.1 us -> 7.01 us
  transfers between devices with their start and end apart: 17 -> 17, of which waited for: 7 -> 7; matrix products, arithmetic and copies ran while one was open for 0% -> 0% of each run, Pallas kernels for 12% -> 14%
where the time goes in v2:
time: 109 us
  waiting for transfers between devices  31 us (28%)
  blocking collectives  23.6 us (22%)
  starting transfers between devices  23.3 us (21%)
  Pallas kernels  22.9 us (21%)
  local copies, waits for them, and re-layouts  7.01 us (6%)
    all_to_all x1, blocking collectives, swap(): return lax.all_to_all(value, 'dp', split_axis=0, concat_axis=0, tiled=True)  23.6 us
    pallas_call x14, Pallas kernels, call(): pl.pallas_call(body, name=name, out_shape=[jax.ShapeDtypeStruct(s, d) for...  22.9 us
    ppermute x15, waiting for transfers between devices, hop(): return lax.ppermute(value, 'ctx', [(i, i ^ step) for i in range(cycle)])  18.7 us
    all_to_all x2, waiting for transfers between devices, swap(): return lax.all_to_all(value, 'dp', split_axis=0, concat_axis=0, tiled=True)  12.2 us
    ppermute x15, starting transfers between devices, hop(): return lax.ppermute(value, 'ctx', [(i, i ^ step) for i in range(cycle)])  12 us
    all_to_all x2, starting transfers between devices, swap(): return lax.all_to_all(value, 'dp', split_axis=0, concat_axis=0, tiled=True)  11.3 us
    unnamed x32, local copies, waits for them, and re-layouts  7.01 us
  transfers between devices with their start and end apart: 17, of which 7 were waited for; matrix products, arithmetic and copies ran while one was open for 0% of the time, Pallas kernels for 14%

profile of v2, /device:TPU:0, one launch (start us, length us, event | category | flops | bytes accessed | tf_op | source)
XLA Modules:
  0.0 108.7 jit_solution(3196436859400855163)
XLA Ops:
  0.7 1.1 %copy-done.6 = bf16[256,512]{1,0:T(8,128)(2,1)S(1)} copy-done((bf16[256,512]{1,0:T(8,128)(2,1)S(1)}, bf16[256,512]{1,0:T(8,128)(2,1)}, u32[]{:S(2)}) %copy-start.6) | copy-done | bytes 262168
  1.8 0.7 copy-done.11
  2.4 0.7 copy-done.14
  3.1 0.7 pack.1
  3.8 23.6 %all_to_all.15 = bf16[8,72,512]{2,1,0:T(8,128)(2,1)S(1)} all-to-all(bf16[8,72,512]{2,1,0:T(8,128)(2,1)S(1)} %bitcast.9), channel_id=1, replica_groups=mesh['dp'=8,'ctx'=4] {'dp'}, dimensions={0} | all-to-all | bytes 1179648 | tf_op jit(solution)/shard_map/all_to_all | solution.py:393
  27.5 1.5 %place.1 = (bf16[256,512]{1,0:T(8,128)(2,1)S(1)}, bf16[256,512]{1,0:T(8,128)(2,1)}, s32[1,512]{1,0:T(1,128)S(1)}) custom-call(bf16[576,512]{1,0:T(8,128)(2,1)S(1)} %bitcast.8), custom_call_target="tpu_custom_call" | custom-call | flops 100000000 | bytes 1048576 | tf_op jit(solution)/shard_map/place/pallas_call | solution.py:22
  29.0 1.5 %collective-permute-start = (bf16[256,512]{1,0:T(8,128)(2,1)}, bf16[256,512]{1,0:T(8,128)(2,1)S(1)}, u32[]{:S(2)}, u32[]{:S(2)}) collective-permute-start(bf16[256,512]{1,0:T(8,128)(2,1)} %get-tuple-element.31.normed_ref.n0_ref.refs_0_), channel_id=1, source_target_pairs={{0,2},{1,3},{2,0},{3,1},{4,6},{5,7},{6,4},{7,5},{8,10},{9,11},{10,... | collective-permute-start | bytes 786440 | tf_op jit(solution)/shard_map/ppermute | solution.py:383
  30.5 0.0 collective-permute-start.2
  30.5 5.6 %collective-permute-done.far_ref.n2_ref.refs_2_ = bf16[256,512]{1,0:T(8,128)(2,1)S(1)} collective-permute-done((bf16[256,512]{1,0:T(8,128)(2,1)}, bf16[256,512]{1,0:T(8,128)(2,1)S(1)}, u32[]{:S(2)}, u32[]{:S(2)}) %collective-permute-start) | collective-permute-done | bytes 262176 | tf_op jit(solution)/shard_map/ppermute | solution.py:383
  36.1 0.3 early.1.grad_ref
  36.5 2.6 %own_rows.1 = (bf16[256,512]{1,0:T(8,128)(2,1)S(1)}, f32[256,512]{1,0:T(8,128)S(1)}, bf16[256,512]{1,0:T(8,128)(2,1)S(1)}, f32[256,512]{1,0:T(8,128)S(1)}) custom-call(s32[1]{0:T(128)} %bitcast.me_ref, s32[1,3]{1,0:T(1,128)S(1)} %copy-done.13, bf16[256,512]{1,0:T(8,128)(2,1)} %get-tuple-element.31.normed_ref.n0_ref.refs_0_, bf16[512,2048]{1,0:T(8,128)(2,1)S(1)} %copy-done), custom_call_target="tpu_custom_call" | custom-call | flops 1000000000 | bytes 1048576 | tf_op jit(solution)/shard_map/own_rows/pallas_call | solution.py:22
  39.1 1.0 middle.1.partial_ref
  40.1 2.3 %forward.1 = (bf16[256,512]{1,0:T(8,128)(2,1)}, bf16[256,512]{1,0:T(8,128)(2,1)S(1)}, bf16[256,512]{1,0:T(8,128)(2,1)S(1)}, bf16[256,128]{1,0:T(8,128)(2,1)S(1)}...) custom-call(s32[1]{0:T(128)} %bitcast.me_ref, s32[1,3]{1,0:T(1,128)S(1)} %copy-done.13, ...), custom_call_target="tpu_custom_call" | custom-call | flops 1000000000 | bytes 1048576 | tf_op jit(solution)/shard_map/forward/pallas_call | solution.py:22
  42.5 1.8 %collective-permute-start.3 = (bf16[256,128]{1,0:T(8,128)(2,1)S(1)}, bf16[256,128]{1,0:T(8,128)(2,1)S(1)}, u32[]{:S(2)}, u32[]{:S(2)}) collective-permute-start(bf16[256,128]{1,0:T(8,128)(2,1)S(1)} %get-tuple-element.39), channel_id=1, source_target_pairs={{0,1},{1,0},{2,3},{3,2},{4,5},{5,4},{6,7},{7,6},{8,9},{9,8},{10,11... | collective-permute-start | bytes 196616 | tf_op jit(solution)/shard_map/ppermute | solution.py:383
  44.3 2.3 %collective-permute-start.4 = (bf16[256,128]{1,0:T(8,128)(2,1)S(1)}, bf16[256,128]{1,0:T(8,128)(2,1)S(1)}, u32[]{:S(2)}, u32[]{:S(2)}) collective-permute-start(bf16[256,128]{1,0:T(8,128)(2,1)S(1)} %get-tuple-element.40), channel_id=1, source_target_pairs={{0,2},{1,3},{2,0},{3,1},{4,6},{5,7},{6,4},{7,5},{8,10},{9,11},{10,... | collective-permute-start | bytes 196616 | tf_op jit(solution)/shard_map/ppermute | solution.py:383
  46.6 0.1 collective-permute-start.5
  46.8 0.5 side.1
  47.3 0.0 copy-start.4
  47.4 0.8 copy-done.4
  48.1 0.1 collective-permute-start.9
  48.2 1.9 %collective-permute-start.10 = (bf16[768,128]{1,0:T(8,128)(2,1)S(1)}, bf16[768,128]{1,0:T(8,128)(2,1)S(1)}, u32[]{:S(2)}, u32[]{:S(2)}) collective-permute-start(bf16[768,128]{1,0:T(8,128)(2,1)S(1)} %get-tuple-element.54), channel_id=1, source_target_pairs={{0,2},{1,3},{2,0},{3,1},{4,6},{5,7},{6,4},{7,5},{8,10},{9,11},{10,... | collective-permute-start | bytes 589832 | tf_op jit(solution)/shard_map/ppermute | solution.py:383
  50.1 1.9 %heads.1 = (bf16[1024,384]{1,0:T(8,128)(2,1)S(1)}, f32[1024,384]{1,0:T(8,128)S(1)}) custom-call(s32[1]{0:T(128)} %bitcast.me_ref, bf16[256,512]{1,0:T(8,128)(2,1)} %get-tuple-element.31.normed_ref.n0_ref.refs_0_, bf16[256,512]{1,0:T(8,128)(2,1)} %collective-permute-done.2.near_ref.n1_ref.refs_1_, ...), custom_call_target="tpu_custom_call" | custom-call | flops 1000000000 | bytes 1048576 | tf_op jit(solution)/shard_map/heads/pallas_call | solution.py:22
  52.1 0.1 collective-permute-start.11
  52.2 0.0 collective-permute-done.4.g2_ref
  52.2 5.5 %backward.1 = (bf16[256,384]{1,0:T(8,128)(2,1)S(1)}, bf16[256,384]{1,0:T(8,128)(2,1)S(1)}, bf16[256,384]{1,0:T(8,128)(2,1)S(1)}, bf16[256,384]{1,0:T(8,128)(2,1)S(1)}) custom-call(s32[1]{0:T(128)} %bitcast.me_ref, s32[1,3]{1,0:T(1,128)S(1)} %copy-done.13, bf16[256,128]{1,0:T(8,128)(2,1)S(1)} %get-tuple-element.38.g0_ref, ...), custom_call_target="tpu_custom_call" | custom-call | flops 4000000000 | bytes 1048576 | tf_op jit(solution)/shard_map/backward/pallas_call | solution.py:22
  57.8 0.3 collective-permute-start.6
  58.0 1.4 %collective-permute-done.11.refs_11_ = bf16[768,128]{1,0:T(8,128)(2,1)S(1)} collective-permute-done((bf16[768,128]{1,0:T(8,128)(2,1)S(1)}, bf16[768,128]{1,0:T(8,128)(2,1)S(1)}, u32[]{:S(2)}, u32[]{:S(2)}) %collective-permute-start.11) | collective-permute-done | bytes 196640 | tf_op jit(solution)/shard_map/ppermute | solution.py:383
  59.4 2.2 %weights.1 = bf16[512,640]{1,0:T(8,128)(2,1)S(1)} custom-call(bf16[256,512]{1,0:T(8,128)(2,1)} %get-tuple-element.31.normed_ref.n0_ref.refs_0_, bf16[256,512]{1,0:T(8,128)(2,1)} %collective-permute-done.2.near_ref.n1_ref.refs_1_, bf16[256,512]{1,0:T(8,128)(2,1)S(1)} %collective-permute-done.far_ref.n2_ref.refs_2_, ...), custom_call_target="tpu_custom_call" | custom-call | flops 1000000000 | bytes 1048576 | tf_op jit(solution)/shard_map/weights/pallas_call | solution.py:22
  61.7 0.8 copy-done.3
  62.6 7.7 %all-to-all-start.2 = ((bf16[8,64,640]{2,1,0:T(8,128)(2,1)}), bf16[8,64,640]{2,1,0:T(8,128)(2,1)S(1)}, u32[]{:S(2)}, u32[]{:S(2)}) async-start(bf16[8,64,640]{2,1,0:T(8,128)(2,1)} %bitcast.11), calls=%async_computation.2 | async-start | bytes 1310720 | tf_op jit(solution)/shard_map/all_to_all | solution.py:393
  70.2 1.8 %collective-permute-start.7 = (bf16[256,384]{1,0:T(8,128)(2,1)}, bf16[256,384]{1,0:T(8,128)(2,1)S(1)}, u32[]{:S(2)}, u32[]{:S(2)}) collective-permute-start(bf16[256,384]{1,0:T(8,128)(2,1)} %copy-done.15), channel_id=1, source_target_pairs={{0,2},{1,3},{2,0},{3,1},{4,6},{5,7},{6,4},{7,5},{8,10},{9,11},{10,... | collective-permute-start | bytes 589832 | tf_op jit(solution)/shard_map/ppermute | solution.py:383
  72.0 0.0 collective-permute-start.8
  72.0 6.2 %collective-permute-done.7.g2_ref = bf16[256,384]{1,0:T(8,128)(2,1)S(1)} collective-permute-done((bf16[256,384]{1,0:T(8,128)(2,1)}, bf16[256,384]{1,0:T(8,128)(2,1)S(1)}, u32[]{:S(2)}, u32[]{:S(2)}) %collective-permute-start.7) | collective-permute-done | bytes 196640 | tf_op jit(solution)/shard_map/ppermute | solution.py:383
  78.2 2.6 %collective-permute-done.8.g3_ref = bf16[256,384]{1,0:T(8,128)(2,1)S(1)} collective-permute-done((bf16[256,384]{1,0:T(8,128)(2,1)S(1)}, bf16[256,384]{1,0:T(8,128)(2,1)S(1)}, u32[]{:S(2)}, u32[]{:S(2)}) %collective-permute-start.8) | collective-permute-done | bytes 196640 | tf_op jit(solution)/shard_map/ppermute | solution.py:383
  80.8 1.0 copy-done.5
  81.8 0.9 copy-done.8
  82.8 0.9 copy-done.10
  83.7 2.0 %input_grad.1 = bf16[512,512]{1,0:T(8,128)(2,1)} custom-call(s32[1]{0:T(128)} %bitcast.me_ref, bf16[256,384]{1,0:T(8,128)(2,1)S(1)} %copy-done.8, bf16[256,384]{1,0:T(8,128)(2,1)S(1)} %copy-done.10, bf16[256,384]{1,0:T(8,128)(2,1)S(1)} %collective-permute-done.7.g2_ref, bf16[256,384]{1,0:T(8,128)(2,1)S(1)} %collective-permute-done.8.g3_ref, ...), custom_call_target="tpu_custom_call" | custom-call | flops 1000000000 | bytes 1048576 | tf_op jit(solution)/shard_map/input_grad/pallas_call | solution.py:22
  85.7 2.1 %all-to-all-done.2.parts_ref = bf16[8,64,640]{2,1,0:T(8,128)(2,1)S(1)} async-done(((bf16[8,64,640]{2,1,0:T(8,128)(2,1)}), bf16[8,64,640]{2,1,0:T(8,128)(2,1)S(1)}, u32[]{:S(2)}, u32[]{:S(2)}) %all-to-all-start.2) | async-done | bytes 655392 | tf_op jit(solution)/shard_map/all_to_all | solution.py:393
  87.8 3.6 %all-to-all-start.1 = ((bf16[8,64,512]{2,1,0:T(8,128)(2,1)}), bf16[8,64,512]{2,1,0:T(8,128)(2,1)S(1)}, u32[]{:S(2)}, u32[]{:S(2)}) async-start(bf16[8,64,512]{2,1,0:T(8,128)(2,1)} %bitcast.5), calls=%async_computation.1 | async-start | bytes 1048576 | tf_op jit(solution)/shard_map/all_to_all | solution.py:393
  91.5 0.1 sum.1.w0_ref
  91.6 2.0 %collective-permute-start.13 = (bf16[64,640]{1,0:T(8,128)(2,1)S(1)}, bf16[64,640]{1,0:T(8,128)(2,1)S(1)}, u32[]{:S(2)}, u32[]{:S(2)}) collective-permute-start(bf16[64,640]{1,0:T(8,128)(2,1)S(1)} %sum.1.w0_ref), channel_id=1, source_target_pairs={{0,2},{1,3},{2,0},{3,1},{4,6},{5,7},{6,4},{7,5},{8,10},{9,11},{10,... | collective-permute-start | bytes 245768 | tf_op jit(solution)/shard_map/ppermute | solution.py:383
  93.6 0.1 collective-permute-start.12
  93.6 2.9 %collective-permute-done.13.w2_ref = bf16[64,640]{1,0:T(8,128)(2,1)S(1)} collective-permute-done((bf16[64,640]{1,0:T(8,128)(2,1)S(1)}, bf16[64,640]{1,0:T(8,128)(2,1)S(1)}, u32[]{:S(2)}, u32[]{:S(2)}) %collective-permute-start.13) | collective-permute-done | bytes 81952 | tf_op jit(solution)/shard_map/ppermute | solution.py:383
  96.5 0.0 collective-permute-start.14
  96.5 10.1 %all-to-all-done.1 = bf16[8,64,512]{2,1,0:T(8,128)(2,1)S(1)} async-done(((bf16[8,64,512]{2,1,0:T(8,128)(2,1)}), bf16[8,64,512]{2,1,0:T(8,128)(2,1)S(1)}, u32[]{:S(2)}, u32[]{:S(2)}) %all-to-all-start.1) | async-done | bytes 524320 | tf_op jit(solution)/shard_map/all_to_all | solution.py:393
  106.7 1.2 %give_back.1 = bf16[256,512]{1,0:T(8,128)(2,1)} custom-call(s32[1,256]{1,0:T(1,128)S(1)} %bitcast.13, bf16[512,512]{1,0:T(8,128)(2,1)S(1)} %bitcast.10), custom_call_target="tpu_custom_call" | custom-call | flops 100000000 | bytes 1048576 | tf_op jit(solution)/shard_map/give_back/pallas_call | solution.py:22
  107.8 0.9 finish.1
  (33 shorter events, 0.1 us)
Async XLA Ops:
  0.6 35.5 %copy-start.1 = (bf16[512,512]{1,0:T(8,128)(2,1)S(1)}, bf16[512,512]{1,0:T(8,128)(2,1)}, u32[]{:S(2)}) copy-start(bf16[512,512]{1,0:T(8,128)(2,1)} %outw_ref.3) | copy-start | bytes 1572868
  0.6 35.5 %copy-start.2 = (bf16[256,512]{1,0:T(8,128)(2,1)S(1)}, bf16[256,512]{1,0:T(8,128)(2,1)}, u32[]{:S(2)}) copy-start(bf16[256,512]{1,0:T(8,128)(2,1)} %cot_ref.5) | copy-start | bytes 786436
  0.7 35.8 %copy-start = (bf16[512,2048]{1,0:T(8,128)(2,1)S(1)}, bf16[512,2048]{1,0:T(8,128)(2,1)}, u32[]{:S(2)}) copy-start(bf16[512,2048]{1,0:T(8,128)(2,1)} %proj_ref.11) | copy-start | bytes 6291460
  0.7 1.1 %copy-start.6 = (bf16[256,512]{1,0:T(8,128)(2,1)S(1)}, bf16[256,512]{1,0:T(8,128)(2,1)}, u32[]{:S(2)}) copy-start(bf16[256,512]{1,0:T(8,128)(2,1)} %tokens_hbm.1) | copy-start | bytes 786436
  1.8 0.7 copy-start.11
  2.4 0.7 copy-start.14
  3.1 33.4 %copy-start.13 = (s32[1,3]{1,0:T(1,128)S(1)}, s32[1,3]{1,0:T(1,128)}, u32[]{:S(2)}) copy-start(s32[1,3]{1,0:T(1,128)} %lengths_ref.7) | copy-start | bytes 40
  29.0 7.1 %collective-permute-start = (bf16[256,512]{1,0:T(8,128)(2,1)}, bf16[256,512]{1,0:T(8,128)(2,1)S(1)}, u32[]{:S(2)}, u32[]{:S(2)}) collective-permute-start(bf16[256,512]{1,0:T(8,128)(2,1)} %get-tuple-element.31.normed_ref.n0_ref.refs_0_), channel_id=1, source_target_pairs={{0,2},{1,3},{2,0},{3,1},{4,6},{5,7},{6,4},{7,5},{8,10},{9,11},{10,... | collective-permute-start | bytes 786440 | tf_op jit(solution)/shard_map/ppermute | solution.py:383
  30.5 8.6 %collective-permute-start.2 = (bf16[256,512]{1,0:T(8,128)(2,1)}, bf16[256,512]{1,0:T(8,128)(2,1)}, u32[]{:S(2)}, u32[]{:S(2)}) collective-permute-start(bf16[256,512]{1,0:T(8,128)(2,1)} %get-tuple-element.31.normed_ref.n0_ref.refs_0_), channel_id=1, source_target_pairs={{0,1},{1,0},{2,3},{3,2},{4,5},{5,4},{6,7},{7,6},{8,9},{9,8},{10,11... | collective-permute-start | bytes 786440 | tf_op jit(solution)/shard_map/ppermute | solution.py:383
  36.1 4.0 %collective-permute-start.1 = (bf16[256,512]{1,0:T(8,128)(2,1)S(1)}, bf16[256,512]{1,0:T(8,128)(2,1)}, u32[]{:S(2)}, u32[]{:S(2)}) collective-permute-start(bf16[256,512]{1,0:T(8,128)(2,1)S(1)} %collective-permute-done.far_ref.n2_ref.refs_2_), channel_id=1, source_target_pairs={{0,1},{1,0},{2,3},{3,2},{4,5},{5,4},{6,7},{7,6},{8,9},{9,8},{10,11... | collective-permute-start | bytes 786440 | tf_op jit(solution)/shard_map/ppermute | solution.py:383
  42.5 9.6 %collective-permute-start.3 = (bf16[256,128]{1,0:T(8,128)(2,1)S(1)}, bf16[256,128]{1,0:T(8,128)(2,1)S(1)}, u32[]{:S(2)}, u32[]{:S(2)}) collective-permute-start(bf16[256,128]{1,0:T(8,128)(2,1)S(1)} %get-tuple-element.39), channel_id=1, source_target_pairs={{0,1},{1,0},{2,3},{3,2},{4,5},{5,4},{6,7},{7,6},{8,9},{9,8},{10,11... | collective-permute-start | bytes 196616 | tf_op jit(solution)/shard_map/ppermute | solution.py:383
  44.3 7.9 %collective-permute-start.4 = (bf16[256,128]{1,0:T(8,128)(2,1)S(1)}, bf16[256,128]{1,0:T(8,128)(2,1)S(1)}, u32[]{:S(2)}, u32[]{:S(2)}) collective-permute-start(bf16[256,128]{1,0:T(8,128)(2,1)S(1)} %get-tuple-element.40), channel_id=1, source_target_pairs={{0,2},{1,3},{2,0},{3,1},{4,6},{5,7},{6,4},{7,5},{8,10},{9,11},{10,... | collective-permute-start | bytes 196616 | tf_op jit(solution)/shard_map/ppermute | solution.py:383
  46.6 5.5 %collective-permute-start.5 = (bf16[256,128]{1,0:T(8,128)(2,1)S(1)}, bf16[256,128]{1,0:T(8,128)(2,1)S(1)}, u32[]{:S(2)}, u32[]{:S(2)}) collective-permute-start(bf16[256,128]{1,0:T(8,128)(2,1)S(1)} %get-tuple-element.41), channel_id=1, source_target_pairs={{0,3},{1,2},{2,1},{3,0},{4,7},{5,6},{6,5},{7,4},{8,11},{9,10},{10,... | collective-permute-start | bytes 196616 | tf_op jit(solution)/shard_map/ppermute | solution.py:383
  47.3 0.8 copy-start.4
  48.1 9.9 %collective-permute-start.9 = (bf16[768,128]{1,0:T(8,128)(2,1)S(1)}, bf16[768,128]{1,0:T(8,128)(2,1)S(1)}, u32[]{:S(2)}, u32[]{:S(2)}) collective-permute-start(bf16[768,128]{1,0:T(8,128)(2,1)S(1)} %get-tuple-element.53), channel_id=1, source_target_pairs={{0,1},{1,0},{2,3},{3,2},{4,5},{5,4},{6,7},{7,6},{8,9},{9,8},{10,11... | collective-permute-start | bytes 589832 | tf_op jit(solution)/shard_map/ppermute | solution.py:383
  48.2 9.8 %collective-permute-start.10 = (bf16[768,128]{1,0:T(8,128)(2,1)S(1)}, bf16[768,128]{1,0:T(8,128)(2,1)S(1)}, u32[]{:S(2)}, u32[]{:S(2)}) collective-permute-start(bf16[768,128]{1,0:T(8,128)(2,1)S(1)} %get-tuple-element.54), channel_id=1, source_target_pairs={{0,2},{1,3},{2,0},{3,1},{4,6},{5,7},{6,4},{7,5},{8,10},{9,11},{10,... | collective-permute-start | bytes 589832 | tf_op jit(solution)/shard_map/ppermute | solution.py:383
  52.1 7.3 %collective-permute-start.11 = (bf16[768,128]{1,0:T(8,128)(2,1)S(1)}, bf16[768,128]{1,0:T(8,128)(2,1)S(1)}, u32[]{:S(2)}, u32[]{:S(2)}) collective-permute-start(bf16[768,128]{1,0:T(8,128)(2,1)S(1)} %get-tuple-element.55), channel_id=1, source_target_pairs={{0,3},{1,2},{2,1},{3,0},{4,7},{5,6},{6,5},{7,4},{8,11},{9,10},{10,... | collective-permute-start | bytes 589832 | tf_op jit(solution)/shard_map/ppermute | solution.py:383
  57.7 3.9 %copy-start.15 = (bf16[256,384]{1,0:T(8,128)(2,1)}, bf16[256,384]{1,0:T(8,128)(2,1)S(1)}, u32[]{:S(2)}) copy-start(bf16[256,384]{1,0:T(8,128)(2,1)S(1)} %get-tuple-element.46.refs_6_) | copy-start | bytes 589828
  57.8 4.8 %copy-start.7 = (bf16[256,384]{1,0:T(8,128)(2,1)}, bf16[256,384]{1,0:T(8,128)(2,1)S(1)}, u32[]{:S(2)}) copy-start(bf16[256,384]{1,0:T(8,128)(2,1)S(1)} %get-tuple-element.44.g0_ref.refs_4_) | copy-start | bytes 589828
  57.8 1.7 %collective-permute-start.6 = (bf16[256,384]{1,0:T(8,128)(2,1)S(1)}, bf16[256,384]{1,0:T(8,128)(2,1)S(1)}, u32[]{:S(2)}, u32[]{:S(2)}) collective-permute-start(bf16[256,384]{1,0:T(8,128)(2,1)S(1)} %get-tuple-element.45.refs_5_), channel_id=1, source_target_pairs={{0,1},{1,0},{2,3},{3,2},{4,5},{5,4},{6,7},{7,6},{8,9},{9,8},{10,11... | collective-permute-start | bytes 589832 | tf_op jit(solution)/shard_map/ppermute | solution.py:383
  59.4 2.3 %copy-start.9 = (bf16[256,384]{1,0:T(8,128)(2,1)}, bf16[256,384]{1,0:T(8,128)(2,1)S(1)}, u32[]{:S(2)}) copy-start(bf16[256,384]{1,0:T(8,128)(2,1)S(1)} %collective-permute-done.6.g1_ref.refs_12_) | copy-start | bytes 589828
  61.7 0.9 copy-start.3
  62.6 25.3 %all-to-all-start.2 = ((bf16[8,64,640]{2,1,0:T(8,128)(2,1)}), bf16[8,64,640]{2,1,0:T(8,128)(2,1)S(1)}, u32[]{:S(2)}, u32[]{:S(2)}) async-start(bf16[8,64,640]{2,1,0:T(8,128)(2,1)} %bitcast.11), calls=%async_computation.2 | async-start | bytes 1310720 | tf_op jit(solution)/shard_map/all_to_all | solution.py:393
  70.2 8.0 %collective-permute-start.7 = (bf16[256,384]{1,0:T(8,128)(2,1)}, bf16[256,384]{1,0:T(8,128)(2,1)S(1)}, u32[]{:S(2)}, u32[]{:S(2)}) collective-permute-start(bf16[256,384]{1,0:T(8,128)(2,1)} %copy-done.15), channel_id=1, source_target_pairs={{0,2},{1,3},{2,0},{3,1},{4,6},{5,7},{6,4},{7,5},{8,10},{9,11},{10,... | collective-permute-start | bytes 589832 | tf_op jit(solution)/shard_map/ppermute | solution.py:383
  72.0 8.8 %collective-permute-start.8 = (bf16[256,384]{1,0:T(8,128)(2,1)S(1)}, bf16[256,384]{1,0:T(8,128)(2,1)S(1)}, u32[]{:S(2)}, u32[]{:S(2)}) collective-permute-start(bf16[256,384]{1,0:T(8,128)(2,1)S(1)} %get-tuple-element.47.refs_7_), channel_id=1, source_target_pairs={{0,3},{1,2},{2,1},{3,0},{4,7},{5,6},{6,5},{7,4},{8,11},{9,10},{10,... | collective-permute-start | bytes 589832 | tf_op jit(solution)/shard_map/ppermute | solution.py:383
  80.8 1.0 copy-start.5
  81.8 0.9 copy-start.8
  82.8 0.9 copy-start.10
  83.7 23.0 %copy-start.12 = (s32[256]{0:T(256)S(1)}, s32[256]{0:T(256)}, u32[]{:S(2)}) copy-start(s32[256]{0:T(256)} %param.8) | copy-start | bytes 3076
  87.8 18.8 %all-to-all-start.1 = ((bf16[8,64,512]{2,1,0:T(8,128)(2,1)}), bf16[8,64,512]{2,1,0:T(8,128)(2,1)S(1)}, u32[]{:S(2)}, u32[]{:S(2)}) async-start(bf16[8,64,512]{2,1,0:T(8,128)(2,1)} %bitcast.5), calls=%async_computation.1 | async-start | bytes 1048576 | tf_op jit(solution)/shard_map/all_to_all | solution.py:393
  91.6 5.0 %collective-permute-start.13 = (bf16[64,640]{1,0:T(8,128)(2,1)S(1)}, bf16[64,640]{1,0:T(8,128)(2,1)S(1)}, u32[]{:S(2)}, u32[]{:S(2)}) collective-permute-start(bf16[64,640]{1,0:T(8,128)(2,1)S(1)} %sum.1.w0_ref), channel_id=1, source_target_pairs={{0,2},{1,3},{2,0},{3,1},{4,6},{5,7},{6,4},{7,5},{8,10},{9,11},{10,... | collective-permute-start | bytes 245768 | tf_op jit(solution)/shard_map/ppermute | solution.py:383
  93.6 14.2 %collective-permute-start.12 = (bf16[64,640]{1,0:T(8,128)(2,1)S(1)}, bf16[64,640]{1,0:T(8,128)(2,1)S(1)}, u32[]{:S(2)}, u32[]{:S(2)}) collective-permute-start(bf16[64,640]{1,0:T(8,128)(2,1)S(1)} %sum.1.w0_ref), channel_id=1, source_target_pairs={{0,1},{1,0},{2,3},{3,2},{4,5},{5,4},{6,7},{7,6},{8,9},{9,8},{10,11... | collective-permute-start | bytes 245768 | tf_op jit(solution)/shard_map/ppermute | solution.py:383
  96.5 11.3 %collective-permute-start.14 = (bf16[64,640]{1,0:T(8,128)(2,1)S(1)}, bf16[64,640]{1,0:T(8,128)(2,1)S(1)}, u32[]{:S(2)}, u32[]{:S(2)}) collective-permute-start(bf16[64,640]{1,0:T(8,128)(2,1)S(1)} %collective-permute-done.13.w2_ref), channel_id=1, source_target_pairs={{0,1},{1,0},{2,3},{3,2},{4,5},{5,4},{6,7},{7,6},{8,9},{9,8},{10,11... | collective-permute-start | bytes 245768 | tf_op jit(solution)/shard_map/ppermute | solution.py:383

commit v3 on v2

--- a/solution.py
+++ b/solution.py
@@ -90,21 +90,28 @@
         copy.wait()
 
 
-def pack_body(
-    capacity, stride, owner_hbm, slot_hbm, tokens_hbm, out_ref, owner_ref, slot_ref, tokens_ref, sems
-):
+def store_blocks(refs, value):
+    size = refs[0].shape[0]
+    for i, ref in enumerate(refs):
+        ref[...] = value[i * size : (i + 1) * size].astype(ref.dtype)
+
+
+def load_blocks(refs):
+    return jnp.concatenate([ref[...].astype(F32) for ref in refs], axis=0).astype(BF16)
+
+
+def pack_body(capacity, stride, outs, mask_ref, owner_hbm, slot_hbm, tokens_hbm, *rest):
+    out_refs, (owner_ref, slot_ref, tokens_ref, sems) = rest[:outs], rest[outs:]
     fetch((owner_hbm, slot_hbm, tokens_hbm), (owner_ref, slot_ref, tokens_ref), sems)
-    owner = owner_ref[...]
+    owner = owner_ref[...] ^ mask_ref[0]
     rows = owner.shape[1]
     rank_row, rank_col = rank_rows(owner)
-    total, width = out_ref.shape
+    total, width = outs * out_refs[0].shape[0], out_refs[0].shape[1]
     place = iota((total, rows), 0)
     chosen = hot(place == owner * stride + rank_row)
     slots = jnp.where(place == owner * stride + capacity, slot_ref[...] + 1, 0)
     by_rank = hot(rank_col == iota((rows, width), 1))
-    out_ref[...] = (mm(chosen, tokens_ref[...]) + mm(slots.astype(F32).astype(BF16), by_rank)).astype(
-        BF16
-    )
+    store_blocks(out_refs, mm(chosen, tokens_ref[...]) + mm(slots.astype(F32).astype(BF16), by_rank))
 
 
 def block_rem(owners, stride):
@@ -122,9 +129,10 @@
     return jnp.sum(jnp.where(inside, spread, 0.0), axis=0, keepdims=True)
 
 
-def place_body(owners, capacity, stride, arrived_ref, owned_ref, normed_ref, landing_ref):
+def place_body(owners, capacity, stride, *refs):
+    owned_ref, normed_ref, landing_ref = refs[-3:]
     rows = owned_ref.shape[0]
-    arrived = arrived_ref[...]
+    arrived = load_blocks(refs[:-3])
     total = arrived.shape[0]
     pick = hot(iota((owners, total), 1) == iota((owners, total), 0) * stride + capacity)
     table = mm(pick, arrived).astype(BF16)
@@ -308,21 +316,44 @@
         ref[...] = (total_ref[at, :] * slope_ref[at, :]).astype(BF16)
 
 
-def weight_body(*refs):
-    normed, grads, sides, out_ref = refs[:4], refs[4:8], refs[8:12], refs[-1]
+def weight_body(sources, pairs, dp_ref, *refs):
+    normed, grads, sides = refs[:sources], refs[sources : 2 * sources], refs[2 * sources : 3 * sources]
+    outs, total_ref = refs[3 * sources : -1], refs[-1]
     rows, piece = normed[0].shape[0], sides[0].shape[1]
     qkv, gate, outw = 0.0, 0.0, 0.0
     for n_ref, g_ref, s_ref in zip(normed, grads, sides):
         qkv += t_mm(n_ref[...], g_ref[...])
         gate += t_mm(n_ref[...], s_ref[:rows, :])
         outw += s_ref[rows:, :].astype(F32)
-    out_ref[:, :piece] = gate.astype(BF16)
-    out_ref[:, piece : 4 * piece] = qkv.astype(BF16)
-    out_ref[:, 4 * piece :] = outw.astype(BF16)
+    total_ref[:, :piece] = gate
+    total_ref[:, piece : 4 * piece] = qkv
+    total_ref[:, 4 * piece :] = outw
+    if len(outs) == 1:
+        outs[0][...] = total_ref[...].astype(BF16)
+        return
+    kept_ref, sent_ref = outs
+    half = kept_ref.shape[0]
+    share = half // pairs
+    for j in range(pairs):
+        at = slice(j * share, (j + 1) * share)
+        for ref, k in ((kept_ref, 2 * j), (sent_ref, 2 * j + 1)):
+            source = pl.ds(pl.multiple_of((dp_ref[0] ^ k) * share, share), share)
+            ref[at, :] = total_ref[source, :].astype(BF16)
+
+
+def halve_body(pairs, kept_ref, came_ref, *refs):
+    keep_ref, send_ref = refs[-2:]
+    share = kept_ref.shape[0] // pairs
+    for j in range(pairs):
+        at = slice(j * share, (j + 1) * share)
+        to = slice(j // 2 * share, (j // 2 + 1) * share)
+        total = kept_ref[at, :].astype(F32) + came_ref[at, :].astype(F32)
+        (send_ref if j % 2 else keep_ref)[to, :] = total.astype(BF16)
 
 
 def input_body(
-    me_ref, g0_ref, g1_ref, g2_ref, g3_ref, gate_in_ref, owned_ref, cot_ref, landing_ref, proj_ref, out_ref
+    blocks, me_ref, mask_ref, g0_ref, g1_ref, g2_ref, g3_ref,
+    gate_in_ref, owned_ref, cot_ref, landing_ref, proj_ref, out_ref,
 ):
     rows, width = owned_ref.shape
     me = me_ref[0]
@@ -335,23 +366,27 @@
         total += mm_t(ref[...], jnp.concatenate(cols, axis=1))
     centred, inv_scale = normalize(owned_ref[...].astype(F32))
     grad = (norm_back(total, centred, inv_scale) + cot_ref[...].astype(F32)).astype(BF16)
-    select = hot(iota((rows, out_ref.shape[0]), 0) + 1 == landing_ref[...])
-    out_ref[...] = t_mm(select, grad).astype(BF16)
+    select = hot(iota((rows, landing_ref.shape[1]), 0) + 1 == landing_ref[...])
+    value = t_mm(select, grad)
+    size = value.shape[0] // blocks
+    for k in range(blocks):
+        at = pl.ds(pl.multiple_of((mask_ref[0] ^ k) * size, size), size)
+        out_ref[at, :] = value[k * size : (k + 1) * size].astype(BF16)
 
 
 def return_body(capacity, owner_ref, back_ref, out_ref):
     owner = owner_ref[...]
     rank_row, _ = rank_rows(owner)
-    total = back_ref.shape[0]
-    chosen = hot(iota((total, owner.shape[1]), 0) == owner * capacity + rank_row)
+    chosen = hot(iota((back_ref.shape[0], owner.shape[1]), 0) == owner * capacity + rank_row)
     out_ref[...] = t_mm(chosen, back_ref[...]).astype(BF16)
 
 
-def sum_body(parts_ref, out_ref):
-    total = parts_ref[0].astype(F32)
-    for i in range(1, parts_ref.shape[0]):
-        total += parts_ref[i].astype(F32)
-    out_ref[...] = total.astype(BF16)
+def sum_body(*refs):
+    total = 0.0
+    for ref in refs[:-1]:
+        parts = ref[...].astype(F32)
+        total += parts if ref.ndim == 2 else jnp.sum(parts, axis=0)
+    refs[-1][...] = total.astype(BF16)
 
 
 def finish_body(me_ref, w0_ref, w1_ref, w2_ref, w3_ref, proj_ref, outw_ref):
@@ -389,12 +424,31 @@
     def exchange(values):
         return [values[0]] + [hop(values[step], step) for step in (2, 3, 1)]
 
-    def swap(value):
-        return lax.all_to_all(value, "dp", split_axis=0, concat_axis=0, tiled=True)
-
-    (outgoing,) = call(
-        functools.partial(pack_body, capacity, stride),
-        "pack", [((owners * stride, width), BF16)], [], [], far=[owner_row, slot_row, tokens],
+    by_hops = owners <= 8
+    blocks = owners if by_hops else 1
+    dp = lax.axis_index("dp").astype(jnp.int32).reshape(1)
+    mask = dp if by_hops else jnp.zeros_like(dp)
+
+    def dp_hop(value, step):
+        return lax.ppermute(value, "dp", [(i, i ^ step) for i in range(owners)])
+
+    def swap_whole(value):
+        split = value.reshape(owners, value.shape[0] // owners, value.shape[1])
+        return lax.all_to_all(split, "dp", split_axis=0, concat_axis=0, tiled=True).reshape(value.shape)
+
+    def swap(values):
+        if by_hops:
+            order = sorted(range(1, owners), key=lambda k: -k)
+            moved = {k: dp_hop(values[k], k) for k in order}
+            return [values[0]] + [moved[k] for k in range(1, owners)]
+        return [swap_whole(values[0])]
+
+    def block_shapes(height, columns, dtype):
+        return [((owners * height // blocks, columns), dtype)] * blocks
+
+    outgoing = call(
+        functools.partial(pack_body, capacity, stride, blocks),
+        "pack", block_shapes(stride, width, BF16), [mask], [], far=[owner_row, slot_row, tokens],
         scratch=[
             pltpu.VMEM((1, rows), jnp.int32),
             pltpu.VMEM((1, rows), jnp.int32),
@@ -402,61 +456,80 @@
             pltpu.SemaphoreType.DMA((3,)),
         ],
     )
-    arrived = swap(outgoing.reshape(owners, stride, width)).reshape(owners * stride, width)
+    arrived = swap(outgoing)
     owned, normed, landing = call(
         functools.partial(place_body, owners, capacity, stride),
-        "place", [square, square, ((1, owners * capacity), jnp.int32)], [], [arrived],
+        "place", [square, square, ((1, owners * capacity), jnp.int32)], [], arrived,
     )
     near, far, cross = gather(normed)
     wide = ((rows, width), F32)
     (grad_gated,) = call(early_body, "early", [wide], [], [cotangent, out_weight], flops=10**8)
     gate, slope, query, partial = call(
         own_body, "own_rows", [square, wide, square, wide],
-        [me, lengths], [normed, proj_weight], flops=10**9, vmem=16,
+        [me, lengths], [normed, proj_weight], flops=10**10, vmem=16,
     )
     (partial,) = call(
         middle_body, "middle", [wide], [me, lengths], [near, far, proj_weight, query, partial],
-        flops=10**9, vmem=16,
+        flops=10**10, vmem=16,
     )
     layer_out, gated, gate_grad, *grad_pieces = call(
         forward_body, "forward",
         [square, square, square] + [((rows, piece), BF16)] * cycle,
         [me, lengths],
         [cross, proj_weight, out_weight, owned, gate, slope, query, partial, grad_gated],
-        scratch=[pltpu.VMEM((rows, width), F32)], flops=10**9, vmem=16,
+        scratch=[pltpu.VMEM((rows, width), F32)], flops=10**10, vmem=16,
     )
     r0, r2, r3, r1 = exchange(grad_pieces)
     *sides, gate_in = call(
         side_body, "side", [((rows + width, piece), BF16)] * cycle + [((rows, width), F32)],
         [me], [gated, cotangent, gate_grad, proj_weight],
-        scratch=[pltpu.VMEM((width, width), F32), pltpu.VMEM((rows, width), F32)], flops=10**9,
+        scratch=[pltpu.VMEM((width, width), F32), pltpu.VMEM((rows, width), F32)], flops=10**10,
     )
     parts, slopes = call(
         heads_body, "heads",
         [((rows * cycle, 3 * piece), BF16), ((rows * cycle, 3 * piece), F32)],
-        [me], [normed, near, far, cross, proj_weight], flops=10**9, vmem=16,
+        [me], [normed, near, far, cross, proj_weight], flops=10**10, vmem=16,
     )
     s0, s2, s3, s1 = exchange(sides)
     grads = call(
         backward_body, "backward", [((rows, 3 * piece), BF16)] * cycle,
         [me, lengths], [r0, r1, r2, r3, parts, slopes],
         scratch=[pltpu.VMEM((rows * cycle, piece), BF16), pltpu.VMEM((rows * cycle, 3 * piece), F32)],
-        flops=4 * 10**9, vmem=16,
+        flops=4 * 10**10, vmem=16,
     )
     p0, p2, p3, p1 = exchange(grads)
-    (weight_part,) = call(
-        weight_body, "weights", [((width, 5 * piece), BF16)], [],
-        [normed, near, far, cross, *grads, s0, s1, s2, s3], flops=10**9, vmem=16, far=[p1],
-    )
     share = width // owners
-    summed_parts = swap(weight_part.reshape(owners, share, 5 * piece))
+    pairs = owners // 2
+    half = ((pairs * share, 5 * piece), BF16)
+    weight_parts = call(
+        functools.partial(weight_body, cycle, pairs), "weights",
+        [half, half] if by_hops else [((width, 5 * piece), BF16)], [dp],
+        [normed, near, far, cross, *grads, s0, s1, s2, s3], flops=10**10, vmem=16,
+        scratch=[pltpu.VMEM((width, 5 * piece), F32)],
+    )
+    if by_hops:
+        kept, sent = weight_parts
+        came = dp_hop(sent, 1)
+    else:
+        summed_parts = swap_whole(weight_parts[0])
+        summed_parts = [summed_parts.reshape(owners, share, 5 * piece)]
     (back,) = call(
-        input_body, "input_grad", [((owners * capacity, width), BF16)], [me],
-        [p0, p1, p2, p3, gate_in, owned, cotangent, landing, proj_weight], flops=10**9, vmem=16,
-    )
-    returned = swap(back.reshape(owners, capacity, width)).reshape(owners * capacity, width)
-    (mine,) = call(sum_body, "sum", [((share, 5 * piece), BF16)], [], [summed_parts])
-    w1, w2, w3 = gather(mine)
+        functools.partial(input_body, blocks), "input_grad", [((owners * capacity, width), BF16)], [me, mask],
+        [p0, p1, p2, p3, gate_in, owned, cotangent, landing, proj_weight], flops=2 * 10**10, vmem=16,
+    )
+    returned = swap_whole(back)
+    if by_hops:
+        behind, bit = [back], 2
+        while bit < owners:
+            kept, sent = call(
+                functools.partial(halve_body, pairs), "halve",
+                [((pairs * share // 2, 5 * piece), BF16)] * 2, [], [kept, came], far=behind,
+            )
+            came = dp_hop(sent, bit)
+            behind, bit, pairs = [], 2 * bit, pairs // 2
+        summed_parts = [kept, came]
+    (mine,) = call(sum_body, "sum", [((share, 5 * piece), BF16)], [], summed_parts)
+    w1, w2, w3 = (hop(mine, step) for step in range(1, cycle))
     (grad_tokens,) = call(
         functools.partial(return_body, capacity), "give_back", [square], [], [owner_row, returned]
     )

time: 109 us -> 110 us (level)
  blocking collectives: 23.6 us -> 0 us
  starting transfers between devices: 23.3 us -> 42.2 us
  waiting for transfers between devices: 31 us -> 40 us
  Pallas kernels: 22.9 us -> 19 us
    all_to_all x1 -> x0, blocking collectives: 23.6 us -> none  [swap(): return lax.all_to_all(value, 'dp', split_axis=0, concat_axis=0, tiled=True)]
    ppermute x0 -> x10, waiting for transfers between devices: none -> 23.5 us  [dp_hop(): return lax.ppermute(value, 'dp', [(i, i ^ step) for i in range(owners)])]
    ppermute x0 -> x10, starting transfers between devices: none -> 20.7 us  [dp_hop(): return lax.ppermute(value, 'dp', [(i, i ^ step) for i in range(owners)])]
    all_to_all x2 -> x1, waiting for transfers between devices: 12.2 us -> 0.01 us  [swap_whole(): lax.all_to_all(split, 'dp', split_axis=0, concat_axis=0, tiled=True)]
    pallas_call x14 -> x16, Pallas kernels: 22.9 us -> 19 us  [call(): pl.pallas_call(body, name=name, out_shape=[jax.ShapeDtypeStruct(s, d) for...]
    ppermute x15, waiting for transfers between devices: 18.7 us -> 16.5 us  [hop(): return lax.ppermute(value, 'ctx', [(i, i ^ step) for i in range(cycle)])]
    all_to_all x2 -> x1, starting transfers between devices: 11.3 us -> 10.3 us  [swap_whole(): lax.all_to_all(split, 'dp', split_axis=0, concat_axis=0, tiled=True)]
    unnamed x32 -> x30, local copies, waits for them, and re-layouts: 7.01 us -> 7.77 us
  transfers between devices with their start and end apart: 17 -> 26, of which waited for: 7 -> 13; matrix products, arithmetic and copies ran while one was open for 0% -> 0% of each run, Pallas kernels for 14% -> 8%
where the time goes in v3:
time: 110 us
  starting transfers between devices  42.2 us (38%)
  waiting for transfers between devices  40 us (36%)
  Pallas kernels  19 us (17%)
  local copies, waits for them, and re-layouts  7.77 us (7%)
    ppermute x10, waiting for transfers between devices, dp_hop(): return lax.ppermute(value, 'dp', [(i, i ^ step) for i in range(owners)])  23.5 us
    ppermute x10, starting transfers between devices, dp_hop(): return lax.ppermute(value, 'dp', [(i, i ^ step) for i in range(owners)])  20.7 us
    pallas_call x16, Pallas kernels, call(): pl.pallas_call(body, name=name, out_shape=[jax.ShapeDtypeStruct(s, d) for...  19 us
    ppermute x15, waiting for transfers between devices, hop(): return lax.ppermute(value, 'ctx', [(i, i ^ step) for i in range(cycle)])  16.5 us
    ppermute x15, starting transfers between devices, hop(): return lax.ppermute(value, 'ctx', [(i, i ^ step) for i in range(cycle)])  11.2 us
    all_to_all x1, starting transfers between devices, swap_whole(): lax.all_to_all(split, 'dp', split_axis=0, concat_axis=0, tiled=True)  10.3 us
    unnamed x30, local copies, waits for them, and re-layouts  7.77 us
  transfers between devices with their start and end apart: 26, of which 13 were waited for; matrix products, arithmetic and copies ran while one was open for 0% of the time, Pallas kernels for 8%

profile of v3, /device:TPU:0, one launch (start us, length us, event | category | flops | bytes accessed | tf_op | source)
XLA Modules:
  0.0 109.8 jit_solution(5213510190061006856)
XLA Ops:
  0.7 0.7 copy-done.4
  1.3 0.9 copy-done.8
  2.3 0.7 copy-done.9
  3.0 0.7 pack.1
  3.7 3.0 %collective-permute-start = (bf16[72,512]{1,0:T(8,128)(2,1)S(1)}, bf16[72,512]{1,0:T(8,128)(2,1)S(1)}, u32[]{:S(2)}, u32[]{:S(2)}) collective-permute-start(bf16[72,512]{1,0:T(8,128)(2,1)S(1)} %get-tuple-element.46), channel_id=1, source_target_pairs={{0,4},{4,0},{8,12},{12,8},{16,20},{20,16},{24,28},{28,24},{1,5},{5... | collective-permute-start | bytes 221192 | tf_op jit(solution)/shard_map/ppermute | solution.py:433
  6.7 1.6 %collective-permute-start.1 = (bf16[72,512]{1,0:T(8,128)(2,1)S(1)}, bf16[72,512]{1,0:T(8,128)(2,1)S(1)}, u32[]{:S(2)}, u32[]{:S(2)}) collective-permute-start(bf16[72,512]{1,0:T(8,128)(2,1)S(1)} %get-tuple-element.47), channel_id=1, source_target_pairs={{0,8},{4,12},{8,0},{12,4},{16,24},{20,28},{24,16},{28,20},{1,9},{5... | collective-permute-start | bytes 221192 | tf_op jit(solution)/shard_map/ppermute | solution.py:433
  8.3 3.0 %collective-permute-start.3 = (bf16[72,512]{1,0:T(8,128)(2,1)S(1)}, bf16[72,512]{1,0:T(8,128)(2,1)S(1)}, u32[]{:S(2)}, u32[]{:S(2)}) collective-permute-start(bf16[72,512]{1,0:T(8,128)(2,1)S(1)} %get-tuple-element.49), channel_id=1, source_target_pairs={{0,16},{4,20},{8,24},{12,28},{16,0},{20,4},{24,8},{28,12},{1,17},{... | collective-permute-start | bytes 221192 | tf_op jit(solution)/shard_map/ppermute | solution.py:433
  11.3 1.3 %collective-permute-start.4 = (bf16[72,512]{1,0:T(8,128)(2,1)S(1)}, bf16[72,512]{1,0:T(8,128)(2,1)S(1)}, u32[]{:S(2)}, u32[]{:S(2)}) collective-permute-start(bf16[72,512]{1,0:T(8,128)(2,1)S(1)} %get-tuple-element.50), channel_id=1, source_target_pairs={{0,20},{4,16},{8,28},{12,24},{16,4},{20,0},{24,12},{28,8},{1,21},{... | collective-permute-start | bytes 221192 | tf_op jit(solution)/shard_map/ppermute | solution.py:433
  12.6 3.6 %collective-permute-start.5 = (bf16[72,512]{1,0:T(8,128)(2,1)S(1)}, bf16[72,512]{1,0:T(8,128)(2,1)S(1)}, u32[]{:S(2)}, u32[]{:S(2)}) collective-permute-start(bf16[72,512]{1,0:T(8,128)(2,1)S(1)} %get-tuple-element.51), channel_id=1, source_target_pairs={{0,24},{4,28},{8,16},{12,20},{16,8},{20,12},{24,0},{28,4},{1,25},{... | collective-permute-start | bytes 221192 | tf_op jit(solution)/shard_map/ppermute | solution.py:433
  16.2 1.0 copy-done
  17.2 0.9 copy-done.2
  18.5 4.0 %collective-permute-done.4.refs_5_ = bf16[72,512]{1,0:T(8,128)(2,1)S(1)} collective-permute-done((bf16[72,512]{1,0:T(8,128)(2,1)S(1)}, bf16[72,512]{1,0:T(8,128)(2,1)S(1)}, u32[]{:S(2)}, u32[]{:S(2)}) %collective-permute-start.4) | collective-permute-done | bytes 73760 | tf_op jit(solution)/shard_map/ppermute | solution.py:433
  22.5 0.8 collective-permute-done.6.refs_7_
  23.3 0.8 place.1
  24.2 1.6 %collective-permute-start.7 = (bf16[256,512]{1,0:T(8,128)(2,1)S(1)}, bf16[256,512]{1,0:T(8,128)(2,1)S(1)}, u32[]{:S(2)}, u32[]{:S(2)}) collective-permute-start(bf16[256,512]{1,0:T(8,128)(2,1)S(1)} %get-tuple-element.53.normed_ref.n0_ref.refs_0_), channel_id=1, source_target_pairs={{0,2},{1,3},{2,0},{3,1},{4,6},{5,7},{6,4},{7,5},{8,10},{9,11},{10,... | collective-permute-start | bytes 786440 | tf_op jit(solution)/shard_map/ppermute | solution.py:418
  25.7 1.6 %copy-done.6 = bf16[512,2048]{1,0:T(8,128)(2,1)S(1)} copy-done((bf16[512,2048]{1,0:T(8,128)(2,1)S(1)}, bf16[512,2048]{1,0:T(8,128)(2,1)}, u32[]{:S(2)}) %copy-start.6) | copy-done | bytes 2097176
  27.3 2.2 %own_rows.1 = (bf16[256,512]{1,0:T(8,128)(2,1)S(1)}, f32[256,512]{1,0:T(8,128)S(1)}, bf16[256,512]{1,0:T(8,128)(2,1)S(1)}, f32[256,512]{1,0:T(8,128)S(1)}) custom-call(s32[1]{0:T(128)} %bitcast.me_ref, s32[1,3]{1,0:T(1,128)S(1)} %copy-done.10, bf16[256,512]{1,0:T(8,128)(2,1)S(1)} %get-tuple-element.53.normed_ref.n0_ref.refs_0_, bf16[512,2048]{1,0:T(8,128)(2,1)S(1)} %copy-done.6), custom_call_target="tpu_custom_call" | custom-call | flops 10000000000 | bytes 1048576 | tf_op jit(solution)/shard_map/own_rows/pallas_call | solution.py:22
  29.5 1.1 collective-permute-done.7.far_ref.n2_ref.refs_2_
  31.2 0.9 collective-permute-done.8.cross_ref.n3_ref.refs_3_
  32.1 1.9 %forward.1 = (bf16[256,512]{1,0:T(8,128)(2,1)}, bf16[256,512]{1,0:T(8,128)(2,1)S(1)}, bf16[256,512]{1,0:T(8,128)(2,1)S(1)}, bf16[256,128]{1,0:T(8,128)(2,1)S(1)}...) custom-call(s32[1]{0:T(128)} %bitcast.me_ref, s32[1,3]{1,0:T(1,128)S(1)} %copy-done.10, ...), custom_call_target="tpu_custom_call" | custom-call | flops 10000000000 | bytes 1048576 | tf_op jit(solution)/shard_map/forward/pallas_call | solution.py:22
  34.2 3.7 %collective-permute-start.11 = (bf16[256,128]{1,0:T(8,128)(2,1)S(1)}, bf16[256,128]{1,0:T(8,128)(2,1)S(1)}, u32[]{:S(2)}, u32[]{:S(2)}) collective-permute-start(bf16[256,128]{1,0:T(8,128)(2,1)S(1)} %get-tuple-element.62), channel_id=1, source_target_pairs={{0,2},{1,3},{2,0},{3,1},{4,6},{5,7},{6,4},{7,5},{8,10},{9,11},{10,... | collective-permute-start | bytes 196616 | tf_op jit(solution)/shard_map/ppermute | solution.py:418
  37.9 0.8 heads.1
  38.7 1.4 %collective-permute-done.11.g2_ref = bf16[256,128]{1,0:T(8,128)(2,1)S(1)} collective-permute-done((bf16[256,128]{1,0:T(8,128)(2,1)S(1)}, bf16[256,128]{1,0:T(8,128)(2,1)S(1)}, u32[]{:S(2)}, u32[]{:S(2)}) %collective-permute-start.11) | collective-permute-done | bytes 65568 | tf_op jit(solution)/shard_map/ppermute | solution.py:418
  40.1 2.0 %collective-permute-done.12.g3_ref = bf16[256,128]{1,0:T(8,128)(2,1)S(1)} collective-permute-done((bf16[256,128]{1,0:T(8,128)(2,1)S(1)}, bf16[256,128]{1,0:T(8,128)(2,1)S(1)}, u32[]{:S(2)}, u32[]{:S(2)}) %collective-permute-start.12) | collective-permute-done | bytes 65568 | tf_op jit(solution)/shard_map/ppermute | solution.py:418
  42.2 5.7 %backward.1 = (bf16[256,384]{1,0:T(8,128)(2,1)S(1)}, bf16[256,384]{1,0:T(8,128)(2,1)S(1)}, bf16[256,384]{1,0:T(8,128)(2,1)S(1)}, bf16[256,384]{1,0:T(8,128)(2,1)S(1)}) custom-call(s32[1]{0:T(128)} %bitcast.me_ref, s32[1,3]{1,0:T(1,128)S(1)} %copy-done.10, bf16[256,128]{1,0:T(8,128)(2,1)S(1)} %get-tuple-element.60.g0_ref, ...), custom_call_target="tpu_custom_call" | custom-call | flops 40000000000 | bytes 1048576 | tf_op jit(solution)/shard_map/backward/pallas_call | solution.py:22
  48.0 0.9 collective-permute-start.14
  48.9 0.9 collective-permute-start.15
  50.8 0.9 collective-permute-start.17
  51.7 0.7 collective-permute-start.18
  52.4 3.4 %collective-permute-done.14.g2_ref = bf16[256,384]{1,0:T(8,128)(2,1)S(1)} collective-permute-done((bf16[256,384]{1,0:T(8,128)(2,1)S(1)}, bf16[256,384]{1,0:T(8,128)(2,1)S(1)}, u32[]{:S(2)}, u32[]{:S(2)}) %collective-permute-start.14) | collective-permute-done | bytes 196640 | tf_op jit(solution)/shard_map/ppermute | solution.py:418
  55.8 3.3 %collective-permute-done.15.g3_ref = bf16[256,384]{1,0:T(8,128)(2,1)S(1)} collective-permute-done((bf16[256,384]{1,0:T(8,128)(2,1)S(1)}, bf16[256,384]{1,0:T(8,128)(2,1)S(1)}, u32[]{:S(2)}, u32[]{:S(2)}) %collective-permute-start.15) | collective-permute-done | bytes 196640 | tf_op jit(solution)/shard_map/ppermute | solution.py:418
  59.1 2.0 %input_grad.1.refs_0_ = bf16[512,512]{1,0:T(8,128)(2,1)} custom-call(s32[1]{0:T(128)} %bitcast.me_ref, s32[1]{0:T(128)} %bitcast.1.mask_ref.dp_ref, bf16[256,384]{1,0:T(8,128)(2,1)S(1)} %get-tuple-element.66.g0_ref.refs_4_, bf16[256,384]{1,0:T(8,128)(2,1)S(1)} %collective-permute-done.13.g1_ref, bf16[256,384]{1,0:T(8,128)(2,1)S(1)} %collective-permute-done.14.g2_ref, ...), custom_call_target="tpu_custom_call" | custom-call | flops 20000000000 | bytes 1048576 | tf_op jit(solution)/shard_map/input_grad/pallas_call | solution.py:22
  61.1 10.3 %all-to-all-start = ((bf16[8,64,512]{2,1,0:T(8,128)(2,1)}), bf16[8,64,512]{2,1,0:T(8,128)(2,1)S(1)}, u32[]{:S(2)}, u32[]{:S(2)}) async-start(bf16[8,64,512]{2,1,0:T(8,128)(2,1)} %bitcast.4), calls=%async_computation | async-start | bytes 1048576 | tf_op jit(solution)/shard_map/all_to_all | solution.py:437
  71.4 0.9 copy-done.12
  72.4 0.9 copy-done.14
  73.3 1.1 weights.1
  74.4 2.1 %collective-permute-start.19 = (bf16[256,640]{1,0:T(8,128)(2,1)S(1)}, bf16[256,640]{1,0:T(8,128)(2,1)S(1)}, u32[]{:S(2)}, u32[]{:S(2)}) collective-permute-start(bf16[256,640]{1,0:T(8,128)(2,1)S(1)} %get-tuple-element.79), channel_id=1, source_target_pairs={{0,4},{4,0},{8,12},{12,8},{16,20},{20,16},{24,28},{28,24},{1,5},{5... | collective-permute-start | bytes 983048 | tf_op jit(solution)/shard_map/ppermute | solution.py:433
  76.5 11.3 %collective-permute-done.19.came_ref = bf16[256,640]{1,0:T(8,128)(2,1)S(1)} collective-permute-done((bf16[256,640]{1,0:T(8,128)(2,1)S(1)}, bf16[256,640]{1,0:T(8,128)(2,1)S(1)}, u32[]{:S(2)}, u32[]{:S(2)}) %collective-permute-start.19) | collective-permute-done | bytes 327712 | tf_op jit(solution)/shard_map/ppermute | solution.py:433
  87.8 2.2 %collective-permute-start.20 = (bf16[128,640]{1,0:T(8,128)(2,1)S(1)}, bf16[128,640]{1,0:T(8,128)(2,1)S(1)}, u32[]{:S(2)}, u32[]{:S(2)}) collective-permute-start(bf16[128,640]{1,0:T(8,128)(2,1)S(1)} %get-tuple-element.81), channel_id=1, source_target_pairs={{0,8},{4,12},{8,0},{12,4},{16,24},{20,28},{24,16},{28,20},{1,9},{5... | collective-permute-start | bytes 491528 | tf_op jit(solution)/shard_map/ppermute | solution.py:433
  90.1 4.1 %collective-permute-done.20.came_ref = bf16[128,640]{1,0:T(8,128)(2,1)S(1)} collective-permute-done((bf16[128,640]{1,0:T(8,128)(2,1)S(1)}, bf16[128,640]{1,0:T(8,128)(2,1)S(1)}, u32[]{:S(2)}, u32[]{:S(2)}) %collective-permute-start.20) | collective-permute-done | bytes 163872 | tf_op jit(solution)/shard_map/ppermute | solution.py:433
  94.3 3.9 %collective-permute-start.21 = (bf16[64,640]{1,0:T(8,128)(2,1)S(1)}, bf16[64,640]{1,0:T(8,128)(2,1)S(1)}, u32[]{:S(2)}, u32[]{:S(2)}) collective-permute-start(bf16[64,640]{1,0:T(8,128)(2,1)S(1)} %get-tuple-element.83), channel_id=1, source_target_pairs={{0,16},{4,20},{8,24},{12,28},{16,0},{20,4},{24,8},{28,12},{1,17},{... | collective-permute-start | bytes 245768 | tf_op jit(solution)/shard_map/ppermute | solution.py:433
  98.2 3.3 %collective-permute-done.21.refs_1_ = bf16[64,640]{1,0:T(8,128)(2,1)S(1)} collective-permute-done((bf16[64,640]{1,0:T(8,128)(2,1)S(1)}, bf16[64,640]{1,0:T(8,128)(2,1)S(1)}, u32[]{:S(2)}, u32[]{:S(2)}) %collective-permute-start.21) | collective-permute-done | bytes 81952 | tf_op jit(solution)/shard_map/ppermute | solution.py:433
  101.6 0.9 collective-permute-start.23
  102.5 0.9 collective-permute-start.24
  103.4 3.4 %collective-permute-done.23.w2_ref = bf16[64,640]{1,0:T(8,128)(2,1)S(1)} collective-permute-done((bf16[64,640]{1,0:T(8,128)(2,1)S(1)}, bf16[64,640]{1,0:T(8,128)(2,1)S(1)}, u32[]{:S(2)}, u32[]{:S(2)}) %collective-permute-start.23) | collective-permute-done | bytes 81952 | tf_op jit(solution)/shard_map/ppermute | solution.py:418
  106.9 0.8 collective-permute-done.24.w3_ref
  107.7 0.9 finish.1
  108.6 1.2 %give_back.1 = bf16[256,512]{1,0:T(8,128)(2,1)} custom-call(s32[1,256]{1,0:T(1,128)S(1)} %bitcast.8, bf16[512,512]{1,0:T(8,128)(2,1)S(1)} %bitcast.6), custom_call_target="tpu_custom_call" | custom-call | flops 100000000 | bytes 1048576 | tf_op jit(solution)/shard_map/give_back/pallas_call | solution.py:22
  (50 shorter events, 2.4 us)
Async XLA Ops:
  0.6 25.1 %copy-start.10 = (s32[1,3]{1,0:T(1,128)S(1)}, s32[1,3]{1,0:T(1,128)}, u32[]{:S(2)}) copy-start(s32[1,3]{1,0:T(1,128)} %lengths_ref.7) | copy-start | bytes 40
  0.6 0.7 copy-start.4
  1.3 0.9 copy-start.8
  2.3 0.7 copy-start.9
  3.7 8.9 %collective-permute-start = (bf16[72,512]{1,0:T(8,128)(2,1)S(1)}, bf16[72,512]{1,0:T(8,128)(2,1)S(1)}, u32[]{:S(2)}, u32[]{:S(2)}) collective-permute-start(bf16[72,512]{1,0:T(8,128)(2,1)S(1)} %get-tuple-element.46), channel_id=1, source_target_pairs={{0,4},{4,0},{8,12},{12,8},{16,20},{20,16},{24,28},{28,24},{1,5},{5... | collective-permute-start | bytes 221192 | tf_op jit(solution)/shard_map/ppermute | solution.py:433
  6.7 9.5 %collective-permute-start.1 = (bf16[72,512]{1,0:T(8,128)(2,1)S(1)}, bf16[72,512]{1,0:T(8,128)(2,1)S(1)}, u32[]{:S(2)}, u32[]{:S(2)}) collective-permute-start(bf16[72,512]{1,0:T(8,128)(2,1)S(1)} %get-tuple-element.47), channel_id=1, source_target_pairs={{0,8},{4,12},{8,0},{12,4},{16,24},{20,28},{24,16},{28,20},{1,9},{5... | collective-permute-start | bytes 221192 | tf_op jit(solution)/shard_map/ppermute | solution.py:433
  8.3 10.2 %collective-permute-start.2 = (bf16[72,512]{1,0:T(8,128)(2,1)S(1)}, bf16[72,512]{1,0:T(8,128)(2,1)S(1)}, u32[]{:S(2)}, u32[]{:S(2)}) collective-permute-start(bf16[72,512]{1,0:T(8,128)(2,1)S(1)} %get-tuple-element.48), channel_id=1, source_target_pairs={{0,12},{4,8},{8,4},{12,0},{16,28},{20,24},{24,20},{28,16},{1,13},{... | collective-permute-start | bytes 221192 | tf_op jit(solution)/shard_map/ppermute | solution.py:433
  8.3 10.2 %collective-permute-start.3 = (bf16[72,512]{1,0:T(8,128)(2,1)S(1)}, bf16[72,512]{1,0:T(8,128)(2,1)S(1)}, u32[]{:S(2)}, u32[]{:S(2)}) collective-permute-start(bf16[72,512]{1,0:T(8,128)(2,1)S(1)} %get-tuple-element.49), channel_id=1, source_target_pairs={{0,16},{4,20},{8,24},{12,28},{16,0},{20,4},{24,8},{28,12},{1,17},{... | collective-permute-start | bytes 221192 | tf_op jit(solution)/shard_map/ppermute | solution.py:433
  11.3 11.3 %collective-permute-start.4 = (bf16[72,512]{1,0:T(8,128)(2,1)S(1)}, bf16[72,512]{1,0:T(8,128)(2,1)S(1)}, u32[]{:S(2)}, u32[]{:S(2)}) collective-permute-start(bf16[72,512]{1,0:T(8,128)(2,1)S(1)} %get-tuple-element.50), channel_id=1, source_target_pairs={{0,20},{4,16},{8,28},{12,24},{16,4},{20,0},{24,12},{28,8},{1,21},{... | collective-permute-start | bytes 221192 | tf_op jit(solution)/shard_map/ppermute | solution.py:433
  12.6 10.0 %collective-permute-start.5 = (bf16[72,512]{1,0:T(8,128)(2,1)S(1)}, bf16[72,512]{1,0:T(8,128)(2,1)S(1)}, u32[]{:S(2)}, u32[]{:S(2)}) collective-permute-start(bf16[72,512]{1,0:T(8,128)(2,1)S(1)} %get-tuple-element.51), channel_id=1, source_target_pairs={{0,24},{4,28},{8,16},{12,20},{16,8},{20,12},{24,0},{28,4},{1,25},{... | collective-permute-start | bytes 221192 | tf_op jit(solution)/shard_map/ppermute | solution.py:433
  16.2 7.2 %collective-permute-start.6 = (bf16[72,512]{1,0:T(8,128)(2,1)S(1)}, bf16[72,512]{1,0:T(8,128)(2,1)S(1)}, u32[]{:S(2)}, u32[]{:S(2)}) collective-permute-start(bf16[72,512]{1,0:T(8,128)(2,1)S(1)} %get-tuple-element.52), channel_id=1, source_target_pairs={{0,28},{4,24},{8,20},{12,16},{16,12},{20,8},{24,4},{28,0},{1,29},{... | collective-permute-start | bytes 221192 | tf_op jit(solution)/shard_map/ppermute | solution.py:433
  16.2 1.0 copy-start
  17.2 0.9 copy-start.2
  24.2 6.4 %collective-permute-start.7 = (bf16[256,512]{1,0:T(8,128)(2,1)S(1)}, bf16[256,512]{1,0:T(8,128)(2,1)S(1)}, u32[]{:S(2)}, u32[]{:S(2)}) collective-permute-start(bf16[256,512]{1,0:T(8,128)(2,1)S(1)} %get-tuple-element.53.normed_ref.n0_ref.refs_0_), channel_id=1, source_target_pairs={{0,2},{1,3},{2,0},{3,1},{4,6},{5,7},{6,4},{7,5},{8,10},{9,11},{10,... | collective-permute-start | bytes 786440 | tf_op jit(solution)/shard_map/ppermute | solution.py:418
  25.7 4.9 %collective-permute-start.9 = (bf16[256,512]{1,0:T(8,128)(2,1)S(1)}, bf16[256,512]{1,0:T(8,128)(2,1)S(1)}, u32[]{:S(2)}, u32[]{:S(2)}) collective-permute-start(bf16[256,512]{1,0:T(8,128)(2,1)S(1)} %get-tuple-element.53.normed_ref.n0_ref.refs_0_), channel_id=1, source_target_pairs={{0,1},{1,0},{2,3},{3,2},{4,5},{5,4},{6,7},{7,6},{8,9},{9,8},{10,11... | collective-permute-start | bytes 786440 | tf_op jit(solution)/shard_map/ppermute | solution.py:418
  25.7 1.6 %copy-start.6 = (bf16[512,2048]{1,0:T(8,128)(2,1)S(1)}, bf16[512,2048]{1,0:T(8,128)(2,1)}, u32[]{:S(2)}) copy-start(bf16[512,2048]{1,0:T(8,128)(2,1)} %proj_ref.11) | copy-start | bytes 6291460
  27.3 3.3 %copy-start.7 = (bf16[512,2048]{1,0:T(8,128)(2,1)S(1)}, bf16[512,2048]{1,0:T(8,128)(2,1)}, u32[]{:S(2)}) copy-start(bf16[512,2048]{1,0:T(8,128)(2,1)} %proj_ref.11) | copy-start | bytes 6291460
  30.6 1.5 %collective-permute-start.8 = (bf16[256,512]{1,0:T(8,128)(2,1)S(1)}, bf16[256,512]{1,0:T(8,128)(2,1)S(1)}, u32[]{:S(2)}, u32[]{:S(2)}) collective-permute-start(bf16[256,512]{1,0:T(8,128)(2,1)S(1)} %collective-permute-done.7.far_ref.n2_ref.refs_2_), channel_id=1, source_target_pairs={{0,1},{1,0},{2,3},{3,2},{4,5},{5,4},{6,7},{7,6},{8,9},{9,8},{10,11... | collective-permute-start | bytes 786440 | tf_op jit(solution)/shard_map/ppermute | solution.py:418
  30.6 1.5 %copy-start.1 = (bf16[512,512]{1,0:T(8,128)(2,1)S(1)}, bf16[512,512]{1,0:T(8,128)(2,1)}, u32[]{:S(2)}) copy-start(bf16[512,512]{1,0:T(8,128)(2,1)} %outw_ref.3) | copy-start | bytes 1572868
  34.1 4.7 %collective-permute-start.10 = (bf16[256,128]{1,0:T(8,128)(2,1)S(1)}, bf16[256,128]{1,0:T(8,128)(2,1)S(1)}, u32[]{:S(2)}, u32[]{:S(2)}) collective-permute-start(bf16[256,128]{1,0:T(8,128)(2,1)S(1)} %get-tuple-element.61), channel_id=1, source_target_pairs={{0,1},{1,0},{2,3},{3,2},{4,5},{5,4},{6,7},{7,6},{8,9},{9,8},{10,11... | collective-permute-start | bytes 196616 | tf_op jit(solution)/shard_map/ppermute | solution.py:418
  34.2 5.9 %collective-permute-start.11 = (bf16[256,128]{1,0:T(8,128)(2,1)S(1)}, bf16[256,128]{1,0:T(8,128)(2,1)S(1)}, u32[]{:S(2)}, u32[]{:S(2)}) collective-permute-start(bf16[256,128]{1,0:T(8,128)(2,1)S(1)} %get-tuple-element.62), channel_id=1, source_target_pairs={{0,2},{1,3},{2,0},{3,1},{4,6},{5,7},{6,4},{7,5},{8,10},{9,11},{10,... | collective-permute-start | bytes 196616 | tf_op jit(solution)/shard_map/ppermute | solution.py:418
  37.9 4.3 %collective-permute-start.12 = (bf16[256,128]{1,0:T(8,128)(2,1)S(1)}, bf16[256,128]{1,0:T(8,128)(2,1)S(1)}, u32[]{:S(2)}, u32[]{:S(2)}) collective-permute-start(bf16[256,128]{1,0:T(8,128)(2,1)S(1)} %get-tuple-element.63), channel_id=1, source_target_pairs={{0,3},{1,2},{2,1},{3,0},{4,7},{5,6},{6,5},{7,4},{8,11},{9,10},{10,... | collective-permute-start | bytes 196616 | tf_op jit(solution)/shard_map/ppermute | solution.py:418
  42.2 7.7 %copy-start.3 = (bf16[256,512]{1,0:T(8,128)(2,1)S(1)}, bf16[256,512]{1,0:T(8,128)(2,1)}, u32[]{:S(2)}) copy-start(bf16[256,512]{1,0:T(8,128)(2,1)} %cot_ref.5) | copy-start | bytes 786436
  47.9 11.2 %copy-start.13 = (bf16[256,384]{1,0:T(8,128)(2,1)}, bf16[256,384]{1,0:T(8,128)(2,1)S(1)}, u32[]{:S(2)}) copy-start(bf16[256,384]{1,0:T(8,128)(2,1)S(1)} %get-tuple-element.66.g0_ref.refs_4_) | copy-start | bytes 589828
  47.9 3.8 %collective-permute-start.13 = (bf16[256,384]{1,0:T(8,128)(2,1)S(1)}, bf16[256,384]{1,0:T(8,128)(2,1)S(1)}, u32[]{:S(2)}, u32[]{:S(2)}) collective-permute-start(bf16[256,384]{1,0:T(8,128)(2,1)S(1)} %get-tuple-element.67.refs_5_), channel_id=1, source_target_pairs={{0,1},{1,0},{2,3},{3,2},{4,5},{5,4},{6,7},{7,6},{8,9},{9,8},{10,11... | collective-permute-start | bytes 589832 | tf_op jit(solution)/shard_map/ppermute | solution.py:418
  48.0 7.8 %collective-permute-start.14 = (bf16[256,384]{1,0:T(8,128)(2,1)S(1)}, bf16[256,384]{1,0:T(8,128)(2,1)S(1)}, u32[]{:S(2)}, u32[]{:S(2)}) collective-permute-start(bf16[256,384]{1,0:T(8,128)(2,1)S(1)} %get-tuple-element.68.refs_6_), channel_id=1, source_target_pairs={{0,2},{1,3},{2,0},{3,1},{4,6},{5,7},{6,4},{7,5},{8,10},{9,11},{10,... | collective-permute-start | bytes 589832 | tf_op jit(solution)/shard_map/ppermute | solution.py:418
  48.9 10.2 %collective-permute-start.15 = (bf16[256,384]{1,0:T(8,128)(2,1)S(1)}, bf16[256,384]{1,0:T(8,128)(2,1)S(1)}, u32[]{:S(2)}, u32[]{:S(2)}) collective-permute-start(bf16[256,384]{1,0:T(8,128)(2,1)S(1)} %get-tuple-element.69.refs_7_), channel_id=1, source_target_pairs={{0,3},{1,2},{2,1},{3,0},{4,7},{5,6},{6,5},{7,4},{8,11},{9,10},{10,... | collective-permute-start | bytes 589832 | tf_op jit(solution)/shard_map/ppermute | solution.py:418
  50.4 10.7 %copy-start.11 = (bf16[768,128]{1,0:T(8,128)(2,1)}, bf16[768,128]{1,0:T(8,128)(2,1)S(1)}, u32[]{:S(2)}) copy-start(bf16[768,128]{1,0:T(8,128)(2,1)S(1)} %get-tuple-element.74.refs_8_) | copy-start | bytes 589828
  50.4 21.0 %collective-permute-start.16 = (bf16[768,128]{1,0:T(8,128)(2,1)S(1)}, bf16[768,128]{1,0:T(8,128)(2,1)S(1)}, u32[]{:S(2)}, u32[]{:S(2)}) collective-permute-start(bf16[768,128]{1,0:T(8,128)(2,1)S(1)} %get-tuple-element.75), channel_id=1, source_target_pairs={{0,1},{1,0},{2,3},{3,2},{4,5},{5,4},{6,7},{7,6},{8,9},{9,8},{10,11... | collective-permute-start | bytes 589832 | tf_op jit(solution)/shard_map/ppermute | solution.py:418
  50.8 20.6 %collective-permute-start.17 = (bf16[768,128]{1,0:T(8,128)(2,1)S(1)}, bf16[768,128]{1,0:T(8,128)(2,1)S(1)}, u32[]{:S(2)}, u32[]{:S(2)}) collective-permute-start(bf16[768,128]{1,0:T(8,128)(2,1)S(1)} %get-tuple-element.76), channel_id=1, source_target_pairs={{0,2},{1,3},{2,0},{3,1},{4,6},{5,7},{6,4},{7,5},{8,10},{9,11},{10,... | collective-permute-start | bytes 589832 | tf_op jit(solution)/shard_map/ppermute | solution.py:418
  51.7 19.7 %collective-permute-start.18 = (bf16[768,128]{1,0:T(8,128)(2,1)S(1)}, bf16[768,128]{1,0:T(8,128)(2,1)S(1)}, u32[]{:S(2)}, u32[]{:S(2)}) collective-permute-start(bf16[768,128]{1,0:T(8,128)(2,1)S(1)} %get-tuple-element.77), channel_id=1, source_target_pairs={{0,3},{1,2},{2,1},{3,0},{4,7},{5,6},{6,5},{7,4},{8,11},{9,10},{10,... | collective-permute-start | bytes 589832 | tf_op jit(solution)/shard_map/ppermute | solution.py:418
  61.1 47.5 %all-to-all-start = ((bf16[8,64,512]{2,1,0:T(8,128)(2,1)}), bf16[8,64,512]{2,1,0:T(8,128)(2,1)S(1)}, u32[]{:S(2)}, u32[]{:S(2)}) async-start(bf16[8,64,512]{2,1,0:T(8,128)(2,1)} %bitcast.4), calls=%async_computation | async-start | bytes 1048576 | tf_op jit(solution)/shard_map/all_to_all | solution.py:437
  71.4 0.9 copy-start.12
  72.4 0.9 copy-start.14
  74.4 34.3 %copy-start.5 = (s32[256]{0:T(256)S(1)}, s32[256]{0:T(256)}, u32[]{:S(2)}) copy-start(s32[256]{0:T(256)} %param.8) | copy-start | bytes 3076
  74.4 13.4 %collective-permute-start.19 = (bf16[256,640]{1,0:T(8,128)(2,1)S(1)}, bf16[256,640]{1,0:T(8,128)(2,1)S(1)}, u32[]{:S(2)}, u32[]{:S(2)}) collective-permute-start(bf16[256,640]{1,0:T(8,128)(2,1)S(1)} %get-tuple-element.79), channel_id=1, source_target_pairs={{0,4},{4,0},{8,12},{12,8},{16,20},{20,16},{24,28},{28,24},{1,5},{5... | collective-permute-start | bytes 983048 | tf_op jit(solution)/shard_map/ppermute | solution.py:433
  87.8 6.4 %collective-permute-start.20 = (bf16[128,640]{1,0:T(8,128)(2,1)S(1)}, bf16[128,640]{1,0:T(8,128)(2,1)S(1)}, u32[]{:S(2)}, u32[]{:S(2)}) collective-permute-start(bf16[128,640]{1,0:T(8,128)(2,1)S(1)} %get-tuple-element.81), channel_id=1, source_target_pairs={{0,8},{4,12},{8,0},{12,4},{16,24},{20,28},{24,16},{28,20},{1,9},{5... | collective-permute-start | bytes 491528 | tf_op jit(solution)/shard_map/ppermute | solution.py:433
  94.3 7.2 %collective-permute-start.21 = (bf16[64,640]{1,0:T(8,128)(2,1)S(1)}, bf16[64,640]{1,0:T(8,128)(2,1)S(1)}, u32[]{:S(2)}, u32[]{:S(2)}) collective-permute-start(bf16[64,640]{1,0:T(8,128)(2,1)S(1)} %get-tuple-element.83), channel_id=1, source_target_pairs={{0,16},{4,20},{8,24},{12,28},{16,0},{20,4},{24,8},{28,12},{1,17},{... | collective-permute-start | bytes 245768 | tf_op jit(solution)/shard_map/ppermute | solution.py:433
  101.5 1.9 %collective-permute-start.22 = (bf16[64,640]{1,0:T(8,128)(2,1)S(1)}, bf16[64,640]{1,0:T(8,128)(2,1)S(1)}, u32[]{:S(2)}, u32[]{:S(2)}) collective-permute-start(bf16[64,640]{1,0:T(8,128)(2,1)S(1)} %sum.1.w0_ref), channel_id=1, source_target_pairs={{0,1},{1,0},{2,3},{3,2},{4,5},{5,4},{6,7},{7,6},{8,9},{9,8},{10,11... | collective-permute-start | bytes 245768 | tf_op jit(solution)/shard_map/ppermute | solution.py:418
  101.6 5.3 %collective-permute-start.23 = (bf16[64,640]{1,0:T(8,128)(2,1)S(1)}, bf16[64,640]{1,0:T(8,128)(2,1)S(1)}, u32[]{:S(2)}, u32[]{:S(2)}) collective-permute-start(bf16[64,640]{1,0:T(8,128)(2,1)S(1)} %sum.1.w0_ref), channel_id=1, source_target_pairs={{0,2},{1,3},{2,0},{3,1},{4,6},{5,7},{6,4},{7,5},{8,10},{9,11},{10,... | collective-permute-start | bytes 245768 | tf_op jit(solution)/shard_map/ppermute | solution.py:418
  102.5 5.2 %collective-permute-start.24 = (bf16[64,640]{1,0:T(8,128)(2,1)S(1)}, bf16[64,640]{1,0:T(8,128)(2,1)S(1)}, u32[]{:S(2)}, u32[]{:S(2)}) collective-permute-start(bf16[64,640]{1,0:T(8,128)(2,1)S(1)} %sum.1.w0_ref), channel_id=1, source_target_pairs={{0,3},{1,2},{2,1},{3,0},{4,7},{5,6},{6,5},{7,4},{8,11},{9,10},{10,... | collective-permute-start | bytes 245768 | tf_op jit(solution)/shard_map/ppermute | solution.py:418

commit v4 on v3

--- a/solution.py
+++ b/solution.py
@@ -233,18 +233,12 @@
     gate_grad_ref[...] = (grad_gated * normed * slope_ref[...]).astype(BF16)
 
 
-def side_body(me_ref, gated_ref, cot_ref, gate_grad_ref, proj_ref, *rest):
-    pieces, gate_in_ref, scratch_ref, narrow_ref = rest[:-3], rest[-3], rest[-2], rest[-1]
-    rows, width = gated_ref.shape
-    me = me_ref[0]
-    piece = width // len(pieces)
-    scratch_ref[...] = t_mm(gated_ref[...], cot_ref[...])
-    narrow_ref[...] = gate_grad_ref[...].astype(F32)
-    for step, ref in enumerate(pieces):
-        cols = pl.ds(pl.multiple_of((me ^ step) * piece, LANES), piece)
-        ref[:rows, :] = narrow_ref[:, cols].astype(BF16)
-        ref[rows:, :] = scratch_ref[:, cols].astype(BF16)
-    gate_in_ref[...] = mm_t(gate_grad_ref[...], proj_ref[:, :width])
+def side_body(normed_ref, gated_ref, cot_ref, gate_grad_ref, proj_ref, part_ref, gate_in_ref):
+    width = gated_ref.shape[1]
+    gate_grad = gate_grad_ref[...]
+    part_ref[:, :width] = t_mm(normed_ref[...], gate_grad).astype(BF16)
+    part_ref[:, width:] = t_mm(gated_ref[...], cot_ref[...]).astype(BF16)
+    gate_in_ref[...] = mm_t(gate_grad, proj_ref[:, :width])
 
 
 def heads_body(me_ref, n0_ref, n1_ref, n2_ref, n3_ref, proj_ref, part_ref, slope_ref):
@@ -263,7 +257,7 @@
 def backward_body(
     me_ref, lengths_ref, g0_ref, g1_ref, g2_ref, g3_ref, part_ref, slope_ref, *rest
 ):
-    outs, grad_ref, total_ref = rest[:4], rest[4], rest[5]
+    outs, (grad_ref, total_ref) = rest[-6:-2], rest[-2:]
     rows, piece = g0_ref.shape
     me = me_ref[0]
     for step, ref in enumerate((g0_ref, g1_ref, g2_ref, g3_ref)):
@@ -317,23 +311,17 @@
 
 
 def weight_body(sources, pairs, dp_ref, *refs):
-    normed, grads, sides = refs[:sources], refs[sources : 2 * sources], refs[2 * sources : 3 * sources]
-    outs, total_ref = refs[3 * sources : -1], refs[-1]
-    rows, piece = normed[0].shape[0], sides[0].shape[1]
-    qkv, gate, outw = 0.0, 0.0, 0.0
-    for n_ref, g_ref, s_ref in zip(normed, grads, sides):
-        qkv += t_mm(n_ref[...], g_ref[...])
-        gate += t_mm(n_ref[...], s_ref[:rows, :])
-        outw += s_ref[rows:, :].astype(F32)
-    total_ref[:, :piece] = gate
-    total_ref[:, piece : 4 * piece] = qkv
-    total_ref[:, 4 * piece :] = outw
+    normed, grads = refs[:sources], refs[sources : 2 * sources]
+    outs, total_ref = refs[2 * sources : -1], refs[-1]
+    total = 0.0
+    for n_ref, g_ref in zip(normed, grads):
+        total += t_mm(n_ref[...], g_ref[...])
     if len(outs) == 1:
-        outs[0][...] = total_ref[...].astype(BF16)
+        outs[0][...] = total.astype(BF16)
         return
+    total_ref[...] = total
     kept_ref, sent_ref = outs
-    half = kept_ref.shape[0]
-    share = half // pairs
+    share = kept_ref.shape[0] // pairs
     for j in range(pairs):
         at = slice(j * share, (j + 1) * share)
         for ref, k in ((kept_ref, 2 * j), (sent_ref, 2 * j + 1)):
@@ -341,20 +329,15 @@
             ref[at, :] = total_ref[source, :].astype(BF16)
 
 
-def halve_body(pairs, kept_ref, came_ref, *refs):
-    keep_ref, send_ref = refs[-2:]
-    share = kept_ref.shape[0] // pairs
-    for j in range(pairs):
-        at = slice(j * share, (j + 1) * share)
-        to = slice(j // 2 * share, (j // 2 + 1) * share)
-        total = kept_ref[at, :].astype(F32) + came_ref[at, :].astype(F32)
-        (send_ref if j % 2 else keep_ref)[to, :] = total.astype(BF16)
+def pair_body(kept_ref, came_ref, *outs):
+    store_blocks(outs, kept_ref[...].astype(F32) + came_ref[...].astype(F32))
 
 
 def input_body(
     blocks, me_ref, mask_ref, g0_ref, g1_ref, g2_ref, g3_ref,
-    gate_in_ref, owned_ref, cot_ref, landing_ref, proj_ref, out_ref,
+    gate_in_ref, owned_ref, cot_ref, landing_ref, proj_ref, *rest,
 ):
+    out_ref = rest[-1]
     rows, width = owned_ref.shape
     me = me_ref[0]
     piece = width // 4
@@ -389,16 +372,16 @@
     refs[-1][...] = total.astype(BF16)
 
 
-def finish_body(me_ref, w0_ref, w1_ref, w2_ref, w3_ref, proj_ref, outw_ref):
+def finish_body(me_ref, w0_ref, w1_ref, w2_ref, w3_ref, rest_ref, proj_ref, outw_ref):
     me = me_ref[0]
     width = outw_ref.shape[1]
     piece = width // 4
+    proj_ref[:, :width] = rest_ref[:, :width].astype(F32)
+    outw_ref[...] = rest_ref[:, width:].astype(F32)
     for step, ref in enumerate((w0_ref, w1_ref, w2_ref, w3_ref)):
-        for b in range(4):
-            at = pl.ds(pl.multiple_of(b * width + (me ^ step) * piece, LANES), piece)
+        for b in range(3):
+            at = pl.ds(pl.multiple_of((b + 1) * width + (me ^ step) * piece, LANES), piece)
             proj_ref[:, at] = ref[:, b * piece : (b + 1) * piece].astype(F32)
-        at = pl.ds(pl.multiple_of((me ^ step) * piece, LANES), piece)
-        outw_ref[:, at] = ref[:, 4 * piece :].astype(F32)
 
 
 def on_device(tokens, dest_owner, dest_slot, lengths, proj_weight, out_weight, cotangent):
@@ -480,62 +463,55 @@
         scratch=[pltpu.VMEM((rows, width), F32)], flops=10**10, vmem=16,
     )
     r0, r2, r3, r1 = exchange(grad_pieces)
-    *sides, gate_in = call(
-        side_body, "side", [((rows + width, piece), BF16)] * cycle + [((rows, width), F32)],
-        [me], [gated, cotangent, gate_grad, proj_weight],
-        scratch=[pltpu.VMEM((width, width), F32), pltpu.VMEM((rows, width), F32)], flops=10**10,
-    )
+    side_part, gate_in = call(
+        side_body, "side", [((width, 2 * width), BF16), wide],
+        [], [normed, gated, cotangent, gate_grad, proj_weight], flops=10**10,
+    )
+    side_sum = lax.psum(lax.psum_scatter(side_part, "dp", scatter_dimension=0, tiled=True), "ctx")
     parts, slopes = call(
         heads_body, "heads",
         [((rows * cycle, 3 * piece), BF16), ((rows * cycle, 3 * piece), F32)],
         [me], [normed, near, far, cross, proj_weight], flops=10**10, vmem=16,
     )
-    s0, s2, s3, s1 = exchange(sides)
     grads = call(
         backward_body, "backward", [((rows, 3 * piece), BF16)] * cycle,
         [me, lengths], [r0, r1, r2, r3, parts, slopes],
         scratch=[pltpu.VMEM((rows * cycle, piece), BF16), pltpu.VMEM((rows * cycle, 3 * piece), F32)],
-        flops=4 * 10**10, vmem=16,
+        flops=4 * 10**10, vmem=16, far=[side_part],
     )
     p0, p2, p3, p1 = exchange(grads)
     share = width // owners
     pairs = owners // 2
-    half = ((pairs * share, 5 * piece), BF16)
+    columns = 3 * piece
     weight_parts = call(
         functools.partial(weight_body, cycle, pairs), "weights",
-        [half, half] if by_hops else [((width, 5 * piece), BF16)], [dp],
-        [normed, near, far, cross, *grads, s0, s1, s2, s3], flops=10**10, vmem=16,
-        scratch=[pltpu.VMEM((width, 5 * piece), F32)],
+        [((pairs * share, columns), BF16)] * 2 if by_hops else [((width, columns), BF16)], [dp],
+        [normed, near, far, cross, *grads], flops=10**10, vmem=16,
+        scratch=[pltpu.VMEM((width, columns), F32)],
     )
     if by_hops:
         kept, sent = weight_parts
-        came = dp_hop(sent, 1)
+        halves = call(
+            pair_body, "pair_sum", [((share, columns), BF16)] * pairs, [], [kept, dp_hop(sent, 1)]
+        )
+        summed_parts = [halves[0]] + [dp_hop(halves[j], 2 * j) for j in range(1, pairs)]
     else:
-        summed_parts = swap_whole(weight_parts[0])
-        summed_parts = [summed_parts.reshape(owners, share, 5 * piece)]
+        halves = weight_parts
+        summed_parts = [swap_whole(weight_parts[0]).reshape(owners, share, columns)]
     (back,) = call(
         functools.partial(input_body, blocks), "input_grad", [((owners * capacity, width), BF16)], [me, mask],
         [p0, p1, p2, p3, gate_in, owned, cotangent, landing, proj_weight], flops=2 * 10**10, vmem=16,
+        far=[halves[0]],
     )
     returned = swap_whole(back)
-    if by_hops:
-        behind, bit = [back], 2
-        while bit < owners:
-            kept, sent = call(
-                functools.partial(halve_body, pairs), "halve",
-                [((pairs * share // 2, 5 * piece), BF16)] * 2, [], [kept, came], far=behind,
-            )
-            came = dp_hop(sent, bit)
-            behind, bit, pairs = [], 2 * bit, pairs // 2
-        summed_parts = [kept, came]
-    (mine,) = call(sum_body, "sum", [((share, 5 * piece), BF16)], [], summed_parts)
+    (mine,) = call(sum_body, "sum", [((share, columns), BF16)], [], summed_parts)
     w1, w2, w3 = (hop(mine, step) for step in range(1, cycle))
     (grad_tokens,) = call(
         functools.partial(return_body, capacity), "give_back", [square], [], [owner_row, returned]
     )
     grad_proj, grad_outw = call(
         finish_body, "finish", [((share, 4 * width), F32), ((share, width), F32)],
-        [me], [mine, w1, w2, w3],
+        [me], [mine, w1, w2, w3, side_sum],
     )
     return layer_out, grad_tokens, grad_proj, grad_outw
 

time: 110 us -> 184 us (1.67)
  waiting for transfers between devices: 40 us -> 89 us
  between operations: 0.86 us -> 14.3 us
  local copies, waits for them, and re-layouts: 7.77 us -> 19.8 us
  starting transfers between devices: 42.2 us -> 36.6 us
  Pallas kernels: 19 us -> 23.1 us
    reduce_scatter x0 -> x1, waiting for transfers between devices: none -> 43.5 us  [on_device(): lax.psum_scatter(side_part, 'dp', scatter_dimension=0, tiled=True)]
    psum x0 -> x1, waiting for transfers between devices: none -> 27.4 us  [on_device(): lax.psum(lax.psum_scatter(side_part, 'dp', scatter_dimension=0, tiled=Tru...]
    ppermute x10 -> x11, waiting for transfers between devices: 23.5 us -> 9.71 us  [dp_hop(): return lax.ppermute(value, 'dp', [(i, i ^ step) for i in range(owners)])]
    unnamed x30 -> x68, local copies, waits for them, and re-layouts: 7.77 us -> 19.8 us
    ppermute x15 -> x12, waiting for transfers between devices: 16.5 us -> 8.25 us  [hop(): return lax.ppermute(value, 'ctx', [(i, i ^ step) for i in range(cycle)])]
    pallas_call x16 -> x15, Pallas kernels: 19 us -> 23.1 us  [call(): pl.pallas_call(body, name=name, out_shape=[jax.ShapeDtypeStruct(s, d) for...]
    ppermute x10 -> x11, starting transfers between devices: 20.7 us -> 17.4 us  [dp_hop(): return lax.ppermute(value, 'dp', [(i, i ^ step) for i in range(owners)])]
    ppermute x15 -> x12, starting transfers between devices: 11.2 us -> 9.21 us  [hop(): return lax.ppermute(value, 'ctx', [(i, i ^ step) for i in range(cycle)])]
  transfers between devices with their start and end apart: 26 -> 26, of which waited for: 13 -> 11; matrix products, arithmetic and copies ran while one was open for 0% -> 0% of each run, Pallas kernels for 8% -> 5%
where the time goes in v4:
time: 184 us; the launch traced here: 183 us
  waiting for transfers between devices  89 us (48%)
  starting transfers between devices  36.6 us (20%)
  Pallas kernels  23.1 us (13%)
  local copies, waits for them, and re-layouts  19.8 us (11%)
  between operations  14.3 us (8%)
    reduce_scatter x1, waiting for transfers between devices, on_device(): lax.psum_scatter(side_part, 'dp', scatter_dimension=0, tiled=True)  43.5 us
    psum x1, waiting for transfers between devices, on_device(): lax.psum(lax.psum_scatter(side_part, 'dp', scatter_dimension=0, tiled=Tru...  27.4 us
    pallas_call x15, Pallas kernels, call(): pl.pallas_call(body, name=name, out_shape=[jax.ShapeDtypeStruct(s, d) for...  23.1 us
    unnamed x68, local copies, waits for them, and re-layouts  19.8 us
    ppermute x11, starting transfers between devices, dp_hop(): return lax.ppermute(value, 'dp', [(i, i ^ step) for i in range(owners)])  17.4 us
    all_to_all x1, starting transfers between devices, swap_whole(): lax.all_to_all(split, 'dp', split_axis=0, concat_axis=0, tiled=True)  9.93 us
    ppermute x11, waiting for transfers between devices, dp_hop(): return lax.ppermute(value, 'dp', [(i, i ^ step) for i in range(owners)])  9.71 us
    ppermute x12, starting transfers between devices, hop(): return lax.ppermute(value, 'ctx', [(i, i ^ step) for i in range(cycle)])  9.21 us
  transfers between devices with their start and end apart: 26, of which 11 were waited for; matrix products, arithmetic and copies ran while one was open for 0% of the time, Pallas kernels for 5%

profile of v4, /device:TPU:0, one launch (start us, length us, event | category | flops | bytes accessed | tf_op | source)
XLA Modules:
  0.0 182.7 jit_solution(17363775045122887455)
XLA Ops:
  7.9 0.9 copy-done.8
  9.5 0.7 pack.1
  10.2 3.0 %collective-permute-start = (bf16[72,512]{1,0:T(8,128)(2,1)S(1)}, bf16[72,512]{1,0:T(8,128)(2,1)S(1)}, u32[]{:S(2)}, u32[]{:S(2)}) collective-permute-start(bf16[72,512]{1,0:T(8,128)(2,1)S(1)} %get-tuple-element.43), channel_id=1, source_target_pairs={{0,4},{4,0},{8,12},{12,8},{16,20},{20,16},{24,28},{28,24},{1,5},{5... | collective-permute-start | bytes 221192 | tf_op jit(solution)/shard_map/ppermute | solution.py:416
  13.3 1.6 collective-permute-start.1
  14.9 3.0 %collective-permute-start.3 = (bf16[72,512]{1,0:T(8,128)(2,1)S(1)}, bf16[72,512]{1,0:T(8,128)(2,1)S(1)}, u32[]{:S(2)}, u32[]{:S(2)}) collective-permute-start(bf16[72,512]{1,0:T(8,128)(2,1)S(1)} %get-tuple-element.46), channel_id=1, source_target_pairs={{0,16},{4,20},{8,24},{12,28},{16,0},{20,4},{24,8},{28,12},{1,17},{... | collective-permute-start | bytes 221192 | tf_op jit(solution)/shard_map/ppermute | solution.py:416
  17.8 1.3 collective-permute-start.4
  19.1 3.6 %collective-permute-start.5 = (bf16[72,512]{1,0:T(8,128)(2,1)S(1)}, bf16[72,512]{1,0:T(8,128)(2,1)S(1)}, u32[]{:S(2)}, u32[]{:S(2)}) collective-permute-start(bf16[72,512]{1,0:T(8,128)(2,1)S(1)} %get-tuple-element.48), channel_id=1, source_target_pairs={{0,24},{4,28},{8,16},{12,20},{16,8},{20,12},{24,0},{28,4},{1,25},{... | collective-permute-start | bytes 221192 | tf_op jit(solution)/shard_map/ppermute | solution.py:416
  22.8 1.0 copy-done
  23.8 0.9 copy-done.2
  25.1 4.0 %collective-permute-done.4.refs_5_ = bf16[72,512]{1,0:T(8,128)(2,1)S(1)} collective-permute-done((bf16[72,512]{1,0:T(8,128)(2,1)S(1)}, bf16[72,512]{1,0:T(8,128)(2,1)S(1)}, u32[]{:S(2)}, u32[]{:S(2)}) %collective-permute-start.4) | collective-permute-done | bytes 73760 | tf_op jit(solution)/shard_map/ppermute | solution.py:416
  29.1 0.8 collective-permute-done.6.refs_7_
  29.9 0.8 place.1
  30.7 1.6 collective-permute-start.7
  32.3 1.6 copy-done.6
  33.9 2.2 %own_rows.1 = (bf16[256,512]{1,0:T(8,128)(2,1)S(1)}, f32[256,512]{1,0:T(8,128)S(1)}, bf16[256,512]{1,0:T(8,128)(2,1)S(1)}, f32[256,512]{1,0:T(8,128)S(1)}) custom-call(s32[1]{0:T(128)} %bitcast.me_ref, s32[1,3]{1,0:T(1,128)S(1)} %copy-done.23, bf16[256,512]{1,0:T(8,128)(2,1)S(1)} %get-tuple-element.50.normed_ref.n0_ref.refs_0_, bf16[512,2048]{1,0:T(8,128)(2,1)S(1)} %copy-done.6), custom_call_target="tpu_custom_call" | custom-call | flops 10000000000 | bytes 1048576 | tf_op jit(solution)/shard_map/own_rows/pallas_call | solution.py:22
  36.1 1.1 collective-permute-done.7.far_ref.n2_ref.refs_2_
  37.8 0.9 collective-permute-done.8.cross_ref.n3_ref.refs_3_
  38.7 1.9 %forward.1 = (bf16[256,512]{1,0:T(8,128)(2,1)}, bf16[256,512]{1,0:T(8,128)(2,1)S(1)}, bf16[256,512]{1,0:T(8,128)(2,1)S(1)}, bf16[256,128]{1,0:T(8,128)(2,1)S(1)}...) custom-call(s32[1]{0:T(128)} %bitcast.me_ref, s32[1,3]{1,0:T(1,128)S(1)} %copy-done.23, ...), custom_call_target="tpu_custom_call" | custom-call | flops 10000000000 | bytes 1048576 | tf_op jit(solution)/shard_map/forward/pallas_call | solution.py:22
  41.4 3.7 %collective-permute-start.11 = (bf16[256,128]{1,0:T(8,128)(2,1)S(1)}, bf16[256,128]{1,0:T(8,128)(2,1)S(1)}, u32[]{:S(2)}, u32[]{:S(2)}) collective-permute-start(bf16[256,128]{1,0:T(8,128)(2,1)S(1)} %get-tuple-element.59), channel_id=1, source_target_pairs={{0,2},{1,3},{2,0},{3,1},{4,6},{5,7},{6,4},{7,5},{8,10},{9,11},{10,... | collective-permute-start | bytes 196616 | tf_op jit(solution)/shard_map/ppermute | solution.py:401
  45.1 1.5 side.1
  46.6 0.8 copy-done.28
  47.4 0.8 heads.1
  48.2 1.2 copy-done.24
  49.4 0.9 copy-done.26
  51.5 0.8 copy-done.15
  52.4 0.8 copy-done.17
  53.2 1.4 copy-done.25
  54.6 1.1 copy-done.27
  55.8 0.8 copy-done.33
  56.6 6.5 %backward.1 = (bf16[256,384]{1,0:T(8,128)(2,1)S(1)}, bf16[256,384]{1,0:T(8,128)(2,1)}, bf16[256,384]{1,0:T(8,128)(2,1)}, bf16[256,384]{1,0:T(8,128)(2,1)}) custom-call(s32[1]{0:T(128)} %bitcast.me_ref, s32[1,3]{1,0:T(1,128)S(1)} %copy-done.23, bf16[256,128]{1,0:T(8,128)(2,1)S(1)} %copy-done.33, bf16[256,128]{1,0:T(8,128)(2,1)S(1)} %collective-permute-done.10.g1_ref, ...), custom_call_target="tpu_custom_call" | custom-call | flops 40000000000 | bytes 1048576 | tf_op jit(solution)/shard_map/backward/pallas_call | solution.py:22
  63.1 2.6 %weights.1 = (bf16[256,384]{1,0:T(8,128)(2,1)S(1)}, bf16[256,384]{1,0:T(8,128)(2,1)}) custom-call(s32[1]{0:T(128)} %bitcast.1.mask_ref.dp_ref, bf16[256,512]{1,0:T(8,128)(2,1)S(1)} %get-tuple-element.50.normed_ref.n0_ref.refs_0_, bf16[256,512]{1,0:T(8,128)(2,1)S(1)} %copy-done.10, bf16[256,512]{1,0:T(8,128)(2,1)S(1)} %collective-permute-done.7.far_ref.n2_ref.refs_2_, ...), custom_call_target="tpu_custom_call" | custom-call | flops 10000000000 | bytes 1048576 | tf_op jit(solution)/shard_map/weights/pallas_call | solution.py:22
  66.1 1.8 collective-permute-start.14
  68.0 4.9 %collective-permute-done.16.came_ref = bf16[256,384]{1,0:T(8,128)(2,1)S(1)} collective-permute-done((bf16[256,384]{1,0:T(8,128)(2,1)}, bf16[256,384]{1,0:T(8,128)(2,1)S(1)}, u32[]{:S(2)}, u32[]{:S(2)}) %collective-permute-start.16) | collective-permute-done | bytes 196640 | tf_op jit(solution)/shard_map/ppermute | solution.py:416
  74.0 3.5 %collective-permute-done.15.g3_ref = bf16[256,384]{1,0:T(8,128)(2,1)} collective-permute-done((bf16[256,384]{1,0:T(8,128)(2,1)}, bf16[256,384]{1,0:T(8,128)(2,1)}, u32[]{:S(2)}, u32[]{:S(2)}) %collective-permute-start.15) | collective-permute-done | bytes 196640 | tf_op jit(solution)/shard_map/ppermute | solution.py:401
  78.2 1.0 copy-done.29
  79.2 0.9 copy-done.31
  80.2 3.0 %input_grad.1 = bf16[512,512]{1,0:T(8,128)(2,1)} custom-call(s32[1]{0:T(128)} %bitcast.me_ref, s32[1]{0:T(128)} %bitcast.1.mask_ref.dp_ref, bf16[256,384]{1,0:T(8,128)(2,1)S(1)} %copy-done.31, bf16[256,384]{1,0:T(8,128)(2,1)S(1)} %collective-permute-done.13.g1_ref, bf16[256,384]{1,0:T(8,128)(2,1)S(1)} %collective-permute-done.14.g2_ref, ...), custom_call_target="tpu_custom_call" | custom-call | flops 20000000000 | bytes 1048576 | tf_op jit(solution)/shard_map/input_grad/pallas_call | solution.py:22
  83.2 9.9 %all-to-all-start = ((bf16[8,64,512]{2,1,0:T(8,128)(2,1)}), bf16[8,64,512]{2,1,0:T(8,128)(2,1)S(1)}, u32[]{:S(2)}, u32[]{:S(2)}) async-start(bf16[8,64,512]{2,1,0:T(8,128)(2,1)} %bitcast.4), calls=%async_computation | async-start | bytes 1048576 | tf_op jit(solution)/shard_map/all_to_all | solution.py:420
  93.1 2.1 %collective-permute-start.17 = (bf16[64,384]{1,0:T(8,128)(2,1)S(1)}, bf16[64,384]{1,0:T(8,128)(2,1)S(1)}, u32[]{:S(2)}, u32[]{:S(2)}) collective-permute-start(bf16[64,384]{1,0:T(8,128)(2,1)S(1)} %copy-done.19), channel_id=1, source_target_pairs={{0,8},{4,12},{8,0},{12,4},{16,24},{20,28},{24,16},{28,20},{1,9},{5... | collective-permute-start | bytes 147464 | tf_op jit(solution)/shard_map/ppermute | solution.py:416
  95.2 2.3 %collective-permute-start.18 = (bf16[64,384]{1,0:T(8,128)(2,1)S(1)}, bf16[64,384]{1,0:T(8,128)(2,1)S(1)}, u32[]{:S(2)}, u32[]{:S(2)}) collective-permute-start(bf16[64,384]{1,0:T(8,128)(2,1)S(1)} %get-tuple-element.76), channel_id=1, source_target_pairs={{0,16},{4,20},{8,24},{12,28},{16,0},{20,4},{24,8},{28,12},{1,17},{... | collective-permute-start | bytes 147464 | tf_op jit(solution)/shard_map/ppermute | solution.py:416
  97.6 43.5 %reduce-scatter.2.cloned.1.call-done = bf16[64,1024]{1,0:T(8,128)(2,1)} async-done(((bf16[512,1024]{1,0:T(8,128)(2,1)}), bf16[64,1024]{1,0:T(8,128)(2,1)}) %reduce-scatter.2.cloned.1.call-update) | async-done | bytes 131088 | tf_op jit(solution)/shard_map/reduce_scatter | solution.py:470
  141.3 1.6 collective-permute-start.21
  143.2 1.2 give_back.1
  144.4 1.1 collective-permute-done.21.w2_ref
  145.5 1.1 collective-permute-done.22.w3_ref
  146.6 27.4 %all-reduce.2.cloned.1.call-done.rest_ref = bf16[64,1024]{1,0:T(8,128)(2,1)} async-done(((bf16[64,1024]{1,0:T(8,128)(2,1)}), bf16[64,1024]{1,0:T(8,128)(2,1)}) %all-reduce.2.cloned.1.call-update) | async-done | bytes 131088 | tf_op jit(solution)/shard_map/psum | solution.py:470
  174.1 0.9 copy-done.13
  175.0 0.9 finish.1
  (89 shorter events, 7.2 us)
Async XLA Ops:
  7.2 25.1 %copy-start.23 = (s32[1,3]{1,0:T(1,128)S(1)}, s32[1,3]{1,0:T(1,128)}, u32[]{:S(2)}) copy-start(s32[1,3]{1,0:T(1,128)} %lengths_ref.7) | copy-start | bytes 40
  7.2 134.0 %reduce-scatter.2.cloned.1.call-start = ((), (), s32[]{:S(2)}) async-start(), calls=%async_computation.2 | async-start | bytes 1179648 | tf_op jit(solution)/shard_map/reduce_scatter | solution.py:470
  7.9 0.9 copy-start.8
  10.2 8.9 %collective-permute-start = (bf16[72,512]{1,0:T(8,128)(2,1)S(1)}, bf16[72,512]{1,0:T(8,128)(2,1)S(1)}, u32[]{:S(2)}, u32[]{:S(2)}) collective-permute-start(bf16[72,512]{1,0:T(8,128)(2,1)S(1)} %get-tuple-element.43), channel_id=1, source_target_pairs={{0,4},{4,0},{8,12},{12,8},{16,20},{20,16},{24,28},{28,24},{1,5},{5... | collective-permute-start | bytes 221192 | tf_op jit(solution)/shard_map/ppermute | solution.py:416
  13.3 9.5 %collective-permute-start.1 = (bf16[72,512]{1,0:T(8,128)(2,1)S(1)}, bf16[72,512]{1,0:T(8,128)(2,1)S(1)}, u32[]{:S(2)}, u32[]{:S(2)}) collective-permute-start(bf16[72,512]{1,0:T(8,128)(2,1)S(1)} %get-tuple-element.44), channel_id=1, source_target_pairs={{0,8},{4,12},{8,0},{12,4},{16,24},{20,28},{24,16},{28,20},{1,9},{5... | collective-permute-start | bytes 221192 | tf_op jit(solution)/shard_map/ppermute | solution.py:416
  14.9 10.2 %collective-permute-start.2 = (bf16[72,512]{1,0:T(8,128)(2,1)S(1)}, bf16[72,512]{1,0:T(8,128)(2,1)S(1)}, u32[]{:S(2)}, u32[]{:S(2)}) collective-permute-start(bf16[72,512]{1,0:T(8,128)(2,1)S(1)} %get-tuple-element.45), channel_id=1, source_target_pairs={{0,12},{4,8},{8,4},{12,0},{16,28},{20,24},{24,20},{28,16},{1,13},{... | collective-permute-start | bytes 221192 | tf_op jit(solution)/shard_map/ppermute | solution.py:416
  14.9 10.2 %collective-permute-start.3 = (bf16[72,512]{1,0:T(8,128)(2,1)S(1)}, bf16[72,512]{1,0:T(8,128)(2,1)S(1)}, u32[]{:S(2)}, u32[]{:S(2)}) collective-permute-start(bf16[72,512]{1,0:T(8,128)(2,1)S(1)} %get-tuple-element.46), channel_id=1, source_target_pairs={{0,16},{4,20},{8,24},{12,28},{16,0},{20,4},{24,8},{28,12},{1,17},{... | collective-permute-start | bytes 221192 | tf_op jit(solution)/shard_map/ppermute | solution.py:416
  17.8 11.3 %collective-permute-start.4 = (bf16[72,512]{1,0:T(8,128)(2,1)S(1)}, bf16[72,512]{1,0:T(8,128)(2,1)S(1)}, u32[]{:S(2)}, u32[]{:S(2)}) collective-permute-start(bf16[72,512]{1,0:T(8,128)(2,1)S(1)} %get-tuple-element.47), channel_id=1, source_target_pairs={{0,20},{4,16},{8,28},{12,24},{16,4},{20,0},{24,12},{28,8},{1,21},{... | collective-permute-start | bytes 221192 | tf_op jit(solution)/shard_map/ppermute | solution.py:416
  19.1 10.0 %collective-permute-start.5 = (bf16[72,512]{1,0:T(8,128)(2,1)S(1)}, bf16[72,512]{1,0:T(8,128)(2,1)S(1)}, u32[]{:S(2)}, u32[]{:S(2)}) collective-permute-start(bf16[72,512]{1,0:T(8,128)(2,1)S(1)} %get-tuple-element.48), channel_id=1, source_target_pairs={{0,24},{4,28},{8,16},{12,20},{16,8},{20,12},{24,0},{28,4},{1,25},{... | collective-permute-start | bytes 221192 | tf_op jit(solution)/shard_map/ppermute | solution.py:416
  22.7 7.2 %collective-permute-start.6 = (bf16[72,512]{1,0:T(8,128)(2,1)S(1)}, bf16[72,512]{1,0:T(8,128)(2,1)S(1)}, u32[]{:S(2)}, u32[]{:S(2)}) collective-permute-start(bf16[72,512]{1,0:T(8,128)(2,1)S(1)} %get-tuple-element.49), channel_id=1, source_target_pairs={{0,28},{4,24},{8,20},{12,16},{16,12},{20,8},{24,4},{28,0},{1,29},{... | collective-permute-start | bytes 221192 | tf_op jit(solution)/shard_map/ppermute | solution.py:416
  22.8 1.0 copy-start
  23.8 0.9 copy-start.2
  30.7 5.4 %copy-start.20 = (s32[1,512]{1,0:T(1,128)}, s32[1,512]{1,0:T(1,128)S(1)}, u32[]{:S(2)}) copy-start(s32[1,512]{1,0:T(1,128)S(1)} %get-tuple-element.71.landing_ref) | copy-start | bytes 6148
  30.7 6.4 %collective-permute-start.7 = (bf16[256,512]{1,0:T(8,128)(2,1)S(1)}, bf16[256,512]{1,0:T(8,128)(2,1)S(1)}, u32[]{:S(2)}, u32[]{:S(2)}) collective-permute-start(bf16[256,512]{1,0:T(8,128)(2,1)S(1)} %get-tuple-element.50.normed_ref.n0_ref.refs_0_), channel_id=1, source_target_pairs={{0,2},{1,3},{2,0},{3,1},{4,6},{5,7},{6,4},{7,5},{8,10},{9,11},{10,... | collective-permute-start | bytes 786440 | tf_op jit(solution)/shard_map/ppermute | solution.py:401
  32.3 4.9 %collective-permute-start.9 = (bf16[256,512]{1,0:T(8,128)(2,1)S(1)}, bf16[256,512]{1,0:T(8,128)(2,1)S(1)}, u32[]{:S(2)}, u32[]{:S(2)}) collective-permute-start(bf16[256,512]{1,0:T(8,128)(2,1)S(1)} %get-tuple-element.50.normed_ref.n0_ref.refs_0_), channel_id=1, source_target_pairs={{0,1},{1,0},{2,3},{3,2},{4,5},{5,4},{6,7},{7,6},{8,9},{9,8},{10,11... | collective-permute-start | bytes 786440 | tf_op jit(solution)/shard_map/ppermute | solution.py:401
  32.3 1.6 copy-start.6
  33.9 3.3 %copy-start.7 = (bf16[512,2048]{1,0:T(8,128)(2,1)S(1)}, bf16[512,2048]{1,0:T(8,128)(2,1)}, u32[]{:S(2)}) copy-start(bf16[512,2048]{1,0:T(8,128)(2,1)} %proj_ref.11) | copy-start | bytes 6291460
  37.2 1.5 collective-permute-start.8
  37.2 9.4 %copy-start.9 = (bf16[256,512]{1,0:T(8,128)(2,1)}, bf16[256,512]{1,0:T(8,128)(2,1)S(1)}, u32[]{:S(2)}) copy-start(bf16[256,512]{1,0:T(8,128)(2,1)S(1)} %collective-permute-done.9.near_ref.n1_ref.refs_1_) | copy-start | bytes 786436
  37.2 1.5 copy-start.1
  38.7 7.9 %copy-start.11 = (bf16[256,512]{1,0:T(8,128)(2,1)}, bf16[256,512]{1,0:T(8,128)(2,1)S(1)}, u32[]{:S(2)}) copy-start(bf16[256,512]{1,0:T(8,128)(2,1)S(1)} %collective-permute-done.8.cross_ref.n3_ref.refs_3_) | copy-start | bytes 786436
  38.7 6.4 %copy-start.3 = (bf16[256,512]{1,0:T(8,128)(2,1)S(1)}, bf16[256,512]{1,0:T(8,128)(2,1)}, u32[]{:S(2)}) copy-start(bf16[256,512]{1,0:T(8,128)(2,1)} %cot_ref.5) | copy-start | bytes 786436
  41.3 9.0 %collective-permute-start.10 = (bf16[256,128]{1,0:T(8,128)(2,1)S(1)}, bf16[256,128]{1,0:T(8,128)(2,1)S(1)}, u32[]{:S(2)}, u32[]{:S(2)}) collective-permute-start(bf16[256,128]{1,0:T(8,128)(2,1)S(1)} %get-tuple-element.58), channel_id=1, source_target_pairs={{0,1},{1,0},{2,3},{3,2},{4,5},{5,4},{6,7},{7,6},{8,9},{9,8},{10,11... | collective-permute-start | bytes 196616 | tf_op jit(solution)/shard_map/ppermute | solution.py:401
  41.4 8.9 %collective-permute-start.11 = (bf16[256,128]{1,0:T(8,128)(2,1)S(1)}, bf16[256,128]{1,0:T(8,128)(2,1)S(1)}, u32[]{:S(2)}, u32[]{:S(2)}) collective-permute-start(bf16[256,128]{1,0:T(8,128)(2,1)S(1)} %get-tuple-element.59), channel_id=1, source_target_pairs={{0,2},{1,3},{2,0},{3,1},{4,6},{5,7},{6,4},{7,5},{8,10},{9,11},{10,... | collective-permute-start | bytes 196616 | tf_op jit(solution)/shard_map/ppermute | solution.py:401
  45.1 5.8 %collective-permute-start.12 = (bf16[256,128]{1,0:T(8,128)(2,1)S(1)}, bf16[256,128]{1,0:T(8,128)(2,1)S(1)}, u32[]{:S(2)}, u32[]{:S(2)}) collective-permute-start(bf16[256,128]{1,0:T(8,128)(2,1)S(1)} %get-tuple-element.60), channel_id=1, source_target_pairs={{0,3},{1,2},{2,1},{3,0},{4,7},{5,6},{6,5},{7,4},{8,11},{9,10},{10,... | collective-permute-start | bytes 196616 | tf_op jit(solution)/shard_map/ppermute | solution.py:401
  48.2 1.2 copy-start.24
  53.2 1.4 copy-start.25
  54.6 1.1 copy-start.27
  56.6 6.5 %copy-start.10 = (bf16[256,512]{1,0:T(8,128)(2,1)S(1)}, bf16[256,512]{1,0:T(8,128)(2,1)}, u32[]{:S(2)}) copy-start(bf16[256,512]{1,0:T(8,128)(2,1)} %copy-done.9) | copy-start | bytes 786436
  56.6 6.5 %copy-start.12 = (bf16[256,512]{1,0:T(8,128)(2,1)S(1)}, bf16[256,512]{1,0:T(8,128)(2,1)}, u32[]{:S(2)}) copy-start(bf16[256,512]{1,0:T(8,128)(2,1)} %copy-done.11) | copy-start | bytes 786436
  63.1 2.7 %copy-start.30 = (bf16[256,384]{1,0:T(8,128)(2,1)}, bf16[256,384]{1,0:T(8,128)(2,1)S(1)}, u32[]{:S(2)}) copy-start(bf16[256,384]{1,0:T(8,128)(2,1)S(1)} %get-tuple-element.66.refs_4_.g0_ref) | copy-start | bytes 589828
  65.7 7.2 %collective-permute-start.16 = (bf16[256,384]{1,0:T(8,128)(2,1)}, bf16[256,384]{1,0:T(8,128)(2,1)S(1)}, u32[]{:S(2)}, u32[]{:S(2)}) collective-permute-start(bf16[256,384]{1,0:T(8,128)(2,1)} %get-tuple-element.73), channel_id=1, source_target_pairs={{0,4},{4,0},{8,12},{12,8},{16,20},{20,16},{24,28},{28,24},{1,5},{5... | collective-permute-start | bytes 589832 | tf_op jit(solution)/shard_map/ppermute | solution.py:416
  66.1 7.5 %collective-permute-start.13 = (bf16[256,384]{1,0:T(8,128)(2,1)}, bf16[256,384]{1,0:T(8,128)(2,1)S(1)}, u32[]{:S(2)}, u32[]{:S(2)}) collective-permute-start(bf16[256,384]{1,0:T(8,128)(2,1)} %get-tuple-element.67.refs_5_), channel_id=1, source_target_pairs={{0,1},{1,0},{2,3},{3,2},{4,5},{5,4},{6,7},{7,6},{8,9},{9,8},{10,11... | collective-permute-start | bytes 589832 | tf_op jit(solution)/shard_map/ppermute | solution.py:401
  66.1 7.9 %collective-permute-start.14 = (bf16[256,384]{1,0:T(8,128)(2,1)}, bf16[256,384]{1,0:T(8,128)(2,1)S(1)}, u32[]{:S(2)}, u32[]{:S(2)}) collective-permute-start(bf16[256,384]{1,0:T(8,128)(2,1)} %get-tuple-element.68.refs_6_), channel_id=1, source_target_pairs={{0,2},{1,3},{2,0},{3,1},{4,6},{5,7},{6,4},{7,5},{8,10},{9,11},{10,... | collective-permute-start | bytes 589832 | tf_op jit(solution)/shard_map/ppermute | solution.py:401
  67.9 9.7 %collective-permute-start.15 = (bf16[256,384]{1,0:T(8,128)(2,1)}, bf16[256,384]{1,0:T(8,128)(2,1)}, u32[]{:S(2)}, u32[]{:S(2)}) collective-permute-start(bf16[256,384]{1,0:T(8,128)(2,1)} %get-tuple-element.69.refs_7_), channel_id=1, source_target_pairs={{0,3},{1,2},{2,1},{3,0},{4,7},{5,6},{6,5},{7,4},{8,11},{9,10},{10,... | collective-permute-start | bytes 589832 | tf_op jit(solution)/shard_map/ppermute | solution.py:401
  78.2 1.0 copy-start.29
  79.2 0.9 copy-start.31
  80.2 13.0 %copy-start.19 = (bf16[64,384]{1,0:T(8,128)(2,1)S(1)}, bf16[64,384]{1,0:T(8,128)(2,1)}, u32[]{:S(2)}) copy-start(bf16[64,384]{1,0:T(8,128)(2,1)} %copy-done.18) | copy-start | bytes 147460
  80.2 63.0 %copy-start.5 = (s32[256]{0:T(256)S(1)}, s32[256]{0:T(256)}, u32[]{:S(2)}) copy-start(s32[256]{0:T(256)} %param.8) | copy-start | bytes 3076
  83.2 60.0 %all-to-all-start = ((bf16[8,64,512]{2,1,0:T(8,128)(2,1)}), bf16[8,64,512]{2,1,0:T(8,128)(2,1)S(1)}, u32[]{:S(2)}, u32[]{:S(2)}) async-start(bf16[8,64,512]{2,1,0:T(8,128)(2,1)} %bitcast.4), calls=%async_computation | async-start | bytes 1048576 | tf_op jit(solution)/shard_map/all_to_all | solution.py:420
  93.1 81.0 %all-reduce.2.cloned.1.call-start = ((), (), s32[]{:S(2)}) async-start(), calls=%async_computation.3 | async-start | bytes 262144 | tf_op jit(solution)/shard_map/psum | solution.py:470
  93.1 48.0 %collective-permute-start.17 = (bf16[64,384]{1,0:T(8,128)(2,1)S(1)}, bf16[64,384]{1,0:T(8,128)(2,1)S(1)}, u32[]{:S(2)}, u32[]{:S(2)}) collective-permute-start(bf16[64,384]{1,0:T(8,128)(2,1)S(1)} %copy-done.19), channel_id=1, source_target_pairs={{0,8},{4,12},{8,0},{12,4},{16,24},{20,28},{24,16},{28,20},{1,9},{5... | collective-permute-start | bytes 147464 | tf_op jit(solution)/shard_map/ppermute | solution.py:416
  95.2 46.0 %collective-permute-start.18 = (bf16[64,384]{1,0:T(8,128)(2,1)S(1)}, bf16[64,384]{1,0:T(8,128)(2,1)S(1)}, u32[]{:S(2)}, u32[]{:S(2)}) collective-permute-start(bf16[64,384]{1,0:T(8,128)(2,1)S(1)} %get-tuple-element.76), channel_id=1, source_target_pairs={{0,16},{4,20},{8,24},{12,28},{16,0},{20,4},{24,8},{28,12},{1,17},{... | collective-permute-start | bytes 147464 | tf_op jit(solution)/shard_map/ppermute | solution.py:416
  97.6 43.7 %collective-permute-start.19 = (bf16[64,384]{1,0:T(8,128)(2,1)S(1)}, bf16[64,384]{1,0:T(8,128)(2,1)S(1)}, u32[]{:S(2)}, u32[]{:S(2)}) collective-permute-start(bf16[64,384]{1,0:T(8,128)(2,1)S(1)} %get-tuple-element.77), channel_id=1, source_target_pairs={{0,24},{4,28},{8,16},{12,20},{16,8},{20,12},{24,0},{28,4},{1,25},{... | collective-permute-start | bytes 147464 | tf_op jit(solution)/shard_map/ppermute | solution.py:416
  141.3 3.1 %collective-permute-start.20 = (bf16[64,384]{1,0:T(8,128)(2,1)S(1)}, bf16[64,384]{1,0:T(8,128)(2,1)S(1)}, u32[]{:S(2)}, u32[]{:S(2)}) collective-permute-start(bf16[64,384]{1,0:T(8,128)(2,1)S(1)} %sum.1.w0_ref), channel_id=1, source_target_pairs={{0,1},{1,0},{2,3},{3,2},{4,5},{5,4},{6,7},{7,6},{8,9},{9,8},{10,11... | collective-permute-start | bytes 147464 | tf_op jit(solution)/shard_map/ppermute | solution.py:401
  141.3 4.2 %collective-permute-start.21 = (bf16[64,384]{1,0:T(8,128)(2,1)S(1)}, bf16[64,384]{1,0:T(8,128)(2,1)S(1)}, u32[]{:S(2)}, u32[]{:S(2)}) collective-permute-start(bf16[64,384]{1,0:T(8,128)(2,1)S(1)} %sum.1.w0_ref), channel_id=1, source_target_pairs={{0,2},{1,3},{2,0},{3,1},{4,6},{5,7},{6,4},{7,5},{8,10},{9,11},{10,... | collective-permute-start | bytes 147464 | tf_op jit(solution)/shard_map/ppermute | solution.py:401
  142.9 3.7 %collective-permute-start.22 = (bf16[64,384]{1,0:T(8,128)(2,1)S(1)}, bf16[64,384]{1,0:T(8,128)(2,1)S(1)}, u32[]{:S(2)}, u32[]{:S(2)}) collective-permute-start(bf16[64,384]{1,0:T(8,128)(2,1)S(1)} %sum.1.w0_ref), channel_id=1, source_target_pairs={{0,3},{1,2},{2,1},{3,0},{4,7},{5,6},{6,5},{7,4},{8,11},{9,10},{10,... | collective-permute-start | bytes 147464 | tf_op jit(solution)/shard_map/ppermute | solution.py:401
  174.1 0.9 copy-start.13
  (12 other events, 8.7 us)
Sparse Core Ops, SparseCore 0:
  68.1 72.9 reduce-scatter.1
  143.6 30.4 all-reduce.1

commit v5 on v4

--- a/solution.py
+++ b/solution.py
@@ -233,12 +233,27 @@
     gate_grad_ref[...] = (grad_gated * normed * slope_ref[...]).astype(BF16)
 
 
-def side_body(normed_ref, gated_ref, cot_ref, gate_grad_ref, proj_ref, part_ref, gate_in_ref):
+def side_body(me_ref, normed_ref, gated_ref, cot_ref, gate_grad_ref, proj_ref, kept_ref, sent_ref, gate_in_ref, part_ref):
     width = gated_ref.shape[1]
+    me = me_ref[0]
     gate_grad = gate_grad_ref[...]
-    part_ref[:, :width] = t_mm(normed_ref[...], gate_grad).astype(BF16)
-    part_ref[:, width:] = t_mm(gated_ref[...], cot_ref[...]).astype(BF16)
+    part_ref[:, :width] = t_mm(normed_ref[...], gate_grad)
+    part_ref[:, width:] = t_mm(gated_ref[...], cot_ref[...])
     gate_in_ref[...] = mm_t(gate_grad, proj_ref[:, :width])
+    for ref, steps in ((kept_ref, (0, 2)), (sent_ref, (1, 3))):
+        place = 0
+        for step in steps:
+            for base in (0, width):
+                source = pl.ds(pl.multiple_of(base + (me ^ step) * LANES, LANES), LANES)
+                ref[:, place : place + LANES] = part_ref[:, source].astype(BF16)
+                place += LANES
+
+
+def side_sum_body(kept_ref, came_ref, keep_ref, send_ref):
+    total = kept_ref[...].astype(F32) + came_ref[...].astype(F32)
+    half = total.shape[1] // 2
+    keep_ref[...] = total[:, :half].astype(BF16)
+    send_ref[...] = total[:, half:].astype(BF16)
 
 
 def heads_body(me_ref, n0_ref, n1_ref, n2_ref, n3_ref, proj_ref, part_ref, slope_ref):
@@ -254,20 +269,17 @@
         slope_ref[at, :] = slope
 
 
-def backward_body(
-    me_ref, lengths_ref, g0_ref, g1_ref, g2_ref, g3_ref, part_ref, slope_ref, *rest
-):
-    outs, (grad_ref, total_ref) = rest[-6:-2], rest[-2:]
-    rows, piece = g0_ref.shape
-    me = me_ref[0]
-    for step, ref in enumerate((g0_ref, g1_ref, g2_ref, g3_ref)):
-        grad_ref[pl.ds(pl.multiple_of((me ^ step) * rows, rows), rows), :] = ref[...]
-    total_ref[...] = jnp.zeros_like(total_ref)
-    left = iota((1, LANES), 1) < LANES // 2
-    blocks = len(outs)
-
-    def visit(q_block, k_block):
-        q_at, k_at = slice(q_block * rows, (q_block + 1) * rows), slice(k_block * rows, (k_block + 1) * rows)
+def block_at(block, rows):
+    return pl.ds(pl.multiple_of(block * rows, rows), rows)
+
+
+def visit(first, second, same, lengths_ref, part_ref, grad_ref, total_ref):
+    rows, piece = grad_ref.shape[0] // 4, grad_ref.shape[1]
+    q_block, k_block = jnp.maximum(first, second), jnp.minimum(first, second)
+
+    def work():
+        q_at, k_at = block_at(q_block, rows), block_at(k_block, rows)
+        left = iota((1, LANES), 1) < LANES // 2
         query_pos = q_block * rows + iota((1, rows), 1)
         start = history_start(query_pos, lengths_ref)
         key_pos = k_block * rows + iota((rows, 1), 0)
@@ -296,30 +308,69 @@
         total_ref[q_at, piece : 2 * piece] += d_query
         total_ref[k_at, 2 * piece :] += d_key
 
-    for q_block in range(blocks):
-        visit(q_block, q_block)
-        for k_block in range(q_block):
-            reach = history_start(q_block * rows, lengths_ref)
-
-            @pl.when((k_block + 1) * rows > reach)
-            def _():
-                visit(q_block, k_block)
-
-    for step, ref in enumerate(outs):
-        at = pl.ds(pl.multiple_of((me ^ step) * rows, rows), rows)
+    if same:
+        work()
+    else:
+        pl.when((k_block + 1) * rows > history_start(q_block * rows, lengths_ref))(work)
+
+
+def backward_rows(steps, finished, me, lengths_ref, part_ref, slope_ref, grad_ref, total_ref, refs):
+    done = list(finished)
+    for step, ref in zip(steps, refs):
+        for other in range(4):
+            if other not in done:
+                visit(me ^ step, me ^ other, other == step, lengths_ref, part_ref, grad_ref, total_ref)
+        done.append(step)
+        at = block_at(me ^ step, ref.shape[0])
         ref[...] = (total_ref[at, :] * slope_ref[at, :]).astype(BF16)
 
 
-def weight_body(sources, pairs, dp_ref, *refs):
+def backward_far_body(
+    me_ref, lengths_ref, g0_ref, g1_ref, g2_ref, g3_ref, part_ref, slope_ref, *rest
+):
+    o2_ref, o3_ref, total_ref, grad_ref = rest[-4:]
+    rows = g0_ref.shape[0]
+    me = me_ref[0]
+    for step, ref in enumerate((g0_ref, g1_ref, g2_ref, g3_ref)):
+        grad_ref[block_at(me ^ step, rows), :] = ref[...]
+    total_ref[...] = jnp.zeros_like(total_ref)
+    backward_rows(
+        (2, 3), (), me, lengths_ref, part_ref, slope_ref, grad_ref, total_ref, (o2_ref, o3_ref)
+    )
+
+
+def backward_rest_body(
+    me_ref, lengths_ref, part_ref, slope_ref, grad_ref, sums_ref, o0_ref, o1_ref, total_ref
+):
+    total_ref[...] = sums_ref[...]
+    backward_rows(
+        (1, 0), (2, 3), me_ref[0], lengths_ref, part_ref, slope_ref, grad_ref, total_ref, (o1_ref, o0_ref)
+    )
+
+
+def relay(value, after):
+    return pl.pallas_call(
+        lambda *refs: None,
+        name="relay",
+        out_shape=jax.ShapeDtypeStruct(value.shape, value.dtype),
+        in_specs=[ANYWHERE] * (1 + len(after)),
+        out_specs=ANYWHERE,
+        input_output_aliases={0: 0},
+    )(value, *after)
+
+
+def weight_body(sources, pairs, dp_ref, kept_side_ref, came_side_ref, *refs):
     normed, grads = refs[:sources], refs[sources : 2 * sources]
     outs, total_ref = refs[2 * sources : -1], refs[-1]
+    side = kept_side_ref.shape[1]
     total = 0.0
     for n_ref, g_ref in zip(normed, grads):
         total += t_mm(n_ref[...], g_ref[...])
+    total_ref[:, :side] = kept_side_ref[...].astype(F32) + came_side_ref[...].astype(F32)
+    total_ref[:, side:] = total
     if len(outs) == 1:
-        outs[0][...] = total.astype(BF16)
+        outs[0][...] = total_ref[...].astype(BF16)
         return
-    total_ref[...] = total
     kept_ref, sent_ref = outs
     share = kept_ref.shape[0] // pairs
     for j in range(pairs):
@@ -372,16 +423,15 @@
     refs[-1][...] = total.astype(BF16)
 
 
-def finish_body(me_ref, w0_ref, w1_ref, w2_ref, w3_ref, rest_ref, proj_ref, outw_ref):
+def finish_body(me_ref, w0_ref, w1_ref, w2_ref, w3_ref, proj_ref, outw_ref):
     me = me_ref[0]
     width = outw_ref.shape[1]
-    piece = width // 4
-    proj_ref[:, :width] = rest_ref[:, :width].astype(F32)
-    outw_ref[...] = rest_ref[:, width:].astype(F32)
     for step, ref in enumerate((w0_ref, w1_ref, w2_ref, w3_ref)):
-        for b in range(3):
-            at = pl.ds(pl.multiple_of((b + 1) * width + (me ^ step) * piece, LANES), piece)
-            proj_ref[:, at] = ref[:, b * piece : (b + 1) * piece].astype(F32)
+        at = pl.ds(pl.multiple_of((me ^ step) * LANES, LANES), LANES)
+        outw_ref[:, at] = ref[:, LANES : 2 * LANES].astype(F32)
+        for b, source in enumerate((0, 2, 3, 4)):
+            at = pl.ds(pl.multiple_of(b * width + (me ^ step) * LANES, LANES), LANES)
+            proj_ref[:, at] = ref[:, source * LANES : (source + 1) * LANES].astype(F32)
 
 
 def on_device(tokens, dest_owner, dest_slot, lengths, proj_weight, out_weight, cotangent):
@@ -453,46 +503,61 @@
     )
     (partial,) = call(
         middle_body, "middle", [wide], [me, lengths], [near, far, proj_weight, query, partial],
-        flops=10**10, vmem=16,
+        vmem=16,
     )
     layer_out, gated, gate_grad, *grad_pieces = call(
         forward_body, "forward",
         [square, square, square] + [((rows, piece), BF16)] * cycle,
         [me, lengths],
         [cross, proj_weight, out_weight, owned, gate, slope, query, partial, grad_gated],
-        scratch=[pltpu.VMEM((rows, width), F32)], flops=10**10, vmem=16,
+        scratch=[pltpu.VMEM((rows, width), F32)], vmem=16,
     )
     r0, r2, r3, r1 = exchange(grad_pieces)
-    side_part, gate_in = call(
-        side_body, "side", [((width, 2 * width), BF16), wide],
-        [], [normed, gated, cotangent, gate_grad, proj_weight], flops=10**10,
-    )
-    side_sum = lax.psum(lax.psum_scatter(side_part, "dp", scatter_dimension=0, tiled=True), "ctx")
+    side_half = ((width, 4 * piece), BF16)
+    side_piece = ((width, 2 * piece), BF16)
+    side_kept, side_sent, gate_in = call(
+        side_body, "side", [side_half, side_half, wide],
+        [me], [normed, gated, cotangent, gate_grad, proj_weight],
+        scratch=[pltpu.VMEM((width, 2 * width), F32)], vmem=16,
+    )
+    side_came = hop(side_sent, 1)
     parts, slopes = call(
         heads_body, "heads",
         [((rows * cycle, 3 * piece), BF16), ((rows * cycle, 3 * piece), F32)],
-        [me], [normed, near, far, cross, proj_weight], flops=10**10, vmem=16,
-    )
-    grads = call(
-        backward_body, "backward", [((rows, 3 * piece), BF16)] * cycle,
-        [me, lengths], [r0, r1, r2, r3, parts, slopes],
-        scratch=[pltpu.VMEM((rows * cycle, piece), BF16), pltpu.VMEM((rows * cycle, 3 * piece), F32)],
-        flops=4 * 10**10, vmem=16, far=[side_part],
-    )
-    p0, p2, p3, p1 = exchange(grads)
+        [me], [normed, near, far, cross, proj_weight], vmem=16,
+    )
+    side_keep, side_send = call(
+        side_sum_body, "side_sum", [side_piece, side_piece], [], [side_kept, side_came]
+    )
+    side_last = hop(side_send, 2)
+    grad_block = ((rows, 3 * piece), BF16)
+    sums = ((rows * cycle, 3 * piece), F32)
+    grad_rows = ((rows * cycle, piece), BF16)
+    far_block, cross_block, totals, grad_all = call(
+        backward_far_body, "backward_far", [grad_block, grad_block, sums, grad_rows],
+        [me, lengths], [r0, r1, r2, r3, parts, slopes], vmem=16, far=[side_send],
+    )
+    p2, p3 = hop(far_block, 2), hop(cross_block, 3)
+    own_block, near_block = call(
+        backward_rest_body, "backward_rest", [grad_block] * 2,
+        [me, lengths], [parts, slopes, grad_all, totals], vmem=16,
+        scratch=[pltpu.VMEM(*sums)],
+    )
+    p1 = hop(near_block, 1)
+    p0, grads = own_block, [own_block, near_block, far_block, cross_block]
     share = width // owners
     pairs = owners // 2
-    columns = 3 * piece
+    columns = 5 * piece
     weight_parts = call(
         functools.partial(weight_body, cycle, pairs), "weights",
         [((pairs * share, columns), BF16)] * 2 if by_hops else [((width, columns), BF16)], [dp],
-        [normed, near, far, cross, *grads], flops=10**10, vmem=16,
+        [side_keep, side_last, normed, near, far, cross, *grads], vmem=16,
         scratch=[pltpu.VMEM((width, columns), F32)],
     )
     if by_hops:
         kept, sent = weight_parts
         halves = call(
-            pair_body, "pair_sum", [((share, columns), BF16)] * pairs, [], [kept, dp_hop(sent, 1)]
+            pair_body, "pair_sum", [((share, columns), BF16)] * pairs, [], [kept, dp_hop(relay(sent, [p2, p3]), 1)]
         )
         summed_parts = [halves[0]] + [dp_hop(halves[j], 2 * j) for j in range(1, pairs)]
     else:
@@ -500,8 +565,7 @@
         summed_parts = [swap_whole(weight_parts[0]).reshape(owners, share, columns)]
     (back,) = call(
         functools.partial(input_body, blocks), "input_grad", [((owners * capacity, width), BF16)], [me, mask],
-        [p0, p1, p2, p3, gate_in, owned, cotangent, landing, proj_weight], flops=2 * 10**10, vmem=16,
-        far=[halves[0]],
+        [p0, p1, p2, p3, gate_in, owned, cotangent, landing, proj_weight], vmem=16,
     )
     returned = swap_whole(back)
     (mine,) = call(sum_body, "sum", [((share, columns), BF16)], [], summed_parts)
@@ -511,7 +575,7 @@
     )
     grad_proj, grad_outw = call(
         finish_body, "finish", [((share, 4 * width), F32), ((share, width), F32)],
-        [me], [mine, w1, w2, w3, side_sum],
+        [me], [mine, w1, w2, w3],
     )
     return layer_out, grad_tokens, grad_proj, grad_outw
 

time: 184 us -> 118 us (0.64)
  waiting for transfers between devices: 89 us -> 45.9 us
  between operations: 14.3 us -> 0.94 us
  local copies, waits for them, and re-layouts: 19.8 us -> 12.4 us
  Pallas kernels: 23.1 us -> 18.7 us
  starting transfers between devices: 36.6 us -> 39.4 us
    reduce_scatter x1 -> x0, waiting for transfers between devices: 43.5 us -> none  [on_device(): lax.psum_scatter(side_part, 'dp', scatter_dimension=0, tiled=True)]
    psum x1 -> x0, waiting for transfers between devices: 27.4 us -> none  [on_device(): lax.psum(lax.psum_scatter(side_part, 'dp', scatter_dimension=0, tiled=Tru...]
    ppermute x12 -> x14, waiting for transfers between devices: 8.25 us -> 25.7 us  [hop(): return lax.ppermute(value, 'ctx', [(i, i ^ step) for i in range(cycle)])]
    ppermute x11, waiting for transfers between devices: 9.71 us -> 20.2 us  [dp_hop(): return lax.ppermute(value, 'dp', [(i, i ^ step) for i in range(owners)])]
    unnamed x68 -> x52, local copies, waits for them, and re-layouts: 19.8 us -> 12.4 us
    pallas_call x15 -> x17, Pallas kernels: 23.1 us -> 18.7 us  [call(): pl.pallas_call(body, name=name, out_shape=[jax.ShapeDtypeStruct(s, d) for...]
    ppermute x12 -> x14, starting transfers between devices: 9.21 us -> 11.1 us  [hop(): return lax.ppermute(value, 'ctx', [(i, i ^ step) for i in range(cycle)])]
  transfers between devices with their start and end apart: 26 -> 26, of which waited for: 11 -> 14; matrix products, arithmetic and copies ran while one was open for 0% -> 0% of each run, Pallas kernels for 5% -> 5%
where the time goes in v5:
time: 118 us; the launch traced here: 117 us
  waiting for transfers between devices  45.9 us (39%)
  starting transfers between devices  39.4 us (33%)
  Pallas kernels  18.7 us (16%)
  local copies, waits for them, and re-layouts  12.4 us (11%)
    ppermute x14, waiting for transfers between devices, hop(): return lax.ppermute(value, 'ctx', [(i, i ^ step) for i in range(cycle)])  25.7 us
    ppermute x11, waiting for transfers between devices, dp_hop(): return lax.ppermute(value, 'dp', [(i, i ^ step) for i in range(owners)])  20.2 us
    pallas_call x17, Pallas kernels, call(): pl.pallas_call(body, name=name, out_shape=[jax.ShapeDtypeStruct(s, d) for...  18.7 us
    ppermute x11, starting transfers between devices, dp_hop(): return lax.ppermute(value, 'dp', [(i, i ^ step) for i in range(owners)])  18.7 us
    unnamed x52, local copies, waits for them, and re-layouts  12.4 us
    ppermute x14, starting transfers between devices, hop(): return lax.ppermute(value, 'ctx', [(i, i ^ step) for i in range(cycle)])  11.1 us
    all_to_all x1, starting transfers between devices, swap_whole(): lax.all_to_all(split, 'dp', split_axis=0, concat_axis=0, tiled=True)  9.61 us
  transfers between devices with their start and end apart: 26, of which 14 were waited for; matrix products, arithmetic and copies ran while one was open for 0% of the time, Pallas kernels for 5%

profile of v5, /device:TPU:0, one launch (start us, length us, event | category | flops | bytes accessed | tf_op | source)
XLA Modules:
  0.0 117.4 jit_solution(4106603833459847292)
XLA Ops:
  0.7 0.8 copy-done.22
  1.5 0.9 copy-done.24
  3.8 3.0 %collective-permute-start = (bf16[72,512]{1,0:T(8,128)(2,1)S(1)}, bf16[72,512]{1,0:T(8,128)(2,1)S(1)}, u32[]{:S(2)}, u32[]{:S(2)}) collective-permute-start(bf16[72,512]{1,0:T(8,128)(2,1)S(1)} %get-tuple-element.48), channel_id=1, source_target_pairs={{0,4},{4,0},{8,12},{12,8},{16,20},{20,16},{24,28},{28,24},{1,5},{5... | collective-permute-start | bytes 221192 | tf_op jit(solution)/shard_map/ppermute | solution.py:466
  6.8 1.6 %collective-permute-start.1 = (bf16[72,512]{1,0:T(8,128)(2,1)S(1)}, bf16[72,512]{1,0:T(8,128)(2,1)S(1)}, u32[]{:S(2)}, u32[]{:S(2)}) collective-permute-start(bf16[72,512]{1,0:T(8,128)(2,1)S(1)} %get-tuple-element.49), channel_id=1, source_target_pairs={{0,8},{4,12},{8,0},{12,4},{16,24},{20,28},{24,16},{28,20},{1,9},{5... | collective-permute-start | bytes 221192 | tf_op jit(solution)/shard_map/ppermute | solution.py:466
  8.4 3.0 %collective-permute-start.3 = (bf16[72,512]{1,0:T(8,128)(2,1)S(1)}, bf16[72,512]{1,0:T(8,128)(2,1)S(1)}, u32[]{:S(2)}, u32[]{:S(2)}) collective-permute-start(bf16[72,512]{1,0:T(8,128)(2,1)S(1)} %get-tuple-element.51), channel_id=1, source_target_pairs={{0,16},{4,20},{8,24},{12,28},{16,0},{20,4},{24,8},{28,12},{1,17},{... | collective-permute-start | bytes 221192 | tf_op jit(solution)/shard_map/ppermute | solution.py:466
  11.4 1.3 %collective-permute-start.4 = (bf16[72,512]{1,0:T(8,128)(2,1)S(1)}, bf16[72,512]{1,0:T(8,128)(2,1)S(1)}, u32[]{:S(2)}, u32[]{:S(2)}) collective-permute-start(bf16[72,512]{1,0:T(8,128)(2,1)S(1)} %get-tuple-element.52), channel_id=1, source_target_pairs={{0,20},{4,16},{8,28},{12,24},{16,4},{20,0},{24,12},{28,8},{1,21},{... | collective-permute-start | bytes 221192 | tf_op jit(solution)/shard_map/ppermute | solution.py:466
  12.7 3.6 %collective-permute-start.5 = (bf16[72,512]{1,0:T(8,128)(2,1)S(1)}, bf16[72,512]{1,0:T(8,128)(2,1)S(1)}, u32[]{:S(2)}, u32[]{:S(2)}) collective-permute-start(bf16[72,512]{1,0:T(8,128)(2,1)S(1)} %get-tuple-element.53), channel_id=1, source_target_pairs={{0,24},{4,28},{8,16},{12,20},{16,8},{20,12},{24,0},{28,4},{1,25},{... | collective-permute-start | bytes 221192 | tf_op jit(solution)/shard_map/ppermute | solution.py:466
  16.3 6.4 %collective-permute-done.4.refs_5_ = bf16[72,512]{1,0:T(8,128)(2,1)S(1)} collective-permute-done((bf16[72,512]{1,0:T(8,128)(2,1)S(1)}, bf16[72,512]{1,0:T(8,128)(2,1)S(1)}, u32[]{:S(2)}, u32[]{:S(2)}) %collective-permute-start.4) | collective-permute-done | bytes 73760 | tf_op jit(solution)/shard_map/ppermute | solution.py:466
  22.7 0.8 collective-permute-done.6.refs_7_
  23.5 0.8 place.1
  24.3 1.6 %collective-permute-start.7 = (bf16[256,512]{1,0:T(8,128)(2,1)S(1)}, bf16[256,512]{1,0:T(8,128)(2,1)S(1)}, u32[]{:S(2)}, u32[]{:S(2)}) collective-permute-start(bf16[256,512]{1,0:T(8,128)(2,1)S(1)} %get-tuple-element.55.normed_ref.n0_ref.refs_0_), channel_id=1, source_target_pairs={{0,2},{1,3},{2,0},{3,1},{4,6},{5,7},{6,4},{7,5},{8,10},{9,11},{10,... | collective-permute-start | bytes 786440 | tf_op jit(solution)/shard_map/ppermute | solution.py:451
  25.9 0.9 copy-done.1
  26.8 1.0 copy-done.4
  28.3 2.5 %collective-permute-done.7.far_ref.n2_ref.refs_2_ = bf16[256,512]{1,0:T(8,128)(2,1)S(1)} collective-permute-done((bf16[256,512]{1,0:T(8,128)(2,1)S(1)}, bf16[256,512]{1,0:T(8,128)(2,1)S(1)}, u32[]{:S(2)}, u32[]{:S(2)}) %collective-permute-start.7) | collective-permute-done | bytes 262176 | tf_op jit(solution)/shard_map/ppermute | solution.py:451
  31.4 2.2 %own_rows.1 = (bf16[256,512]{1,0:T(8,128)(2,1)S(1)}, f32[256,512]{1,0:T(8,128)S(1)}, bf16[256,512]{1,0:T(8,128)(2,1)S(1)}, f32[256,512]{1,0:T(8,128)S(1)}) custom-call(s32[1]{0:T(128)} %bitcast.me_ref, s32[1,3]{1,0:T(1,128)S(1)} %copy-done.20, bf16[256,512]{1,0:T(8,128)(2,1)S(1)} %get-tuple-element.55.normed_ref.n0_ref.refs_0_, bf16[512,2048]{1,0:T(8,128)(2,1)S(1)} %copy-done), custom_call_target="tpu_custom_call" | custom-call | flops 10000000000 | bytes 1048576 | tf_op jit(solution)/shard_map/own_rows/pallas_call | solution.py:22
  34.6 1.9 %forward.1 = (bf16[256,512]{1,0:T(8,128)(2,1)}, bf16[256,512]{1,0:T(8,128)(2,1)S(1)}, bf16[256,512]{1,0:T(8,128)(2,1)S(1)}, bf16[256,128]{1,0:T(8,128)(2,1)S(1)}...) custom-call(s32[1]{0:T(128)} %bitcast.me_ref, s32[1,3]{1,0:T(1,128)S(1)} %copy-done.21, ...), custom_call_target="tpu_custom_call" | custom-call | flops 100000000 | bytes 1048576 | tf_op jit(solution)/shard_map/forward/pallas_call | solution.py:22
  36.5 0.8 side.1
  38.0 3.8 %collective-permute-start.11 = (bf16[256,128]{1,0:T(8,128)(2,1)S(1)}, bf16[256,128]{1,0:T(8,128)(2,1)S(1)}, u32[]{:S(2)}, u32[]{:S(2)}) collective-permute-start(bf16[256,128]{1,0:T(8,128)(2,1)S(1)} %get-tuple-element.66), channel_id=1, source_target_pairs={{0,2},{1,3},{2,0},{3,1},{4,6},{5,7},{6,4},{7,5},{8,10},{9,11},{10,... | collective-permute-start | bytes 196616 | tf_op jit(solution)/shard_map/ppermute | solution.py:451
  41.8 0.8 heads.1
  43.5 0.9 collective-permute-done.11.g2_ref
  44.4 1.4 %collective-permute-done.12.g3_ref = bf16[256,128]{1,0:T(8,128)(2,1)S(1)} collective-permute-done((bf16[256,128]{1,0:T(8,128)(2,1)S(1)}, bf16[256,128]{1,0:T(8,128)(2,1)S(1)}, u32[]{:S(2)}, u32[]{:S(2)}) %collective-permute-start.12) | collective-permute-done | bytes 65568 | tf_op jit(solution)/shard_map/ppermute | solution.py:451
  45.9 4.4 %backward_far.1 = (bf16[256,384]{1,0:T(8,128)(2,1)S(1)}, bf16[256,384]{1,0:T(8,128)(2,1)S(1)}, f32[1024,384]{1,0:T(8,128)S(1)}, bf16[1024,128]{1,0:T(8,128)(2,1)S(1)}) custom-call(s32[1]{0:T(128)} %bitcast.me_ref, s32[1,3]{1,0:T(1,128)S(1)} %copy-done.21, bf16[256,128]{1,0:T(8,128)(2,1)S(1)} %get-tuple-element.64.g0_ref, ...), custom_call_target="tpu_custom_call" | custom-call | flops 100000000 | bytes 1048576 | tf_op jit(solution)/shard_map/backward_far/pallas_call | solution.py:22
  50.3 1.9 %backward_rest.1 = (bf16[256,384]{1,0:T(8,128)(2,1)S(1)}, bf16[256,384]{1,0:T(8,128)(2,1)S(1)}) custom-call(s32[1]{0:T(128)} %bitcast.me_ref, s32[1,3]{1,0:T(1,128)S(1)} %copy-done.21, bf16[1024,384]{1,0:T(8,128)(2,1)S(1)} %get-tuple-element.62.part_ref, f32[1024,384]{1,0:T(8,128)S(1)} %get-tuple-element.63.slope_ref, ...), custom_call_target="tpu_custom_call" | custom-call | flops 100000000 | bytes 1048576 | tf_op jit(solution)/shard_map/backward_rest/pallas_call | solution.py:22
  52.4 1.4 %collective-permute-start.15 = (bf16[256,384]{1,0:T(8,128)(2,1)S(1)}, bf16[256,384]{1,0:T(8,128)(2,1)S(1)}, u32[]{:S(2)}, u32[]{:S(2)}) collective-permute-start(bf16[256,384]{1,0:T(8,128)(2,1)S(1)} %get-tuple-element.77.refs_6_), channel_id=1, source_target_pairs={{0,2},{1,3},{2,0},{3,1},{4,6},{5,7},{6,4},{7,5},{8,10},{9,11},{10,... | collective-permute-start | bytes 589832 | tf_op jit(solution)/shard_map/ppermute | solution.py:451
  54.2 6.0 %collective-permute-done.15.g2_ref.refs_1_ = bf16[256,384]{1,0:T(8,128)(2,1)S(1)} collective-permute-done((bf16[256,384]{1,0:T(8,128)(2,1)S(1)}, bf16[256,384]{1,0:T(8,128)(2,1)S(1)}, u32[]{:S(2)}, u32[]{:S(2)}) %collective-permute-start.15) | collective-permute-done | bytes 196640 | tf_op jit(solution)/shard_map/ppermute | solution.py:451
  60.2 3.1 %collective-permute-done.16.g3_ref.refs_2_ = bf16[256,384]{1,0:T(8,128)(2,1)S(1)} collective-permute-done((bf16[256,384]{1,0:T(8,128)(2,1)S(1)}, bf16[256,384]{1,0:T(8,128)(2,1)S(1)}, u32[]{:S(2)}, u32[]{:S(2)}) %collective-permute-start.16) | collective-permute-done | bytes 196640 | tf_op jit(solution)/shard_map/ppermute | solution.py:451
  63.3 1.2 %input_grad.1 = bf16[512,512]{1,0:T(8,128)(2,1)S(1)} custom-call(s32[1]{0:T(128)} %bitcast.me_ref, s32[1]{0:T(128)} %bitcast.1.mask_ref.dp_ref, bf16[256,384]{1,0:T(8,128)(2,1)S(1)} %get-tuple-element.75.g0_ref.refs_4_, bf16[256,384]{1,0:T(8,128)(2,1)S(1)} %collective-permute-done.14.g1_ref, bf16[256,384]{1,0:T(8,128)(2,1)S(1)} %collective-permute-done.15.g2_ref.refs_1_, ...), custom_call_target="tpu_custom_call" | custom-call | flops 100000000 | bytes 1048576 | tf_op jit(solution)/shard_map/input_grad/pallas_call | solution.py:22
  64.5 0.8 copy-done.3
  65.4 9.6 %all-to-all-start = ((bf16[8,64,512]{2,1,0:T(8,128)(2,1)}), bf16[8,64,512]{2,1,0:T(8,128)(2,1)S(1)}, u32[]{:S(2)}, u32[]{:S(2)}) async-start(bf16[8,64,512]{2,1,0:T(8,128)(2,1)} %bitcast.6), calls=%async_computation | async-start | bytes 1048576 | tf_op jit(solution)/shard_map/all_to_all | solution.py:470
  75.0 1.1 collective-permute-start.17
  76.1 7.4 %collective-permute-done.17.came_side_ref = bf16[512,256]{1,0:T(8,128)(2,1)S(1)} collective-permute-done((bf16[512,256]{1,0:T(8,128)(2,1)}, bf16[512,256]{1,0:T(8,128)(2,1)S(1)}, u32[]{:S(2)}, u32[]{:S(2)}) %collective-permute-start.17) | collective-permute-done | bytes 262176 | tf_op jit(solution)/shard_map/ppermute | solution.py:451
  83.5 0.9 copy-done.7
  84.4 0.9 copy-done.12
  85.3 0.9 copy-done.15
  86.3 0.9 copy-done.17
  87.2 0.9 copy-done.19
  88.1 0.8 weights.1
  89.7 1.7 %collective-permute-start.18 = (bf16[256,640]{1,0:T(8,128)(2,1)}, bf16[256,640]{1,0:T(8,128)(2,1)S(1)}, u32[]{:S(2)}, u32[]{:S(2)}) collective-permute-start(bf16[256,640]{1,0:T(8,128)(2,1)} %relay.1), channel_id=1, source_target_pairs={{0,4},{4,0},{8,12},{12,8},{16,20},{20,16},{24,28},{28,24},{1,5},{5... | collective-permute-start | bytes 983048 | tf_op jit(solution)/shard_map/ppermute | solution.py:466
  91.4 7.3 %collective-permute-done.18.came_ref = bf16[256,640]{1,0:T(8,128)(2,1)S(1)} collective-permute-done((bf16[256,640]{1,0:T(8,128)(2,1)}, bf16[256,640]{1,0:T(8,128)(2,1)S(1)}, u32[]{:S(2)}, u32[]{:S(2)}) %collective-permute-start.18) | collective-permute-done | bytes 327712 | tf_op jit(solution)/shard_map/ppermute | solution.py:466
  98.8 1.7 %collective-permute-start.19 = (bf16[64,640]{1,0:T(8,128)(2,1)S(1)}, bf16[64,640]{1,0:T(8,128)(2,1)S(1)}, u32[]{:S(2)}, u32[]{:S(2)}) collective-permute-start(bf16[64,640]{1,0:T(8,128)(2,1)S(1)} %get-tuple-element.85), channel_id=1, source_target_pairs={{0,8},{4,12},{8,0},{12,4},{16,24},{20,28},{24,16},{28,20},{1,9},{5... | collective-permute-start | bytes 245768 | tf_op jit(solution)/shard_map/ppermute | solution.py:466
  100.5 2.2 %collective-permute-start.20 = (bf16[64,640]{1,0:T(8,128)(2,1)S(1)}, bf16[64,640]{1,0:T(8,128)(2,1)S(1)}, u32[]{:S(2)}, u32[]{:S(2)}) collective-permute-start(bf16[64,640]{1,0:T(8,128)(2,1)S(1)} %get-tuple-element.86), channel_id=1, source_target_pairs={{0,16},{4,20},{8,24},{12,28},{16,0},{20,4},{24,8},{28,12},{1,17},{... | collective-permute-start | bytes 245768 | tf_op jit(solution)/shard_map/ppermute | solution.py:466
  103.8 3.6 %collective-permute-done.20.refs_2_ = bf16[64,640]{1,0:T(8,128)(2,1)S(1)} collective-permute-done((bf16[64,640]{1,0:T(8,128)(2,1)S(1)}, bf16[64,640]{1,0:T(8,128)(2,1)S(1)}, u32[]{:S(2)}, u32[]{:S(2)}) %collective-permute-start.20) | collective-permute-done | bytes 81952 | tf_op jit(solution)/shard_map/ppermute | solution.py:466
  107.4 1.7 %collective-permute-done.21.refs_3_ = bf16[64,640]{1,0:T(8,128)(2,1)S(1)} collective-permute-done((bf16[64,640]{1,0:T(8,128)(2,1)S(1)}, bf16[64,640]{1,0:T(8,128)(2,1)S(1)}, u32[]{:S(2)}, u32[]{:S(2)}) %collective-permute-start.21) | collective-permute-done | bytes 81952 | tf_op jit(solution)/shard_map/ppermute | solution.py:466
  109.2 1.5 %collective-permute-start.23 = (bf16[64,640]{1,0:T(8,128)(2,1)S(1)}, bf16[64,640]{1,0:T(8,128)(2,1)S(1)}, u32[]{:S(2)}, u32[]{:S(2)}) collective-permute-start(bf16[64,640]{1,0:T(8,128)(2,1)S(1)} %sum.1.w0_ref), channel_id=1, source_target_pairs={{0,2},{1,3},{2,0},{3,1},{4,6},{5,7},{6,4},{7,5},{8,10},{9,11},{10,... | collective-permute-start | bytes 245768 | tf_op jit(solution)/shard_map/ppermute | solution.py:451
  111.0 3.4 %collective-permute-done.23.w2_ref = bf16[64,640]{1,0:T(8,128)(2,1)S(1)} collective-permute-done((bf16[64,640]{1,0:T(8,128)(2,1)S(1)}, bf16[64,640]{1,0:T(8,128)(2,1)S(1)}, u32[]{:S(2)}, u32[]{:S(2)}) %collective-permute-start.23) | collective-permute-done | bytes 81952 | tf_op jit(solution)/shard_map/ppermute | solution.py:451
  114.4 0.9 collective-permute-done.24.w3_ref
  115.4 0.9 finish.1
  116.3 1.2 give_back.1
  (74 shorter events, 8.0 us)
Async XLA Ops:
  0.6 30.1 %copy-start = (bf16[512,2048]{1,0:T(8,128)(2,1)S(1)}, bf16[512,2048]{1,0:T(8,128)(2,1)}, u32[]{:S(2)}) copy-start(bf16[512,2048]{1,0:T(8,128)(2,1)} %proj_ref.11) | copy-start | bytes 6291460
  0.6 0.8 copy-start.22
  1.5 0.9 copy-start.24
  3.8 8.9 %collective-permute-start = (bf16[72,512]{1,0:T(8,128)(2,1)S(1)}, bf16[72,512]{1,0:T(8,128)(2,1)S(1)}, u32[]{:S(2)}, u32[]{:S(2)}) collective-permute-start(bf16[72,512]{1,0:T(8,128)(2,1)S(1)} %get-tuple-element.48), channel_id=1, source_target_pairs={{0,4},{4,0},{8,12},{12,8},{16,20},{20,16},{24,28},{28,24},{1,5},{5... | collective-permute-start | bytes 221192 | tf_op jit(solution)/shard_map/ppermute | solution.py:466
  6.8 9.5 %collective-permute-start.1 = (bf16[72,512]{1,0:T(8,128)(2,1)S(1)}, bf16[72,512]{1,0:T(8,128)(2,1)S(1)}, u32[]{:S(2)}, u32[]{:S(2)}) collective-permute-start(bf16[72,512]{1,0:T(8,128)(2,1)S(1)} %get-tuple-element.49), channel_id=1, source_target_pairs={{0,8},{4,12},{8,0},{12,4},{16,24},{20,28},{24,16},{28,20},{1,9},{5... | collective-permute-start | bytes 221192 | tf_op jit(solution)/shard_map/ppermute | solution.py:466
  8.4 7.9 %collective-permute-start.2 = (bf16[72,512]{1,0:T(8,128)(2,1)S(1)}, bf16[72,512]{1,0:T(8,128)(2,1)S(1)}, u32[]{:S(2)}, u32[]{:S(2)}) collective-permute-start(bf16[72,512]{1,0:T(8,128)(2,1)S(1)} %get-tuple-element.50), channel_id=1, source_target_pairs={{0,12},{4,8},{8,4},{12,0},{16,28},{20,24},{24,20},{28,16},{1,13},{... | collective-permute-start | bytes 221192 | tf_op jit(solution)/shard_map/ppermute | solution.py:466
  8.4 7.9 %collective-permute-start.3 = (bf16[72,512]{1,0:T(8,128)(2,1)S(1)}, bf16[72,512]{1,0:T(8,128)(2,1)S(1)}, u32[]{:S(2)}, u32[]{:S(2)}) collective-permute-start(bf16[72,512]{1,0:T(8,128)(2,1)S(1)} %get-tuple-element.51), channel_id=1, source_target_pairs={{0,16},{4,20},{8,24},{12,28},{16,0},{20,4},{24,8},{28,12},{1,17},{... | collective-permute-start | bytes 221192 | tf_op jit(solution)/shard_map/ppermute | solution.py:466
  11.4 11.3 %collective-permute-start.4 = (bf16[72,512]{1,0:T(8,128)(2,1)S(1)}, bf16[72,512]{1,0:T(8,128)(2,1)S(1)}, u32[]{:S(2)}, u32[]{:S(2)}) collective-permute-start(bf16[72,512]{1,0:T(8,128)(2,1)S(1)} %get-tuple-element.52), channel_id=1, source_target_pairs={{0,20},{4,16},{8,28},{12,24},{16,4},{20,0},{24,12},{28,8},{1,21},{... | collective-permute-start | bytes 221192 | tf_op jit(solution)/shard_map/ppermute | solution.py:466
  12.7 10.0 %collective-permute-start.5 = (bf16[72,512]{1,0:T(8,128)(2,1)S(1)}, bf16[72,512]{1,0:T(8,128)(2,1)S(1)}, u32[]{:S(2)}, u32[]{:S(2)}) collective-permute-start(bf16[72,512]{1,0:T(8,128)(2,1)S(1)} %get-tuple-element.53), channel_id=1, source_target_pairs={{0,24},{4,28},{8,16},{12,20},{16,8},{20,12},{24,0},{28,4},{1,25},{... | collective-permute-start | bytes 221192 | tf_op jit(solution)/shard_map/ppermute | solution.py:466
  16.3 7.2 %collective-permute-start.6 = (bf16[72,512]{1,0:T(8,128)(2,1)S(1)}, bf16[72,512]{1,0:T(8,128)(2,1)S(1)}, u32[]{:S(2)}, u32[]{:S(2)}) collective-permute-start(bf16[72,512]{1,0:T(8,128)(2,1)S(1)} %get-tuple-element.54), channel_id=1, source_target_pairs={{0,28},{4,24},{8,20},{12,16},{16,12},{20,8},{24,4},{28,0},{1,29},{... | collective-permute-start | bytes 221192 | tf_op jit(solution)/shard_map/ppermute | solution.py:466
  24.3 6.4 %collective-permute-start.7 = (bf16[256,512]{1,0:T(8,128)(2,1)S(1)}, bf16[256,512]{1,0:T(8,128)(2,1)S(1)}, u32[]{:S(2)}, u32[]{:S(2)}) collective-permute-start(bf16[256,512]{1,0:T(8,128)(2,1)S(1)} %get-tuple-element.55.normed_ref.n0_ref.refs_0_), channel_id=1, source_target_pairs={{0,2},{1,3},{2,0},{3,1},{4,6},{5,7},{6,4},{7,5},{8,10},{9,11},{10,... | collective-permute-start | bytes 786440 | tf_op jit(solution)/shard_map/ppermute | solution.py:451
  25.9 0.9 copy-start.1
  26.8 1.0 copy-start.4
  28.2 5.4 %collective-permute-start.9 = (bf16[256,512]{1,0:T(8,128)(2,1)S(1)}, bf16[256,512]{1,0:T(8,128)(2,1)S(1)}, u32[]{:S(2)}, u32[]{:S(2)}) collective-permute-start(bf16[256,512]{1,0:T(8,128)(2,1)S(1)} %get-tuple-element.55.normed_ref.n0_ref.refs_0_), channel_id=1, source_target_pairs={{0,1},{1,0},{2,3},{3,2},{4,5},{5,4},{6,7},{7,6},{8,9},{9,8},{10,11... | collective-permute-start | bytes 786440 | tf_op jit(solution)/shard_map/ppermute | solution.py:451
  30.7 3.5 %collective-permute-start.8 = (bf16[256,512]{1,0:T(8,128)(2,1)S(1)}, bf16[256,512]{1,0:T(8,128)(2,1)S(1)}, u32[]{:S(2)}, u32[]{:S(2)}) collective-permute-start(bf16[256,512]{1,0:T(8,128)(2,1)S(1)} %collective-permute-done.7.far_ref.n2_ref.refs_2_), channel_id=1, source_target_pairs={{0,1},{1,0},{2,3},{3,2},{4,5},{5,4},{6,7},{7,6},{8,9},{9,8},{10,11... | collective-permute-start | bytes 786440 | tf_op jit(solution)/shard_map/ppermute | solution.py:451
  33.6 1.0 copy-start.5
  33.6 1.0 copy-start.21
  34.6 1.9 %copy-start.2 = (bf16[256,512]{1,0:T(8,128)(2,1)S(1)}, bf16[256,512]{1,0:T(8,128)(2,1)}, u32[]{:S(2)}) copy-start(bf16[256,512]{1,0:T(8,128)(2,1)} %cot_ref.5) | copy-start | bytes 786436
  37.3 5.3 %collective-permute-start.13 = (bf16[512,512]{1,0:T(8,128)(2,1)S(1)}, bf16[512,512]{1,0:T(8,128)(2,1)S(1)}, u32[]{:S(2)}, u32[]{:S(2)}) collective-permute-start(bf16[512,512]{1,0:T(8,128)(2,1)S(1)} %get-tuple-element.71), channel_id=1, source_target_pairs={{0,1},{1,0},{2,3},{3,2},{4,5},{5,4},{6,7},{7,6},{8,9},{9,8},{10,11... | collective-permute-start | bytes 1572872 | tf_op jit(solution)/shard_map/ppermute | solution.py:451
  37.9 5.6 %collective-permute-start.10 = (bf16[256,128]{1,0:T(8,128)(2,1)S(1)}, bf16[256,128]{1,0:T(8,128)(2,1)S(1)}, u32[]{:S(2)}, u32[]{:S(2)}) collective-permute-start(bf16[256,128]{1,0:T(8,128)(2,1)S(1)} %get-tuple-element.65), channel_id=1, source_target_pairs={{0,1},{1,0},{2,3},{3,2},{4,5},{5,4},{6,7},{7,6},{8,9},{9,8},{10,11... | collective-permute-start | bytes 196616 | tf_op jit(solution)/shard_map/ppermute | solution.py:451
  38.0 6.5 %collective-permute-start.11 = (bf16[256,128]{1,0:T(8,128)(2,1)S(1)}, bf16[256,128]{1,0:T(8,128)(2,1)S(1)}, u32[]{:S(2)}, u32[]{:S(2)}) collective-permute-start(bf16[256,128]{1,0:T(8,128)(2,1)S(1)} %get-tuple-element.66), channel_id=1, source_target_pairs={{0,2},{1,3},{2,0},{3,1},{4,6},{5,7},{6,4},{7,5},{8,10},{9,11},{10,... | collective-permute-start | bytes 196616 | tf_op jit(solution)/shard_map/ppermute | solution.py:451
  41.8 4.1 %collective-permute-start.12 = (bf16[256,128]{1,0:T(8,128)(2,1)S(1)}, bf16[256,128]{1,0:T(8,128)(2,1)S(1)}, u32[]{:S(2)}, u32[]{:S(2)}) collective-permute-start(bf16[256,128]{1,0:T(8,128)(2,1)S(1)} %get-tuple-element.67), channel_id=1, source_target_pairs={{0,3},{1,2},{2,1},{3,0},{4,7},{5,6},{6,5},{7,4},{8,11},{9,10},{10,... | collective-permute-start | bytes 196616 | tf_op jit(solution)/shard_map/ppermute | solution.py:451
  43.5 6.8 %copy-start.13 = (bf16[512,256]{1,0:T(8,128)(2,1)}, bf16[512,256]{1,0:T(8,128)(2,1)S(1)}, u32[]{:S(2)}) copy-start(bf16[512,256]{1,0:T(8,128)(2,1)S(1)} %get-tuple-element.72.rest_0_) | copy-start | bytes 786436
  50.3 2.1 %copy-start.14 = (bf16[256,384]{1,0:T(8,128)(2,1)}, bf16[256,384]{1,0:T(8,128)(2,1)S(1)}, u32[]{:S(2)}) copy-start(bf16[256,384]{1,0:T(8,128)(2,1)S(1)} %get-tuple-element.77.refs_6_) | copy-start | bytes 589828
  50.3 3.5 %copy-start.16 = (bf16[256,384]{1,0:T(8,128)(2,1)}, bf16[256,384]{1,0:T(8,128)(2,1)S(1)}, u32[]{:S(2)}) copy-start(bf16[256,384]{1,0:T(8,128)(2,1)S(1)} %get-tuple-element.78.refs_7_) | copy-start | bytes 589828
  52.2 12.3 %copy-start.6 = (bf16[256,384]{1,0:T(8,128)(2,1)}, bf16[256,384]{1,0:T(8,128)(2,1)S(1)}, u32[]{:S(2)}) copy-start(bf16[256,384]{1,0:T(8,128)(2,1)S(1)} %get-tuple-element.75.g0_ref.refs_4_) | copy-start | bytes 589828
  52.2 12.3 %copy-start.18 = (bf16[256,384]{1,0:T(8,128)(2,1)}, bf16[256,384]{1,0:T(8,128)(2,1)S(1)}, u32[]{:S(2)}) copy-start(bf16[256,384]{1,0:T(8,128)(2,1)S(1)} %get-tuple-element.76.refs_5_) | copy-start | bytes 589828
  52.2 1.9 %collective-permute-start.14 = (bf16[256,384]{1,0:T(8,128)(2,1)S(1)}, bf16[256,384]{1,0:T(8,128)(2,1)S(1)}, u32[]{:S(2)}, u32[]{:S(2)}) collective-permute-start(bf16[256,384]{1,0:T(8,128)(2,1)S(1)} %get-tuple-element.76.refs_5_), channel_id=1, source_target_pairs={{0,1},{1,0},{2,3},{3,2},{4,5},{5,4},{6,7},{7,6},{8,9},{9,8},{10,11... | collective-permute-start | bytes 589832 | tf_op jit(solution)/shard_map/ppermute | solution.py:451
  52.4 7.7 %collective-permute-start.15 = (bf16[256,384]{1,0:T(8,128)(2,1)S(1)}, bf16[256,384]{1,0:T(8,128)(2,1)S(1)}, u32[]{:S(2)}, u32[]{:S(2)}) collective-permute-start(bf16[256,384]{1,0:T(8,128)(2,1)S(1)} %get-tuple-element.77.refs_6_), channel_id=1, source_target_pairs={{0,2},{1,3},{2,0},{3,1},{4,6},{5,7},{6,4},{7,5},{8,10},{9,11},{10,... | collective-permute-start | bytes 589832 | tf_op jit(solution)/shard_map/ppermute | solution.py:451
  53.8 9.4 %collective-permute-start.16 = (bf16[256,384]{1,0:T(8,128)(2,1)S(1)}, bf16[256,384]{1,0:T(8,128)(2,1)S(1)}, u32[]{:S(2)}, u32[]{:S(2)}) collective-permute-start(bf16[256,384]{1,0:T(8,128)(2,1)S(1)} %get-tuple-element.78.refs_7_), channel_id=1, source_target_pairs={{0,3},{1,2},{2,1},{3,0},{4,7},{5,6},{6,5},{7,4},{8,11},{9,10},{10,... | collective-permute-start | bytes 589832 | tf_op jit(solution)/shard_map/ppermute | solution.py:451
  60.2 4.4 %copy-start.8 = (bf16[256,384]{1,0:T(8,128)(2,1)}, bf16[256,384]{1,0:T(8,128)(2,1)S(1)}, u32[]{:S(2)}) copy-start(bf16[256,384]{1,0:T(8,128)(2,1)S(1)} %collective-permute-done.15.g2_ref.refs_1_) | copy-start | bytes 589828
  63.3 1.3 %copy-start.9 = (bf16[256,384]{1,0:T(8,128)(2,1)}, bf16[256,384]{1,0:T(8,128)(2,1)S(1)}, u32[]{:S(2)}) copy-start(bf16[256,384]{1,0:T(8,128)(2,1)S(1)} %collective-permute-done.16.g3_ref.refs_2_) | copy-start | bytes 589828
  64.5 0.8 copy-start.3
  65.4 50.9 %all-to-all-start = ((bf16[8,64,512]{2,1,0:T(8,128)(2,1)}), bf16[8,64,512]{2,1,0:T(8,128)(2,1)S(1)}, u32[]{:S(2)}, u32[]{:S(2)}) async-start(bf16[8,64,512]{2,1,0:T(8,128)(2,1)} %bitcast.6), calls=%async_computation | async-start | bytes 1048576 | tf_op jit(solution)/shard_map/all_to_all | solution.py:470
  75.0 8.5 %collective-permute-start.17 = (bf16[512,256]{1,0:T(8,128)(2,1)}, bf16[512,256]{1,0:T(8,128)(2,1)S(1)}, u32[]{:S(2)}, u32[]{:S(2)}) collective-permute-start(bf16[512,256]{1,0:T(8,128)(2,1)} %copy-done.13), channel_id=1, source_target_pairs={{0,2},{1,3},{2,0},{3,1},{4,6},{5,7},{6,4},{7,5},{8,10},{9,11},{10,... | collective-permute-start | bytes 786440 | tf_op jit(solution)/shard_map/ppermute | solution.py:451
  83.5 0.9 copy-start.7
  84.4 0.9 copy-start.12
  85.3 0.9 copy-start.15
  86.3 0.9 copy-start.17
  87.2 0.9 copy-start.19
  89.7 26.6 %copy-start.23 = (s32[256]{0:T(256)S(1)}, s32[256]{0:T(256)}, u32[]{:S(2)}) copy-start(s32[256]{0:T(256)} %param.8) | copy-start | bytes 3076
  89.7 9.1 %collective-permute-start.18 = (bf16[256,640]{1,0:T(8,128)(2,1)}, bf16[256,640]{1,0:T(8,128)(2,1)S(1)}, u32[]{:S(2)}, u32[]{:S(2)}) collective-permute-start(bf16[256,640]{1,0:T(8,128)(2,1)} %relay.1), channel_id=1, source_target_pairs={{0,4},{4,0},{8,12},{12,8},{16,20},{20,16},{24,28},{28,24},{1,5},{5... | collective-permute-start | bytes 983048 | tf_op jit(solution)/shard_map/ppermute | solution.py:466
  98.8 5.0 %collective-permute-start.19 = (bf16[64,640]{1,0:T(8,128)(2,1)S(1)}, bf16[64,640]{1,0:T(8,128)(2,1)S(1)}, u32[]{:S(2)}, u32[]{:S(2)}) collective-permute-start(bf16[64,640]{1,0:T(8,128)(2,1)S(1)} %get-tuple-element.85), channel_id=1, source_target_pairs={{0,8},{4,12},{8,0},{12,4},{16,24},{20,28},{24,16},{28,20},{1,9},{5... | collective-permute-start | bytes 245768 | tf_op jit(solution)/shard_map/ppermute | solution.py:466
  100.5 6.9 %collective-permute-start.20 = (bf16[64,640]{1,0:T(8,128)(2,1)S(1)}, bf16[64,640]{1,0:T(8,128)(2,1)S(1)}, u32[]{:S(2)}, u32[]{:S(2)}) collective-permute-start(bf16[64,640]{1,0:T(8,128)(2,1)S(1)} %get-tuple-element.86), channel_id=1, source_target_pairs={{0,16},{4,20},{8,24},{12,28},{16,0},{20,4},{24,8},{28,12},{1,17},{... | collective-permute-start | bytes 245768 | tf_op jit(solution)/shard_map/ppermute | solution.py:466
  102.7 6.3 %collective-permute-start.21 = (bf16[64,640]{1,0:T(8,128)(2,1)S(1)}, bf16[64,640]{1,0:T(8,128)(2,1)S(1)}, u32[]{:S(2)}, u32[]{:S(2)}) collective-permute-start(bf16[64,640]{1,0:T(8,128)(2,1)S(1)} %get-tuple-element.87), channel_id=1, source_target_pairs={{0,24},{4,28},{8,16},{12,20},{16,8},{20,12},{24,0},{28,4},{1,25},{... | collective-permute-start | bytes 245768 | tf_op jit(solution)/shard_map/ppermute | solution.py:466
  109.1 1.9 %collective-permute-start.22 = (bf16[64,640]{1,0:T(8,128)(2,1)S(1)}, bf16[64,640]{1,0:T(8,128)(2,1)S(1)}, u32[]{:S(2)}, u32[]{:S(2)}) collective-permute-start(bf16[64,640]{1,0:T(8,128)(2,1)S(1)} %sum.1.w0_ref), channel_id=1, source_target_pairs={{0,1},{1,0},{2,3},{3,2},{4,5},{5,4},{6,7},{7,6},{8,9},{9,8},{10,11... | collective-permute-start | bytes 245768 | tf_op jit(solution)/shard_map/ppermute | solution.py:451
  109.2 5.3 %collective-permute-start.23 = (bf16[64,640]{1,0:T(8,128)(2,1)S(1)}, bf16[64,640]{1,0:T(8,128)(2,1)S(1)}, u32[]{:S(2)}, u32[]{:S(2)}) collective-permute-start(bf16[64,640]{1,0:T(8,128)(2,1)S(1)} %sum.1.w0_ref), channel_id=1, source_target_pairs={{0,2},{1,3},{2,0},{3,1},{4,6},{5,7},{6,4},{7,5},{8,10},{9,11},{10,... | collective-permute-start | bytes 245768 | tf_op jit(solution)/shard_map/ppermute | solution.py:451
  110.6 4.7 %collective-permute-start.24 = (bf16[64,640]{1,0:T(8,128)(2,1)S(1)}, bf16[64,640]{1,0:T(8,128)(2,1)S(1)}, u32[]{:S(2)}, u32[]{:S(2)}) collective-permute-start(bf16[64,640]{1,0:T(8,128)(2,1)S(1)} %sum.1.w0_ref), channel_id=1, source_target_pairs={{0,3},{1,2},{2,1},{3,0},{4,7},{5,6},{6,5},{7,4},{8,11},{9,10},{10,... | collective-permute-start | bytes 245768 | tf_op jit(solution)/shard_map/ppermute | solution.py:451
  (4 other events, 2.8 us)

commit v6 on v5

--- a/solution.py
+++ b/solution.py
@@ -132,7 +132,7 @@
 def place_body(owners, capacity, stride, *refs):
     owned_ref, normed_ref, landing_ref = refs[-3:]
     rows = owned_ref.shape[0]
-    arrived = load_blocks(refs[:-3])
+    arrived = load_blocks(refs[:-4])
     total = arrived.shape[0]
     pick = hot(iota((owners, total), 1) == iota((owners, total), 0) * stride + capacity)
     table = mm(pick, arrived).astype(BF16)
@@ -143,7 +143,7 @@
     landing_ref[...] = landing_row(table, owners, capacity, capacity).astype(jnp.int32)
 
 
-def early_body(cot_ref, outw_ref, grad_ref):
+def early_body(cot_ref, outw_ref, proj_ref, grad_ref):
     grad_ref[...] = mm_t(cot_ref[...], outw_ref[...])
 
 
@@ -214,7 +214,7 @@
     gate_ref, slope_ref, query_ref, partial_ref, grad_ref,
     out_ref, gated_ref, gate_grad_ref, *rest,
 ):
-    grads, acc_ref = rest[:-1], rest[-1]
+    pieces_ref, acc_ref = rest
     rows, width = query_ref.shape
     me = me_ref[0]
     acc_ref[...] = partial_ref[...]
@@ -225,15 +225,16 @@
     gated_ref[...] = gated
     grad_gated = grad_ref[...]
     grad_attended = norm_back(grad_gated * gate, normed, inv_dev).astype(BF16)
-    acc_ref[...] = grad_attended.astype(F32)
-    piece = width // len(grads)
-    for step, ref in enumerate(grads):
-        ref[...] = acc_ref[:, pl.ds(pl.multiple_of((me ^ step) * piece, LANES), piece)].astype(BF16)
+    piece = pieces_ref.shape[2]
+    for i in range(pieces_ref.shape[0]):
+        pieces_ref[i] = grad_attended[:, i * piece : (i + 1) * piece]
     out_ref[...] = (mm(gated, outw_ref[...]) + owned_ref[...].astype(F32)).astype(BF16)
     gate_grad_ref[...] = (grad_gated * normed * slope_ref[...]).astype(BF16)
 
 
-def side_body(me_ref, normed_ref, gated_ref, cot_ref, gate_grad_ref, proj_ref, kept_ref, sent_ref, gate_in_ref, part_ref):
+def side_body(
+    me_ref, normed_ref, gated_ref, cot_ref, gate_grad_ref, proj_ref, kept_ref, sent_ref, gate_in_ref, part_ref
+):
     width = gated_ref.shape[1]
     me = me_ref[0]
     gate_grad = gate_grad_ref[...]
@@ -325,38 +326,25 @@
         ref[...] = (total_ref[at, :] * slope_ref[at, :]).astype(BF16)
 
 
-def backward_far_body(
-    me_ref, lengths_ref, g0_ref, g1_ref, g2_ref, g3_ref, part_ref, slope_ref, *rest
-):
-    o2_ref, o3_ref, total_ref, grad_ref = rest[-4:]
-    rows = g0_ref.shape[0]
-    me = me_ref[0]
-    for step, ref in enumerate((g0_ref, g1_ref, g2_ref, g3_ref)):
-        grad_ref[block_at(me ^ step, rows), :] = ref[...]
+def backward_far_body(me_ref, lengths_ref, grad_ref, part_ref, slope_ref, *rest):
+    sent_ref, o2_ref, o3_ref, total_ref = rest[-4:]
+    me = me_ref[0]
     total_ref[...] = jnp.zeros_like(total_ref)
     backward_rows(
         (2, 3), (), me, lengths_ref, part_ref, slope_ref, grad_ref, total_ref, (o2_ref, o3_ref)
     )
+    for step, ref in ((0, None), (1, None), (2, o2_ref), (3, o3_ref)):
+        sent_ref[me ^ step] = jnp.zeros_like(o2_ref) if ref is None else ref[...]
 
 
 def backward_rest_body(
-    me_ref, lengths_ref, part_ref, slope_ref, grad_ref, sums_ref, o0_ref, o1_ref, total_ref
+    me_ref, lengths_ref, grad_ref, part_ref, slope_ref, sums_ref, *rest
 ):
+    o0_ref, o1_ref, total_ref = rest[-3:]
     total_ref[...] = sums_ref[...]
     backward_rows(
         (1, 0), (2, 3), me_ref[0], lengths_ref, part_ref, slope_ref, grad_ref, total_ref, (o1_ref, o0_ref)
     )
-
-
-def relay(value, after):
-    return pl.pallas_call(
-        lambda *refs: None,
-        name="relay",
-        out_shape=jax.ShapeDtypeStruct(value.shape, value.dtype),
-        in_specs=[ANYWHERE] * (1 + len(after)),
-        out_specs=ANYWHERE,
-        input_output_aliases={0: 0},
-    )(value, *after)
 
 
 def weight_body(sources, pairs, dp_ref, kept_side_ref, came_side_ref, *refs):
@@ -385,7 +373,7 @@
 
 
 def input_body(
-    blocks, me_ref, mask_ref, g0_ref, g1_ref, g2_ref, g3_ref,
+    blocks, me_ref, mask_ref, own_ref, near_ref, far_ref,
     gate_in_ref, owned_ref, cot_ref, landing_ref, proj_ref, *rest,
 ):
     out_ref = rest[-1]
@@ -393,11 +381,12 @@
     me = me_ref[0]
     piece = width // 4
     total = gate_in_ref[...]
-    for step, ref in enumerate((g0_ref, g1_ref, g2_ref, g3_ref)):
+    came = (own_ref[...], near_ref[...], far_ref[me ^ 2], far_ref[me ^ 3])
+    for step, value in enumerate(came):
         cols = [
             proj_ref[:, pl.ds(pl.multiple_of(b * width + (me ^ step) * piece, LANES), piece)] for b in (1, 2, 3)
         ]
-        total += mm_t(ref[...], jnp.concatenate(cols, axis=1))
+        total += mm_t(value, jnp.concatenate(cols, axis=1))
     centred, inv_scale = normalize(owned_ref[...].astype(F32))
     grad = (norm_back(total, centred, inv_scale) + cot_ref[...].astype(F32)).astype(BF16)
     select = hot(iota((rows, landing_ref.shape[1]), 0) + 1 == landing_ref[...])
@@ -454,8 +443,8 @@
         near, far = hop(value, 1), hop(value, 2)
         return near, far, hop(far, 1)
 
-    def exchange(values):
-        return [values[0]] + [hop(values[step], step) for step in (2, 3, 1)]
+    def trade(value):
+        return lax.all_to_all(value, "ctx", split_axis=0, concat_axis=0, tiled=True)
 
     by_hops = owners <= 8
     blocks = owners if by_hops else 1
@@ -490,29 +479,29 @@
         ],
     )
     arrived = swap(outgoing)
+    wide = ((rows, width), F32)
+    (grad_gated,) = call(early_body, "early", [wide], [], [cotangent, out_weight, proj_weight])
     owned, normed, landing = call(
         functools.partial(place_body, owners, capacity, stride),
-        "place", [square, square, ((1, owners * capacity), jnp.int32)], [], arrived,
+        "place", [square, square, ((1, owners * capacity), jnp.int32)], [], arrived, far=[grad_gated],
     )
     near, far, cross = gather(normed)
-    wide = ((rows, width), F32)
-    (grad_gated,) = call(early_body, "early", [wide], [], [cotangent, out_weight], flops=10**8)
     gate, slope, query, partial = call(
         own_body, "own_rows", [square, wide, square, wide],
         [me, lengths], [normed, proj_weight], flops=10**10, vmem=16,
     )
     (partial,) = call(
         middle_body, "middle", [wide], [me, lengths], [near, far, proj_weight, query, partial],
-        vmem=16,
-    )
-    layer_out, gated, gate_grad, *grad_pieces = call(
+        flops=10**10, vmem=16,
+    )
+    layer_out, gated, gate_grad, grad_pieces = call(
         forward_body, "forward",
-        [square, square, square] + [((rows, piece), BF16)] * cycle,
+        [square, square, square, ((cycle, rows, piece), BF16)],
         [me, lengths],
         [cross, proj_weight, out_weight, owned, gate, slope, query, partial, grad_gated],
         scratch=[pltpu.VMEM((rows, width), F32)], vmem=16,
     )
-    r0, r2, r3, r1 = exchange(grad_pieces)
+    grad_all = trade(grad_pieces).reshape(cycle * rows, piece)
     side_half = ((width, 4 * piece), BF16)
     side_piece = ((width, 2 * piece), BF16)
     side_kept, side_sent, gate_in = call(
@@ -532,19 +521,19 @@
     side_last = hop(side_send, 2)
     grad_block = ((rows, 3 * piece), BF16)
     sums = ((rows * cycle, 3 * piece), F32)
-    grad_rows = ((rows * cycle, piece), BF16)
-    far_block, cross_block, totals, grad_all = call(
-        backward_far_body, "backward_far", [grad_block, grad_block, sums, grad_rows],
-        [me, lengths], [r0, r1, r2, r3, parts, slopes], vmem=16, far=[side_send],
-    )
-    p2, p3 = hop(far_block, 2), hop(cross_block, 3)
+    sent_blocks, far_block, cross_block, totals = call(
+        backward_far_body, "backward_far",
+        [((cycle, rows, 3 * piece), BF16), grad_block, grad_block, sums],
+        [me, lengths], [grad_all, parts, slopes], vmem=16,
+    )
+    far_came = trade(sent_blocks)
     own_block, near_block = call(
         backward_rest_body, "backward_rest", [grad_block] * 2,
-        [me, lengths], [parts, slopes, grad_all, totals], vmem=16,
+        [me, lengths], [grad_all, parts, slopes, totals], vmem=16, far=[side_last],
         scratch=[pltpu.VMEM(*sums)],
     )
     p1 = hop(near_block, 1)
-    p0, grads = own_block, [own_block, near_block, far_block, cross_block]
+    grads = [own_block, near_block, far_block, cross_block]
     share = width // owners
     pairs = owners // 2
     columns = 5 * piece
@@ -557,7 +546,7 @@
     if by_hops:
         kept, sent = weight_parts
         halves = call(
-            pair_body, "pair_sum", [((share, columns), BF16)] * pairs, [], [kept, dp_hop(relay(sent, [p2, p3]), 1)]
+            pair_body, "pair_sum", [((share, columns), BF16)] * pairs, [], [kept, dp_hop(sent, 1)]
         )
         summed_parts = [halves[0]] + [dp_hop(halves[j], 2 * j) for j in range(1, pairs)]
     else:
@@ -565,7 +554,8 @@
         summed_parts = [swap_whole(weight_parts[0]).reshape(owners, share, columns)]
     (back,) = call(
         functools.partial(input_body, blocks), "input_grad", [((owners * capacity, width), BF16)], [me, mask],
-        [p0, p1, p2, p3, gate_in, owned, cotangent, landing, proj_weight], vmem=16,
+        [own_block, p1, far_came, gate_in, owned, cotangent, landing, proj_weight], vmem=16,
+        far=[halves[0]],
     )
     returned = swap_whole(back)
     (mine,) = call(sum_body, "sum", [((share, columns), BF16)], [], summed_parts)

time: 118 us -> 129 us (1.093)
  local copies, waits for them, and re-layouts: 12.4 us -> 24.4 us
  waiting for transfers between devices: 45.9 us -> 38.6 us
  Pallas kernels: 18.7 us -> 23.9 us
  starting transfers between devices: 39.4 us -> 41.1 us
    ppermute x14 -> x9, waiting for transfers between devices: 25.7 us -> 10.1 us  [hop(): return lax.ppermute(value, 'ctx', [(i, i ^ step) for i in range(cycle)])]
    unnamed x52 -> x84, local copies, waits for them, and re-layouts: 12.4 us -> 24.4 us
    all_to_all x0 -> x2, starting transfers between devices: none -> 8.47 us  [trade(): return lax.all_to_all(value, 'ctx', split_axis=0, concat_axis=0, tiled=True)]
    ppermute x11, waiting for transfers between devices: 20.2 us -> 28.5 us  [dp_hop(): return lax.ppermute(value, 'dp', [(i, i ^ step) for i in range(owners)])]
    pallas_call x17, Pallas kernels: 18.7 us -> 23.9 us  [call(): pl.pallas_call(body, name=name, out_shape=[jax.ShapeDtypeStruct(s, d) for...]
    ppermute x14 -> x9, starting transfers between devices: 11.1 us -> 6.01 us  [hop(): return lax.ppermute(value, 'ctx', [(i, i ^ step) for i in range(cycle)])]
  transfers between devices with their start and end apart: 26 -> 23, of which waited for: 14 -> 9; matrix products, arithmetic and copies ran while one was open for 0% -> 0% of each run, Pallas kernels for 5% -> 12%
where the time goes in v6:
time: 129 us
  starting transfers between devices  41.1 us (32%)
  waiting for transfers between devices  38.6 us (30%)
  local copies, waits for them, and re-layouts  24.4 us (19%)
  Pallas kernels  23.9 us (19%)
    ppermute x11, waiting for transfers between devices, dp_hop(): return lax.ppermute(value, 'dp', [(i, i ^ step) for i in range(owners)])  28.5 us
    unnamed x84, local copies, waits for them, and re-layouts  24.4 us
    pallas_call x17, Pallas kernels, call(): pl.pallas_call(body, name=name, out_shape=[jax.ShapeDtypeStruct(s, d) for...  23.9 us
    ppermute x11, starting transfers between devices, dp_hop(): return lax.ppermute(value, 'dp', [(i, i ^ step) for i in range(owners)])  17.7 us
    ppermute x9, waiting for transfers between devices, hop(): return lax.ppermute(value, 'ctx', [(i, i ^ step) for i in range(cycle)])  10.1 us
    all_to_all x1, starting transfers between devices, swap_whole(): lax.all_to_all(split, 'dp', split_axis=0, concat_axis=0, tiled=True)  8.95 us
    all_to_all x2, starting transfers between devices, trade(): return lax.all_to_all(value, 'ctx', split_axis=0, concat_axis=0, tiled=True)  8.47 us
    ppermute x9, starting transfers between devices, hop(): return lax.ppermute(value, 'ctx', [(i, i ^ step) for i in range(cycle)])  6.01 us
  transfers between devices with their start and end apart: 23, of which 9 were waited for; matrix products, arithmetic and copies ran while one was open for 0% of the time, Pallas kernels for 12%

profile of v6, /device:TPU:0, one launch (start us, length us, event | category | flops | bytes accessed | tf_op | source)
XLA Modules:
  0.0 129.0 jit_solution(5290654198502356680)
XLA Ops:
  1.3 0.9 copy-done.40
  3.7 3.0 %collective-permute-start = (bf16[72,512]{1,0:T(8,128)(2,1)S(1)}, bf16[72,512]{1,0:T(8,128)(2,1)S(1)}, u32[]{:S(2)}, u32[]{:S(2)}) collective-permute-start(bf16[72,512]{1,0:T(8,128)(2,1)S(1)} %get-tuple-element.45), channel_id=1, source_target_pairs={{0,4},{4,0},{8,12},{12,8},{16,20},{20,16},{24,28},{28,24},{1,5},{5... | collective-permute-start | bytes 221192 | tf_op jit(solution)/shard_map/ppermute | solution.py:455
  6.7 1.6 %collective-permute-start.1 = (bf16[72,512]{1,0:T(8,128)(2,1)S(1)}, bf16[72,512]{1,0:T(8,128)(2,1)S(1)}, u32[]{:S(2)}, u32[]{:S(2)}) collective-permute-start(bf16[72,512]{1,0:T(8,128)(2,1)S(1)} %get-tuple-element.46), channel_id=1, source_target_pairs={{0,8},{4,12},{8,0},{12,4},{16,24},{20,28},{24,16},{28,20},{1,9},{5... | collective-permute-start | bytes 221192 | tf_op jit(solution)/shard_map/ppermute | solution.py:455
  8.3 3.0 %collective-permute-start.3 = (bf16[72,512]{1,0:T(8,128)(2,1)S(1)}, bf16[72,512]{1,0:T(8,128)(2,1)S(1)}, u32[]{:S(2)}, u32[]{:S(2)}) collective-permute-start(bf16[72,512]{1,0:T(8,128)(2,1)S(1)} %get-tuple-element.48), channel_id=1, source_target_pairs={{0,16},{4,20},{8,24},{12,28},{16,0},{20,4},{24,8},{28,12},{1,17},{... | collective-permute-start | bytes 221192 | tf_op jit(solution)/shard_map/ppermute | solution.py:455
  11.2 1.3 %collective-permute-start.4 = (bf16[72,512]{1,0:T(8,128)(2,1)S(1)}, bf16[72,512]{1,0:T(8,128)(2,1)S(1)}, u32[]{:S(2)}, u32[]{:S(2)}) collective-permute-start(bf16[72,512]{1,0:T(8,128)(2,1)S(1)} %get-tuple-element.49), channel_id=1, source_target_pairs={{0,20},{4,16},{8,28},{12,24},{16,4},{20,0},{24,12},{28,8},{1,21},{... | collective-permute-start | bytes 221192 | tf_op jit(solution)/shard_map/ppermute | solution.py:455
  12.5 3.6 %collective-permute-start.5 = (bf16[72,512]{1,0:T(8,128)(2,1)S(1)}, bf16[72,512]{1,0:T(8,128)(2,1)S(1)}, u32[]{:S(2)}, u32[]{:S(2)}) collective-permute-start(bf16[72,512]{1,0:T(8,128)(2,1)S(1)} %get-tuple-element.50), channel_id=1, source_target_pairs={{0,24},{4,28},{8,16},{12,20},{16,8},{20,12},{24,0},{28,4},{1,25},{... | collective-permute-start | bytes 221192 | tf_op jit(solution)/shard_map/ppermute | solution.py:455
  16.2 1.6 %copy-done = bf16[512,2048]{1,0:T(8,128)(2,1)S(1)} copy-done((bf16[512,2048]{1,0:T(8,128)(2,1)S(1)}, bf16[512,2048]{1,0:T(8,128)(2,1)}, u32[]{:S(2)}) %copy-start) | copy-done | bytes 2097176
  17.8 0.9 copy-done.7
  18.7 1.0 copy-done.14
  20.1 2.4 %collective-permute-done.4.refs_5_ = bf16[72,512]{1,0:T(8,128)(2,1)S(1)} collective-permute-done((bf16[72,512]{1,0:T(8,128)(2,1)S(1)}, bf16[72,512]{1,0:T(8,128)(2,1)S(1)}, u32[]{:S(2)}, u32[]{:S(2)}) %collective-permute-start.4) | collective-permute-done | bytes 73760 | tf_op jit(solution)/shard_map/ppermute | solution.py:455
  23.3 0.8 place.1
  24.2 1.6 %collective-permute-start.7 = (bf16[256,512]{1,0:T(8,128)(2,1)S(1)}, bf16[256,512]{1,0:T(8,128)(2,1)S(1)}, u32[]{:S(2)}, u32[]{:S(2)}) collective-permute-start(bf16[256,512]{1,0:T(8,128)(2,1)S(1)} %get-tuple-element.52.normed_ref.n0_ref.refs_0_), channel_id=1, source_target_pairs={{0,2},{1,3},{2,0},{3,1},{4,6},{5,7},{6,4},{7,5},{8,10},{9,11},{10,... | collective-permute-start | bytes 786440 | tf_op jit(solution)/shard_map/ppermute | solution.py:440
  25.8 2.2 %own_rows.1 = (bf16[256,512]{1,0:T(8,128)(2,1)S(1)}, f32[256,512]{1,0:T(8,128)S(1)}, bf16[256,512]{1,0:T(8,128)(2,1)S(1)}, f32[256,512]{1,0:T(8,128)S(1)}) custom-call(s32[1]{0:T(128)} %bitcast.me_ref, s32[1,3]{1,0:T(1,128)S(1)} %copy-done.37, bf16[256,512]{1,0:T(8,128)(2,1)S(1)} %get-tuple-element.52.normed_ref.n0_ref.refs_0_, bf16[512,2048]{1,0:T(8,128)(2,1)S(1)} %copy-done.1), custom_call_target="tpu_custom_call" | custom-call | flops 10000000000 | bytes 1048576 | tf_op jit(solution)/shard_map/own_rows/pallas_call | solution.py:22
  28.0 5.0 %collective-permute-done.7.far_ref.n2_ref.refs_2_ = bf16[256,512]{1,0:T(8,128)(2,1)S(1)} collective-permute-done((bf16[256,512]{1,0:T(8,128)(2,1)S(1)}, bf16[256,512]{1,0:T(8,128)(2,1)S(1)}, u32[]{:S(2)}, u32[]{:S(2)}) %collective-permute-start.7) | collective-permute-done | bytes 262176 | tf_op jit(solution)/shard_map/ppermute | solution.py:440
  34.5 1.9 %forward.1 = (bf16[256,512]{1,0:T(8,128)(2,1)}, bf16[256,512]{1,0:T(8,128)(2,1)S(1)}, bf16[256,512]{1,0:T(8,128)(2,1)S(1)}, bf16[4,256,128]{2,1,0:T(8,128)(2,1)}) custom-call(s32[1]{0:T(128)} %bitcast.me_ref, s32[1,3]{1,0:T(1,128)S(1)} %copy-done.37, bf16[256,512]{1,0:T(8,128)(2,1)S(1)} %collective-permute-done.8.cross_ref.n3_ref.refs_3_, ...), custom_call_target="tpu_custom_call" | custom-call | flops 100000000 | bytes 1048576 | tf_op jit(solution)/shard_map/forward/pallas_call | solution.py:22
  36.4 1.6 %side.1 = (bf16[512,512]{1,0:T(8,128)(2,1)S(1)}, bf16[512,512]{1,0:T(8,128)(2,1)}, f32[256,512]{1,0:T(8,128)S(1)}) custom-call(s32[1]{0:T(128)} %bitcast.me_ref, bf16[256,512]{1,0:T(8,128)(2,1)S(1)} %get-tuple-element.52.normed_ref.n0_ref.refs_0_, bf16[256,512]{1,0:T(8,128)(2,1)S(1)} %get-tuple-element.63.gated_ref, bf16[256,512]{1,0:T(8,128)(2,1)S(1)} %copy-done.8, ...), custom_call_target="tpu_custom_call" | custom-call | flops 100000000 | bytes 1048576 | tf_op jit(solution)/shard_map/side/pallas_call | solution.py:22
  38.9 5.0 %all-to-all-start = ((bf16[4,256,128]{2,1,0:T(8,128)(2,1)}), bf16[4,256,128]{2,1,0:T(8,128)(2,1)S(1)}, u32[]{:S(2)}, u32[]{:S(2)}) async-start(bf16[4,256,128]{2,1,0:T(8,128)(2,1)} %get-tuple-element.59), calls=%async_computation | async-start | bytes 524288 | tf_op jit(solution)/shard_map/all_to_all | solution.py:447
  43.9 1.8 %side_sum.1 = (bf16[512,256]{1,0:T(8,128)(2,1)S(1)}, bf16[512,256]{1,0:T(8,128)(2,1)}) custom-call(bf16[512,512]{1,0:T(8,128)(2,1)S(1)} %get-tuple-element.65.kept_ref, bf16[512,512]{1,0:T(8,128)(2,1)} %collective-permute-done.10.came_ref), custom_call_target="tpu_custom_call" | custom-call | flops 100000000 | bytes 1048576 | tf_op jit(solution)/shard_map/side_sum/pallas_call | solution.py:22
  46.4 2.1 %collective-permute-start.11 = (bf16[512,256]{1,0:T(8,128)(2,1)}, bf16[512,256]{1,0:T(8,128)(2,1)}, u32[]{:S(2)}, u32[]{:S(2)}) collective-permute-start(bf16[512,256]{1,0:T(8,128)(2,1)} %get-tuple-element.67), channel_id=1, source_target_pairs={{0,2},{1,3},{2,0},{3,1},{4,6},{5,7},{6,4},{7,5},{8,10},{9,11},{10,... | collective-permute-start | bytes 786440 | tf_op jit(solution)/shard_map/ppermute | solution.py:440
  48.6 0.9 copy-done.11
  49.5 0.9 copy-done.21
  50.5 0.9 copy-done.24
  52.3 1.1 copy-done.2
  53.4 1.7 %copy-done.3 = f32[1024,384]{1,0:T(8,128)S(1)} copy-done((f32[1024,384]{1,0:T(8,128)S(1)}, f32[1024,384]{1,0:T(8,128)}, u32[]{:S(2)}) %copy-start.3) | copy-done | bytes 1572888
  55.1 4.4 %backward_far.1 = (bf16[4,256,384]{2,1,0:T(8,128)(2,1)S(1)}, bf16[256,384]{1,0:T(8,128)(2,1)S(1)}, bf16[256,384]{1,0:T(8,128)(2,1)S(1)}, f32[1024,384]{1,0:T(8,128)S(1)}) custom-call(s32[1]{0:T(128)} %bitcast.me_ref, s32[1,3]{1,0:T(1,128)S(1)} %copy-done.37, bf16[1024,128]{1,0:T(8,128)(2,1)S(1)} %bitcast.7, ...), custom_call_target="tpu_custom_call" | custom-call | flops 100000000 | bytes 1048576 | tf_op jit(solution)/shard_map/backward_far/pallas_call | solution.py:22
  59.5 1.2 copy-done.16
  60.7 0.9 copy-done.28
  63.0 3.5 %all-to-all-start.1 = ((bf16[4,256,384]{2,1,0:T(8,128)(2,1)}), bf16[4,256,384]{2,1,0:T(8,128)(2,1)S(1)}, u32[]{:S(2)}, u32[]{:S(2)}) async-start(bf16[4,256,384]{2,1,0:T(8,128)(2,1)} %copy-done.28), calls=%async_computation.1 | async-start | bytes 1572864 | tf_op jit(solution)/shard_map/all_to_all | solution.py:447
  66.5 1.4 %copy-done.4 = f32[1024,384]{1,0:T(8,128)S(1)} copy-done((f32[1024,384]{1,0:T(8,128)S(1)}, f32[1024,384]{1,0:T(8,128)}, u32[]{:S(2)}) %copy-start.4) | copy-done | bytes 1572888
  67.9 1.1 copy-done.6
  69.0 1.4 %copy-done.17 = f32[1024,384]{1,0:T(8,128)S(1)} copy-done((f32[1024,384]{1,0:T(8,128)S(1)}, f32[1024,384]{1,0:T(8,128)}, u32[]{:S(2)}) %copy-start.17) | copy-done | bytes 1572888
  70.5 2.4 %backward_rest.1 = (bf16[256,384]{1,0:T(8,128)(2,1)S(1)}, bf16[256,384]{1,0:T(8,128)(2,1)}) custom-call(s32[1]{0:T(128)} %bitcast.me_ref, s32[1,3]{1,0:T(1,128)S(1)} %copy-done.37, bf16[1024,128]{1,0:T(8,128)(2,1)S(1)} %bitcast.8, bf16[1024,384]{1,0:T(8,128)(2,1)S(1)} %copy-done.6, f32[1024,384]{1,0:T(8,128)S(1)} %copy-done.4, f32[1024,384]{1,0:T(8,128)S(1)} %copy-done.17, ...), custom_call_target="tpu_custom_call" | custom-call | flops 100000000 | bytes 1048576 | tf_op jit(solution)/shard_map/backward_rest/pallas_call | solution.py:22
  72.9 1.9 %weights.1 = (bf16[256,640]{1,0:T(8,128)(2,1)S(1)}, bf16[256,640]{1,0:T(8,128)(2,1)S(1)}) custom-call(s32[1]{0:T(128)} %bitcast.1.mask_ref.dp_ref, bf16[512,256]{1,0:T(8,128)(2,1)S(1)} %copy-done.32, bf16[512,256]{1,0:T(8,128)(2,1)} %collective-permute-done.11.rest_0_.came_side_ref, bf16[256,512]{1,0:T(8,128)(2,1)S(1)} %copy-done.12, ...), custom_call_target="tpu_custom_call" | custom-call | flops 100000000 | bytes 1048576 | tf_op jit(solution)/shard_map/weights/pallas_call | solution.py:22
  75.8 9.2 %collective-permute-done.13.came_ref = bf16[256,640]{1,0:T(8,128)(2,1)S(1)} collective-permute-done((bf16[256,640]{1,0:T(8,128)(2,1)S(1)}, bf16[256,640]{1,0:T(8,128)(2,1)S(1)}, u32[]{:S(2)}, u32[]{:S(2)}) %collective-permute-start.13) | collective-permute-done | bytes 327712 | tf_op jit(solution)/shard_map/ppermute | solution.py:455
  85.2 0.9 copy-done.19
  86.1 0.9 copy-done.27
  87.0 1.0 copy-done.30
  88.1 2.1 %input_grad.1 = bf16[512,512]{1,0:T(8,128)(2,1)S(1)} custom-call(s32[1]{0:T(128)} %bitcast.me_ref, s32[1]{0:T(128)} %bitcast.1.mask_ref.dp_ref, bf16[256,384]{1,0:T(8,128)(2,1)S(1)} %copy-done.27, bf16[256,384]{1,0:T(8,128)(2,1)} %collective-permute-done.12.near_ref, bf16[4,256,384]{2,1,0:T(8,128)(2,1)S(1)} %all-to-all-done.1.far_ref, ...), custom_call_target="tpu_custom_call" | custom-call | flops 100000000 | bytes 1048576 | tf_op jit(solution)/shard_map/input_grad/pallas_call | solution.py:22
  91.1 8.9 %all-to-all-start.2 = ((bf16[8,64,512]{2,1,0:T(8,128)(2,1)}), bf16[8,64,512]{2,1,0:T(8,128)(2,1)S(1)}, u32[]{:S(2)}, u32[]{:S(2)}) async-start(bf16[8,64,512]{2,1,0:T(8,128)(2,1)} %bitcast.9), calls=%async_computation.2 | async-start | bytes 1048576 | tf_op jit(solution)/shard_map/all_to_all | solution.py:459
  100.0 2.0 %collective-permute-start.14 = (bf16[64,640]{1,0:T(8,128)(2,1)S(1)}, bf16[64,640]{1,0:T(8,128)(2,1)S(1)}, u32[]{:S(2)}, u32[]{:S(2)}) collective-permute-start(bf16[64,640]{1,0:T(8,128)(2,1)S(1)} %get-tuple-element.79), channel_id=1, source_target_pairs={{0,8},{4,12},{8,0},{12,4},{16,24},{20,28},{24,16},{28,20},{1,9},{5... | collective-permute-start | bytes 245768 | tf_op jit(solution)/shard_map/ppermute | solution.py:455
  102.0 2.4 %collective-permute-start.15 = (bf16[64,640]{1,0:T(8,128)(2,1)S(1)}, bf16[64,640]{1,0:T(8,128)(2,1)S(1)}, u32[]{:S(2)}, u32[]{:S(2)}) collective-permute-start(bf16[64,640]{1,0:T(8,128)(2,1)S(1)} %get-tuple-element.80), channel_id=1, source_target_pairs={{0,16},{4,20},{8,24},{12,28},{16,0},{20,4},{24,8},{28,12},{1,17},{... | collective-permute-start | bytes 245768 | tf_op jit(solution)/shard_map/ppermute | solution.py:455
  104.4 7.2 %collective-permute-done.14.refs_1_ = bf16[64,640]{1,0:T(8,128)(2,1)S(1)} collective-permute-done((bf16[64,640]{1,0:T(8,128)(2,1)S(1)}, bf16[64,640]{1,0:T(8,128)(2,1)S(1)}, u32[]{:S(2)}, u32[]{:S(2)}) %collective-permute-start.14) | collective-permute-done | bytes 81952 | tf_op jit(solution)/shard_map/ppermute | solution.py:455
  111.6 8.9 %collective-permute-done.15.refs_2_ = bf16[64,640]{1,0:T(8,128)(2,1)S(1)} collective-permute-done((bf16[64,640]{1,0:T(8,128)(2,1)S(1)}, bf16[64,640]{1,0:T(8,128)(2,1)S(1)}, u32[]{:S(2)}, u32[]{:S(2)}) %collective-permute-start.15) | collective-permute-done | bytes 81952 | tf_op jit(solution)/shard_map/ppermute | solution.py:455
  120.6 1.4 %collective-permute-start.18 = (bf16[64,640]{1,0:T(8,128)(2,1)S(1)}, bf16[64,640]{1,0:T(8,128)(2,1)S(1)}, u32[]{:S(2)}, u32[]{:S(2)}) collective-permute-start(bf16[64,640]{1,0:T(8,128)(2,1)S(1)} %sum.1.w0_ref), channel_id=1, source_target_pairs={{0,2},{1,3},{2,0},{3,1},{4,6},{5,7},{6,4},{7,5},{8,10},{9,11},{10,... | collective-permute-start | bytes 245768 | tf_op jit(solution)/shard_map/ppermute | solution.py:440
  122.5 2.9 %collective-permute-done.19.w3_ref = bf16[64,640]{1,0:T(8,128)(2,1)S(1)} collective-permute-done((bf16[64,640]{1,0:T(8,128)(2,1)S(1)}, bf16[64,640]{1,0:T(8,128)(2,1)S(1)}, u32[]{:S(2)}, u32[]{:S(2)}) %collective-permute-start.19) | collective-permute-done | bytes 81952 | tf_op jit(solution)/shard_map/ppermute | solution.py:440
  125.4 1.5 %collective-permute-done.18.w2_ref = bf16[64,640]{1,0:T(8,128)(2,1)S(1)} collective-permute-done((bf16[64,640]{1,0:T(8,128)(2,1)S(1)}, bf16[64,640]{1,0:T(8,128)(2,1)S(1)}, u32[]{:S(2)}, u32[]{:S(2)}) %collective-permute-start.18) | collective-permute-done | bytes 81952 | tf_op jit(solution)/shard_map/ppermute | solution.py:440
  126.9 0.9 finish.1
  127.8 1.2 give_back.1
  (99 shorter events, 11.1 us)
Async XLA Ops:
  3.7 8.9 %collective-permute-start = (bf16[72,512]{1,0:T(8,128)(2,1)S(1)}, bf16[72,512]{1,0:T(8,128)(2,1)S(1)}, u32[]{:S(2)}, u32[]{:S(2)}) collective-permute-start(bf16[72,512]{1,0:T(8,128)(2,1)S(1)} %get-tuple-element.45), channel_id=1, source_target_pairs={{0,4},{4,0},{8,12},{12,8},{16,20},{20,16},{24,28},{28,24},{1,5},{5... | collective-permute-start | bytes 221192 | tf_op jit(solution)/shard_map/ppermute | solution.py:455
  6.7 9.5 %collective-permute-start.1 = (bf16[72,512]{1,0:T(8,128)(2,1)S(1)}, bf16[72,512]{1,0:T(8,128)(2,1)S(1)}, u32[]{:S(2)}, u32[]{:S(2)}) collective-permute-start(bf16[72,512]{1,0:T(8,128)(2,1)S(1)} %get-tuple-element.46), channel_id=1, source_target_pairs={{0,8},{4,12},{8,0},{12,4},{16,24},{20,28},{24,16},{28,20},{1,9},{5... | collective-permute-start | bytes 221192 | tf_op jit(solution)/shard_map/ppermute | solution.py:455
  8.3 11.8 %collective-permute-start.2 = (bf16[72,512]{1,0:T(8,128)(2,1)S(1)}, bf16[72,512]{1,0:T(8,128)(2,1)S(1)}, u32[]{:S(2)}, u32[]{:S(2)}) collective-permute-start(bf16[72,512]{1,0:T(8,128)(2,1)S(1)} %get-tuple-element.47), channel_id=1, source_target_pairs={{0,12},{4,8},{8,4},{12,0},{16,28},{20,24},{24,20},{28,16},{1,13},{... | collective-permute-start | bytes 221192 | tf_op jit(solution)/shard_map/ppermute | solution.py:455
  8.3 11.8 %collective-permute-start.3 = (bf16[72,512]{1,0:T(8,128)(2,1)S(1)}, bf16[72,512]{1,0:T(8,128)(2,1)S(1)}, u32[]{:S(2)}, u32[]{:S(2)}) collective-permute-start(bf16[72,512]{1,0:T(8,128)(2,1)S(1)} %get-tuple-element.48), channel_id=1, source_target_pairs={{0,16},{4,20},{8,24},{12,28},{16,0},{20,4},{24,8},{28,12},{1,17},{... | collective-permute-start | bytes 221192 | tf_op jit(solution)/shard_map/ppermute | solution.py:455
  11.2 11.3 %collective-permute-start.4 = (bf16[72,512]{1,0:T(8,128)(2,1)S(1)}, bf16[72,512]{1,0:T(8,128)(2,1)S(1)}, u32[]{:S(2)}, u32[]{:S(2)}) collective-permute-start(bf16[72,512]{1,0:T(8,128)(2,1)S(1)} %get-tuple-element.49), channel_id=1, source_target_pairs={{0,20},{4,16},{8,28},{12,24},{16,4},{20,0},{24,12},{28,8},{1,21},{... | collective-permute-start | bytes 221192 | tf_op jit(solution)/shard_map/ppermute | solution.py:455
  12.5 10.0 %collective-permute-start.5 = (bf16[72,512]{1,0:T(8,128)(2,1)S(1)}, bf16[72,512]{1,0:T(8,128)(2,1)S(1)}, u32[]{:S(2)}, u32[]{:S(2)}) collective-permute-start(bf16[72,512]{1,0:T(8,128)(2,1)S(1)} %get-tuple-element.50), channel_id=1, source_target_pairs={{0,24},{4,28},{8,16},{12,20},{16,8},{20,12},{24,0},{28,4},{1,25},{... | collective-permute-start | bytes 221192 | tf_op jit(solution)/shard_map/ppermute | solution.py:455
  16.1 7.2 %collective-permute-start.6 = (bf16[72,512]{1,0:T(8,128)(2,1)S(1)}, bf16[72,512]{1,0:T(8,128)(2,1)S(1)}, u32[]{:S(2)}, u32[]{:S(2)}) collective-permute-start(bf16[72,512]{1,0:T(8,128)(2,1)S(1)} %get-tuple-element.51), channel_id=1, source_target_pairs={{0,28},{4,24},{8,20},{12,16},{16,12},{20,8},{24,4},{28,0},{1,29},{... | collective-permute-start | bytes 221192 | tf_op jit(solution)/shard_map/ppermute | solution.py:455
  16.2 1.6 %copy-start = (bf16[512,2048]{1,0:T(8,128)(2,1)S(1)}, bf16[512,2048]{1,0:T(8,128)(2,1)}, u32[]{:S(2)}) copy-start(bf16[512,2048]{1,0:T(8,128)(2,1)} %proj_ref.13) | copy-start | bytes 6291460
  18.7 1.0 copy-start.14
  19.7 6.1 %copy-start.1 = (bf16[512,2048]{1,0:T(8,128)(2,1)S(1)}, bf16[512,2048]{1,0:T(8,128)(2,1)}, u32[]{:S(2)}) copy-start(bf16[512,2048]{1,0:T(8,128)(2,1)} %proj_ref.13) | copy-start | bytes 6291460
  19.7 6.1 %copy-start.37 = (s32[1,3]{1,0:T(1,128)S(1)}, s32[1,3]{1,0:T(1,128)}, u32[]{:S(2)}) copy-start(s32[1,3]{1,0:T(1,128)} %lengths_ref.9) | copy-start | bytes 40
  24.1 10.4 %copy-start.18 = (bf16[256,512]{1,0:T(8,128)(2,1)}, bf16[256,512]{1,0:T(8,128)(2,1)S(1)}, u32[]{:S(2)}) copy-start(bf16[256,512]{1,0:T(8,128)(2,1)S(1)} %get-tuple-element.53.owned_ref) | copy-start | bytes 786436
  24.2 12.3 %copy-start.10 = (bf16[256,512]{1,0:T(8,128)(2,1)}, bf16[256,512]{1,0:T(8,128)(2,1)S(1)}, u32[]{:S(2)}) copy-start(bf16[256,512]{1,0:T(8,128)(2,1)S(1)} %get-tuple-element.52.normed_ref.n0_ref.refs_0_) | copy-start | bytes 786436
  24.2 8.8 %collective-permute-start.9 = (bf16[256,512]{1,0:T(8,128)(2,1)S(1)}, bf16[256,512]{1,0:T(8,128)(2,1)S(1)}, u32[]{:S(2)}, u32[]{:S(2)}) collective-permute-start(bf16[256,512]{1,0:T(8,128)(2,1)S(1)} %get-tuple-element.52.normed_ref.n0_ref.refs_0_), channel_id=1, source_target_pairs={{0,1},{1,0},{2,3},{3,2},{4,5},{5,4},{6,7},{7,6},{8,9},{9,8},{10,11... | collective-permute-start | bytes 786440 | tf_op jit(solution)/shard_map/ppermute | solution.py:440
  24.2 8.7 %collective-permute-start.7 = (bf16[256,512]{1,0:T(8,128)(2,1)S(1)}, bf16[256,512]{1,0:T(8,128)(2,1)S(1)}, u32[]{:S(2)}, u32[]{:S(2)}) collective-permute-start(bf16[256,512]{1,0:T(8,128)(2,1)S(1)} %get-tuple-element.52.normed_ref.n0_ref.refs_0_), channel_id=1, source_target_pairs={{0,2},{1,3},{2,0},{3,1},{4,6},{5,7},{6,4},{7,5},{8,10},{9,11},{10,... | collective-permute-start | bytes 786440 | tf_op jit(solution)/shard_map/ppermute | solution.py:440
  33.0 1.5 %collective-permute-start.8 = (bf16[256,512]{1,0:T(8,128)(2,1)S(1)}, bf16[256,512]{1,0:T(8,128)(2,1)S(1)}, u32[]{:S(2)}, u32[]{:S(2)}) collective-permute-start(bf16[256,512]{1,0:T(8,128)(2,1)S(1)} %collective-permute-done.7.far_ref.n2_ref.refs_2_), channel_id=1, source_target_pairs={{0,1},{1,0},{2,3},{3,2},{4,5},{5,4},{6,7},{7,6},{8,9},{9,8},{10,11... | collective-permute-start | bytes 786440 | tf_op jit(solution)/shard_map/ppermute | solution.py:440
  33.0 1.5 %copy-start.15 = (bf16[512,512]{1,0:T(8,128)(2,1)S(1)}, bf16[512,512]{1,0:T(8,128)(2,1)}, u32[]{:S(2)}) copy-start(bf16[512,512]{1,0:T(8,128)(2,1)} %outw_ref.3) | copy-start | bytes 1572868
  34.5 1.9 %copy-start.8 = (bf16[256,512]{1,0:T(8,128)(2,1)S(1)}, bf16[256,512]{1,0:T(8,128)(2,1)}, u32[]{:S(2)}) copy-start(bf16[256,512]{1,0:T(8,128)(2,1)} %cot_ref.5) | copy-start | bytes 786436
  38.8 5.1 %collective-permute-start.10 = (bf16[512,512]{1,0:T(8,128)(2,1)}, bf16[512,512]{1,0:T(8,128)(2,1)}, u32[]{:S(2)}, u32[]{:S(2)}) collective-permute-start(bf16[512,512]{1,0:T(8,128)(2,1)} %get-tuple-element.66), channel_id=1, source_target_pairs={{0,1},{1,0},{2,3},{3,2},{4,5},{5,4},{6,7},{7,6},{8,9},{9,8},{10,11... | collective-permute-start | bytes 1572872 | tf_op jit(solution)/shard_map/ppermute | solution.py:440
  38.9 14.5 %all-to-all-start = ((bf16[4,256,128]{2,1,0:T(8,128)(2,1)}), bf16[4,256,128]{2,1,0:T(8,128)(2,1)S(1)}, u32[]{:S(2)}, u32[]{:S(2)}) async-start(bf16[4,256,128]{2,1,0:T(8,128)(2,1)} %get-tuple-element.59), calls=%async_computation | async-start | bytes 524288 | tf_op jit(solution)/shard_map/all_to_all | solution.py:447
  46.4 20.0 %collective-permute-start.11 = (bf16[512,256]{1,0:T(8,128)(2,1)}, bf16[512,256]{1,0:T(8,128)(2,1)}, u32[]{:S(2)}, u32[]{:S(2)}) collective-permute-start(bf16[512,256]{1,0:T(8,128)(2,1)} %get-tuple-element.67), channel_id=1, source_target_pairs={{0,2},{1,3},{2,0},{3,1},{4,6},{5,7},{6,4},{7,5},{8,10},{9,11},{10,... | collective-permute-start | bytes 786440 | tf_op jit(solution)/shard_map/ppermute | solution.py:440
  52.3 1.2 copy-start.2
  53.4 9.6 %copy-start.5 = (bf16[1024,384]{1,0:T(8,128)(2,1)}, bf16[1024,384]{1,0:T(8,128)(2,1)S(1)}, u32[]{:S(2)}) copy-start(bf16[1024,384]{1,0:T(8,128)(2,1)S(1)} %get-tuple-element.60.part_ref) | copy-start | bytes 2359300
  53.4 1.7 %copy-start.3 = (f32[1024,384]{1,0:T(8,128)S(1)}, f32[1024,384]{1,0:T(8,128)}, u32[]{:S(2)}) copy-start(f32[1024,384]{1,0:T(8,128)} %copy-done.2) | copy-start | bytes 4718596
  59.5 1.2 copy-start.16
  63.0 22.2 %all-to-all-start.1 = ((bf16[4,256,384]{2,1,0:T(8,128)(2,1)}), bf16[4,256,384]{2,1,0:T(8,128)(2,1)S(1)}, u32[]{:S(2)}, u32[]{:S(2)}) async-start(bf16[4,256,384]{2,1,0:T(8,128)(2,1)} %copy-done.28), calls=%async_computation.1 | async-start | bytes 1572864 | tf_op jit(solution)/shard_map/all_to_all | solution.py:447
  66.5 1.4 %copy-start.4 = (f32[1024,384]{1,0:T(8,128)S(1)}, f32[1024,384]{1,0:T(8,128)}, u32[]{:S(2)}) copy-start(f32[1024,384]{1,0:T(8,128)} %copy-done.2) | copy-start | bytes 4718596
  67.9 1.1 copy-start.6
  69.0 1.4 %copy-start.17 = (f32[1024,384]{1,0:T(8,128)S(1)}, f32[1024,384]{1,0:T(8,128)}, u32[]{:S(2)}) copy-start(f32[1024,384]{1,0:T(8,128)} %copy-done.16) | copy-start | bytes 4718596
  70.4 2.5 %copy-start.12 = (bf16[256,512]{1,0:T(8,128)(2,1)S(1)}, bf16[256,512]{1,0:T(8,128)(2,1)}, u32[]{:S(2)}) copy-start(bf16[256,512]{1,0:T(8,128)(2,1)} %copy-done.10) | copy-start | bytes 786436
  70.4 2.5 %copy-start.22 = (bf16[256,512]{1,0:T(8,128)(2,1)S(1)}, bf16[256,512]{1,0:T(8,128)(2,1)}, u32[]{:S(2)}) copy-start(bf16[256,512]{1,0:T(8,128)(2,1)} %copy-done.20) | copy-start | bytes 786436
  70.4 2.5 %copy-start.25 = (bf16[256,512]{1,0:T(8,128)(2,1)S(1)}, bf16[256,512]{1,0:T(8,128)(2,1)}, u32[]{:S(2)}) copy-start(bf16[256,512]{1,0:T(8,128)(2,1)} %copy-done.23) | copy-start | bytes 786436
  70.4 2.5 %copy-start.32 = (bf16[512,256]{1,0:T(8,128)(2,1)S(1)}, bf16[512,256]{1,0:T(8,128)(2,1)}, u32[]{:S(2)}) copy-start(bf16[512,256]{1,0:T(8,128)(2,1)} %copy-done.31) | copy-start | bytes 786436
  70.4 2.5 %copy-start.34 = (bf16[256,384]{1,0:T(8,128)(2,1)S(1)}, bf16[256,384]{1,0:T(8,128)(2,1)}, u32[]{:S(2)}) copy-start(bf16[256,384]{1,0:T(8,128)(2,1)} %copy-done.33) | copy-start | bytes 589828
  70.5 2.5 %copy-start.36 = (bf16[256,384]{1,0:T(8,128)(2,1)S(1)}, bf16[256,384]{1,0:T(8,128)(2,1)}, u32[]{:S(2)}) copy-start(bf16[256,384]{1,0:T(8,128)(2,1)} %copy-done.35) | copy-start | bytes 589828
  72.9 12.2 %copy-start.26 = (bf16[256,384]{1,0:T(8,128)(2,1)}, bf16[256,384]{1,0:T(8,128)(2,1)S(1)}, u32[]{:S(2)}) copy-start(bf16[256,384]{1,0:T(8,128)(2,1)S(1)} %get-tuple-element.68.refs_4_.own_ref) | copy-start | bytes 589828
  72.9 12.3 %copy-start.9 = (bf16[256,512]{1,0:T(8,128)(2,1)S(1)}, bf16[256,512]{1,0:T(8,128)(2,1)}, u32[]{:S(2)}) copy-start(bf16[256,512]{1,0:T(8,128)(2,1)} %cot_ref.5) | copy-start | bytes 786436
  74.9 10.1 %collective-permute-start.13 = (bf16[256,640]{1,0:T(8,128)(2,1)S(1)}, bf16[256,640]{1,0:T(8,128)(2,1)S(1)}, u32[]{:S(2)}, u32[]{:S(2)}) collective-permute-start(bf16[256,640]{1,0:T(8,128)(2,1)S(1)} %get-tuple-element.77), channel_id=1, source_target_pairs={{0,4},{4,0},{8,12},{12,8},{16,20},{20,16},{24,28},{28,24},{1,5},{5... | collective-permute-start | bytes 983048 | tf_op jit(solution)/shard_map/ppermute | solution.py:455
  75.7 9.5 %collective-permute-start.12 = (bf16[256,384]{1,0:T(8,128)(2,1)}, bf16[256,384]{1,0:T(8,128)(2,1)}, u32[]{:S(2)}, u32[]{:S(2)}) collective-permute-start(bf16[256,384]{1,0:T(8,128)(2,1)} %get-tuple-element.69.refs_5_), channel_id=1, source_target_pairs={{0,1},{1,0},{2,3},{3,2},{4,5},{5,4},{6,7},{7,6},{8,9},{9,8},{10,11... | collective-permute-start | bytes 589832 | tf_op jit(solution)/shard_map/ppermute | solution.py:440
  87.0 1.0 copy-start.30
  91.1 36.8 %copy-start.39 = (s32[256]{0:T(256)S(1)}, s32[256]{0:T(256)}, u32[]{:S(2)}) copy-start(s32[256]{0:T(256)} %param.8) | copy-start | bytes 3076
  91.1 36.7 %all-to-all-start.2 = ((bf16[8,64,512]{2,1,0:T(8,128)(2,1)}), bf16[8,64,512]{2,1,0:T(8,128)(2,1)S(1)}, u32[]{:S(2)}, u32[]{:S(2)}) async-start(bf16[8,64,512]{2,1,0:T(8,128)(2,1)} %bitcast.9), calls=%async_computation.2 | async-start | bytes 1048576 | tf_op jit(solution)/shard_map/all_to_all | solution.py:459
  100.0 11.6 %collective-permute-start.14 = (bf16[64,640]{1,0:T(8,128)(2,1)S(1)}, bf16[64,640]{1,0:T(8,128)(2,1)S(1)}, u32[]{:S(2)}, u32[]{:S(2)}) collective-permute-start(bf16[64,640]{1,0:T(8,128)(2,1)S(1)} %get-tuple-element.79), channel_id=1, source_target_pairs={{0,8},{4,12},{8,0},{12,4},{16,24},{20,28},{24,16},{28,20},{1,9},{5... | collective-permute-start | bytes 245768 | tf_op jit(solution)/shard_map/ppermute | solution.py:455
  102.0 18.5 %collective-permute-start.15 = (bf16[64,640]{1,0:T(8,128)(2,1)S(1)}, bf16[64,640]{1,0:T(8,128)(2,1)S(1)}, u32[]{:S(2)}, u32[]{:S(2)}) collective-permute-start(bf16[64,640]{1,0:T(8,128)(2,1)S(1)} %get-tuple-element.80), channel_id=1, source_target_pairs={{0,16},{4,20},{8,24},{12,28},{16,0},{20,4},{24,8},{28,12},{1,17},{... | collective-permute-start | bytes 245768 | tf_op jit(solution)/shard_map/ppermute | solution.py:455
  104.4 16.1 %collective-permute-start.16 = (bf16[64,640]{1,0:T(8,128)(2,1)S(1)}, bf16[64,640]{1,0:T(8,128)(2,1)S(1)}, u32[]{:S(2)}, u32[]{:S(2)}) collective-permute-start(bf16[64,640]{1,0:T(8,128)(2,1)S(1)} %get-tuple-element.81), channel_id=1, source_target_pairs={{0,24},{4,28},{8,16},{12,20},{16,8},{20,12},{24,0},{28,4},{1,25},{... | collective-permute-start | bytes 245768 | tf_op jit(solution)/shard_map/ppermute | solution.py:455
  120.6 4.8 %collective-permute-start.19 = (bf16[64,640]{1,0:T(8,128)(2,1)S(1)}, bf16[64,640]{1,0:T(8,128)(2,1)S(1)}, u32[]{:S(2)}, u32[]{:S(2)}) collective-permute-start(bf16[64,640]{1,0:T(8,128)(2,1)S(1)} %sum.1.w0_ref), channel_id=1, source_target_pairs={{0,3},{1,2},{2,1},{3,0},{4,7},{5,6},{6,5},{7,4},{8,11},{9,10},{10,... | collective-permute-start | bytes 245768 | tf_op jit(solution)/shard_map/ppermute | solution.py:440
  120.6 6.3 %collective-permute-start.18 = (bf16[64,640]{1,0:T(8,128)(2,1)S(1)}, bf16[64,640]{1,0:T(8,128)(2,1)S(1)}, u32[]{:S(2)}, u32[]{:S(2)}) collective-permute-start(bf16[64,640]{1,0:T(8,128)(2,1)S(1)} %sum.1.w0_ref), channel_id=1, source_target_pairs={{0,2},{1,3},{2,0},{3,1},{4,6},{5,7},{6,4},{7,5},{8,10},{9,11},{10,... | collective-permute-start | bytes 245768 | tf_op jit(solution)/shard_map/ppermute | solution.py:440
  122.0 4.9 %collective-permute-start.17 = (bf16[64,640]{1,0:T(8,128)(2,1)S(1)}, bf16[64,640]{1,0:T(8,128)(2,1)S(1)}, u32[]{:S(2)}, u32[]{:S(2)}) collective-permute-start(bf16[64,640]{1,0:T(8,128)(2,1)S(1)} %sum.1.w0_ref), channel_id=1, source_target_pairs={{0,1},{1,0},{2,3},{3,2},{4,5},{5,4},{6,7},{7,6},{8,9},{9,8},{10,11... | collective-permute-start | bytes 245768 | tf_op jit(solution)/shard_map/ppermute | solution.py:440
  (17 other events, 14.1 us)

commit v7 on v5

--- a/solution.py
+++ b/solution.py
@@ -96,8 +96,15 @@
         ref[...] = value[i * size : (i + 1) * size].astype(ref.dtype)
 
 
+def hop_order(count):
+    return sorted(range(count), key=lambda k: (0 < k < count // 2, k))
+
+
 def load_blocks(refs):
-    return jnp.concatenate([ref[...].astype(F32) for ref in refs], axis=0).astype(BF16)
+    order = hop_order(len(refs))
+    return jnp.concatenate(
+        [refs[order.index(k)][...].astype(F32) for k in range(len(refs))], axis=0
+    ).astype(BF16)
 
 
 def pack_body(capacity, stride, outs, mask_ref, owner_hbm, slot_hbm, tokens_hbm, *rest):
@@ -132,7 +139,7 @@
 def place_body(owners, capacity, stride, *refs):
     owned_ref, normed_ref, landing_ref = refs[-3:]
     rows = owned_ref.shape[0]
-    arrived = load_blocks(refs[:-3])
+    arrived = load_blocks(refs[:-4])
     total = arrived.shape[0]
     pick = hot(iota((owners, total), 1) == iota((owners, total), 0) * stride + capacity)
     table = mm(pick, arrived).astype(BF16)
@@ -143,7 +150,7 @@
     landing_ref[...] = landing_row(table, owners, capacity, capacity).astype(jnp.int32)
 
 
-def early_body(cot_ref, outw_ref, grad_ref):
+def early_body(cot_ref, outw_ref, proj_ref, grad_ref):
     grad_ref[...] = mm_t(cot_ref[...], outw_ref[...])
 
 
@@ -348,17 +355,6 @@
     )
 
 
-def relay(value, after):
-    return pl.pallas_call(
-        lambda *refs: None,
-        name="relay",
-        out_shape=jax.ShapeDtypeStruct(value.shape, value.dtype),
-        in_specs=[ANYWHERE] * (1 + len(after)),
-        out_specs=ANYWHERE,
-        input_output_aliases={0: 0},
-    )(value, *after)
-
-
 def weight_body(sources, pairs, dp_ref, kept_side_ref, came_side_ref, *refs):
     normed, grads = refs[:sources], refs[sources : 2 * sources]
     outs, total_ref = refs[2 * sources : -1], refs[-1]
@@ -380,39 +376,41 @@
             ref[at, :] = total_ref[source, :].astype(BF16)
 
 
-def pair_body(kept_ref, came_ref, *outs):
+def pair_body(kept_ref, came_ref, _, *outs):
     store_blocks(outs, kept_ref[...].astype(F32) + came_ref[...].astype(F32))
 
 
+def head_columns(owner, proj_ref):
+    width = proj_ref.shape[0]
+    cols = [proj_ref[:, pl.ds(pl.multiple_of(b * width + owner * LANES, LANES), LANES)] for b in (1, 2, 3)]
+    return jnp.concatenate(cols, axis=1)
+
+
+def input_far_body(me_ref, far_ref, cross_ref, gate_in_ref, proj_ref, out_ref):
+    me = me_ref[0]
+    total = gate_in_ref[...] + mm_t(far_ref[...], head_columns(me ^ 2, proj_ref))
+    out_ref[...] = total + mm_t(cross_ref[...], head_columns(me ^ 3, proj_ref))
+
+
 def input_body(
-    blocks, me_ref, mask_ref, g0_ref, g1_ref, g2_ref, g3_ref,
-    gate_in_ref, owned_ref, cot_ref, landing_ref, proj_ref, *rest,
+    blocks, me_ref, own_ref, near_ref, partial_ref, owned_ref, cot_ref, landing_ref, proj_ref, *rest
 ):
-    out_ref = rest[-1]
-    rows, width = owned_ref.shape
-    me = me_ref[0]
-    piece = width // 4
-    total = gate_in_ref[...]
-    for step, ref in enumerate((g0_ref, g1_ref, g2_ref, g3_ref)):
-        cols = [
-            proj_ref[:, pl.ds(pl.multiple_of(b * width + (me ^ step) * piece, LANES), piece)] for b in (1, 2, 3)
-        ]
-        total += mm_t(ref[...], jnp.concatenate(cols, axis=1))
+    rows = owned_ref.shape[0]
+    me = me_ref[0]
+    total = partial_ref[...] + mm_t(own_ref[...], head_columns(me, proj_ref))
+    total += mm_t(near_ref[...], head_columns(me ^ 1, proj_ref))
     centred, inv_scale = normalize(owned_ref[...].astype(F32))
     grad = (norm_back(total, centred, inv_scale) + cot_ref[...].astype(F32)).astype(BF16)
     select = hot(iota((rows, landing_ref.shape[1]), 0) + 1 == landing_ref[...])
-    value = t_mm(select, grad)
-    size = value.shape[0] // blocks
-    for k in range(blocks):
-        at = pl.ds(pl.multiple_of((mask_ref[0] ^ k) * size, size), size)
-        out_ref[at, :] = value[k * size : (k + 1) * size].astype(BF16)
-
-
-def return_body(capacity, owner_ref, back_ref, out_ref):
-    owner = owner_ref[...]
+    store_blocks(rest[-blocks:], t_mm(select, grad))
+
+
+def return_body(capacity, mask_ref, owner_ref, *refs):
+    owner = owner_ref[...] ^ mask_ref[0]
     rank_row, _ = rank_rows(owner)
-    chosen = hot(iota((back_ref.shape[0], owner.shape[1]), 0) == owner * capacity + rank_row)
-    out_ref[...] = t_mm(chosen, back_ref[...]).astype(BF16)
+    back = load_blocks(refs[:-1])
+    chosen = hot(iota((back.shape[0], owner.shape[1]), 0) == owner * capacity + rank_row)
+    refs[-1][...] = t_mm(chosen, back).astype(BF16)
 
 
 def sum_body(*refs):
@@ -471,9 +469,7 @@
 
     def swap(values):
         if by_hops:
-            order = sorted(range(1, owners), key=lambda k: -k)
-            moved = {k: dp_hop(values[k], k) for k in order}
-            return [values[0]] + [moved[k] for k in range(1, owners)]
+            return [dp_hop(values[k], k) if k else values[k] for k in hop_order(owners)]
         return [swap_whole(values[0])]
 
     def block_shapes(height, columns, dtype):
@@ -490,20 +486,20 @@
         ],
     )
     arrived = swap(outgoing)
+    wide = ((rows, width), F32)
+    (grad_gated,) = call(early_body, "early", [wide], [], [cotangent, out_weight, proj_weight])
     owned, normed, landing = call(
         functools.partial(place_body, owners, capacity, stride),
-        "place", [square, square, ((1, owners * capacity), jnp.int32)], [], arrived,
+        "place", [square, square, ((1, owners * capacity), jnp.int32)], [], arrived, far=[grad_gated],
     )
     near, far, cross = gather(normed)
-    wide = ((rows, width), F32)
-    (grad_gated,) = call(early_body, "early", [wide], [], [cotangent, out_weight], flops=10**8)
     gate, slope, query, partial = call(
         own_body, "own_rows", [square, wide, square, wide],
         [me, lengths], [normed, proj_weight], flops=10**10, vmem=16,
     )
     (partial,) = call(
         middle_body, "middle", [wide], [me, lengths], [near, far, proj_weight, query, partial],
-        vmem=16,
+        flops=10**10, vmem=16,
     )
     layer_out, gated, gate_grad, *grad_pieces = call(
         forward_body, "forward",
@@ -535,7 +531,7 @@
     grad_rows = ((rows * cycle, piece), BF16)
     far_block, cross_block, totals, grad_all = call(
         backward_far_body, "backward_far", [grad_block, grad_block, sums, grad_rows],
-        [me, lengths], [r0, r1, r2, r3, parts, slopes], vmem=16, far=[side_send],
+        [me, lengths], [r0, r1, r2, r3, parts, slopes], flops=10**10, vmem=16,
     )
     p2, p3 = hop(far_block, 2), hop(cross_block, 3)
     own_block, near_block = call(
@@ -544,7 +540,7 @@
         scratch=[pltpu.VMEM(*sums)],
     )
     p1 = hop(near_block, 1)
-    p0, grads = own_block, [own_block, near_block, far_block, cross_block]
+    grads = [own_block, near_block, far_block, cross_block]
     share = width // owners
     pairs = owners // 2
     columns = 5 * piece
@@ -554,24 +550,29 @@
         [side_keep, side_last, normed, near, far, cross, *grads], vmem=16,
         scratch=[pltpu.VMEM((width, columns), F32)],
     )
+    (partial_in,) = call(
+        input_far_body, "input_far", [wide], [me], [p2, p3, gate_in, proj_weight], flops=6 * 10**9,
+    )
     if by_hops:
         kept, sent = weight_parts
         halves = call(
-            pair_body, "pair_sum", [((share, columns), BF16)] * pairs, [], [kept, dp_hop(relay(sent, [p2, p3]), 1)]
+            pair_body, "pair_sum", [((share, columns), BF16)] * pairs, [], [kept, dp_hop(sent, 1)],
+            far=[partial_in],
         )
         summed_parts = [halves[0]] + [dp_hop(halves[j], 2 * j) for j in range(1, pairs)]
     else:
         halves = weight_parts
         summed_parts = [swap_whole(weight_parts[0]).reshape(owners, share, columns)]
-    (back,) = call(
-        functools.partial(input_body, blocks), "input_grad", [((owners * capacity, width), BF16)], [me, mask],
-        [p0, p1, p2, p3, gate_in, owned, cotangent, landing, proj_weight], vmem=16,
-    )
-    returned = swap_whole(back)
+    back = call(
+        functools.partial(input_body, blocks), "input_grad", block_shapes(capacity, width, BF16), [me],
+        [own_block, p1, partial_in, owned, cotangent, landing, proj_weight], vmem=16,
+        far=[halves[0]],
+    )
+    returned = swap(back)
     (mine,) = call(sum_body, "sum", [((share, columns), BF16)], [], summed_parts)
     w1, w2, w3 = (hop(mine, step) for step in range(1, cycle))
     (grad_tokens,) = call(
-        functools.partial(return_body, capacity), "give_back", [square], [], [owner_row, returned]
+        functools.partial(return_body, capacity), "give_back", [square], [mask], [owner_row, *returned]
     )
     grad_proj, grad_outw = call(
         finish_body, "finish", [((share, 4 * width), F32), ((share, width), F32)],

time: 118 us -> 98.8 us (0.84)
  waiting for transfers between devices: 45.9 us -> 26.8 us
  starting transfers between devices: 39.4 us -> 46.2 us
  local copies, waits for them, and re-layouts: 12.4 us -> 5.9 us
    ppermute x14, waiting for transfers between devices: 25.7 us -> 7.02 us  [hop(): return lax.ppermute(value, 'ctx', [(i, i ^ step) for i in range(cycle)])]
    ppermute x11 -> x18, starting transfers between devices: 18.7 us -> 35.8 us  [dp_hop(): return lax.ppermute(value, 'dp', [(i, i ^ step) for i in range(owners)])]
    all_to_all x1 -> x0, starting transfers between devices: 9.61 us -> none  [swap_whole(): lax.all_to_all(split, 'dp', split_axis=0, concat_axis=0, tiled=True)]
    unnamed x52 -> x22, local copies, waits for them, and re-layouts: 12.4 us -> 5.9 us
    ppermute x11 -> x18, waiting for transfers between devices: 20.2 us -> 19.8 us  [dp_hop(): return lax.ppermute(value, 'dp', [(i, i ^ step) for i in range(owners)])]
    pallas_call x17 -> x18, Pallas kernels: 18.7 us -> 19.1 us  [call(): pl.pallas_call(body, name=name, out_shape=[jax.ShapeDtypeStruct(s, d) for...]
  transfers between devices with their start and end apart: 26 -> 32, of which waited for: 14 -> 12; matrix products, arithmetic and copies ran while one was open for 0% -> 0% of each run, Pallas kernels for 5% -> 14%
where the time goes in v7:
time: 98.8 us; the launch traced here: 98.9 us
  starting transfers between devices  46.2 us (47%)
  waiting for transfers between devices  26.8 us (27%)
  Pallas kernels  19.1 us (19%)
  local copies, waits for them, and re-layouts  5.9 us (6%)
    ppermute x18, starting transfers between devices, dp_hop(): return lax.ppermute(value, 'dp', [(i, i ^ step) for i in range(owners)])  35.8 us
    ppermute x18, waiting for transfers between devices, dp_hop(): return lax.ppermute(value, 'dp', [(i, i ^ step) for i in range(owners)])  19.8 us
    pallas_call x18, Pallas kernels, call(): pl.pallas_call(body, name=name, out_shape=[jax.ShapeDtypeStruct(s, d) for...  19.1 us
    ppermute x14, starting transfers between devices, hop(): return lax.ppermute(value, 'ctx', [(i, i ^ step) for i in range(cycle)])  10.4 us
    ppermute x14, waiting for transfers between devices, hop(): return lax.ppermute(value, 'ctx', [(i, i ^ step) for i in range(cycle)])  7.02 us
    unnamed x22, local copies, waits for them, and re-layouts  5.9 us
  transfers between devices with their start and end apart: 32, of which 12 were waited for; matrix products, arithmetic and copies ran while one was open for 0% of the time, Pallas kernels for 14%

profile of v7, /device:TPU:0, one launch (start us, length us, event | category | flops | bytes accessed | tf_op | source)
XLA Modules:
  0.0 98.9 jit_solution(8267278866016210431)
XLA Ops:
  1.3 0.9 copy-done.9
  3.7 4.1 %collective-permute-start = (bf16[72,512]{1,0:T(8,128)(2,1)S(1)}, bf16[72,512]{1,0:T(8,128)(2,1)S(1)}, u32[]{:S(2)}, u32[]{:S(2)}) collective-permute-start(bf16[72,512]{1,0:T(8,128)(2,1)S(1)} %get-tuple-element.56), channel_id=1, source_target_pairs={{0,16},{4,20},{8,24},{12,28},{16,0},{20,4},{24,8},{28,12},{1,17},{... | collective-permute-start | bytes 221192 | tf_op jit(solution)/shard_map/ppermute | solution.py:464
  7.8 1.3 %collective-permute-start.1 = (bf16[72,512]{1,0:T(8,128)(2,1)S(1)}, bf16[72,512]{1,0:T(8,128)(2,1)S(1)}, u32[]{:S(2)}, u32[]{:S(2)}) collective-permute-start(bf16[72,512]{1,0:T(8,128)(2,1)S(1)} %get-tuple-element.57), channel_id=1, source_target_pairs={{0,20},{4,16},{8,28},{12,24},{16,4},{20,0},{24,12},{28,8},{1,21},{... | collective-permute-start | bytes 221192 | tf_op jit(solution)/shard_map/ppermute | solution.py:464
  9.1 3.6 %collective-permute-start.2 = (bf16[72,512]{1,0:T(8,128)(2,1)S(1)}, bf16[72,512]{1,0:T(8,128)(2,1)S(1)}, u32[]{:S(2)}, u32[]{:S(2)}) collective-permute-start(bf16[72,512]{1,0:T(8,128)(2,1)S(1)} %get-tuple-element.58), channel_id=1, source_target_pairs={{0,24},{4,28},{8,16},{12,20},{16,8},{20,12},{24,0},{28,4},{1,25},{... | collective-permute-start | bytes 221192 | tf_op jit(solution)/shard_map/ppermute | solution.py:464
  12.7 1.7 %collective-permute-start.4 = (bf16[72,512]{1,0:T(8,128)(2,1)S(1)}, bf16[72,512]{1,0:T(8,128)(2,1)S(1)}, u32[]{:S(2)}, u32[]{:S(2)}) collective-permute-start(bf16[72,512]{1,0:T(8,128)(2,1)S(1)} %get-tuple-element.60), channel_id=1, source_target_pairs={{0,4},{4,0},{8,12},{12,8},{16,20},{20,16},{24,28},{28,24},{1,5},{5... | collective-permute-start | bytes 221192 | tf_op jit(solution)/shard_map/ppermute | solution.py:464
  14.3 1.6 %collective-permute-start.5 = (bf16[72,512]{1,0:T(8,128)(2,1)S(1)}, bf16[72,512]{1,0:T(8,128)(2,1)S(1)}, u32[]{:S(2)}, u32[]{:S(2)}) collective-permute-start(bf16[72,512]{1,0:T(8,128)(2,1)S(1)} %get-tuple-element.61), channel_id=1, source_target_pairs={{0,8},{4,12},{8,0},{12,4},{16,24},{20,28},{24,16},{28,20},{1,9},{5... | collective-permute-start | bytes 221192 | tf_op jit(solution)/shard_map/ppermute | solution.py:464
  15.9 2.9 %collective-permute-done.1.refs_2_ = bf16[72,512]{1,0:T(8,128)(2,1)S(1)} collective-permute-done((bf16[72,512]{1,0:T(8,128)(2,1)S(1)}, bf16[72,512]{1,0:T(8,128)(2,1)S(1)}, u32[]{:S(2)}, u32[]{:S(2)}) %collective-permute-start.1) | collective-permute-done | bytes 73760 | tf_op jit(solution)/shard_map/ppermute | solution.py:464
  18.8 0.9 collective-permute-start.6
  19.7 1.6 %copy-done = bf16[512,2048]{1,0:T(8,128)(2,1)S(1)} copy-done((bf16[512,2048]{1,0:T(8,128)(2,1)S(1)}, bf16[512,2048]{1,0:T(8,128)(2,1)}, u32[]{:S(2)}) %copy-start) | copy-done | bytes 2097176
  21.3 0.9 copy-done.2
  22.2 1.0 %copy-done.4 = bf16[512,512]{1,0:T(8,128)(2,1)S(1)} copy-done((bf16[512,512]{1,0:T(8,128)(2,1)S(1)}, bf16[512,512]{1,0:T(8,128)(2,1)}, u32[]{:S(2)}) %copy-start.4) | copy-done | bytes 524312
  24.1 0.8 place.1
  24.9 1.5 %collective-permute-start.7 = (bf16[256,512]{1,0:T(8,128)(2,1)S(1)}, bf16[256,512]{1,0:T(8,128)(2,1)S(1)}, u32[]{:S(2)}, u32[]{:S(2)}) collective-permute-start(bf16[256,512]{1,0:T(8,128)(2,1)S(1)} %get-tuple-element.63.normed_ref.n0_ref.refs_0_), channel_id=1, source_target_pairs={{0,2},{1,3},{2,0},{3,1},{4,6},{5,7},{6,4},{7,5},{8,10},{9,11},{10,... | collective-permute-start | bytes 786440 | tf_op jit(solution)/shard_map/ppermute | solution.py:449
  26.5 2.2 %own_rows.1 = (bf16[256,512]{1,0:T(8,128)(2,1)S(1)}, f32[256,512]{1,0:T(8,128)S(1)}, bf16[256,512]{1,0:T(8,128)(2,1)S(1)}, f32[256,512]{1,0:T(8,128)S(1)}) custom-call(s32[1]{0:T(128)} %bitcast.me_ref, s32[1,3]{1,0:T(1,128)S(1)} %copy-done.6, bf16[256,512]{1,0:T(8,128)(2,1)S(1)} %get-tuple-element.63.normed_ref.n0_ref.refs_0_, bf16[512,2048]{1,0:T(8,128)(2,1)S(1)} %copy-done.1), custom_call_target="tpu_custom_call" | custom-call | flops 10000000000 | bytes 1048576 | tf_op jit(solution)/shard_map/own_rows/pallas_call | solution.py:22
  28.6 3.8 %collective-permute-done.7.far_ref.n2_ref.refs_2_ = bf16[256,512]{1,0:T(8,128)(2,1)S(1)} collective-permute-done((bf16[256,512]{1,0:T(8,128)(2,1)S(1)}, bf16[256,512]{1,0:T(8,128)(2,1)S(1)}, u32[]{:S(2)}, u32[]{:S(2)}) %collective-permute-start.7) | collective-permute-done | bytes 262176 | tf_op jit(solution)/shard_map/ppermute | solution.py:449
  33.0 0.9 collective-permute-done.8.cross_ref.n3_ref.refs_3_
  34.0 1.9 %forward.1 = (bf16[256,512]{1,0:T(8,128)(2,1)}, bf16[256,512]{1,0:T(8,128)(2,1)S(1)}, bf16[256,512]{1,0:T(8,128)(2,1)S(1)}, bf16[256,128]{1,0:T(8,128)(2,1)S(1)}...) custom-call(s32[1]{0:T(128)} %bitcast.me_ref, s32[1,3]{1,0:T(1,128)S(1)} %copy-done.6, ...), custom_call_target="tpu_custom_call" | custom-call | flops 100000000 | bytes 1048576 | tf_op jit(solution)/shard_map/forward/pallas_call | solution.py:22
  35.9 0.8 side.1
  36.7 1.0 %collective-permute-start.16 = (bf16[512,512]{1,0:T(8,128)(2,1)S(1)}, bf16[512,512]{1,0:T(8,128)(2,1)S(1)}, u32[]{:S(2)}, u32[]{:S(2)}) collective-permute-start(bf16[512,512]{1,0:T(8,128)(2,1)S(1)} %get-tuple-element.87), channel_id=1, source_target_pairs={{0,1},{1,0},{2,3},{3,2},{4,5},{5,4},{6,7},{7,6},{8,9},{9,8},{10,11... | collective-permute-start | bytes 1572872 | tf_op jit(solution)/shard_map/ppermute | solution.py:449
  37.8 2.8 %collective-permute-start.11 = (bf16[256,128]{1,0:T(8,128)(2,1)S(1)}, bf16[256,128]{1,0:T(8,128)(2,1)S(1)}, u32[]{:S(2)}, u32[]{:S(2)}) collective-permute-start(bf16[256,128]{1,0:T(8,128)(2,1)S(1)} %get-tuple-element.74), channel_id=1, source_target_pairs={{0,2},{1,3},{2,0},{3,1},{4,6},{5,7},{6,4},{7,5},{8,10},{9,11},{10,... | collective-permute-start | bytes 196616 | tf_op jit(solution)/shard_map/ppermute | solution.py:449
  40.6 0.8 heads.1
  41.6 1.5 %collective-permute-start.17 = (bf16[512,256]{1,0:T(8,128)(2,1)S(1)}, bf16[512,256]{1,0:T(8,128)(2,1)S(1)}, u32[]{:S(2)}, u32[]{:S(2)}) collective-permute-start(bf16[512,256]{1,0:T(8,128)(2,1)S(1)} %get-tuple-element.89), channel_id=1, source_target_pairs={{0,2},{1,3},{2,0},{3,1},{4,6},{5,7},{6,4},{7,5},{8,10},{9,11},{10,... | collective-permute-start | bytes 786440 | tf_op jit(solution)/shard_map/ppermute | solution.py:449
  43.1 1.9 %collective-permute-done.12.g3_ref = bf16[256,128]{1,0:T(8,128)(2,1)S(1)} collective-permute-done((bf16[256,128]{1,0:T(8,128)(2,1)S(1)}, bf16[256,128]{1,0:T(8,128)(2,1)S(1)}, u32[]{:S(2)}, u32[]{:S(2)}) %collective-permute-start.12) | collective-permute-done | bytes 65568 | tf_op jit(solution)/shard_map/ppermute | solution.py:449
  45.0 3.7 %backward_far.1 = (bf16[256,384]{1,0:T(8,128)(2,1)S(1)}, bf16[256,384]{1,0:T(8,128)(2,1)S(1)}, f32[1024,384]{1,0:T(8,128)S(1)}, bf16[1024,128]{1,0:T(8,128)(2,1)S(1)}) custom-call(s32[1]{0:T(128)} %bitcast.me_ref, s32[1,3]{1,0:T(1,128)S(1)} %copy-done.6, bf16[256,128]{1,0:T(8,128)(2,1)S(1)} %get-tuple-element.72.g0_ref, ...), custom_call_target="tpu_custom_call" | custom-call | flops 10000000000 | bytes 1048576 | tf_op jit(solution)/shard_map/backward_far/pallas_call | solution.py:22
  48.7 1.2 %collective-permute-start.14 = (bf16[256,384]{1,0:T(8,128)(2,1)S(1)}, bf16[256,384]{1,0:T(8,128)(2,1)S(1)}, u32[]{:S(2)}, u32[]{:S(2)}) collective-permute-start(bf16[256,384]{1,0:T(8,128)(2,1)S(1)} %get-tuple-element.80.refs_6_), channel_id=1, source_target_pairs={{0,2},{1,3},{2,0},{3,1},{4,6},{5,7},{6,4},{7,5},{8,10},{9,11},{10,... | collective-permute-start | bytes 589832 | tf_op jit(solution)/shard_map/ppermute | solution.py:449
  50.2 2.6 %backward_rest.1 = (bf16[256,384]{1,0:T(8,128)(2,1)S(1)}, bf16[256,384]{1,0:T(8,128)(2,1)S(1)}) custom-call(s32[1]{0:T(128)} %bitcast.me_ref, s32[1,3]{1,0:T(1,128)S(1)} %copy-done.6, bf16[1024,384]{1,0:T(8,128)(2,1)S(1)} %get-tuple-element.70.part_ref, f32[1024,384]{1,0:T(8,128)S(1)} %get-tuple-element.71.slope_ref, ...), custom_call_target="tpu_custom_call" | custom-call | flops 100000000 | bytes 1048576 | tf_op jit(solution)/shard_map/backward_rest/pallas_call | solution.py:22
  52.8 0.8 collective-permute-start.13
  53.6 0.8 weights.1
  54.4 4.2 %collective-permute-start.18 = (bf16[256,640]{1,0:T(8,128)(2,1)S(1)}, bf16[256,640]{1,0:T(8,128)(2,1)S(1)}, u32[]{:S(2)}, u32[]{:S(2)}) collective-permute-start(bf16[256,640]{1,0:T(8,128)(2,1)S(1)} %get-tuple-element.91), channel_id=1, source_target_pairs={{0,4},{4,0},{8,12},{12,8},{16,20},{20,16},{24,28},{28,24},{1,5},{5... | collective-permute-start | bytes 983048 | tf_op jit(solution)/shard_map/ppermute | solution.py:464
  59.5 7.0 %collective-permute-done.18.came_ref = bf16[256,640]{1,0:T(8,128)(2,1)S(1)} collective-permute-done((bf16[256,640]{1,0:T(8,128)(2,1)S(1)}, bf16[256,640]{1,0:T(8,128)(2,1)S(1)}, u32[]{:S(2)}, u32[]{:S(2)}) %collective-permute-start.18) | collective-permute-done | bytes 327712 | tf_op jit(solution)/shard_map/ppermute | solution.py:464
  66.6 2.0 %collective-permute-start.26 = (bf16[64,640]{1,0:T(8,128)(2,1)S(1)}, bf16[64,640]{1,0:T(8,128)(2,1)S(1)}, u32[]{:S(2)}, u32[]{:S(2)}) collective-permute-start(bf16[64,640]{1,0:T(8,128)(2,1)S(1)} %get-tuple-element.101), channel_id=1, source_target_pairs={{0,8},{4,12},{8,0},{12,4},{16,24},{20,28},{24,16},{28,20},{1,9},{5... | collective-permute-start | bytes 245768 | tf_op jit(solution)/shard_map/ppermute | solution.py:464
  68.6 2.2 %collective-permute-start.27 = (bf16[64,640]{1,0:T(8,128)(2,1)S(1)}, bf16[64,640]{1,0:T(8,128)(2,1)S(1)}, u32[]{:S(2)}, u32[]{:S(2)}) collective-permute-start(bf16[64,640]{1,0:T(8,128)(2,1)S(1)} %get-tuple-element.102), channel_id=1, source_target_pairs={{0,16},{4,20},{8,24},{12,28},{16,0},{20,4},{24,8},{28,12},{1,17},{... | collective-permute-start | bytes 245768 | tf_op jit(solution)/shard_map/ppermute | solution.py:464
  70.8 1.4 %collective-permute-start.28 = (bf16[64,640]{1,0:T(8,128)(2,1)S(1)}, bf16[64,640]{1,0:T(8,128)(2,1)S(1)}, u32[]{:S(2)}, u32[]{:S(2)}) collective-permute-start(bf16[64,640]{1,0:T(8,128)(2,1)S(1)} %get-tuple-element.103), channel_id=1, source_target_pairs={{0,24},{4,28},{8,16},{12,20},{16,8},{20,12},{24,0},{28,4},{1,25},{... | collective-permute-start | bytes 245768 | tf_op jit(solution)/shard_map/ppermute | solution.py:464
  72.2 0.9 input_grad.1
  73.2 2.1 %collective-permute-start.19 = (bf16[64,512]{1,0:T(8,128)(2,1)S(1)}, bf16[64,512]{1,0:T(8,128)(2,1)S(1)}, u32[]{:S(2)}, u32[]{:S(2)}) collective-permute-start(bf16[64,512]{1,0:T(8,128)(2,1)S(1)} %get-tuple-element.94), channel_id=1, source_target_pairs={{0,16},{4,20},{8,24},{12,28},{16,0},{20,4},{24,8},{28,12},{1,17},{... | collective-permute-start | bytes 196616 | tf_op jit(solution)/shard_map/ppermute | solution.py:464
  75.2 2.1 %collective-permute-start.20 = (bf16[64,512]{1,0:T(8,128)(2,1)S(1)}, bf16[64,512]{1,0:T(8,128)(2,1)S(1)}, u32[]{:S(2)}, u32[]{:S(2)}) collective-permute-start(bf16[64,512]{1,0:T(8,128)(2,1)S(1)} %get-tuple-element.95), channel_id=1, source_target_pairs={{0,20},{4,16},{8,28},{12,24},{16,4},{20,0},{24,12},{28,8},{1,21},{... | collective-permute-start | bytes 196616 | tf_op jit(solution)/shard_map/ppermute | solution.py:464
  77.3 2.4 %collective-permute-start.21 = (bf16[64,512]{1,0:T(8,128)(2,1)S(1)}, bf16[64,512]{1,0:T(8,128)(2,1)S(1)}, u32[]{:S(2)}, u32[]{:S(2)}) collective-permute-start(bf16[64,512]{1,0:T(8,128)(2,1)S(1)} %get-tuple-element.96), channel_id=1, source_target_pairs={{0,24},{4,28},{8,16},{12,20},{16,8},{20,12},{24,0},{28,4},{1,25},{... | collective-permute-start | bytes 196616 | tf_op jit(solution)/shard_map/ppermute | solution.py:464
  79.8 1.2 %collective-permute-done.27.refs_2_ = bf16[64,640]{1,0:T(8,128)(2,1)S(1)} collective-permute-done((bf16[64,640]{1,0:T(8,128)(2,1)S(1)}, bf16[64,640]{1,0:T(8,128)(2,1)S(1)}, u32[]{:S(2)}, u32[]{:S(2)}) %collective-permute-start.27) | collective-permute-done | bytes 81952 | tf_op jit(solution)/shard_map/ppermute | solution.py:464
  81.0 3.6 %collective-permute-start.22 = (bf16[64,512]{1,0:T(8,128)(2,1)S(1)}, bf16[64,512]{1,0:T(8,128)(2,1)S(1)}, u32[]{:S(2)}, u32[]{:S(2)}) collective-permute-start(bf16[64,512]{1,0:T(8,128)(2,1)S(1)} %get-tuple-element.97), channel_id=1, source_target_pairs={{0,28},{4,24},{8,20},{12,16},{16,12},{20,8},{24,4},{28,0},{1,29},{... | collective-permute-start | bytes 196616 | tf_op jit(solution)/shard_map/ppermute | solution.py:464
  84.6 2.3 %collective-permute-done.19.refs_1_ = bf16[64,512]{1,0:T(8,128)(2,1)S(1)} collective-permute-done((bf16[64,512]{1,0:T(8,128)(2,1)S(1)}, bf16[64,512]{1,0:T(8,128)(2,1)S(1)}, u32[]{:S(2)}, u32[]{:S(2)}) %collective-permute-start.19) | collective-permute-done | bytes 65568 | tf_op jit(solution)/shard_map/ppermute | solution.py:464
  86.9 1.8 %collective-permute-done.20.refs_2_ = bf16[64,512]{1,0:T(8,128)(2,1)S(1)} collective-permute-done((bf16[64,512]{1,0:T(8,128)(2,1)S(1)}, bf16[64,512]{1,0:T(8,128)(2,1)S(1)}, u32[]{:S(2)}, u32[]{:S(2)}) %collective-permute-start.20) | collective-permute-done | bytes 65568 | tf_op jit(solution)/shard_map/ppermute | solution.py:464
  88.7 1.2 %collective-permute-start.30 = (bf16[64,640]{1,0:T(8,128)(2,1)S(1)}, bf16[64,640]{1,0:T(8,128)(2,1)S(1)}, u32[]{:S(2)}, u32[]{:S(2)}) collective-permute-start(bf16[64,640]{1,0:T(8,128)(2,1)S(1)} %sum.1.w0_ref), channel_id=1, source_target_pairs={{0,2},{1,3},{2,0},{3,1},{4,6},{5,7},{6,4},{7,5},{8,10},{9,11},{10,... | collective-permute-start | bytes 245768 | tf_op jit(solution)/shard_map/ppermute | solution.py:449
  90.0 1.5 %collective-permute-start.24 = (bf16[64,512]{1,0:T(8,128)(2,1)S(1)}, bf16[64,512]{1,0:T(8,128)(2,1)S(1)}, u32[]{:S(2)}, u32[]{:S(2)}) collective-permute-start(bf16[64,512]{1,0:T(8,128)(2,1)S(1)} %get-tuple-element.99), channel_id=1, source_target_pairs={{0,8},{4,12},{8,0},{12,4},{16,24},{20,28},{24,16},{28,20},{1,9},{5... | collective-permute-start | bytes 196616 | tf_op jit(solution)/shard_map/ppermute | solution.py:464
  91.5 1.1 %collective-permute-start.25 = (bf16[64,512]{1,0:T(8,128)(2,1)S(1)}, bf16[64,512]{1,0:T(8,128)(2,1)S(1)}, u32[]{:S(2)}, u32[]{:S(2)}) collective-permute-start(bf16[64,512]{1,0:T(8,128)(2,1)S(1)} %get-tuple-element.100), channel_id=1, source_target_pairs={{0,12},{4,8},{8,4},{12,0},{16,28},{20,24},{24,20},{28,16},{1,13},{... | collective-permute-start | bytes 196616 | tf_op jit(solution)/shard_map/ppermute | solution.py:464
  92.6 2.4 %collective-permute-done.24.refs_6_ = bf16[64,512]{1,0:T(8,128)(2,1)S(1)} collective-permute-done((bf16[64,512]{1,0:T(8,128)(2,1)S(1)}, bf16[64,512]{1,0:T(8,128)(2,1)S(1)}, u32[]{:S(2)}, u32[]{:S(2)}) %collective-permute-start.24) | collective-permute-done | bytes 65568 | tf_op jit(solution)/shard_map/ppermute | solution.py:464
  95.0 1.8 %collective-permute-done.25.refs_7_ = bf16[64,512]{1,0:T(8,128)(2,1)S(1)} collective-permute-done((bf16[64,512]{1,0:T(8,128)(2,1)S(1)}, bf16[64,512]{1,0:T(8,128)(2,1)S(1)}, u32[]{:S(2)}, u32[]{:S(2)}) %collective-permute-start.25) | collective-permute-done | bytes 65568 | tf_op jit(solution)/shard_map/ppermute | solution.py:464
  96.8 1.2 %give_back.1 = bf16[256,512]{1,0:T(8,128)(2,1)} custom-call(s32[1]{0:T(128)} %bitcast.1.mask_ref.dp_ref, s32[1,256]{1,0:T(1,128)S(1)} %bitcast.5, bf16[64,512]{1,0:T(8,128)(2,1)S(1)} %get-tuple-element.93.refs_0_, bf16[64,512]{1,0:T(8,128)(2,1)S(1)} %collective-permute-done.19.refs_1_, bf16[64,512]{1,0:T(8,128)(2,1)S(1)} %collective-permute-done.20.refs_2_, ...), custom_call_target="tpu_custom_call" | custom-call | flops 100000000 | bytes 1048576 | tf_op jit(solution)/shard_map/give_back/pallas_call | solution.py:22
  98.0 0.9 finish.1
  (56 shorter events, 5.0 us)
Async XLA Ops:
  0.6 0.7 copy-start.7
  1.3 0.9 copy-start.9
  2.3 0.7 copy-start.10
  3.7 10.7 %collective-permute-start = (bf16[72,512]{1,0:T(8,128)(2,1)S(1)}, bf16[72,512]{1,0:T(8,128)(2,1)S(1)}, u32[]{:S(2)}, u32[]{:S(2)}) collective-permute-start(bf16[72,512]{1,0:T(8,128)(2,1)S(1)} %get-tuple-element.56), channel_id=1, source_target_pairs={{0,16},{4,20},{8,24},{12,28},{16,0},{20,4},{24,8},{28,12},{1,17},{... | collective-permute-start | bytes 221192 | tf_op jit(solution)/shard_map/ppermute | solution.py:464
  7.8 11.1 %collective-permute-start.1 = (bf16[72,512]{1,0:T(8,128)(2,1)S(1)}, bf16[72,512]{1,0:T(8,128)(2,1)S(1)}, u32[]{:S(2)}, u32[]{:S(2)}) collective-permute-start(bf16[72,512]{1,0:T(8,128)(2,1)S(1)} %get-tuple-element.57), channel_id=1, source_target_pairs={{0,20},{4,16},{8,28},{12,24},{16,4},{20,0},{24,12},{28,8},{1,21},{... | collective-permute-start | bytes 221192 | tf_op jit(solution)/shard_map/ppermute | solution.py:464
  9.1 14.6 %collective-permute-start.2 = (bf16[72,512]{1,0:T(8,128)(2,1)S(1)}, bf16[72,512]{1,0:T(8,128)(2,1)S(1)}, u32[]{:S(2)}, u32[]{:S(2)}) collective-permute-start(bf16[72,512]{1,0:T(8,128)(2,1)S(1)} %get-tuple-element.58), channel_id=1, source_target_pairs={{0,24},{4,28},{8,16},{12,20},{16,8},{20,12},{24,0},{28,4},{1,25},{... | collective-permute-start | bytes 221192 | tf_op jit(solution)/shard_map/ppermute | solution.py:464
  12.7 11.0 %collective-permute-start.3 = (bf16[72,512]{1,0:T(8,128)(2,1)S(1)}, bf16[72,512]{1,0:T(8,128)(2,1)S(1)}, u32[]{:S(2)}, u32[]{:S(2)}) collective-permute-start(bf16[72,512]{1,0:T(8,128)(2,1)S(1)} %get-tuple-element.59), channel_id=1, source_target_pairs={{0,28},{4,24},{8,20},{12,16},{16,12},{20,8},{24,4},{28,0},{1,29},{... | collective-permute-start | bytes 221192 | tf_op jit(solution)/shard_map/ppermute | solution.py:464
  12.7 11.0 %collective-permute-start.4 = (bf16[72,512]{1,0:T(8,128)(2,1)S(1)}, bf16[72,512]{1,0:T(8,128)(2,1)S(1)}, u32[]{:S(2)}, u32[]{:S(2)}) collective-permute-start(bf16[72,512]{1,0:T(8,128)(2,1)S(1)} %get-tuple-element.60), channel_id=1, source_target_pairs={{0,4},{4,0},{8,12},{12,8},{16,20},{20,16},{24,28},{28,24},{1,5},{5... | collective-permute-start | bytes 221192 | tf_op jit(solution)/shard_map/ppermute | solution.py:464
  14.3 9.3 %collective-permute-start.5 = (bf16[72,512]{1,0:T(8,128)(2,1)S(1)}, bf16[72,512]{1,0:T(8,128)(2,1)S(1)}, u32[]{:S(2)}, u32[]{:S(2)}) collective-permute-start(bf16[72,512]{1,0:T(8,128)(2,1)S(1)} %get-tuple-element.61), channel_id=1, source_target_pairs={{0,8},{4,12},{8,0},{12,4},{16,24},{20,28},{24,16},{28,20},{1,9},{5... | collective-permute-start | bytes 221192 | tf_op jit(solution)/shard_map/ppermute | solution.py:464
  18.8 5.3 %collective-permute-start.6 = (bf16[72,512]{1,0:T(8,128)(2,1)S(1)}, bf16[72,512]{1,0:T(8,128)(2,1)S(1)}, u32[]{:S(2)}, u32[]{:S(2)}) collective-permute-start(bf16[72,512]{1,0:T(8,128)(2,1)S(1)} %get-tuple-element.62), channel_id=1, source_target_pairs={{0,12},{4,8},{8,4},{12,0},{16,28},{20,24},{24,20},{28,16},{1,13},{... | collective-permute-start | bytes 221192 | tf_op jit(solution)/shard_map/ppermute | solution.py:464
  19.7 1.6 %copy-start = (bf16[512,2048]{1,0:T(8,128)(2,1)S(1)}, bf16[512,2048]{1,0:T(8,128)(2,1)}, u32[]{:S(2)}) copy-start(bf16[512,2048]{1,0:T(8,128)(2,1)} %proj_ref.15) | copy-start | bytes 6291460
  21.3 0.9 copy-start.2
  22.2 1.0 %copy-start.4 = (bf16[512,512]{1,0:T(8,128)(2,1)S(1)}, bf16[512,512]{1,0:T(8,128)(2,1)}, u32[]{:S(2)}) copy-start(bf16[512,512]{1,0:T(8,128)(2,1)} %outw_ref.3) | copy-start | bytes 1572868
  23.3 3.2 %copy-start.1 = (bf16[512,2048]{1,0:T(8,128)(2,1)S(1)}, bf16[512,2048]{1,0:T(8,128)(2,1)}, u32[]{:S(2)}) copy-start(bf16[512,2048]{1,0:T(8,128)(2,1)} %proj_ref.15) | copy-start | bytes 6291460
  23.3 3.2 %copy-start.6 = (s32[1,3]{1,0:T(1,128)S(1)}, s32[1,3]{1,0:T(1,128)}, u32[]{:S(2)}) copy-start(s32[1,3]{1,0:T(1,128)} %lengths_ref.9) | copy-start | bytes 40
  24.9 7.5 %collective-permute-start.7 = (bf16[256,512]{1,0:T(8,128)(2,1)S(1)}, bf16[256,512]{1,0:T(8,128)(2,1)S(1)}, u32[]{:S(2)}, u32[]{:S(2)}) collective-permute-start(bf16[256,512]{1,0:T(8,128)(2,1)S(1)} %get-tuple-element.63.normed_ref.n0_ref.refs_0_), channel_id=1, source_target_pairs={{0,2},{1,3},{2,0},{3,1},{4,6},{5,7},{6,4},{7,5},{8,10},{9,11},{10,... | collective-permute-start | bytes 786440 | tf_op jit(solution)/shard_map/ppermute | solution.py:449
  26.4 6.0 %collective-permute-start.9 = (bf16[256,512]{1,0:T(8,128)(2,1)S(1)}, bf16[256,512]{1,0:T(8,128)(2,1)S(1)}, u32[]{:S(2)}, u32[]{:S(2)}) collective-permute-start(bf16[256,512]{1,0:T(8,128)(2,1)S(1)} %get-tuple-element.63.normed_ref.n0_ref.refs_0_), channel_id=1, source_target_pairs={{0,1},{1,0},{2,3},{3,2},{4,5},{5,4},{6,7},{7,6},{8,9},{9,8},{10,11... | collective-permute-start | bytes 786440 | tf_op jit(solution)/shard_map/ppermute | solution.py:449
  32.4 1.5 %collective-permute-start.8 = (bf16[256,512]{1,0:T(8,128)(2,1)S(1)}, bf16[256,512]{1,0:T(8,128)(2,1)S(1)}, u32[]{:S(2)}, u32[]{:S(2)}) collective-permute-start(bf16[256,512]{1,0:T(8,128)(2,1)S(1)} %collective-permute-done.7.far_ref.n2_ref.refs_2_), channel_id=1, source_target_pairs={{0,1},{1,0},{2,3},{3,2},{4,5},{5,4},{6,7},{7,6},{8,9},{9,8},{10,11... | collective-permute-start | bytes 786440 | tf_op jit(solution)/shard_map/ppermute | solution.py:449
  32.4 1.5 %copy-start.5 = (bf16[512,512]{1,0:T(8,128)(2,1)S(1)}, bf16[512,512]{1,0:T(8,128)(2,1)}, u32[]{:S(2)}) copy-start(bf16[512,512]{1,0:T(8,128)(2,1)} %outw_ref.3) | copy-start | bytes 1572868
  34.0 1.9 %copy-start.3 = (bf16[256,512]{1,0:T(8,128)(2,1)S(1)}, bf16[256,512]{1,0:T(8,128)(2,1)}, u32[]{:S(2)}) copy-start(bf16[256,512]{1,0:T(8,128)(2,1)} %cot_ref.5) | copy-start | bytes 786436
  36.7 4.7 %collective-permute-start.16 = (bf16[512,512]{1,0:T(8,128)(2,1)S(1)}, bf16[512,512]{1,0:T(8,128)(2,1)S(1)}, u32[]{:S(2)}, u32[]{:S(2)}) collective-permute-start(bf16[512,512]{1,0:T(8,128)(2,1)S(1)} %get-tuple-element.87), channel_id=1, source_target_pairs={{0,1},{1,0},{2,3},{3,2},{4,5},{5,4},{6,7},{7,6},{8,9},{9,8},{10,11... | collective-permute-start | bytes 1572872 | tf_op jit(solution)/shard_map/ppermute | solution.py:449
  37.7 5.3 %collective-permute-start.10 = (bf16[256,128]{1,0:T(8,128)(2,1)S(1)}, bf16[256,128]{1,0:T(8,128)(2,1)S(1)}, u32[]{:S(2)}, u32[]{:S(2)}) collective-permute-start(bf16[256,128]{1,0:T(8,128)(2,1)S(1)} %get-tuple-element.73), channel_id=1, source_target_pairs={{0,1},{1,0},{2,3},{3,2},{4,5},{5,4},{6,7},{7,6},{8,9},{9,8},{10,11... | collective-permute-start | bytes 196616 | tf_op jit(solution)/shard_map/ppermute | solution.py:449
  37.8 5.3 %collective-permute-start.11 = (bf16[256,128]{1,0:T(8,128)(2,1)S(1)}, bf16[256,128]{1,0:T(8,128)(2,1)S(1)}, u32[]{:S(2)}, u32[]{:S(2)}) collective-permute-start(bf16[256,128]{1,0:T(8,128)(2,1)S(1)} %get-tuple-element.74), channel_id=1, source_target_pairs={{0,2},{1,3},{2,0},{3,1},{4,6},{5,7},{6,4},{7,5},{8,10},{9,11},{10,... | collective-permute-start | bytes 196616 | tf_op jit(solution)/shard_map/ppermute | solution.py:449
  40.6 4.4 %collective-permute-start.12 = (bf16[256,128]{1,0:T(8,128)(2,1)S(1)}, bf16[256,128]{1,0:T(8,128)(2,1)S(1)}, u32[]{:S(2)}, u32[]{:S(2)}) collective-permute-start(bf16[256,128]{1,0:T(8,128)(2,1)S(1)} %get-tuple-element.75), channel_id=1, source_target_pairs={{0,3},{1,2},{2,1},{3,0},{4,7},{5,6},{6,5},{7,4},{8,11},{9,10},{10,... | collective-permute-start | bytes 196616 | tf_op jit(solution)/shard_map/ppermute | solution.py:449
  41.6 12.0 %collective-permute-start.17 = (bf16[512,256]{1,0:T(8,128)(2,1)S(1)}, bf16[512,256]{1,0:T(8,128)(2,1)S(1)}, u32[]{:S(2)}, u32[]{:S(2)}) collective-permute-start(bf16[512,256]{1,0:T(8,128)(2,1)S(1)} %get-tuple-element.89), channel_id=1, source_target_pairs={{0,2},{1,3},{2,0},{3,1},{4,6},{5,7},{6,4},{7,5},{8,10},{9,11},{10,... | collective-permute-start | bytes 786440 | tf_op jit(solution)/shard_map/ppermute | solution.py:449
  48.7 9.9 %collective-permute-start.14 = (bf16[256,384]{1,0:T(8,128)(2,1)S(1)}, bf16[256,384]{1,0:T(8,128)(2,1)S(1)}, u32[]{:S(2)}, u32[]{:S(2)}) collective-permute-start(bf16[256,384]{1,0:T(8,128)(2,1)S(1)} %get-tuple-element.80.refs_6_), channel_id=1, source_target_pairs={{0,2},{1,3},{2,0},{3,1},{4,6},{5,7},{6,4},{7,5},{8,10},{9,11},{10,... | collective-permute-start | bytes 589832 | tf_op jit(solution)/shard_map/ppermute | solution.py:449
  49.9 9.1 %collective-permute-start.15 = (bf16[256,384]{1,0:T(8,128)(2,1)S(1)}, bf16[256,384]{1,0:T(8,128)(2,1)S(1)}, u32[]{:S(2)}, u32[]{:S(2)}) collective-permute-start(bf16[256,384]{1,0:T(8,128)(2,1)S(1)} %get-tuple-element.81.refs_7_), channel_id=1, source_target_pairs={{0,3},{1,2},{2,1},{3,0},{4,7},{5,6},{6,5},{7,4},{8,11},{9,10},{10,... | collective-permute-start | bytes 589832 | tf_op jit(solution)/shard_map/ppermute | solution.py:449
  52.8 19.4 %collective-permute-start.13 = (bf16[256,384]{1,0:T(8,128)(2,1)S(1)}, bf16[256,384]{1,0:T(8,128)(2,1)S(1)}, u32[]{:S(2)}, u32[]{:S(2)}) collective-permute-start(bf16[256,384]{1,0:T(8,128)(2,1)S(1)} %get-tuple-element.79.refs_5_), channel_id=1, source_target_pairs={{0,1},{1,0},{2,3},{3,2},{4,5},{5,4},{6,7},{7,6},{8,9},{9,8},{10,11... | collective-permute-start | bytes 589832 | tf_op jit(solution)/shard_map/ppermute | solution.py:449
  54.4 12.1 %collective-permute-start.18 = (bf16[256,640]{1,0:T(8,128)(2,1)S(1)}, bf16[256,640]{1,0:T(8,128)(2,1)S(1)}, u32[]{:S(2)}, u32[]{:S(2)}) collective-permute-start(bf16[256,640]{1,0:T(8,128)(2,1)S(1)} %get-tuple-element.91), channel_id=1, source_target_pairs={{0,4},{4,0},{8,12},{12,8},{16,20},{20,16},{24,28},{28,24},{1,5},{5... | collective-permute-start | bytes 983048 | tf_op jit(solution)/shard_map/ppermute | solution.py:464
  66.6 10.7 %collective-permute-start.26 = (bf16[64,640]{1,0:T(8,128)(2,1)S(1)}, bf16[64,640]{1,0:T(8,128)(2,1)S(1)}, u32[]{:S(2)}, u32[]{:S(2)}) collective-permute-start(bf16[64,640]{1,0:T(8,128)(2,1)S(1)} %get-tuple-element.101), channel_id=1, source_target_pairs={{0,8},{4,12},{8,0},{12,4},{16,24},{20,28},{24,16},{28,20},{1,9},{5... | collective-permute-start | bytes 245768 | tf_op jit(solution)/shard_map/ppermute | solution.py:464
  68.6 12.4 %collective-permute-start.27 = (bf16[64,640]{1,0:T(8,128)(2,1)S(1)}, bf16[64,640]{1,0:T(8,128)(2,1)S(1)}, u32[]{:S(2)}, u32[]{:S(2)}) collective-permute-start(bf16[64,640]{1,0:T(8,128)(2,1)S(1)} %get-tuple-element.102), channel_id=1, source_target_pairs={{0,16},{4,20},{8,24},{12,28},{16,0},{20,4},{24,8},{28,12},{1,17},{... | collective-permute-start | bytes 245768 | tf_op jit(solution)/shard_map/ppermute | solution.py:464
  70.8 13.8 %collective-permute-start.28 = (bf16[64,640]{1,0:T(8,128)(2,1)S(1)}, bf16[64,640]{1,0:T(8,128)(2,1)S(1)}, u32[]{:S(2)}, u32[]{:S(2)}) collective-permute-start(bf16[64,640]{1,0:T(8,128)(2,1)S(1)} %get-tuple-element.103), channel_id=1, source_target_pairs={{0,24},{4,28},{8,16},{12,20},{16,8},{20,12},{24,0},{28,4},{1,25},{... | collective-permute-start | bytes 245768 | tf_op jit(solution)/shard_map/ppermute | solution.py:464
  72.2 24.6 %copy-start.8 = (s32[256]{0:T(256)S(1)}, s32[256]{0:T(256)}, u32[]{:S(2)}) copy-start(s32[256]{0:T(256)} %param.8) | copy-start | bytes 3076
  73.2 13.8 %collective-permute-start.19 = (bf16[64,512]{1,0:T(8,128)(2,1)S(1)}, bf16[64,512]{1,0:T(8,128)(2,1)S(1)}, u32[]{:S(2)}, u32[]{:S(2)}) collective-permute-start(bf16[64,512]{1,0:T(8,128)(2,1)S(1)} %get-tuple-element.94), channel_id=1, source_target_pairs={{0,16},{4,20},{8,24},{12,28},{16,0},{20,4},{24,8},{28,12},{1,17},{... | collective-permute-start | bytes 196616 | tf_op jit(solution)/shard_map/ppermute | solution.py:464
  75.2 13.5 %collective-permute-start.20 = (bf16[64,512]{1,0:T(8,128)(2,1)S(1)}, bf16[64,512]{1,0:T(8,128)(2,1)S(1)}, u32[]{:S(2)}, u32[]{:S(2)}) collective-permute-start(bf16[64,512]{1,0:T(8,128)(2,1)S(1)} %get-tuple-element.95), channel_id=1, source_target_pairs={{0,20},{4,16},{8,28},{12,24},{16,4},{20,0},{24,12},{28,8},{1,21},{... | collective-permute-start | bytes 196616 | tf_op jit(solution)/shard_map/ppermute | solution.py:464
  77.3 12.6 %collective-permute-start.21 = (bf16[64,512]{1,0:T(8,128)(2,1)S(1)}, bf16[64,512]{1,0:T(8,128)(2,1)S(1)}, u32[]{:S(2)}, u32[]{:S(2)}) collective-permute-start(bf16[64,512]{1,0:T(8,128)(2,1)S(1)} %get-tuple-element.96), channel_id=1, source_target_pairs={{0,24},{4,28},{8,16},{12,20},{16,8},{20,12},{24,0},{28,4},{1,25},{... | collective-permute-start | bytes 196616 | tf_op jit(solution)/shard_map/ppermute | solution.py:464
  81.0 9.0 %collective-permute-start.22 = (bf16[64,512]{1,0:T(8,128)(2,1)S(1)}, bf16[64,512]{1,0:T(8,128)(2,1)S(1)}, u32[]{:S(2)}, u32[]{:S(2)}) collective-permute-start(bf16[64,512]{1,0:T(8,128)(2,1)S(1)} %get-tuple-element.97), channel_id=1, source_target_pairs={{0,28},{4,24},{8,20},{12,16},{16,12},{20,8},{24,4},{28,0},{1,29},{... | collective-permute-start | bytes 196616 | tf_op jit(solution)/shard_map/ppermute | solution.py:464
  84.6 6.9 %collective-permute-start.23 = (bf16[64,512]{1,0:T(8,128)(2,1)S(1)}, bf16[64,512]{1,0:T(8,128)(2,1)S(1)}, u32[]{:S(2)}, u32[]{:S(2)}) collective-permute-start(bf16[64,512]{1,0:T(8,128)(2,1)S(1)} %get-tuple-element.98), channel_id=1, source_target_pairs={{0,4},{4,0},{8,12},{12,8},{16,20},{20,16},{24,28},{28,24},{1,5},{5... | collective-permute-start | bytes 196616 | tf_op jit(solution)/shard_map/ppermute | solution.py:464
  86.9 11.0 %collective-permute-start.29 = (bf16[64,640]{1,0:T(8,128)(2,1)S(1)}, bf16[64,640]{1,0:T(8,128)(2,1)S(1)}, u32[]{:S(2)}, u32[]{:S(2)}) collective-permute-start(bf16[64,640]{1,0:T(8,128)(2,1)S(1)} %sum.1.w0_ref), channel_id=1, source_target_pairs={{0,1},{1,0},{2,3},{3,2},{4,5},{5,4},{6,7},{7,6},{8,9},{9,8},{10,11... | collective-permute-start | bytes 245768 | tf_op jit(solution)/shard_map/ppermute | solution.py:449
  88.7 9.2 %collective-permute-start.30 = (bf16[64,640]{1,0:T(8,128)(2,1)S(1)}, bf16[64,640]{1,0:T(8,128)(2,1)S(1)}, u32[]{:S(2)}, u32[]{:S(2)}) collective-permute-start(bf16[64,640]{1,0:T(8,128)(2,1)S(1)} %sum.1.w0_ref), channel_id=1, source_target_pairs={{0,2},{1,3},{2,0},{3,1},{4,6},{5,7},{6,4},{7,5},{8,10},{9,11},{10,... | collective-permute-start | bytes 245768 | tf_op jit(solution)/shard_map/ppermute | solution.py:449
  90.0 8.0 %collective-permute-start.31 = (bf16[64,640]{1,0:T(8,128)(2,1)S(1)}, bf16[64,640]{1,0:T(8,128)(2,1)S(1)}, u32[]{:S(2)}, u32[]{:S(2)}) collective-permute-start(bf16[64,640]{1,0:T(8,128)(2,1)S(1)} %sum.1.w0_ref), channel_id=1, source_target_pairs={{0,3},{1,2},{2,1},{3,0},{4,7},{5,6},{6,5},{7,4},{8,11},{9,10},{10,... | collective-permute-start | bytes 245768 | tf_op jit(solution)/shard_map/ppermute | solution.py:449
  90.0 5.0 %collective-permute-start.24 = (bf16[64,512]{1,0:T(8,128)(2,1)S(1)}, bf16[64,512]{1,0:T(8,128)(2,1)S(1)}, u32[]{:S(2)}, u32[]{:S(2)}) collective-permute-start(bf16[64,512]{1,0:T(8,128)(2,1)S(1)} %get-tuple-element.99), channel_id=1, source_target_pairs={{0,8},{4,12},{8,0},{12,4},{16,24},{20,28},{24,16},{28,20},{1,9},{5... | collective-permute-start | bytes 196616 | tf_op jit(solution)/shard_map/ppermute | solution.py:464
  91.5 5.3 %collective-permute-start.25 = (bf16[64,512]{1,0:T(8,128)(2,1)S(1)}, bf16[64,512]{1,0:T(8,128)(2,1)S(1)}, u32[]{:S(2)}, u32[]{:S(2)}) collective-permute-start(bf16[64,512]{1,0:T(8,128)(2,1)S(1)} %get-tuple-element.100), channel_id=1, source_target_pairs={{0,12},{4,8},{8,4},{12,0},{16,28},{20,24},{24,20},{28,16},{1,13},{... | collective-permute-start | bytes 196616 | tf_op jit(solution)/shard_map/ppermute | solution.py:464

commit v8 on v7

--- a/solution.py
+++ b/solution.py
@@ -107,18 +107,28 @@
     ).astype(BF16)
 
 
-def pack_body(capacity, stride, outs, mask_ref, owner_hbm, slot_hbm, tokens_hbm, *rest):
-    out_refs, (owner_ref, slot_ref, tokens_ref, sems) = rest[:outs], rest[outs:]
-    fetch((owner_hbm, slot_hbm, tokens_hbm), (owner_ref, slot_ref, tokens_ref), sems)
-    owner = owner_ref[...] ^ mask_ref[0]
+def pack_body(capacity, stride, first, owner_ref, slot_ref, tokens_ref, out_refs):
+    owner = owner_ref[...]
     rows = owner.shape[1]
     rank_row, rank_col = rank_rows(owner)
-    total, width = outs * out_refs[0].shape[0], out_refs[0].shape[1]
-    place = iota((total, rows), 0)
+    total, width = len(out_refs) * out_refs[0].shape[0], out_refs[0].shape[1]
+    place = iota((total, rows), 0) + first * stride
     chosen = hot(place == owner * stride + rank_row)
     slots = jnp.where(place == owner * stride + capacity, slot_ref[...] + 1, 0)
     by_rank = hot(rank_col == iota((rows, width), 1))
     store_blocks(out_refs, mm(chosen, tokens_ref[...]) + mm(slots.astype(F32).astype(BF16), by_rank))
+
+
+def pack_far_body(capacity, stride, first, outs, mask_ref, owner_hbm, slot_hbm, tokens_hbm, *refs):
+    out_refs, kept_refs, sems = refs[:outs], refs[outs:-1], refs[-1]
+    owner_ref, slot_ref, tokens_ref = kept_refs
+    fetch((owner_hbm, slot_hbm, tokens_hbm), (owner_ref, slot_ref, tokens_ref), sems)
+    owner_ref[...] = owner_ref[...] ^ mask_ref[0]
+    pack_body(capacity, stride, first, owner_ref, slot_ref, tokens_ref, out_refs)
+
+
+def pack_near_body(capacity, stride, outs, owner_ref, slot_ref, tokens_ref, *refs):
+    pack_body(capacity, stride, 0, owner_ref, slot_ref, tokens_ref, refs[-outs:])
 
 
 def block_rem(owners, stride):
@@ -139,7 +149,7 @@
 def place_body(owners, capacity, stride, *refs):
     owned_ref, normed_ref, landing_ref = refs[-3:]
     rows = owned_ref.shape[0]
-    arrived = load_blocks(refs[:-4])
+    arrived = load_blocks(refs[:-3])
     total = arrived.shape[0]
     pick = hot(iota((owners, total), 1) == iota((owners, total), 0) * stride + capacity)
     table = mm(pick, arrived).astype(BF16)
@@ -291,7 +301,10 @@
         start = history_start(query_pos, lengths_ref)
         key_pos = k_block * rows + iota((rows, 1), 0)
         inverse = 1.0 / (query_pos - start + 1).astype(F32)
-        shared = jnp.where((key_pos >= start) & (key_pos <= query_pos), inverse, 0.0)
+        allowed = key_pos >= start
+        if same:
+            allowed &= key_pos <= query_pos
+        shared = jnp.where(allowed, inverse, 0.0)
         value = part_ref[k_at, :piece]
         query = part_ref[q_at, piece : 2 * piece]
         key = part_ref[k_at, 2 * piece :]
@@ -376,8 +389,13 @@
             ref[at, :] = total_ref[source, :].astype(BF16)
 
 
-def pair_body(kept_ref, came_ref, _, *outs):
-    store_blocks(outs, kept_ref[...].astype(F32) + came_ref[...].astype(F32))
+def halve_body(pairs, kept_ref, came_ref, *refs):
+    keep_ref, send_ref = refs[-2:]
+    share = kept_ref.shape[0] // pairs
+    total = kept_ref[...].astype(F32) + came_ref[...].astype(F32)
+    for j in range(pairs):
+        at = slice(j // 2 * share, (j // 2 + 1) * share)
+        (send_ref if j % 2 else keep_ref)[at, :] = total[j * share : (j + 1) * share].astype(BF16)
 
 
 def head_columns(owner, proj_ref):
@@ -393,7 +411,8 @@
 
 
 def input_body(
-    blocks, me_ref, own_ref, near_ref, partial_ref, owned_ref, cot_ref, landing_ref, proj_ref, *rest
+    blocks, me_ref, mask_ref, own_ref, near_ref, partial_ref,
+    owned_ref, cot_ref, landing_ref, proj_ref, out_ref,
 ):
     rows = owned_ref.shape[0]
     me = me_ref[0]
@@ -402,15 +421,18 @@
     centred, inv_scale = normalize(owned_ref[...].astype(F32))
     grad = (norm_back(total, centred, inv_scale) + cot_ref[...].astype(F32)).astype(BF16)
     select = hot(iota((rows, landing_ref.shape[1]), 0) + 1 == landing_ref[...])
-    store_blocks(rest[-blocks:], t_mm(select, grad))
-
-
-def return_body(capacity, mask_ref, owner_ref, *refs):
+    value = t_mm(select, grad)
+    size = value.shape[0] // blocks
+    for k in range(blocks):
+        at = pl.ds(pl.multiple_of((mask_ref[0] ^ k) * size, size), size)
+        out_ref[at, :] = value[k * size : (k + 1) * size].astype(BF16)
+
+
+def return_body(capacity, mask_ref, owner_ref, back_ref, out_ref):
     owner = owner_ref[...] ^ mask_ref[0]
     rank_row, _ = rank_rows(owner)
-    back = load_blocks(refs[:-1])
-    chosen = hot(iota((back.shape[0], owner.shape[1]), 0) == owner * capacity + rank_row)
-    refs[-1][...] = t_mm(chosen, back).astype(BF16)
+    chosen = hot(iota((back_ref.shape[0], owner.shape[1]), 0) == owner * capacity + rank_row)
+    out_ref[...] = t_mm(chosen, back_ref[...]).astype(BF16)
 
 
 def sum_body(*refs):
@@ -475,22 +497,25 @@
     def block_shapes(height, columns, dtype):
         return [((owners * height // blocks, columns), dtype)] * blocks
 
-    outgoing = call(
-        functools.partial(pack_body, capacity, stride, blocks),
-        "pack", block_shapes(stride, width, BF16), [mask], [], far=[owner_row, slot_row, tokens],
-        scratch=[
-            pltpu.VMEM((1, rows), jnp.int32),
-            pltpu.VMEM((1, rows), jnp.int32),
-            pltpu.VMEM((rows, width), BF16),
-            pltpu.SemaphoreType.DMA((3,)),
-        ],
-    )
-    arrived = swap(outgoing)
     wide = ((rows, width), F32)
+    late = blocks // 2
+    far_blocks = call(
+        functools.partial(pack_far_body, capacity, stride, late, blocks - late),
+        "pack_far",
+        block_shapes(stride, width, BF16)[late:] + [((1, rows), jnp.int32)] * 2 + [square],
+        [mask], [], far=[owner_row, slot_row, tokens], scratch=[pltpu.SemaphoreType.DMA((3,))],
+    )
+    *far_blocks, owner_here, slot_here, tokens_here = far_blocks
     (grad_gated,) = call(early_body, "early", [wide], [], [cotangent, out_weight, proj_weight])
+    near_blocks = call(
+        functools.partial(pack_near_body, capacity, stride, late),
+        "pack_near", block_shapes(stride, width, BF16)[:late], [],
+        [owner_here, slot_here, tokens_here], far=[grad_gated],
+    ) if late else []
+    arrived = swap([*near_blocks, *far_blocks])
     owned, normed, landing = call(
         functools.partial(place_body, owners, capacity, stride),
-        "place", [square, square, ((1, owners * capacity), jnp.int32)], [], arrived, far=[grad_gated],
+        "place", [square, square, ((1, owners * capacity), jnp.int32)], [], arrived,
     )
     near, far, cross = gather(normed)
     gate, slope, query, partial = call(
@@ -553,26 +578,27 @@
     (partial_in,) = call(
         input_far_body, "input_far", [wide], [me], [p2, p3, gate_in, proj_weight], flops=6 * 10**9,
     )
+    (back,) = call(
+        functools.partial(input_body, blocks), "input_grad", [((owners * capacity, width), BF16)], [me, mask],
+        [own_block, p1, partial_in, owned, cotangent, landing, proj_weight], vmem=16,
+    )
+    returned = swap_whole(back)
     if by_hops:
         kept, sent = weight_parts
-        halves = call(
-            pair_body, "pair_sum", [((share, columns), BF16)] * pairs, [], [kept, dp_hop(sent, 1)],
-            far=[partial_in],
-        )
-        summed_parts = [halves[0]] + [dp_hop(halves[j], 2 * j) for j in range(1, pairs)]
+        came, behind, bit = dp_hop(sent, 1), [back], 2
+        while bit < owners:
+            kept, sent = call(
+                functools.partial(halve_body, pairs), "halve",
+                [((pairs * share // 2, columns), BF16)] * 2, [], [kept, came], far=behind,
+            )
+            came, behind, bit, pairs = dp_hop(sent, bit), [], 2 * bit, pairs // 2
+        summed_parts = [kept, came]
     else:
-        halves = weight_parts
         summed_parts = [swap_whole(weight_parts[0]).reshape(owners, share, columns)]
-    back = call(
-        functools.partial(input_body, blocks), "input_grad", block_shapes(capacity, width, BF16), [me],
-        [own_block, p1, partial_in, owned, cotangent, landing, proj_weight], vmem=16,
-        far=[halves[0]],
-    )
-    returned = swap(back)
     (mine,) = call(sum_body, "sum", [((share, columns), BF16)], [], summed_parts)
     w1, w2, w3 = (hop(mine, step) for step in range(1, cycle))
     (grad_tokens,) = call(
-        functools.partial(return_body, capacity), "give_back", [square], [mask], [owner_row, *returned]
+        functools.partial(return_body, capacity), "give_back", [square], [mask], [owner_here, returned]
     )
     grad_proj, grad_outw = call(
         finish_body, "finish", [((share, 4 * width), F32), ((share, width), F32)],

time: 98.8 us -> 106 us (1.073)
  waiting for transfers between devices: 26.8 us -> 34.6 us
  starting transfers between devices: 46.2 us -> 39.3 us
  local copies, waits for them, and re-layouts: 5.9 us -> 9.65 us
  Pallas kernels: 19.1 us -> 22.4 us
    ppermute x18 -> x10, starting transfers between devices: 35.8 us -> 20.3 us  [dp_hop(): return lax.ppermute(value, 'dp', [(i, i ^ step) for i in range(owners)])]
    all_to_all x0 -> x1, starting transfers between devices: none -> 8.36 us  [swap_whole(): lax.all_to_all(split, 'dp', split_axis=0, concat_axis=0, tiled=True)]
    ppermute x14, waiting for transfers between devices: 7.02 us -> 13.6 us  [hop(): return lax.ppermute(value, 'ctx', [(i, i ^ step) for i in range(cycle)])]
    unnamed x22 -> x40, local copies, waits for them, and re-layouts: 5.9 us -> 9.65 us
    pallas_call x18 -> x20, Pallas kernels: 19.1 us -> 22.4 us  [call(): pl.pallas_call(body, name=name, out_shape=[jax.ShapeDtypeStruct(s, d) for...]
    ppermute x18 -> x10, waiting for transfers between devices: 19.8 us -> 21 us  [dp_hop(): return lax.ppermute(value, 'dp', [(i, i ^ step) for i in range(owners)])]
  transfers between devices with their start and end apart: 32 -> 25, of which waited for: 12 -> 14; matrix products, arithmetic and copies ran while one was open for 0% -> 0% of each run, Pallas kernels for 14% -> 17%
where the time goes in v8:
time: 106 us; the launch traced here: 107 us
  starting transfers between devices  39.3 us (37%)
  waiting for transfers between devices  34.6 us (33%)
  Pallas kernels  22.4 us (21%)
  local copies, waits for them, and re-layouts  9.65 us (9%)
    pallas_call x20, Pallas kernels, call(): pl.pallas_call(body, name=name, out_shape=[jax.ShapeDtypeStruct(s, d) for...  22.4 us
    ppermute x10, waiting for transfers between devices, dp_hop(): return lax.ppermute(value, 'dp', [(i, i ^ step) for i in range(owners)])  21 us
    ppermute x10, starting transfers between devices, dp_hop(): return lax.ppermute(value, 'dp', [(i, i ^ step) for i in range(owners)])  20.3 us
    ppermute x14, waiting for transfers between devices, hop(): return lax.ppermute(value, 'ctx', [(i, i ^ step) for i in range(cycle)])  13.6 us
    ppermute x14, starting transfers between devices, hop(): return lax.ppermute(value, 'ctx', [(i, i ^ step) for i in range(cycle)])  10.6 us
    unnamed x40, local copies, waits for them, and re-layouts  9.65 us
    all_to_all x1, starting transfers between devices, swap_whole(): lax.all_to_all(split, 'dp', split_axis=0, concat_axis=0, tiled=True)  8.36 us
  transfers between devices with their start and end apart: 25, of which 14 were waited for; matrix products, arithmetic and copies ran while one was open for 0% of the time, Pallas kernels for 17%

profile of v8, /device:TPU:0, one launch (start us, length us, event | category | flops | bytes accessed | tf_op | source)
XLA Modules:
  0.0 106.9 jit_solution(9485009752633662935)
XLA Ops:
  0.6 0.9 copy-done.17
  3.5 4.1 %collective-permute-start = (bf16[72,512]{1,0:T(8,128)(2,1)S(1)}, bf16[72,512]{1,0:T(8,128)(2,1)S(1)}, u32[]{:S(2)}, u32[]{:S(2)}) collective-permute-start(bf16[72,512]{1,0:T(8,128)(2,1)S(1)} %get-tuple-element.54), channel_id=1, source_target_pairs={{0,16},{4,20},{8,24},{12,28},{16,0},{20,4},{24,8},{28,12},{1,17},{... | collective-permute-start | bytes 221192 | tf_op jit(solution)/shard_map/ppermute | solution.py:486
  7.6 1.3 %collective-permute-start.1 = (bf16[72,512]{1,0:T(8,128)(2,1)S(1)}, bf16[72,512]{1,0:T(8,128)(2,1)S(1)}, u32[]{:S(2)}, u32[]{:S(2)}) collective-permute-start(bf16[72,512]{1,0:T(8,128)(2,1)S(1)} %get-tuple-element.55), channel_id=1, source_target_pairs={{0,20},{4,16},{8,28},{12,24},{16,4},{20,0},{24,12},{28,8},{1,21},{... | collective-permute-start | bytes 221192 | tf_op jit(solution)/shard_map/ppermute | solution.py:486
  8.9 3.6 %collective-permute-start.2 = (bf16[72,512]{1,0:T(8,128)(2,1)S(1)}, bf16[72,512]{1,0:T(8,128)(2,1)S(1)}, u32[]{:S(2)}, u32[]{:S(2)}) collective-permute-start(bf16[72,512]{1,0:T(8,128)(2,1)S(1)} %get-tuple-element.56), channel_id=1, source_target_pairs={{0,24},{4,28},{8,16},{12,20},{16,8},{20,12},{24,0},{28,4},{1,25},{... | collective-permute-start | bytes 221192 | tf_op jit(solution)/shard_map/ppermute | solution.py:486
  12.5 1.6 %copy-done = bf16[512,2048]{1,0:T(8,128)(2,1)S(1)} copy-done((bf16[512,2048]{1,0:T(8,128)(2,1)S(1)}, bf16[512,2048]{1,0:T(8,128)(2,1)}, u32[]{:S(2)}) %copy-start) | copy-done | bytes 2097176
  14.1 0.9 copy-done.2
  15.0 1.0 copy-done.4
  16.4 1.1 %pack_near.1 = (bf16[72,512]{1,0:T(8,128)(2,1)S(1)}, bf16[72,512]{1,0:T(8,128)(2,1)}, bf16[72,512]{1,0:T(8,128)(2,1)S(1)}, bf16[72,512]{1,0:T(8,128)(2,1)S(1)}) custom-call(s32[1,256]{1,0:T(1,128)S(1)} %get-tuple-element.50.owner_ref, s32[1,256]{1,0:T(1,128)S(1)} %get-tuple-element.51.slot_ref, bf16[256,512]{1,0:T(8,128)(2,1)S(1)} %get-tuple-element.52.tokens_ref, ...), custom_call_target="tpu_custom_call" | custom-call | flops 100000000 | bytes 1048576 | tf_op jit(solution)/shard_map/pack_near/pallas_call | solution.py:22
  17.5 1.7 %collective-permute-start.4 = (bf16[72,512]{1,0:T(8,128)(2,1)}, bf16[72,512]{1,0:T(8,128)(2,1)S(1)}, u32[]{:S(2)}, u32[]{:S(2)}) collective-permute-start(bf16[72,512]{1,0:T(8,128)(2,1)} %get-tuple-element.58), channel_id=1, source_target_pairs={{0,4},{4,0},{8,12},{12,8},{16,20},{20,16},{24,28},{28,24},{1,5},{5... | collective-permute-start | bytes 221192 | tf_op jit(solution)/shard_map/ppermute | solution.py:486
  19.2 1.8 %collective-permute-start.6 = (bf16[72,512]{1,0:T(8,128)(2,1)S(1)}, bf16[72,512]{1,0:T(8,128)(2,1)S(1)}, u32[]{:S(2)}, u32[]{:S(2)}) collective-permute-start(bf16[72,512]{1,0:T(8,128)(2,1)S(1)} %get-tuple-element.60), channel_id=1, source_target_pairs={{0,12},{4,8},{8,4},{12,0},{16,28},{20,24},{24,20},{28,16},{1,13},{... | collective-permute-start | bytes 221192 | tf_op jit(solution)/shard_map/ppermute | solution.py:486
  21.0 1.9 %collective-permute-done.4.refs_5_ = bf16[72,512]{1,0:T(8,128)(2,1)S(1)} collective-permute-done((bf16[72,512]{1,0:T(8,128)(2,1)}, bf16[72,512]{1,0:T(8,128)(2,1)S(1)}, u32[]{:S(2)}, u32[]{:S(2)}) %collective-permute-start.4) | collective-permute-done | bytes 73760 | tf_op jit(solution)/shard_map/ppermute | solution.py:486
  23.6 1.0 collective-permute-done.6.refs_7_
  24.5 0.8 place.1
  25.4 1.6 %collective-permute-start.7 = (bf16[256,512]{1,0:T(8,128)(2,1)S(1)}, bf16[256,512]{1,0:T(8,128)(2,1)S(1)}, u32[]{:S(2)}, u32[]{:S(2)}) collective-permute-start(bf16[256,512]{1,0:T(8,128)(2,1)S(1)} %get-tuple-element.61.normed_ref.n0_ref.refs_0_), channel_id=1, source_target_pairs={{0,2},{1,3},{2,0},{3,1},{4,6},{5,7},{6,4},{7,5},{8,10},{9,11},{10,... | collective-permute-start | bytes 786440 | tf_op jit(solution)/shard_map/ppermute | solution.py:471
  26.9 2.2 %own_rows.1 = (bf16[256,512]{1,0:T(8,128)(2,1)S(1)}, f32[256,512]{1,0:T(8,128)S(1)}, bf16[256,512]{1,0:T(8,128)(2,1)S(1)}, f32[256,512]{1,0:T(8,128)S(1)}) custom-call(s32[1]{0:T(128)} %bitcast.me_ref, s32[1,3]{1,0:T(1,128)S(1)} %copy-done.16, bf16[256,512]{1,0:T(8,128)(2,1)S(1)} %get-tuple-element.61.normed_ref.n0_ref.refs_0_, bf16[512,2048]{1,0:T(8,128)(2,1)S(1)} %copy-done.1), custom_call_target="tpu_custom_call" | custom-call | flops 10000000000 | bytes 1048576 | tf_op jit(solution)/shard_map/own_rows/pallas_call | solution.py:22
  29.1 2.7 %collective-permute-done.7.far_ref.n2_ref.refs_2_ = bf16[256,512]{1,0:T(8,128)(2,1)S(1)} collective-permute-done((bf16[256,512]{1,0:T(8,128)(2,1)S(1)}, bf16[256,512]{1,0:T(8,128)(2,1)S(1)}, u32[]{:S(2)}, u32[]{:S(2)}) %collective-permute-start.7) | collective-permute-done | bytes 262176 | tf_op jit(solution)/shard_map/ppermute | solution.py:471
  32.4 0.9 collective-permute-done.8.cross_ref.n3_ref.refs_3_
  33.4 1.9 %forward.1 = (bf16[256,512]{1,0:T(8,128)(2,1)}, bf16[256,512]{1,0:T(8,128)(2,1)S(1)}, bf16[256,512]{1,0:T(8,128)(2,1)S(1)}, bf16[256,128]{1,0:T(8,128)(2,1)S(1)}...) custom-call(s32[1]{0:T(128)} %bitcast.me_ref, s32[1,3]{1,0:T(1,128)S(1)} %copy-done.16, ...), custom_call_target="tpu_custom_call" | custom-call | flops 100000000 | bytes 1048576 | tf_op jit(solution)/shard_map/forward/pallas_call | solution.py:22
  35.4 3.7 %collective-permute-start.11 = (bf16[256,128]{1,0:T(8,128)(2,1)S(1)}, bf16[256,128]{1,0:T(8,128)(2,1)S(1)}, u32[]{:S(2)}, u32[]{:S(2)}) collective-permute-start(bf16[256,128]{1,0:T(8,128)(2,1)S(1)} %get-tuple-element.72), channel_id=1, source_target_pairs={{0,2},{1,3},{2,0},{3,1},{4,6},{5,7},{6,4},{7,5},{8,10},{9,11},{10,... | collective-permute-start | bytes 196616 | tf_op jit(solution)/shard_map/ppermute | solution.py:471
  39.1 0.8 side.1
  40.1 0.8 heads.1
  41.4 2.0 %collective-permute-done.12.g3_ref = bf16[256,128]{1,0:T(8,128)(2,1)S(1)} collective-permute-done((bf16[256,128]{1,0:T(8,128)(2,1)S(1)}, bf16[256,128]{1,0:T(8,128)(2,1)S(1)}, u32[]{:S(2)}, u32[]{:S(2)}) %collective-permute-start.12) | collective-permute-done | bytes 65568 | tf_op jit(solution)/shard_map/ppermute | solution.py:471
  43.4 4.4 %backward_far.1 = (bf16[256,384]{1,0:T(8,128)(2,1)S(1)}, bf16[256,384]{1,0:T(8,128)(2,1)S(1)}, f32[1024,384]{1,0:T(8,128)S(1)}, bf16[1024,128]{1,0:T(8,128)(2,1)S(1)}) custom-call(s32[1]{0:T(128)} %bitcast.me_ref, s32[1,3]{1,0:T(1,128)S(1)} %copy-done.16, bf16[256,128]{1,0:T(8,128)(2,1)S(1)} %get-tuple-element.70.g0_ref, ...), custom_call_target="tpu_custom_call" | custom-call | flops 10000000000 | bytes 1048576 | tf_op jit(solution)/shard_map/backward_far/pallas_call | solution.py:22
  47.9 1.4 %collective-permute-start.15 = (bf16[256,384]{1,0:T(8,128)(2,1)S(1)}, bf16[256,384]{1,0:T(8,128)(2,1)S(1)}, u32[]{:S(2)}, u32[]{:S(2)}) collective-permute-start(bf16[256,384]{1,0:T(8,128)(2,1)S(1)} %get-tuple-element.79.refs_7_), channel_id=1, source_target_pairs={{0,3},{1,2},{2,1},{3,0},{4,7},{5,6},{6,5},{7,4},{8,11},{9,10},{10,... | collective-permute-start | bytes 589832 | tf_op jit(solution)/shard_map/ppermute | solution.py:471
  49.3 1.9 %backward_rest.1 = (bf16[256,384]{1,0:T(8,128)(2,1)S(1)}, bf16[256,384]{1,0:T(8,128)(2,1)S(1)}) custom-call(s32[1]{0:T(128)} %bitcast.me_ref, s32[1,3]{1,0:T(1,128)S(1)} %copy-done.16, bf16[1024,384]{1,0:T(8,128)(2,1)S(1)} %get-tuple-element.68.part_ref, f32[1024,384]{1,0:T(8,128)S(1)} %get-tuple-element.69.slope_ref, ...), custom_call_target="tpu_custom_call" | custom-call | flops 100000000 | bytes 1048576 | tf_op jit(solution)/shard_map/backward_rest/pallas_call | solution.py:22
  51.2 0.8 collective-permute-start.13
  52.0 0.8 side_sum.1
  52.8 0.8 collective-permute-start.17
  53.6 2.1 %collective-permute-done.14.far_ref = bf16[256,384]{1,0:T(8,128)(2,1)S(1)} collective-permute-done((bf16[256,384]{1,0:T(8,128)(2,1)S(1)}, bf16[256,384]{1,0:T(8,128)(2,1)S(1)}, u32[]{:S(2)}, u32[]{:S(2)}) %collective-permute-start.14) | collective-permute-done | bytes 196640 | tf_op jit(solution)/shard_map/ppermute | solution.py:471
  55.7 2.3 %collective-permute-done.15.cross_ref = bf16[256,384]{1,0:T(8,128)(2,1)S(1)} collective-permute-done((bf16[256,384]{1,0:T(8,128)(2,1)S(1)}, bf16[256,384]{1,0:T(8,128)(2,1)S(1)}, u32[]{:S(2)}, u32[]{:S(2)}) %collective-permute-start.15) | collective-permute-done | bytes 196640 | tf_op jit(solution)/shard_map/ppermute | solution.py:471
  58.6 1.8 %input_grad.1.refs_0_ = bf16[512,512]{1,0:T(8,128)(2,1)} custom-call(s32[1]{0:T(128)} %bitcast.me_ref, s32[1]{0:T(128)} %bitcast.1.mask_ref.dp_ref, bf16[256,384]{1,0:T(8,128)(2,1)S(1)} %get-tuple-element.76.own_ref.refs_4_, bf16[256,384]{1,0:T(8,128)(2,1)S(1)} %collective-permute-done.13.near_ref, f32[256,512]{1,0:T(8,128)S(1)} %input_far.1.partial_ref, ...), custom_call_target="tpu_custom_call" | custom-call | flops 100000000 | bytes 1048576 | tf_op jit(solution)/shard_map/input_grad/pallas_call | solution.py:22
  60.3 8.4 %all-to-all-start = ((bf16[8,64,512]{2,1,0:T(8,128)(2,1)}), bf16[8,64,512]{2,1,0:T(8,128)(2,1)S(1)}, u32[]{:S(2)}, u32[]{:S(2)}) async-start(bf16[8,64,512]{2,1,0:T(8,128)(2,1)} %bitcast.4), calls=%async_computation | async-start | bytes 1048576 | tf_op jit(solution)/shard_map/all_to_all | solution.py:490
  68.7 0.9 copy-done.9
  69.6 0.9 copy-done.11
  70.6 0.9 copy-done.13
  71.5 0.9 copy-done.15
  72.4 1.8 %weights.1 = (bf16[256,640]{1,0:T(8,128)(2,1)S(1)}, bf16[256,640]{1,0:T(8,128)(2,1)S(1)}) custom-call(s32[1]{0:T(128)} %bitcast.1.mask_ref.dp_ref, bf16[512,256]{1,0:T(8,128)(2,1)S(1)} %copy-done.9, bf16[512,256]{1,0:T(8,128)(2,1)} %collective-permute-done.17.came_side_ref, bf16[256,512]{1,0:T(8,128)(2,1)S(1)} %get-tuple-element.61.normed_ref.n0_ref.refs_0_, ...), custom_call_target="tpu_custom_call" | custom-call | flops 100000000 | bytes 1048576 | tf_op jit(solution)/shard_map/weights/pallas_call | solution.py:22
  74.2 2.1 %collective-permute-start.18 = (bf16[256,640]{1,0:T(8,128)(2,1)S(1)}, bf16[256,640]{1,0:T(8,128)(2,1)S(1)}, u32[]{:S(2)}, u32[]{:S(2)}) collective-permute-start(bf16[256,640]{1,0:T(8,128)(2,1)S(1)} %get-tuple-element.89), channel_id=1, source_target_pairs={{0,4},{4,0},{8,12},{12,8},{16,20},{20,16},{24,28},{28,24},{1,5},{5... | collective-permute-start | bytes 983048 | tf_op jit(solution)/shard_map/ppermute | solution.py:486
  76.3 9.6 %collective-permute-done.18.came_ref = bf16[256,640]{1,0:T(8,128)(2,1)S(1)} collective-permute-done((bf16[256,640]{1,0:T(8,128)(2,1)S(1)}, bf16[256,640]{1,0:T(8,128)(2,1)S(1)}, u32[]{:S(2)}, u32[]{:S(2)}) %collective-permute-start.18) | collective-permute-done | bytes 327712 | tf_op jit(solution)/shard_map/ppermute | solution.py:486
  86.0 3.4 %collective-permute-start.19 = (bf16[128,640]{1,0:T(8,128)(2,1)S(1)}, bf16[128,640]{1,0:T(8,128)(2,1)S(1)}, u32[]{:S(2)}, u32[]{:S(2)}) collective-permute-start(bf16[128,640]{1,0:T(8,128)(2,1)S(1)} %get-tuple-element.91), channel_id=1, source_target_pairs={{0,8},{4,12},{8,0},{12,4},{16,24},{20,28},{24,16},{28,20},{1,9},{5... | collective-permute-start | bytes 491528 | tf_op jit(solution)/shard_map/ppermute | solution.py:486
  89.4 4.5 %collective-permute-done.19.came_ref = bf16[128,640]{1,0:T(8,128)(2,1)S(1)} collective-permute-done((bf16[128,640]{1,0:T(8,128)(2,1)S(1)}, bf16[128,640]{1,0:T(8,128)(2,1)S(1)}, u32[]{:S(2)}, u32[]{:S(2)}) %collective-permute-start.19) | collective-permute-done | bytes 163872 | tf_op jit(solution)/shard_map/ppermute | solution.py:486
  93.9 2.4 %collective-permute-start.20 = (bf16[64,640]{1,0:T(8,128)(2,1)S(1)}, bf16[64,640]{1,0:T(8,128)(2,1)S(1)}, u32[]{:S(2)}, u32[]{:S(2)}) collective-permute-start(bf16[64,640]{1,0:T(8,128)(2,1)S(1)} %get-tuple-element.93), channel_id=1, source_target_pairs={{0,16},{4,20},{8,24},{12,28},{16,0},{20,4},{24,8},{28,12},{1,17},{... | collective-permute-start | bytes 245768 | tf_op jit(solution)/shard_map/ppermute | solution.py:486
  96.3 3.4 %collective-permute-done.20.refs_1_ = bf16[64,640]{1,0:T(8,128)(2,1)S(1)} collective-permute-done((bf16[64,640]{1,0:T(8,128)(2,1)S(1)}, bf16[64,640]{1,0:T(8,128)(2,1)S(1)}, u32[]{:S(2)}, u32[]{:S(2)}) %collective-permute-start.20) | collective-permute-done | bytes 81952 | tf_op jit(solution)/shard_map/ppermute | solution.py:486
  100.0 1.7 %collective-permute-start.23 = (bf16[64,640]{1,0:T(8,128)(2,1)S(1)}, bf16[64,640]{1,0:T(8,128)(2,1)S(1)}, u32[]{:S(2)}, u32[]{:S(2)}) collective-permute-start(bf16[64,640]{1,0:T(8,128)(2,1)S(1)} %sum.1.w0_ref), channel_id=1, source_target_pairs={{0,3},{1,2},{2,1},{3,0},{4,7},{5,6},{6,5},{7,4},{8,11},{9,10},{10,... | collective-permute-start | bytes 245768 | tf_op jit(solution)/shard_map/ppermute | solution.py:471
  101.7 1.2 %give_back.1 = bf16[256,512]{1,0:T(8,128)(2,1)} custom-call(s32[1]{0:T(128)} %bitcast.1.mask_ref.dp_ref, s32[1,256]{1,0:T(1,128)S(1)} %get-tuple-element.50.owner_ref, bf16[512,512]{1,0:T(8,128)(2,1)S(1)} %bitcast.6), custom_call_target="tpu_custom_call" | custom-call | flops 100000000 | bytes 1048576 | tf_op jit(solution)/shard_map/give_back/pallas_call | solution.py:22
  102.8 2.3 %collective-permute-done.22.w2_ref = bf16[64,640]{1,0:T(8,128)(2,1)S(1)} collective-permute-done((bf16[64,640]{1,0:T(8,128)(2,1)S(1)}, bf16[64,640]{1,0:T(8,128)(2,1)S(1)}, u32[]{:S(2)}, u32[]{:S(2)}) %collective-permute-start.22) | collective-permute-done | bytes 81952 | tf_op jit(solution)/shard_map/ppermute | solution.py:471
  105.1 0.8 collective-permute-done.23.w3_ref
  106.0 0.9 finish.1
  (62 shorter events, 5.3 us)
Async XLA Ops:
  0.6 1.0 copy-start.17
  1.6 0.7 copy-start.18
  2.3 0.7 copy-start.19
  3.5 15.7 %collective-permute-start = (bf16[72,512]{1,0:T(8,128)(2,1)S(1)}, bf16[72,512]{1,0:T(8,128)(2,1)S(1)}, u32[]{:S(2)}, u32[]{:S(2)}) collective-permute-start(bf16[72,512]{1,0:T(8,128)(2,1)S(1)} %get-tuple-element.54), channel_id=1, source_target_pairs={{0,16},{4,20},{8,24},{12,28},{16,0},{20,4},{24,8},{28,12},{1,17},{... | collective-permute-start | bytes 221192 | tf_op jit(solution)/shard_map/ppermute | solution.py:486
  7.6 11.6 %collective-permute-start.1 = (bf16[72,512]{1,0:T(8,128)(2,1)S(1)}, bf16[72,512]{1,0:T(8,128)(2,1)S(1)}, u32[]{:S(2)}, u32[]{:S(2)}) collective-permute-start(bf16[72,512]{1,0:T(8,128)(2,1)S(1)} %get-tuple-element.55), channel_id=1, source_target_pairs={{0,20},{4,16},{8,28},{12,24},{16,4},{20,0},{24,12},{28,8},{1,21},{... | collective-permute-start | bytes 221192 | tf_op jit(solution)/shard_map/ppermute | solution.py:486
  8.9 12.1 %collective-permute-start.2 = (bf16[72,512]{1,0:T(8,128)(2,1)S(1)}, bf16[72,512]{1,0:T(8,128)(2,1)S(1)}, u32[]{:S(2)}, u32[]{:S(2)}) collective-permute-start(bf16[72,512]{1,0:T(8,128)(2,1)S(1)} %get-tuple-element.56), channel_id=1, source_target_pairs={{0,24},{4,28},{8,16},{12,20},{16,8},{20,12},{24,0},{28,4},{1,25},{... | collective-permute-start | bytes 221192 | tf_op jit(solution)/shard_map/ppermute | solution.py:486
  12.5 8.5 %collective-permute-start.3 = (bf16[72,512]{1,0:T(8,128)(2,1)S(1)}, bf16[72,512]{1,0:T(8,128)(2,1)S(1)}, u32[]{:S(2)}, u32[]{:S(2)}) collective-permute-start(bf16[72,512]{1,0:T(8,128)(2,1)S(1)} %get-tuple-element.57), channel_id=1, source_target_pairs={{0,28},{4,24},{8,20},{12,16},{16,12},{20,8},{24,4},{28,0},{1,29},{... | collective-permute-start | bytes 221192 | tf_op jit(solution)/shard_map/ppermute | solution.py:486
  12.5 1.6 %copy-start = (bf16[512,2048]{1,0:T(8,128)(2,1)S(1)}, bf16[512,2048]{1,0:T(8,128)(2,1)}, u32[]{:S(2)}) copy-start(bf16[512,2048]{1,0:T(8,128)(2,1)} %proj_ref.15) | copy-start | bytes 6291460
  14.1 0.9 copy-start.2
  15.0 1.0 copy-start.4
  16.1 10.8 %copy-start.1 = (bf16[512,2048]{1,0:T(8,128)(2,1)S(1)}, bf16[512,2048]{1,0:T(8,128)(2,1)}, u32[]{:S(2)}) copy-start(bf16[512,2048]{1,0:T(8,128)(2,1)} %proj_ref.15) | copy-start | bytes 6291460
  16.1 10.8 %copy-start.16 = (s32[1,3]{1,0:T(1,128)S(1)}, s32[1,3]{1,0:T(1,128)}, u32[]{:S(2)}) copy-start(s32[1,3]{1,0:T(1,128)} %lengths_ref.9) | copy-start | bytes 40
  17.5 5.4 %collective-permute-start.4 = (bf16[72,512]{1,0:T(8,128)(2,1)}, bf16[72,512]{1,0:T(8,128)(2,1)S(1)}, u32[]{:S(2)}, u32[]{:S(2)}) collective-permute-start(bf16[72,512]{1,0:T(8,128)(2,1)} %get-tuple-element.58), channel_id=1, source_target_pairs={{0,4},{4,0},{8,12},{12,8},{16,20},{20,16},{24,28},{28,24},{1,5},{5... | collective-permute-start | bytes 221192 | tf_op jit(solution)/shard_map/ppermute | solution.py:486
  19.2 4.4 %collective-permute-start.5 = (bf16[72,512]{1,0:T(8,128)(2,1)S(1)}, bf16[72,512]{1,0:T(8,128)(2,1)S(1)}, u32[]{:S(2)}, u32[]{:S(2)}) collective-permute-start(bf16[72,512]{1,0:T(8,128)(2,1)S(1)} %get-tuple-element.59), channel_id=1, source_target_pairs={{0,8},{4,12},{8,0},{12,4},{16,24},{20,28},{24,16},{28,20},{1,9},{5... | collective-permute-start | bytes 221192 | tf_op jit(solution)/shard_map/ppermute | solution.py:486
  19.2 5.3 %collective-permute-start.6 = (bf16[72,512]{1,0:T(8,128)(2,1)S(1)}, bf16[72,512]{1,0:T(8,128)(2,1)S(1)}, u32[]{:S(2)}, u32[]{:S(2)}) collective-permute-start(bf16[72,512]{1,0:T(8,128)(2,1)S(1)} %get-tuple-element.60), channel_id=1, source_target_pairs={{0,12},{4,8},{8,4},{12,0},{16,28},{20,24},{24,20},{28,16},{1,13},{... | collective-permute-start | bytes 221192 | tf_op jit(solution)/shard_map/ppermute | solution.py:486
  25.4 6.4 %collective-permute-start.7 = (bf16[256,512]{1,0:T(8,128)(2,1)S(1)}, bf16[256,512]{1,0:T(8,128)(2,1)S(1)}, u32[]{:S(2)}, u32[]{:S(2)}) collective-permute-start(bf16[256,512]{1,0:T(8,128)(2,1)S(1)} %get-tuple-element.61.normed_ref.n0_ref.refs_0_), channel_id=1, source_target_pairs={{0,2},{1,3},{2,0},{3,1},{4,6},{5,7},{6,4},{7,5},{8,10},{9,11},{10,... | collective-permute-start | bytes 786440 | tf_op jit(solution)/shard_map/ppermute | solution.py:471
  26.9 4.9 %collective-permute-start.9 = (bf16[256,512]{1,0:T(8,128)(2,1)S(1)}, bf16[256,512]{1,0:T(8,128)(2,1)S(1)}, u32[]{:S(2)}, u32[]{:S(2)}) collective-permute-start(bf16[256,512]{1,0:T(8,128)(2,1)S(1)} %get-tuple-element.61.normed_ref.n0_ref.refs_0_), channel_id=1, source_target_pairs={{0,1},{1,0},{2,3},{3,2},{4,5},{5,4},{6,7},{7,6},{8,9},{9,8},{10,11... | collective-permute-start | bytes 786440 | tf_op jit(solution)/shard_map/ppermute | solution.py:471
  31.8 1.5 %collective-permute-start.8 = (bf16[256,512]{1,0:T(8,128)(2,1)S(1)}, bf16[256,512]{1,0:T(8,128)(2,1)S(1)}, u32[]{:S(2)}, u32[]{:S(2)}) collective-permute-start(bf16[256,512]{1,0:T(8,128)(2,1)S(1)} %collective-permute-done.7.far_ref.n2_ref.refs_2_), channel_id=1, source_target_pairs={{0,1},{1,0},{2,3},{3,2},{4,5},{5,4},{6,7},{7,6},{8,9},{9,8},{10,11... | collective-permute-start | bytes 786440 | tf_op jit(solution)/shard_map/ppermute | solution.py:471
  31.8 8.3 %copy-start.6 = (bf16[256,512]{1,0:T(8,128)(2,1)}, bf16[256,512]{1,0:T(8,128)(2,1)S(1)}, u32[]{:S(2)}) copy-start(bf16[256,512]{1,0:T(8,128)(2,1)S(1)} %collective-permute-done.9.near_ref.n1_ref.refs_1_) | copy-start | bytes 786436
  31.8 1.5 %copy-start.5 = (bf16[512,512]{1,0:T(8,128)(2,1)S(1)}, bf16[512,512]{1,0:T(8,128)(2,1)}, u32[]{:S(2)}) copy-start(bf16[512,512]{1,0:T(8,128)(2,1)} %outw_ref.3) | copy-start | bytes 1572868
  33.4 5.8 %copy-start.3 = (bf16[256,512]{1,0:T(8,128)(2,1)S(1)}, bf16[256,512]{1,0:T(8,128)(2,1)}, u32[]{:S(2)}) copy-start(bf16[256,512]{1,0:T(8,128)(2,1)} %cot_ref.5) | copy-start | bytes 786436
  35.3 5.7 %collective-permute-start.10 = (bf16[256,128]{1,0:T(8,128)(2,1)S(1)}, bf16[256,128]{1,0:T(8,128)(2,1)S(1)}, u32[]{:S(2)}, u32[]{:S(2)}) collective-permute-start(bf16[256,128]{1,0:T(8,128)(2,1)S(1)} %get-tuple-element.71), channel_id=1, source_target_pairs={{0,1},{1,0},{2,3},{3,2},{4,5},{5,4},{6,7},{7,6},{8,9},{9,8},{10,11... | collective-permute-start | bytes 196616 | tf_op jit(solution)/shard_map/ppermute | solution.py:471
  35.4 6.0 %collective-permute-start.11 = (bf16[256,128]{1,0:T(8,128)(2,1)S(1)}, bf16[256,128]{1,0:T(8,128)(2,1)S(1)}, u32[]{:S(2)}, u32[]{:S(2)}) collective-permute-start(bf16[256,128]{1,0:T(8,128)(2,1)S(1)} %get-tuple-element.72), channel_id=1, source_target_pairs={{0,2},{1,3},{2,0},{3,1},{4,6},{5,7},{6,4},{7,5},{8,10},{9,11},{10,... | collective-permute-start | bytes 196616 | tf_op jit(solution)/shard_map/ppermute | solution.py:471
  39.1 4.3 %collective-permute-start.12 = (bf16[256,128]{1,0:T(8,128)(2,1)S(1)}, bf16[256,128]{1,0:T(8,128)(2,1)S(1)}, u32[]{:S(2)}, u32[]{:S(2)}) collective-permute-start(bf16[256,128]{1,0:T(8,128)(2,1)S(1)} %get-tuple-element.73), channel_id=1, source_target_pairs={{0,3},{1,2},{2,1},{3,0},{4,7},{5,6},{6,5},{7,4},{8,11},{9,10},{10,... | collective-permute-start | bytes 196616 | tf_op jit(solution)/shard_map/ppermute | solution.py:471
  39.9 12.2 %collective-permute-start.16 = (bf16[512,512]{1,0:T(8,128)(2,1)S(1)}, bf16[512,512]{1,0:T(8,128)(2,1)S(1)}, u32[]{:S(2)}, u32[]{:S(2)}) collective-permute-start(bf16[512,512]{1,0:T(8,128)(2,1)S(1)} %get-tuple-element.85), channel_id=1, source_target_pairs={{0,1},{1,0},{2,3},{3,2},{4,5},{5,4},{6,7},{7,6},{8,9},{9,8},{10,11... | collective-permute-start | bytes 1572872 | tf_op jit(solution)/shard_map/ppermute | solution.py:471
  47.8 3.4 %copy-start.10 = (bf16[256,384]{1,0:T(8,128)(2,1)}, bf16[256,384]{1,0:T(8,128)(2,1)S(1)}, u32[]{:S(2)}) copy-start(bf16[256,384]{1,0:T(8,128)(2,1)S(1)} %get-tuple-element.78.refs_6_) | copy-start | bytes 589828
  47.8 3.4 %copy-start.12 = (bf16[256,384]{1,0:T(8,128)(2,1)}, bf16[256,384]{1,0:T(8,128)(2,1)S(1)}, u32[]{:S(2)}) copy-start(bf16[256,384]{1,0:T(8,128)(2,1)S(1)} %get-tuple-element.79.refs_7_) | copy-start | bytes 589828
  47.8 7.8 %collective-permute-start.14 = (bf16[256,384]{1,0:T(8,128)(2,1)S(1)}, bf16[256,384]{1,0:T(8,128)(2,1)S(1)}, u32[]{:S(2)}, u32[]{:S(2)}) collective-permute-start(bf16[256,384]{1,0:T(8,128)(2,1)S(1)} %get-tuple-element.78.refs_6_), channel_id=1, source_target_pairs={{0,2},{1,3},{2,0},{3,1},{4,6},{5,7},{6,4},{7,5},{8,10},{9,11},{10,... | collective-permute-start | bytes 589832 | tf_op jit(solution)/shard_map/ppermute | solution.py:471
  47.9 10.1 %collective-permute-start.15 = (bf16[256,384]{1,0:T(8,128)(2,1)S(1)}, bf16[256,384]{1,0:T(8,128)(2,1)S(1)}, u32[]{:S(2)}, u32[]{:S(2)}) collective-permute-start(bf16[256,384]{1,0:T(8,128)(2,1)S(1)} %get-tuple-element.79.refs_7_), channel_id=1, source_target_pairs={{0,3},{1,2},{2,1},{3,0},{4,7},{5,6},{6,5},{7,4},{8,11},{9,10},{10,... | collective-permute-start | bytes 589832 | tf_op jit(solution)/shard_map/ppermute | solution.py:471
  51.2 7.3 %copy-start.14 = (bf16[256,384]{1,0:T(8,128)(2,1)}, bf16[256,384]{1,0:T(8,128)(2,1)S(1)}, u32[]{:S(2)}) copy-start(bf16[256,384]{1,0:T(8,128)(2,1)S(1)} %get-tuple-element.77.refs_5_) | copy-start | bytes 589828
  51.2 7.3 %collective-permute-start.13 = (bf16[256,384]{1,0:T(8,128)(2,1)S(1)}, bf16[256,384]{1,0:T(8,128)(2,1)S(1)}, u32[]{:S(2)}, u32[]{:S(2)}) collective-permute-start(bf16[256,384]{1,0:T(8,128)(2,1)S(1)} %get-tuple-element.77.refs_5_), channel_id=1, source_target_pairs={{0,1},{1,0},{2,3},{3,2},{4,5},{5,4},{6,7},{7,6},{8,9},{9,8},{10,11... | collective-permute-start | bytes 589832 | tf_op jit(solution)/shard_map/ppermute | solution.py:471
  52.8 5.7 %copy-start.8 = (bf16[512,256]{1,0:T(8,128)(2,1)}, bf16[512,256]{1,0:T(8,128)(2,1)S(1)}, u32[]{:S(2)}) copy-start(bf16[512,256]{1,0:T(8,128)(2,1)S(1)} %get-tuple-element.86.kept_side_ref) | copy-start | bytes 786436
  52.8 15.9 %collective-permute-start.17 = (bf16[512,256]{1,0:T(8,128)(2,1)}, bf16[512,256]{1,0:T(8,128)(2,1)}, u32[]{:S(2)}, u32[]{:S(2)}) collective-permute-start(bf16[512,256]{1,0:T(8,128)(2,1)} %get-tuple-element.87), channel_id=1, source_target_pairs={{0,2},{1,3},{2,0},{3,1},{4,6},{5,7},{6,4},{7,5},{8,10},{9,11},{10,... | collective-permute-start | bytes 786440 | tf_op jit(solution)/shard_map/ppermute | solution.py:471
  58.5 10.1 %copy-start.7 = (bf16[256,512]{1,0:T(8,128)(2,1)S(1)}, bf16[256,512]{1,0:T(8,128)(2,1)}, u32[]{:S(2)}) copy-start(bf16[256,512]{1,0:T(8,128)(2,1)} %copy-done.6) | copy-start | bytes 786436
  60.3 41.4 %all-to-all-start = ((bf16[8,64,512]{2,1,0:T(8,128)(2,1)}), bf16[8,64,512]{2,1,0:T(8,128)(2,1)S(1)}, u32[]{:S(2)}, u32[]{:S(2)}) async-start(bf16[8,64,512]{2,1,0:T(8,128)(2,1)} %bitcast.4), calls=%async_computation | async-start | bytes 1048576 | tf_op jit(solution)/shard_map/all_to_all | solution.py:490
  68.7 1.0 copy-start.9
  69.6 0.9 copy-start.11
  70.6 0.9 copy-start.13
  71.5 0.9 copy-start.15
  74.2 11.7 %collective-permute-start.18 = (bf16[256,640]{1,0:T(8,128)(2,1)S(1)}, bf16[256,640]{1,0:T(8,128)(2,1)S(1)}, u32[]{:S(2)}, u32[]{:S(2)}) collective-permute-start(bf16[256,640]{1,0:T(8,128)(2,1)S(1)} %get-tuple-element.89), channel_id=1, source_target_pairs={{0,4},{4,0},{8,12},{12,8},{16,20},{20,16},{24,28},{28,24},{1,5},{5... | collective-permute-start | bytes 983048 | tf_op jit(solution)/shard_map/ppermute | solution.py:486
  86.0 7.9 %collective-permute-start.19 = (bf16[128,640]{1,0:T(8,128)(2,1)S(1)}, bf16[128,640]{1,0:T(8,128)(2,1)S(1)}, u32[]{:S(2)}, u32[]{:S(2)}) collective-permute-start(bf16[128,640]{1,0:T(8,128)(2,1)S(1)} %get-tuple-element.91), channel_id=1, source_target_pairs={{0,8},{4,12},{8,0},{12,4},{16,24},{20,28},{24,16},{28,20},{1,9},{5... | collective-permute-start | bytes 491528 | tf_op jit(solution)/shard_map/ppermute | solution.py:486
  93.9 5.8 %collective-permute-start.20 = (bf16[64,640]{1,0:T(8,128)(2,1)S(1)}, bf16[64,640]{1,0:T(8,128)(2,1)S(1)}, u32[]{:S(2)}, u32[]{:S(2)}) collective-permute-start(bf16[64,640]{1,0:T(8,128)(2,1)S(1)} %get-tuple-element.93), channel_id=1, source_target_pairs={{0,16},{4,20},{8,24},{12,28},{16,0},{20,4},{24,8},{28,12},{1,17},{... | collective-permute-start | bytes 245768 | tf_op jit(solution)/shard_map/ppermute | solution.py:486
  99.7 3.1 %collective-permute-start.21 = (bf16[64,640]{1,0:T(8,128)(2,1)S(1)}, bf16[64,640]{1,0:T(8,128)(2,1)S(1)}, u32[]{:S(2)}, u32[]{:S(2)}) collective-permute-start(bf16[64,640]{1,0:T(8,128)(2,1)S(1)} %sum.1.w0_ref), channel_id=1, source_target_pairs={{0,1},{1,0},{2,3},{3,2},{4,5},{5,4},{6,7},{7,6},{8,9},{9,8},{10,11... | collective-permute-start | bytes 245768 | tf_op jit(solution)/shard_map/ppermute | solution.py:471
  99.8 5.3 %collective-permute-start.22 = (bf16[64,640]{1,0:T(8,128)(2,1)S(1)}, bf16[64,640]{1,0:T(8,128)(2,1)S(1)}, u32[]{:S(2)}, u32[]{:S(2)}) collective-permute-start(bf16[64,640]{1,0:T(8,128)(2,1)S(1)} %sum.1.w0_ref), channel_id=1, source_target_pairs={{0,2},{1,3},{2,0},{3,1},{4,6},{5,7},{6,4},{7,5},{8,10},{9,11},{10,... | collective-permute-start | bytes 245768 | tf_op jit(solution)/shard_map/ppermute | solution.py:471
  100.0 6.0 %collective-permute-start.23 = (bf16[64,640]{1,0:T(8,128)(2,1)S(1)}, bf16[64,640]{1,0:T(8,128)(2,1)S(1)}, u32[]{:S(2)}, u32[]{:S(2)}) collective-permute-start(bf16[64,640]{1,0:T(8,128)(2,1)S(1)} %sum.1.w0_ref), channel_id=1, source_target_pairs={{0,3},{1,2},{2,1},{3,0},{4,7},{5,6},{6,5},{7,4},{8,11},{9,10},{10,... | collective-permute-start | bytes 245768 | tf_op jit(solution)/shard_map/ppermute | solution.py:471

commit v9 on v8

--- a/solution.py
+++ b/solution.py
@@ -107,28 +107,30 @@
     ).astype(BF16)
 
 
-def pack_body(capacity, stride, first, owner_ref, slot_ref, tokens_ref, out_refs):
-    owner = owner_ref[...]
+def pack_body(capacity, stride, outs, mask_ref, owner_hbm, slot_hbm, tokens_hbm, *refs):
+    out_refs, (owner_ref, slot_ref, tokens_ref, sems) = refs[:outs], refs[outs:]
+    fetch((owner_hbm, slot_hbm, tokens_hbm), (owner_ref, slot_ref, tokens_ref), sems)
+    owner = owner_ref[...] ^ mask_ref[0]
+    owner_ref[...] = owner
     rows = owner.shape[1]
     rank_row, rank_col = rank_rows(owner)
-    total, width = len(out_refs) * out_refs[0].shape[0], out_refs[0].shape[1]
-    place = iota((total, rows), 0) + first * stride
+    total, width = outs * out_refs[0].shape[0], out_refs[0].shape[1]
+    place = iota((total, rows), 0)
     chosen = hot(place == owner * stride + rank_row)
     slots = jnp.where(place == owner * stride + capacity, slot_ref[...] + 1, 0)
     by_rank = hot(rank_col == iota((rows, width), 1))
     store_blocks(out_refs, mm(chosen, tokens_ref[...]) + mm(slots.astype(F32).astype(BF16), by_rank))
 
 
-def pack_far_body(capacity, stride, first, outs, mask_ref, owner_hbm, slot_hbm, tokens_hbm, *refs):
-    out_refs, kept_refs, sems = refs[:outs], refs[outs:-1], refs[-1]
-    owner_ref, slot_ref, tokens_ref = kept_refs
-    fetch((owner_hbm, slot_hbm, tokens_hbm), (owner_ref, slot_ref, tokens_ref), sems)
-    owner_ref[...] = owner_ref[...] ^ mask_ref[0]
-    pack_body(capacity, stride, first, owner_ref, slot_ref, tokens_ref, out_refs)
-
-
-def pack_near_body(capacity, stride, outs, owner_ref, slot_ref, tokens_ref, *refs):
-    pack_body(capacity, stride, 0, owner_ref, slot_ref, tokens_ref, refs[-outs:])
+def relay(value, after):
+    return pl.pallas_call(
+        lambda *refs: None,
+        name="relay",
+        out_shape=jax.ShapeDtypeStruct(value.shape, value.dtype),
+        in_specs=[ANYWHERE] * (1 + len(after)),
+        out_specs=ANYWHERE,
+        input_output_aliases={0: 0},
+    )(value, *after)
 
 
 def block_rem(owners, stride):
@@ -412,8 +414,9 @@
 
 def input_body(
     blocks, me_ref, mask_ref, own_ref, near_ref, partial_ref,
-    owned_ref, cot_ref, landing_ref, proj_ref, out_ref,
+    owned_ref, cot_ref, landing_ref, proj_ref, *rest,
 ):
+    out_ref = rest[-1]
     rows = owned_ref.shape[0]
     me = me_ref[0]
     total = partial_ref[...] + mm_t(own_ref[...], head_columns(me, proj_ref))
@@ -498,21 +501,20 @@
         return [((owners * height // blocks, columns), dtype)] * blocks
 
     wide = ((rows, width), F32)
-    late = blocks // 2
-    far_blocks = call(
-        functools.partial(pack_far_body, capacity, stride, late, blocks - late),
-        "pack_far",
-        block_shapes(stride, width, BF16)[late:] + [((1, rows), jnp.int32)] * 2 + [square],
-        [mask], [], far=[owner_row, slot_row, tokens], scratch=[pltpu.SemaphoreType.DMA((3,))],
-    )
-    *far_blocks, owner_here, slot_here, tokens_here = far_blocks
+    *outgoing, owner_here = call(
+        functools.partial(pack_body, capacity, stride, blocks),
+        "pack", block_shapes(stride, width, BF16) + [((1, rows), jnp.int32)],
+        [mask], [], far=[owner_row, slot_row, tokens],
+        scratch=[
+            pltpu.VMEM((1, rows), jnp.int32),
+            pltpu.VMEM((rows, width), BF16),
+            pltpu.SemaphoreType.DMA((3,)),
+        ],
+    )
     (grad_gated,) = call(early_body, "early", [wide], [], [cotangent, out_weight, proj_weight])
-    near_blocks = call(
-        functools.partial(pack_near_body, capacity, stride, late),
-        "pack_near", block_shapes(stride, width, BF16)[:late], [],
-        [owner_here, slot_here, tokens_here], far=[grad_gated],
-    ) if late else []
-    arrived = swap([*near_blocks, *far_blocks])
+    if by_hops:
+        outgoing[owners // 4] = relay(outgoing[owners // 4], [grad_gated])
+    arrived = swap(outgoing)
     owned, normed, landing = call(
         functools.partial(place_body, owners, capacity, stride),
         "place", [square, square, ((1, owners * capacity), jnp.int32)], [], arrived,
@@ -578,20 +580,22 @@
     (partial_in,) = call(
         input_far_body, "input_far", [wide], [me], [p2, p3, gate_in, proj_weight], flops=6 * 10**9,
     )
+    came = dp_hop(weight_parts[1], 1) if by_hops else weight_parts[0]
     (back,) = call(
         functools.partial(input_body, blocks), "input_grad", [((owners * capacity, width), BF16)], [me, mask],
         [own_block, p1, partial_in, owned, cotangent, landing, proj_weight], vmem=16,
+        far=[came],
     )
     returned = swap_whole(back)
     if by_hops:
         kept, sent = weight_parts
-        came, behind, bit = dp_hop(sent, 1), [back], 2
+        bit, behind = 2, [back]
         while bit < owners:
             kept, sent = call(
                 functools.partial(halve_body, pairs), "halve",
                 [((pairs * share // 2, columns), BF16)] * 2, [], [kept, came], far=behind,
             )
-            came, behind, bit, pairs = dp_hop(sent, bit), [], 2 * bit, pairs // 2
+            came, bit, pairs, behind = dp_hop(sent, bit), 2 * bit, pairs // 2, []
         summed_parts = [kept, came]
     else:
         summed_parts = [swap_whole(weight_parts[0]).reshape(owners, share, columns)]

time: 106 us -> 103 us (0.972); the launches traced: 107 us -> 103 us
  Pallas kernels: 22.4 us -> 19.9 us
  local copies, waits for them, and re-layouts: 9.65 us -> 7.32 us
  waiting for transfers between devices: 34.6 us -> 35.9 us
    pallas_call x20 -> x19, Pallas kernels: 22.4 us -> 19.9 us  [call(): pl.pallas_call(body, name=name, out_shape=[jax.ShapeDtypeStruct(s, d) for...]
    unnamed x40 -> x26, local copies, waits for them, and re-layouts: 9.65 us -> 7.32 us
    ppermute x10, waiting for transfers between devices: 21 us -> 23.1 us  [dp_hop(): return lax.ppermute(value, 'dp', [(i, i ^ step) for i in range(owners)])]
    ppermute x10, starting transfers between devices: 20.3 us -> 18.8 us  [dp_hop(): return lax.ppermute(value, 'dp', [(i, i ^ step) for i in range(owners)])]
  transfers between devices with their start and end apart: 25 -> 25, of which waited for: 14 -> 12; matrix products, arithmetic and copies ran while one was open for 0% -> 0% of each run, Pallas kernels for 17% -> 12%
where the time goes in v9:
time: 103 us
  starting transfers between devices  38.7 us (38%)
  waiting for transfers between devices  35.9 us (35%)
  Pallas kernels  19.9 us (19%)
  local copies, waits for them, and re-layouts  7.32 us (7%)
    ppermute x10, waiting for transfers between devices, dp_hop(): return lax.ppermute(value, 'dp', [(i, i ^ step) for i in range(owners)])  23.1 us
    pallas_call x19, Pallas kernels, call(): pl.pallas_call(body, name=name, out_shape=[jax.ShapeDtypeStruct(s, d) for...  19.9 us
    ppermute x10, starting transfers between devices, dp_hop(): return lax.ppermute(value, 'dp', [(i, i ^ step) for i in range(owners)])  18.8 us
    ppermute x14, waiting for transfers between devices, hop(): return lax.ppermute(value, 'ctx', [(i, i ^ step) for i in range(cycle)])  12.8 us
    ppermute x14, starting transfers between devices, hop(): return lax.ppermute(value, 'ctx', [(i, i ^ step) for i in range(cycle)])  11.2 us
    all_to_all x1, starting transfers between devices, swap_whole(): lax.all_to_all(split, 'dp', split_axis=0, concat_axis=0, tiled=True)  8.69 us
    unnamed x26, local copies, waits for them, and re-layouts  7.32 us
  transfers between devices with their start and end apart: 25, of which 12 were waited for; matrix products, arithmetic and copies ran while one was open for 0% of the time, Pallas kernels for 12%

profile of v9, /device:TPU:0, one launch (start us, length us, event | category | flops | bytes accessed | tf_op | source)
XLA Modules:
  0.0 102.6 jit_solution(3261787524333690512)
XLA Ops:
  0.6 0.9 copy-done.10
  1.6 0.7 copy-done.11
  2.3 0.7 copy-done.12
  2.9 0.7 pack.1
  3.7 0.6 copy-done.8
  4.3 4.0 %collective-permute-start = (bf16[72,512]{1,0:T(8,128)(2,1)S(1)}, bf16[72,512]{1,0:T(8,128)(2,1)S(1)}, u32[]{:S(2)}, u32[]{:S(2)}) collective-permute-start(bf16[72,512]{1,0:T(8,128)(2,1)S(1)} %get-tuple-element.49), channel_id=1, source_target_pairs={{0,16},{4,20},{8,24},{12,28},{16,0},{20,4},{24,8},{28,12},{1,17},{... | collective-permute-start | bytes 221192 | tf_op jit(solution)/shard_map/ppermute | solution.py:489
  8.3 1.3 %collective-permute-start.1 = (bf16[72,512]{1,0:T(8,128)(2,1)S(1)}, bf16[72,512]{1,0:T(8,128)(2,1)S(1)}, u32[]{:S(2)}, u32[]{:S(2)}) collective-permute-start(bf16[72,512]{1,0:T(8,128)(2,1)S(1)} %get-tuple-element.50), channel_id=1, source_target_pairs={{0,20},{4,16},{8,28},{12,24},{16,4},{20,0},{24,12},{28,8},{1,21},{... | collective-permute-start | bytes 221192 | tf_op jit(solution)/shard_map/ppermute | solution.py:489
  9.6 3.6 %collective-permute-start.2 = (bf16[72,512]{1,0:T(8,128)(2,1)S(1)}, bf16[72,512]{1,0:T(8,128)(2,1)S(1)}, u32[]{:S(2)}, u32[]{:S(2)}) collective-permute-start(bf16[72,512]{1,0:T(8,128)(2,1)S(1)} %get-tuple-element.51), channel_id=1, source_target_pairs={{0,24},{4,28},{8,16},{12,20},{16,8},{20,12},{24,0},{28,4},{1,25},{... | collective-permute-start | bytes 221192 | tf_op jit(solution)/shard_map/ppermute | solution.py:489
  13.2 1.7 %collective-permute-start.4 = (bf16[72,512]{1,0:T(8,128)(2,1)S(1)}, bf16[72,512]{1,0:T(8,128)(2,1)S(1)}, u32[]{:S(2)}, u32[]{:S(2)}) collective-permute-start(bf16[72,512]{1,0:T(8,128)(2,1)S(1)} %get-tuple-element.53), channel_id=1, source_target_pairs={{0,4},{4,0},{8,12},{12,8},{16,20},{20,16},{24,28},{28,24},{1,5},{5... | collective-permute-start | bytes 221192 | tf_op jit(solution)/shard_map/ppermute | solution.py:489
  14.9 1.6 %copy-done = bf16[512,2048]{1,0:T(8,128)(2,1)S(1)} copy-done((bf16[512,2048]{1,0:T(8,128)(2,1)S(1)}, bf16[512,2048]{1,0:T(8,128)(2,1)}, u32[]{:S(2)}) %copy-start) | copy-done | bytes 2097176
  16.5 0.9 copy-done.4
  17.5 1.0 %copy-done.6 = bf16[512,512]{1,0:T(8,128)(2,1)S(1)} copy-done((bf16[512,512]{1,0:T(8,128)(2,1)S(1)}, bf16[512,512]{1,0:T(8,128)(2,1)}, u32[]{:S(2)}) %copy-start.6) | copy-done | bytes 524312
  18.8 0.8 copy-done.2
  19.6 1.8 %collective-permute-start.6 = (bf16[72,512]{1,0:T(8,128)(2,1)S(1)}, bf16[72,512]{1,0:T(8,128)(2,1)S(1)}, u32[]{:S(2)}, u32[]{:S(2)}) collective-permute-start(bf16[72,512]{1,0:T(8,128)(2,1)S(1)} %get-tuple-element.55), channel_id=1, source_target_pairs={{0,12},{4,8},{8,4},{12,0},{16,28},{20,24},{24,20},{28,16},{1,13},{... | collective-permute-start | bytes 221192 | tf_op jit(solution)/shard_map/ppermute | solution.py:489
  21.5 2.7 %collective-permute-done.5.refs_6_ = bf16[72,512]{1,0:T(8,128)(2,1)S(1)} collective-permute-done((bf16[72,512]{1,0:T(8,128)(2,1)}, bf16[72,512]{1,0:T(8,128)(2,1)S(1)}, u32[]{:S(2)}, u32[]{:S(2)}) %collective-permute-start.5) | collective-permute-done | bytes 73760 | tf_op jit(solution)/shard_map/ppermute | solution.py:489
  24.2 0.8 collective-permute-done.6.refs_7_
  25.0 0.8 place.1
  25.8 1.6 %collective-permute-start.7 = (bf16[256,512]{1,0:T(8,128)(2,1)S(1)}, bf16[256,512]{1,0:T(8,128)(2,1)S(1)}, u32[]{:S(2)}, u32[]{:S(2)}) collective-permute-start(bf16[256,512]{1,0:T(8,128)(2,1)S(1)} %get-tuple-element.56.normed_ref.n0_ref.refs_0_), channel_id=1, source_target_pairs={{0,2},{1,3},{2,0},{3,1},{4,6},{5,7},{6,4},{7,5},{8,10},{9,11},{10,... | collective-permute-start | bytes 786440 | tf_op jit(solution)/shard_map/ppermute | solution.py:474
  27.4 2.2 %own_rows.1 = (bf16[256,512]{1,0:T(8,128)(2,1)S(1)}, f32[256,512]{1,0:T(8,128)S(1)}, bf16[256,512]{1,0:T(8,128)(2,1)S(1)}, f32[256,512]{1,0:T(8,128)S(1)}) custom-call(s32[1]{0:T(128)} %bitcast.me_ref, s32[1,3]{1,0:T(1,128)S(1)} %copy-done.9, bf16[256,512]{1,0:T(8,128)(2,1)S(1)} %get-tuple-element.56.normed_ref.n0_ref.refs_0_, bf16[512,2048]{1,0:T(8,128)(2,1)S(1)} %copy-done.1), custom_call_target="tpu_custom_call" | custom-call | flops 10000000000 | bytes 1048576 | tf_op jit(solution)/shard_map/own_rows/pallas_call | solution.py:22
  29.5 2.7 %collective-permute-done.7.far_ref.n2_ref.refs_2_ = bf16[256,512]{1,0:T(8,128)(2,1)S(1)} collective-permute-done((bf16[256,512]{1,0:T(8,128)(2,1)S(1)}, bf16[256,512]{1,0:T(8,128)(2,1)S(1)}, u32[]{:S(2)}, u32[]{:S(2)}) %collective-permute-start.7) | collective-permute-done | bytes 262176 | tf_op jit(solution)/shard_map/ppermute | solution.py:474
  32.9 0.9 collective-permute-done.8.cross_ref.n3_ref.refs_3_
  33.8 1.9 %forward.1 = (bf16[256,512]{1,0:T(8,128)(2,1)}, bf16[256,512]{1,0:T(8,128)(2,1)S(1)}, bf16[256,512]{1,0:T(8,128)(2,1)S(1)}, bf16[256,128]{1,0:T(8,128)(2,1)S(1)}...) custom-call(s32[1]{0:T(128)} %bitcast.me_ref, s32[1,3]{1,0:T(1,128)S(1)} %copy-done.9, ...), custom_call_target="tpu_custom_call" | custom-call | flops 100000000 | bytes 1048576 | tf_op jit(solution)/shard_map/forward/pallas_call | solution.py:22
  35.7 0.8 side.1
  36.5 1.0 %collective-permute-start.16 = (bf16[512,512]{1,0:T(8,128)(2,1)S(1)}, bf16[512,512]{1,0:T(8,128)(2,1)S(1)}, u32[]{:S(2)}, u32[]{:S(2)}) collective-permute-start(bf16[512,512]{1,0:T(8,128)(2,1)S(1)} %get-tuple-element.81), channel_id=1, source_target_pairs={{0,1},{1,0},{2,3},{3,2},{4,5},{5,4},{6,7},{7,6},{8,9},{9,8},{10,11... | collective-permute-start | bytes 1572872 | tf_op jit(solution)/shard_map/ppermute | solution.py:474
  37.6 2.8 %collective-permute-start.11 = (bf16[256,128]{1,0:T(8,128)(2,1)S(1)}, bf16[256,128]{1,0:T(8,128)(2,1)S(1)}, u32[]{:S(2)}, u32[]{:S(2)}) collective-permute-start(bf16[256,128]{1,0:T(8,128)(2,1)S(1)} %get-tuple-element.68), channel_id=1, source_target_pairs={{0,2},{1,3},{2,0},{3,1},{4,6},{5,7},{6,4},{7,5},{8,10},{9,11},{10,... | collective-permute-start | bytes 196616 | tf_op jit(solution)/shard_map/ppermute | solution.py:474
  40.4 0.8 heads.1
  41.4 1.5 %collective-permute-start.17 = (bf16[512,256]{1,0:T(8,128)(2,1)S(1)}, bf16[512,256]{1,0:T(8,128)(2,1)S(1)}, u32[]{:S(2)}, u32[]{:S(2)}) collective-permute-start(bf16[512,256]{1,0:T(8,128)(2,1)S(1)} %get-tuple-element.83), channel_id=1, source_target_pairs={{0,2},{1,3},{2,0},{3,1},{4,6},{5,7},{6,4},{7,5},{8,10},{9,11},{10,... | collective-permute-start | bytes 786440 | tf_op jit(solution)/shard_map/ppermute | solution.py:474
  42.9 1.9 %collective-permute-done.12.g3_ref = bf16[256,128]{1,0:T(8,128)(2,1)S(1)} collective-permute-done((bf16[256,128]{1,0:T(8,128)(2,1)S(1)}, bf16[256,128]{1,0:T(8,128)(2,1)S(1)}, u32[]{:S(2)}, u32[]{:S(2)}) %collective-permute-start.12) | collective-permute-done | bytes 65568 | tf_op jit(solution)/shard_map/ppermute | solution.py:474
  44.8 3.7 %backward_far.1 = (bf16[256,384]{1,0:T(8,128)(2,1)S(1)}, bf16[256,384]{1,0:T(8,128)(2,1)S(1)}, f32[1024,384]{1,0:T(8,128)S(1)}, bf16[1024,128]{1,0:T(8,128)(2,1)S(1)}) custom-call(s32[1]{0:T(128)} %bitcast.me_ref, s32[1,3]{1,0:T(1,128)S(1)} %copy-done.9, bf16[256,128]{1,0:T(8,128)(2,1)S(1)} %get-tuple-element.66.g0_ref, ...), custom_call_target="tpu_custom_call" | custom-call | flops 10000000000 | bytes 1048576 | tf_op jit(solution)/shard_map/backward_far/pallas_call | solution.py:22
  48.5 1.2 %collective-permute-start.14 = (bf16[256,384]{1,0:T(8,128)(2,1)S(1)}, bf16[256,384]{1,0:T(8,128)(2,1)S(1)}, u32[]{:S(2)}, u32[]{:S(2)}) collective-permute-start(bf16[256,384]{1,0:T(8,128)(2,1)S(1)} %get-tuple-element.74.refs_6_), channel_id=1, source_target_pairs={{0,2},{1,3},{2,0},{3,1},{4,6},{5,7},{6,4},{7,5},{8,10},{9,11},{10,... | collective-permute-start | bytes 589832 | tf_op jit(solution)/shard_map/ppermute | solution.py:474
  50.0 2.6 %backward_rest.1 = (bf16[256,384]{1,0:T(8,128)(2,1)S(1)}, bf16[256,384]{1,0:T(8,128)(2,1)S(1)}) custom-call(s32[1]{0:T(128)} %bitcast.me_ref, s32[1,3]{1,0:T(1,128)S(1)} %copy-done.9, bf16[1024,384]{1,0:T(8,128)(2,1)S(1)} %get-tuple-element.64.part_ref, f32[1024,384]{1,0:T(8,128)S(1)} %get-tuple-element.65.slope_ref, ...), custom_call_target="tpu_custom_call" | custom-call | flops 100000000 | bytes 1048576 | tf_op jit(solution)/shard_map/backward_rest/pallas_call | solution.py:22
  52.6 0.8 collective-permute-start.13
  53.4 0.8 weights.1
  54.2 1.6 %collective-permute-start.18 = (bf16[256,640]{1,0:T(8,128)(2,1)S(1)}, bf16[256,640]{1,0:T(8,128)(2,1)S(1)}, u32[]{:S(2)}, u32[]{:S(2)}) collective-permute-start(bf16[256,640]{1,0:T(8,128)(2,1)S(1)} %get-tuple-element.84), channel_id=1, source_target_pairs={{0,4},{4,0},{8,12},{12,8},{16,20},{20,16},{24,28},{28,24},{1,5},{5... | collective-permute-start | bytes 983048 | tf_op jit(solution)/shard_map/ppermute | solution.py:489
  56.3 2.5 %collective-permute-done.15.cross_ref = bf16[256,384]{1,0:T(8,128)(2,1)S(1)} collective-permute-done((bf16[256,384]{1,0:T(8,128)(2,1)S(1)}, bf16[256,384]{1,0:T(8,128)(2,1)S(1)}, u32[]{:S(2)}, u32[]{:S(2)}) %collective-permute-start.15) | collective-permute-done | bytes 196640 | tf_op jit(solution)/shard_map/ppermute | solution.py:474
  59.3 4.6 %collective-permute-done.18.rest_0_.came_ref = bf16[256,640]{1,0:T(8,128)(2,1)S(1)} collective-permute-done((bf16[256,640]{1,0:T(8,128)(2,1)S(1)}, bf16[256,640]{1,0:T(8,128)(2,1)S(1)}, u32[]{:S(2)}, u32[]{:S(2)}) %collective-permute-start.18) | collective-permute-done | bytes 327712 | tf_op jit(solution)/shard_map/ppermute | solution.py:489
  63.9 1.7 %input_grad.1.refs_0_ = bf16[512,512]{1,0:T(8,128)(2,1)} custom-call(s32[1]{0:T(128)} %bitcast.me_ref, s32[1]{0:T(128)} %bitcast.1.mask_ref.dp_ref, bf16[256,384]{1,0:T(8,128)(2,1)S(1)} %get-tuple-element.72.refs_4_.own_ref, bf16[256,384]{1,0:T(8,128)(2,1)S(1)} %collective-permute-done.13.near_ref, f32[256,512]{1,0:T(8,128)S(1)} %input_far.1.partial_ref, ...), custom_call_target="tpu_custom_call" | custom-call | flops 100000000 | bytes 1048576 | tf_op jit(solution)/shard_map/input_grad/pallas_call | solution.py:22
  65.7 8.7 %all-to-all-start = ((bf16[8,64,512]{2,1,0:T(8,128)(2,1)}), bf16[8,64,512]{2,1,0:T(8,128)(2,1)S(1)}, u32[]{:S(2)}, u32[]{:S(2)}) async-start(bf16[8,64,512]{2,1,0:T(8,128)(2,1)} %bitcast.4), calls=%async_computation | async-start | bytes 1048576 | tf_op jit(solution)/shard_map/all_to_all | solution.py:493
  74.5 2.1 %collective-permute-start.19 = (bf16[128,640]{1,0:T(8,128)(2,1)S(1)}, bf16[128,640]{1,0:T(8,128)(2,1)S(1)}, u32[]{:S(2)}, u32[]{:S(2)}) collective-permute-start(bf16[128,640]{1,0:T(8,128)(2,1)S(1)} %get-tuple-element.87), channel_id=1, source_target_pairs={{0,8},{4,12},{8,0},{12,4},{16,24},{20,28},{24,16},{28,20},{1,9},{5... | collective-permute-start | bytes 491528 | tf_op jit(solution)/shard_map/ppermute | solution.py:489
  76.5 11.4 %collective-permute-done.19.came_ref = bf16[128,640]{1,0:T(8,128)(2,1)S(1)} collective-permute-done((bf16[128,640]{1,0:T(8,128)(2,1)S(1)}, bf16[128,640]{1,0:T(8,128)(2,1)S(1)}, u32[]{:S(2)}, u32[]{:S(2)}) %collective-permute-start.19) | collective-permute-done | bytes 163872 | tf_op jit(solution)/shard_map/ppermute | solution.py:489
  88.0 2.7 %collective-permute-start.20 = (bf16[64,640]{1,0:T(8,128)(2,1)S(1)}, bf16[64,640]{1,0:T(8,128)(2,1)S(1)}, u32[]{:S(2)}, u32[]{:S(2)}) collective-permute-start(bf16[64,640]{1,0:T(8,128)(2,1)S(1)} %get-tuple-element.89), channel_id=1, source_target_pairs={{0,16},{4,20},{8,24},{12,28},{16,0},{20,4},{24,8},{28,12},{1,17},{... | collective-permute-start | bytes 245768 | tf_op jit(solution)/shard_map/ppermute | solution.py:489
  90.6 3.6 %collective-permute-done.20.refs_1_ = bf16[64,640]{1,0:T(8,128)(2,1)S(1)} collective-permute-done((bf16[64,640]{1,0:T(8,128)(2,1)S(1)}, bf16[64,640]{1,0:T(8,128)(2,1)S(1)}, u32[]{:S(2)}, u32[]{:S(2)}) %collective-permute-start.20) | collective-permute-done | bytes 81952 | tf_op jit(solution)/shard_map/ppermute | solution.py:489
  94.3 1.3 %collective-permute-start.22 = (bf16[64,640]{1,0:T(8,128)(2,1)S(1)}, bf16[64,640]{1,0:T(8,128)(2,1)S(1)}, u32[]{:S(2)}, u32[]{:S(2)}) collective-permute-start(bf16[64,640]{1,0:T(8,128)(2,1)S(1)} %sum.1.w0_ref), channel_id=1, source_target_pairs={{0,2},{1,3},{2,0},{3,1},{4,6},{5,7},{6,4},{7,5},{8,10},{9,11},{10,... | collective-permute-start | bytes 245768 | tf_op jit(solution)/shard_map/ppermute | solution.py:474
  95.6 0.6 collective-permute-start.23
  96.2 3.4 %collective-permute-done.22.w2_ref = bf16[64,640]{1,0:T(8,128)(2,1)S(1)} collective-permute-done((bf16[64,640]{1,0:T(8,128)(2,1)S(1)}, bf16[64,640]{1,0:T(8,128)(2,1)S(1)}, u32[]{:S(2)}, u32[]{:S(2)}) %collective-permute-start.22) | collective-permute-done | bytes 81952 | tf_op jit(solution)/shard_map/ppermute | solution.py:474
  99.6 0.8 collective-permute-done.23.w3_ref
  100.5 0.9 finish.1
  101.4 1.2 %give_back.1 = bf16[256,512]{1,0:T(8,128)(2,1)} custom-call(s32[1]{0:T(128)} %bitcast.1.mask_ref.dp_ref, s32[1,256]{1,0:T(1,128)S(1)} %get-tuple-element.63.owner_ref, bf16[512,512]{1,0:T(8,128)(2,1)S(1)} %bitcast.6), custom_call_target="tpu_custom_call" | custom-call | flops 100000000 | bytes 1048576 | tf_op jit(solution)/shard_map/give_back/pallas_call | solution.py:22
  (48 shorter events, 2.7 us)
Async XLA Ops:
  0.6 1.0 copy-start.10
  1.6 0.7 copy-start.11
  2.3 0.7 copy-start.12
  3.7 0.6 copy-start.8
  4.3 15.3 %collective-permute-start = (bf16[72,512]{1,0:T(8,128)(2,1)S(1)}, bf16[72,512]{1,0:T(8,128)(2,1)S(1)}, u32[]{:S(2)}, u32[]{:S(2)}) collective-permute-start(bf16[72,512]{1,0:T(8,128)(2,1)S(1)} %get-tuple-element.49), channel_id=1, source_target_pairs={{0,16},{4,20},{8,24},{12,28},{16,0},{20,4},{24,8},{28,12},{1,17},{... | collective-permute-start | bytes 221192 | tf_op jit(solution)/shard_map/ppermute | solution.py:489
  8.3 11.3 %collective-permute-start.1 = (bf16[72,512]{1,0:T(8,128)(2,1)S(1)}, bf16[72,512]{1,0:T(8,128)(2,1)S(1)}, u32[]{:S(2)}, u32[]{:S(2)}) collective-permute-start(bf16[72,512]{1,0:T(8,128)(2,1)S(1)} %get-tuple-element.50), channel_id=1, source_target_pairs={{0,20},{4,16},{8,28},{12,24},{16,4},{20,0},{24,12},{28,8},{1,21},{... | collective-permute-start | bytes 221192 | tf_op jit(solution)/shard_map/ppermute | solution.py:489
  9.6 11.8 %collective-permute-start.2 = (bf16[72,512]{1,0:T(8,128)(2,1)S(1)}, bf16[72,512]{1,0:T(8,128)(2,1)S(1)}, u32[]{:S(2)}, u32[]{:S(2)}) collective-permute-start(bf16[72,512]{1,0:T(8,128)(2,1)S(1)} %get-tuple-element.51), channel_id=1, source_target_pairs={{0,24},{4,28},{8,16},{12,20},{16,8},{20,12},{24,0},{28,4},{1,25},{... | collective-permute-start | bytes 221192 | tf_op jit(solution)/shard_map/ppermute | solution.py:489
  13.2 8.2 %collective-permute-start.3 = (bf16[72,512]{1,0:T(8,128)(2,1)S(1)}, bf16[72,512]{1,0:T(8,128)(2,1)S(1)}, u32[]{:S(2)}, u32[]{:S(2)}) collective-permute-start(bf16[72,512]{1,0:T(8,128)(2,1)S(1)} %get-tuple-element.52), channel_id=1, source_target_pairs={{0,28},{4,24},{8,20},{12,16},{16,12},{20,8},{24,4},{28,0},{1,29},{... | collective-permute-start | bytes 221192 | tf_op jit(solution)/shard_map/ppermute | solution.py:489
  13.2 8.2 %collective-permute-start.4 = (bf16[72,512]{1,0:T(8,128)(2,1)S(1)}, bf16[72,512]{1,0:T(8,128)(2,1)S(1)}, u32[]{:S(2)}, u32[]{:S(2)}) collective-permute-start(bf16[72,512]{1,0:T(8,128)(2,1)S(1)} %get-tuple-element.53), channel_id=1, source_target_pairs={{0,4},{4,0},{8,12},{12,8},{16,20},{20,16},{24,28},{28,24},{1,5},{5... | collective-permute-start | bytes 221192 | tf_op jit(solution)/shard_map/ppermute | solution.py:489
  14.9 1.6 %copy-start = (bf16[512,2048]{1,0:T(8,128)(2,1)S(1)}, bf16[512,2048]{1,0:T(8,128)(2,1)}, u32[]{:S(2)}) copy-start(bf16[512,2048]{1,0:T(8,128)(2,1)} %proj_ref.15) | copy-start | bytes 6291460
  16.5 0.9 copy-start.4
  17.4 1.0 %copy-start.6 = (bf16[512,512]{1,0:T(8,128)(2,1)S(1)}, bf16[512,512]{1,0:T(8,128)(2,1)}, u32[]{:S(2)}) copy-start(bf16[512,512]{1,0:T(8,128)(2,1)} %outw_ref.3) | copy-start | bytes 1572868
  18.5 8.9 %copy-start.1 = (bf16[512,2048]{1,0:T(8,128)(2,1)S(1)}, bf16[512,2048]{1,0:T(8,128)(2,1)}, u32[]{:S(2)}) copy-start(bf16[512,2048]{1,0:T(8,128)(2,1)} %proj_ref.15) | copy-start | bytes 6291460
  18.5 8.9 %copy-start.9 = (s32[1,3]{1,0:T(1,128)S(1)}, s32[1,3]{1,0:T(1,128)}, u32[]{:S(2)}) copy-start(s32[1,3]{1,0:T(1,128)} %lengths_ref.9) | copy-start | bytes 40
  18.8 0.8 copy-start.2
  19.6 4.6 %collective-permute-start.5 = (bf16[72,512]{1,0:T(8,128)(2,1)}, bf16[72,512]{1,0:T(8,128)(2,1)S(1)}, u32[]{:S(2)}, u32[]{:S(2)}) collective-permute-start(bf16[72,512]{1,0:T(8,128)(2,1)} %relay.1), channel_id=1, source_target_pairs={{0,8},{4,12},{8,0},{12,4},{16,24},{20,28},{24,16},{28,20},{1,9},{5... | collective-permute-start | bytes 221192 | tf_op jit(solution)/shard_map/ppermute | solution.py:489
  19.6 5.3 %collective-permute-start.6 = (bf16[72,512]{1,0:T(8,128)(2,1)S(1)}, bf16[72,512]{1,0:T(8,128)(2,1)S(1)}, u32[]{:S(2)}, u32[]{:S(2)}) collective-permute-start(bf16[72,512]{1,0:T(8,128)(2,1)S(1)} %get-tuple-element.55), channel_id=1, source_target_pairs={{0,12},{4,8},{8,4},{12,0},{16,28},{20,24},{24,20},{28,16},{1,13},{... | collective-permute-start | bytes 221192 | tf_op jit(solution)/shard_map/ppermute | solution.py:489
  25.8 6.4 %collective-permute-start.7 = (bf16[256,512]{1,0:T(8,128)(2,1)S(1)}, bf16[256,512]{1,0:T(8,128)(2,1)S(1)}, u32[]{:S(2)}, u32[]{:S(2)}) collective-permute-start(bf16[256,512]{1,0:T(8,128)(2,1)S(1)} %get-tuple-element.56.normed_ref.n0_ref.refs_0_), channel_id=1, source_target_pairs={{0,2},{1,3},{2,0},{3,1},{4,6},{5,7},{6,4},{7,5},{8,10},{9,11},{10,... | collective-permute-start | bytes 786440 | tf_op jit(solution)/shard_map/ppermute | solution.py:474
  27.4 4.9 %collective-permute-start.9 = (bf16[256,512]{1,0:T(8,128)(2,1)S(1)}, bf16[256,512]{1,0:T(8,128)(2,1)S(1)}, u32[]{:S(2)}, u32[]{:S(2)}) collective-permute-start(bf16[256,512]{1,0:T(8,128)(2,1)S(1)} %get-tuple-element.56.normed_ref.n0_ref.refs_0_), channel_id=1, source_target_pairs={{0,1},{1,0},{2,3},{3,2},{4,5},{5,4},{6,7},{7,6},{8,9},{9,8},{10,11... | collective-permute-start | bytes 786440 | tf_op jit(solution)/shard_map/ppermute | solution.py:474
  32.2 1.5 %collective-permute-start.8 = (bf16[256,512]{1,0:T(8,128)(2,1)S(1)}, bf16[256,512]{1,0:T(8,128)(2,1)S(1)}, u32[]{:S(2)}, u32[]{:S(2)}) collective-permute-start(bf16[256,512]{1,0:T(8,128)(2,1)S(1)} %collective-permute-done.7.far_ref.n2_ref.refs_2_), channel_id=1, source_target_pairs={{0,1},{1,0},{2,3},{3,2},{4,5},{5,4},{6,7},{7,6},{8,9},{9,8},{10,11... | collective-permute-start | bytes 786440 | tf_op jit(solution)/shard_map/ppermute | solution.py:474
  32.2 1.5 %copy-start.3 = (f32[256,512]{1,0:T(8,128)S(1)}, f32[256,512]{1,0:T(8,128)}, u32[]{:S(2)}) copy-start(f32[256,512]{1,0:T(8,128)} %copy-done.2) | copy-start | bytes 1572868
  32.3 1.5 %copy-start.7 = (bf16[512,512]{1,0:T(8,128)(2,1)S(1)}, bf16[512,512]{1,0:T(8,128)(2,1)}, u32[]{:S(2)}) copy-start(bf16[512,512]{1,0:T(8,128)(2,1)} %outw_ref.3) | copy-start | bytes 1572868
  33.8 1.9 %copy-start.5 = (bf16[256,512]{1,0:T(8,128)(2,1)S(1)}, bf16[256,512]{1,0:T(8,128)(2,1)}, u32[]{:S(2)}) copy-start(bf16[256,512]{1,0:T(8,128)(2,1)} %cot_ref.5) | copy-start | bytes 786436
  36.5 4.8 %collective-permute-start.16 = (bf16[512,512]{1,0:T(8,128)(2,1)S(1)}, bf16[512,512]{1,0:T(8,128)(2,1)S(1)}, u32[]{:S(2)}, u32[]{:S(2)}) collective-permute-start(bf16[512,512]{1,0:T(8,128)(2,1)S(1)} %get-tuple-element.81), channel_id=1, source_target_pairs={{0,1},{1,0},{2,3},{3,2},{4,5},{5,4},{6,7},{7,6},{8,9},{9,8},{10,11... | collective-permute-start | bytes 1572872 | tf_op jit(solution)/shard_map/ppermute | solution.py:474
  37.5 5.3 %collective-permute-start.10 = (bf16[256,128]{1,0:T(8,128)(2,1)S(1)}, bf16[256,128]{1,0:T(8,128)(2,1)S(1)}, u32[]{:S(2)}, u32[]{:S(2)}) collective-permute-start(bf16[256,128]{1,0:T(8,128)(2,1)S(1)} %get-tuple-element.67), channel_id=1, source_target_pairs={{0,1},{1,0},{2,3},{3,2},{4,5},{5,4},{6,7},{7,6},{8,9},{9,8},{10,11... | collective-permute-start | bytes 196616 | tf_op jit(solution)/shard_map/ppermute | solution.py:474
  37.6 5.3 %collective-permute-start.11 = (bf16[256,128]{1,0:T(8,128)(2,1)S(1)}, bf16[256,128]{1,0:T(8,128)(2,1)S(1)}, u32[]{:S(2)}, u32[]{:S(2)}) collective-permute-start(bf16[256,128]{1,0:T(8,128)(2,1)S(1)} %get-tuple-element.68), channel_id=1, source_target_pairs={{0,2},{1,3},{2,0},{3,1},{4,6},{5,7},{6,4},{7,5},{8,10},{9,11},{10,... | collective-permute-start | bytes 196616 | tf_op jit(solution)/shard_map/ppermute | solution.py:474
  40.4 4.4 %collective-permute-start.12 = (bf16[256,128]{1,0:T(8,128)(2,1)S(1)}, bf16[256,128]{1,0:T(8,128)(2,1)S(1)}, u32[]{:S(2)}, u32[]{:S(2)}) collective-permute-start(bf16[256,128]{1,0:T(8,128)(2,1)S(1)} %get-tuple-element.69), channel_id=1, source_target_pairs={{0,3},{1,2},{2,1},{3,0},{4,7},{5,6},{6,5},{7,4},{8,11},{9,10},{10,... | collective-permute-start | bytes 196616 | tf_op jit(solution)/shard_map/ppermute | solution.py:474
  41.4 12.0 %collective-permute-start.17 = (bf16[512,256]{1,0:T(8,128)(2,1)S(1)}, bf16[512,256]{1,0:T(8,128)(2,1)S(1)}, u32[]{:S(2)}, u32[]{:S(2)}) collective-permute-start(bf16[512,256]{1,0:T(8,128)(2,1)S(1)} %get-tuple-element.83), channel_id=1, source_target_pairs={{0,2},{1,3},{2,0},{3,1},{4,6},{5,7},{6,4},{7,5},{8,10},{9,11},{10,... | collective-permute-start | bytes 786440 | tf_op jit(solution)/shard_map/ppermute | solution.py:474
  48.5 7.8 %collective-permute-start.14 = (bf16[256,384]{1,0:T(8,128)(2,1)S(1)}, bf16[256,384]{1,0:T(8,128)(2,1)S(1)}, u32[]{:S(2)}, u32[]{:S(2)}) collective-permute-start(bf16[256,384]{1,0:T(8,128)(2,1)S(1)} %get-tuple-element.74.refs_6_), channel_id=1, source_target_pairs={{0,2},{1,3},{2,0},{3,1},{4,6},{5,7},{6,4},{7,5},{8,10},{9,11},{10,... | collective-permute-start | bytes 589832 | tf_op jit(solution)/shard_map/ppermute | solution.py:474
  49.7 9.1 %collective-permute-start.15 = (bf16[256,384]{1,0:T(8,128)(2,1)S(1)}, bf16[256,384]{1,0:T(8,128)(2,1)S(1)}, u32[]{:S(2)}, u32[]{:S(2)}) collective-permute-start(bf16[256,384]{1,0:T(8,128)(2,1)S(1)} %get-tuple-element.75.refs_7_), channel_id=1, source_target_pairs={{0,3},{1,2},{2,1},{3,0},{4,7},{5,6},{6,5},{7,4},{8,11},{9,10},{10,... | collective-permute-start | bytes 589832 | tf_op jit(solution)/shard_map/ppermute | solution.py:474
  52.6 6.7 %collective-permute-start.13 = (bf16[256,384]{1,0:T(8,128)(2,1)S(1)}, bf16[256,384]{1,0:T(8,128)(2,1)S(1)}, u32[]{:S(2)}, u32[]{:S(2)}) collective-permute-start(bf16[256,384]{1,0:T(8,128)(2,1)S(1)} %get-tuple-element.73.refs_5_), channel_id=1, source_target_pairs={{0,1},{1,0},{2,3},{3,2},{4,5},{5,4},{6,7},{7,6},{8,9},{9,8},{10,11... | collective-permute-start | bytes 589832 | tf_op jit(solution)/shard_map/ppermute | solution.py:474
  54.2 9.7 %collective-permute-start.18 = (bf16[256,640]{1,0:T(8,128)(2,1)S(1)}, bf16[256,640]{1,0:T(8,128)(2,1)S(1)}, u32[]{:S(2)}, u32[]{:S(2)}) collective-permute-start(bf16[256,640]{1,0:T(8,128)(2,1)S(1)} %get-tuple-element.84), channel_id=1, source_target_pairs={{0,4},{4,0},{8,12},{12,8},{16,20},{20,16},{24,28},{28,24},{1,5},{5... | collective-permute-start | bytes 983048 | tf_op jit(solution)/shard_map/ppermute | solution.py:489
  65.7 35.7 %all-to-all-start = ((bf16[8,64,512]{2,1,0:T(8,128)(2,1)}), bf16[8,64,512]{2,1,0:T(8,128)(2,1)S(1)}, u32[]{:S(2)}, u32[]{:S(2)}) async-start(bf16[8,64,512]{2,1,0:T(8,128)(2,1)} %bitcast.4), calls=%async_computation | async-start | bytes 1048576 | tf_op jit(solution)/shard_map/all_to_all | solution.py:493
  74.5 13.5 %collective-permute-start.19 = (bf16[128,640]{1,0:T(8,128)(2,1)S(1)}, bf16[128,640]{1,0:T(8,128)(2,1)S(1)}, u32[]{:S(2)}, u32[]{:S(2)}) collective-permute-start(bf16[128,640]{1,0:T(8,128)(2,1)S(1)} %get-tuple-element.87), channel_id=1, source_target_pairs={{0,8},{4,12},{8,0},{12,4},{16,24},{20,28},{24,16},{28,20},{1,9},{5... | collective-permute-start | bytes 491528 | tf_op jit(solution)/shard_map/ppermute | solution.py:489
  88.0 6.2 %collective-permute-start.20 = (bf16[64,640]{1,0:T(8,128)(2,1)S(1)}, bf16[64,640]{1,0:T(8,128)(2,1)S(1)}, u32[]{:S(2)}, u32[]{:S(2)}) collective-permute-start(bf16[64,640]{1,0:T(8,128)(2,1)S(1)} %get-tuple-element.89), channel_id=1, source_target_pairs={{0,16},{4,20},{8,24},{12,28},{16,0},{20,4},{24,8},{28,12},{1,17},{... | collective-permute-start | bytes 245768 | tf_op jit(solution)/shard_map/ppermute | solution.py:489
  94.2 1.9 %collective-permute-start.21 = (bf16[64,640]{1,0:T(8,128)(2,1)S(1)}, bf16[64,640]{1,0:T(8,128)(2,1)S(1)}, u32[]{:S(2)}, u32[]{:S(2)}) collective-permute-start(bf16[64,640]{1,0:T(8,128)(2,1)S(1)} %sum.1.w0_ref), channel_id=1, source_target_pairs={{0,1},{1,0},{2,3},{3,2},{4,5},{5,4},{6,7},{7,6},{8,9},{9,8},{10,11... | collective-permute-start | bytes 245768 | tf_op jit(solution)/shard_map/ppermute | solution.py:474
  94.3 5.3 %collective-permute-start.22 = (bf16[64,640]{1,0:T(8,128)(2,1)S(1)}, bf16[64,640]{1,0:T(8,128)(2,1)S(1)}, u32[]{:S(2)}, u32[]{:S(2)}) collective-permute-start(bf16[64,640]{1,0:T(8,128)(2,1)S(1)} %sum.1.w0_ref), channel_id=1, source_target_pairs={{0,2},{1,3},{2,0},{3,1},{4,6},{5,7},{6,4},{7,5},{8,10},{9,11},{10,... | collective-permute-start | bytes 245768 | tf_op jit(solution)/shard_map/ppermute | solution.py:474
  95.6 4.9 %collective-permute-start.23 = (bf16[64,640]{1,0:T(8,128)(2,1)S(1)}, bf16[64,640]{1,0:T(8,128)(2,1)S(1)}, u32[]{:S(2)}, u32[]{:S(2)}) collective-permute-start(bf16[64,640]{1,0:T(8,128)(2,1)S(1)} %sum.1.w0_ref), channel_id=1, source_target_pairs={{0,3},{1,2},{2,1},{3,0},{4,7},{5,6},{6,5},{7,4},{8,11},{9,10},{10,... | collective-permute-start | bytes 245768 | tf_op jit(solution)/shard_map/ppermute | solution.py:474

commit v10 on v9

--- a/solution.py
+++ b/solution.py
@@ -15,7 +15,7 @@
 
 WHOLE = pl.BlockSpec(memory_space=pltpu.VMEM)
 SCALARS = pl.BlockSpec(memory_space=pltpu.SMEM)
-ANYWHERE = pl.BlockSpec(memory_space=pltpu.HBM)
+ANYWHERE = pl.BlockSpec(memory_space=pl.ANY)
 
 
 def call(body, name, outs, scalars, arrays, scratch=(), flops=10**8, vmem=8, far=()):
@@ -391,13 +391,8 @@
             ref[at, :] = total_ref[source, :].astype(BF16)
 
 
-def halve_body(pairs, kept_ref, came_ref, *refs):
-    keep_ref, send_ref = refs[-2:]
-    share = kept_ref.shape[0] // pairs
-    total = kept_ref[...].astype(F32) + came_ref[...].astype(F32)
-    for j in range(pairs):
-        at = slice(j // 2 * share, (j // 2 + 1) * share)
-        (send_ref if j % 2 else keep_ref)[at, :] = total[j * share : (j + 1) * share].astype(BF16)
+def pair_body(kept_ref, came_ref, _, *outs):
+    store_blocks(outs, kept_ref[...].astype(F32) + came_ref[...].astype(F32))
 
 
 def head_columns(owner, proj_ref):
@@ -580,26 +575,21 @@
     (partial_in,) = call(
         input_far_body, "input_far", [wide], [me], [p2, p3, gate_in, proj_weight], flops=6 * 10**9,
     )
-    came = dp_hop(weight_parts[1], 1) if by_hops else weight_parts[0]
     (back,) = call(
         functools.partial(input_body, blocks), "input_grad", [((owners * capacity, width), BF16)], [me, mask],
         [own_block, p1, partial_in, owned, cotangent, landing, proj_weight], vmem=16,
-        far=[came],
-    )
-    returned = swap_whole(back)
+    )
     if by_hops:
         kept, sent = weight_parts
-        bit, behind = 2, [back]
-        while bit < owners:
-            kept, sent = call(
-                functools.partial(halve_body, pairs), "halve",
-                [((pairs * share // 2, columns), BF16)] * 2, [], [kept, came], far=behind,
-            )
-            came, bit, pairs, behind = dp_hop(sent, bit), 2 * bit, pairs // 2, []
-        summed_parts = [kept, came]
+        halves = call(
+            pair_body, "pair_sum", [((share, columns), BF16)] * pairs, [], [kept, dp_hop(sent, 1)],
+            far=[partial_in],
+        )
+        summed_parts = [halves[0]] + [dp_hop(halves[j], 2 * j) for j in range(1, pairs)]
     else:
         summed_parts = [swap_whole(weight_parts[0]).reshape(owners, share, columns)]
     (mine,) = call(sum_body, "sum", [((share, columns), BF16)], [], summed_parts)
+    returned = swap_whole(relay(back, [mine]))
     w1, w2, w3 = (hop(mine, step) for step in range(1, cycle))
     (grad_tokens,) = call(
         functools.partial(return_body, capacity), "give_back", [square], [mask], [owner_here, returned]

time: 103 us -> 98.4 us (0.955)
  waiting for transfers between devices: 35.9 us -> 30.6 us
  local copies, waits for them, and re-layouts: 7.32 us -> 9.63 us
    ppermute x10 -> x11, waiting for transfers between devices: 23.1 us -> 11 us  [dp_hop(): return lax.ppermute(value, 'dp', [(i, i ^ step) for i in range(owners)])]
    all_to_all x1, waiting for transfers between devices: 0.01 us -> 6.1 us  [swap_whole(): lax.all_to_all(split, 'dp', split_axis=0, concat_axis=0, tiled=True)]
    all_to_all x1, starting transfers between devices: 8.69 us -> 3.98 us  [swap_whole(): lax.all_to_all(split, 'dp', split_axis=0, concat_axis=0, tiled=True)]
    ppermute x10 -> x11, starting transfers between devices: 18.8 us -> 23.3 us  [dp_hop(): return lax.ppermute(value, 'dp', [(i, i ^ step) for i in range(owners)])]
    unnamed x26 -> x32, local copies, waits for them, and re-layouts: 7.32 us -> 9.63 us
    pallas_call x19 -> x18, Pallas kernels: 19.9 us -> 19 us  [call(): pl.pallas_call(body, name=name, out_shape=[jax.ShapeDtypeStruct(s, d) for...]
  transfers between devices with their start and end apart: 25 -> 26, of which waited for: 12 -> 12; matrix products, arithmetic and copies ran while one was open for 0% -> 0% of each run, Pallas kernels for 12% -> 14%
where the time goes in v10:
time: 98.4 us; the launch traced here: 98.9 us
  starting transfers between devices  38.8 us (39%)
  waiting for transfers between devices  30.6 us (31%)
  Pallas kernels  19 us (19%)
  local copies, waits for them, and re-layouts  9.63 us (10%)
    ppermute x11, starting transfers between devices, dp_hop(): return lax.ppermute(value, 'dp', [(i, i ^ step) for i in range(owners)])  23.3 us
    pallas_call x18, Pallas kernels, call(): pl.pallas_call(body, name=name, out_shape=[jax.ShapeDtypeStruct(s, d) for...  19 us
    ppermute x14, waiting for transfers between devices, hop(): return lax.ppermute(value, 'ctx', [(i, i ^ step) for i in range(cycle)])  13.5 us
    ppermute x14, starting transfers between devices, hop(): return lax.ppermute(value, 'ctx', [(i, i ^ step) for i in range(cycle)])  11.5 us
    ppermute x11, waiting for transfers between devices, dp_hop(): return lax.ppermute(value, 'dp', [(i, i ^ step) for i in range(owners)])  11 us
    unnamed x32, local copies, waits for them, and re-layouts  9.63 us
    all_to_all x1, waiting for transfers between devices, swap_whole(): lax.all_to_all(split, 'dp', split_axis=0, concat_axis=0, tiled=True)  6.1 us
    all_to_all x1, starting transfers between devices, swap_whole(): lax.all_to_all(split, 'dp', split_axis=0, concat_axis=0, tiled=True)  3.98 us
  transfers between devices with their start and end apart: 26, of which 12 were waited for; matrix products, arithmetic and copies ran while one was open for 0% of the time, Pallas kernels for 14%

profile of v10, /device:TPU:0, one launch (start us, length us, event | category | flops | bytes accessed | tf_op | source)
XLA Modules:
  0.0 98.9 jit_solution(3767964733030757468)
XLA Ops:
  0.6 0.9 copy-done.13
  1.6 0.7 copy-done.14
  2.3 0.7 copy-done.15
  2.9 0.7 pack.1
  4.3 4.0 %collective-permute-start = (bf16[72,512]{1,0:T(8,128)(2,1)S(1)}, bf16[72,512]{1,0:T(8,128)(2,1)S(1)}, u32[]{:S(2)}, u32[]{:S(2)}) collective-permute-start(bf16[72,512]{1,0:T(8,128)(2,1)S(1)} %get-tuple-element.49), channel_id=1, source_target_pairs={{0,16},{4,20},{8,24},{12,28},{16,0},{20,4},{24,8},{28,12},{1,17},{... | collective-permute-start | bytes 221192 | tf_op jit(solution)/shard_map/ppermute | solution.py:484
  8.3 1.3 %collective-permute-start.1 = (bf16[72,512]{1,0:T(8,128)(2,1)S(1)}, bf16[72,512]{1,0:T(8,128)(2,1)S(1)}, u32[]{:S(2)}, u32[]{:S(2)}) collective-permute-start(bf16[72,512]{1,0:T(8,128)(2,1)S(1)} %get-tuple-element.50), channel_id=1, source_target_pairs={{0,20},{4,16},{8,28},{12,24},{16,4},{20,0},{24,12},{28,8},{1,21},{... | collective-permute-start | bytes 221192 | tf_op jit(solution)/shard_map/ppermute | solution.py:484
  9.6 3.6 %collective-permute-start.2 = (bf16[72,512]{1,0:T(8,128)(2,1)S(1)}, bf16[72,512]{1,0:T(8,128)(2,1)S(1)}, u32[]{:S(2)}, u32[]{:S(2)}) collective-permute-start(bf16[72,512]{1,0:T(8,128)(2,1)S(1)} %get-tuple-element.51), channel_id=1, source_target_pairs={{0,24},{4,28},{8,16},{12,20},{16,8},{20,12},{24,0},{28,4},{1,25},{... | collective-permute-start | bytes 221192 | tf_op jit(solution)/shard_map/ppermute | solution.py:484
  13.2 1.7 %collective-permute-start.4 = (bf16[72,512]{1,0:T(8,128)(2,1)S(1)}, bf16[72,512]{1,0:T(8,128)(2,1)S(1)}, u32[]{:S(2)}, u32[]{:S(2)}) collective-permute-start(bf16[72,512]{1,0:T(8,128)(2,1)S(1)} %get-tuple-element.53), channel_id=1, source_target_pairs={{0,4},{4,0},{8,12},{12,8},{16,20},{20,16},{24,28},{28,24},{1,5},{5... | collective-permute-start | bytes 221192 | tf_op jit(solution)/shard_map/ppermute | solution.py:484
  14.9 1.6 %copy-done = bf16[512,2048]{1,0:T(8,128)(2,1)S(1)} copy-done((bf16[512,2048]{1,0:T(8,128)(2,1)S(1)}, bf16[512,2048]{1,0:T(8,128)(2,1)}, u32[]{:S(2)}) %copy-start) | copy-done | bytes 2097176
  16.5 0.9 copy-done.5
  17.5 1.0 %copy-done.7 = bf16[512,512]{1,0:T(8,128)(2,1)S(1)} copy-done((bf16[512,512]{1,0:T(8,128)(2,1)S(1)}, bf16[512,512]{1,0:T(8,128)(2,1)}, u32[]{:S(2)}) %copy-start.7) | copy-done | bytes 524312
  18.8 0.8 copy-done.3
  19.6 1.8 %collective-permute-start.6 = (bf16[72,512]{1,0:T(8,128)(2,1)S(1)}, bf16[72,512]{1,0:T(8,128)(2,1)S(1)}, u32[]{:S(2)}, u32[]{:S(2)}) collective-permute-start(bf16[72,512]{1,0:T(8,128)(2,1)S(1)} %get-tuple-element.55), channel_id=1, source_target_pairs={{0,12},{4,8},{8,4},{12,0},{16,28},{20,24},{24,20},{28,16},{1,13},{... | collective-permute-start | bytes 221192 | tf_op jit(solution)/shard_map/ppermute | solution.py:484
  21.5 2.7 %collective-permute-done.5.refs_6_ = bf16[72,512]{1,0:T(8,128)(2,1)S(1)} collective-permute-done((bf16[72,512]{1,0:T(8,128)(2,1)}, bf16[72,512]{1,0:T(8,128)(2,1)S(1)}, u32[]{:S(2)}, u32[]{:S(2)}) %collective-permute-start.5) | collective-permute-done | bytes 73760 | tf_op jit(solution)/shard_map/ppermute | solution.py:484
  24.2 0.8 collective-permute-done.6.refs_7_
  25.0 0.8 place.1
  25.8 1.6 %collective-permute-start.7 = (bf16[256,512]{1,0:T(8,128)(2,1)S(1)}, bf16[256,512]{1,0:T(8,128)(2,1)S(1)}, u32[]{:S(2)}, u32[]{:S(2)}) collective-permute-start(bf16[256,512]{1,0:T(8,128)(2,1)S(1)} %get-tuple-element.56.normed_ref.n0_ref.refs_0_), channel_id=1, source_target_pairs={{0,2},{1,3},{2,0},{3,1},{4,6},{5,7},{6,4},{7,5},{8,10},{9,11},{10,... | collective-permute-start | bytes 786440 | tf_op jit(solution)/shard_map/ppermute | solution.py:469
  27.4 2.2 %own_rows.1 = (bf16[256,512]{1,0:T(8,128)(2,1)S(1)}, f32[256,512]{1,0:T(8,128)S(1)}, bf16[256,512]{1,0:T(8,128)(2,1)S(1)}, f32[256,512]{1,0:T(8,128)S(1)}) custom-call(s32[1]{0:T(128)} %bitcast.me_ref, s32[1,3]{1,0:T(1,128)S(1)} %copy-done.12, bf16[256,512]{1,0:T(8,128)(2,1)S(1)} %get-tuple-element.56.normed_ref.n0_ref.refs_0_, bf16[512,2048]{1,0:T(8,128)(2,1)S(1)} %copy-done.1), custom_call_target="tpu_custom_call" | custom-call | flops 10000000000 | bytes 1048576 | tf_op jit(solution)/shard_map/own_rows/pallas_call | solution.py:22
  29.5 2.7 %collective-permute-done.7.far_ref.n2_ref.refs_2_ = bf16[256,512]{1,0:T(8,128)(2,1)S(1)} collective-permute-done((bf16[256,512]{1,0:T(8,128)(2,1)S(1)}, bf16[256,512]{1,0:T(8,128)(2,1)S(1)}, u32[]{:S(2)}, u32[]{:S(2)}) %collective-permute-start.7) | collective-permute-done | bytes 262176 | tf_op jit(solution)/shard_map/ppermute | solution.py:469
  32.9 0.9 collective-permute-done.8.cross_ref.n3_ref.refs_3_
  33.8 1.9 %forward.1 = (bf16[256,512]{1,0:T(8,128)(2,1)}, bf16[256,512]{1,0:T(8,128)(2,1)S(1)}, bf16[256,512]{1,0:T(8,128)(2,1)S(1)}, bf16[256,128]{1,0:T(8,128)(2,1)S(1)}...) custom-call(s32[1]{0:T(128)} %bitcast.me_ref, s32[1,3]{1,0:T(1,128)S(1)} %copy-done.12, ...), custom_call_target="tpu_custom_call" | custom-call | flops 100000000 | bytes 1048576 | tf_op jit(solution)/shard_map/forward/pallas_call | solution.py:22
  35.7 0.8 side.1
  37.1 3.4 %collective-permute-start.11 = (bf16[256,128]{1,0:T(8,128)(2,1)S(1)}, bf16[256,128]{1,0:T(8,128)(2,1)S(1)}, u32[]{:S(2)}, u32[]{:S(2)}) collective-permute-start(bf16[256,128]{1,0:T(8,128)(2,1)S(1)} %get-tuple-element.68), channel_id=1, source_target_pairs={{0,2},{1,3},{2,0},{3,1},{4,6},{5,7},{6,4},{7,5},{8,10},{9,11},{10,... | collective-permute-start | bytes 196616 | tf_op jit(solution)/shard_map/ppermute | solution.py:469
  40.5 0.8 heads.1
  41.5 1.8 %collective-permute-start.17 = (bf16[512,256]{1,0:T(8,128)(2,1)S(1)}, bf16[512,256]{1,0:T(8,128)(2,1)S(1)}, u32[]{:S(2)}, u32[]{:S(2)}) collective-permute-start(bf16[512,256]{1,0:T(8,128)(2,1)S(1)} %get-tuple-element.83), channel_id=1, source_target_pairs={{0,2},{1,3},{2,0},{3,1},{4,6},{5,7},{6,4},{7,5},{8,10},{9,11},{10,... | collective-permute-start | bytes 786440 | tf_op jit(solution)/shard_map/ppermute | solution.py:469
  43.3 1.3 %collective-permute-done.12.g3_ref = bf16[256,128]{1,0:T(8,128)(2,1)S(1)} collective-permute-done((bf16[256,128]{1,0:T(8,128)(2,1)S(1)}, bf16[256,128]{1,0:T(8,128)(2,1)S(1)}, u32[]{:S(2)}, u32[]{:S(2)}) %collective-permute-start.12) | collective-permute-done | bytes 65568 | tf_op jit(solution)/shard_map/ppermute | solution.py:469
  44.6 4.4 %backward_far.1 = (bf16[256,384]{1,0:T(8,128)(2,1)S(1)}, bf16[256,384]{1,0:T(8,128)(2,1)S(1)}, f32[1024,384]{1,0:T(8,128)S(1)}, bf16[1024,128]{1,0:T(8,128)(2,1)S(1)}) custom-call(s32[1]{0:T(128)} %bitcast.me_ref, s32[1,3]{1,0:T(1,128)S(1)} %copy-done.12, bf16[256,128]{1,0:T(8,128)(2,1)S(1)} %get-tuple-element.66.g0_ref, ...), custom_call_target="tpu_custom_call" | custom-call | flops 10000000000 | bytes 1048576 | tf_op jit(solution)/shard_map/backward_far/pallas_call | solution.py:22
  49.6 1.1 %collective-permute-start.15 = (bf16[256,384]{1,0:T(8,128)(2,1)S(1)}, bf16[256,384]{1,0:T(8,128)(2,1)S(1)}, u32[]{:S(2)}, u32[]{:S(2)}) collective-permute-start(bf16[256,384]{1,0:T(8,128)(2,1)S(1)} %get-tuple-element.75.refs_7_), channel_id=1, source_target_pairs={{0,3},{1,2},{2,1},{3,0},{4,7},{5,6},{6,5},{7,4},{8,11},{9,10},{10,... | collective-permute-start | bytes 589832 | tf_op jit(solution)/shard_map/ppermute | solution.py:469
  50.8 1.9 %backward_rest.1 = (bf16[256,384]{1,0:T(8,128)(2,1)S(1)}, bf16[256,384]{1,0:T(8,128)(2,1)S(1)}) custom-call(s32[1]{0:T(128)} %bitcast.me_ref, s32[1,3]{1,0:T(1,128)S(1)} %copy-done.12, bf16[1024,384]{1,0:T(8,128)(2,1)S(1)} %get-tuple-element.64.part_ref, f32[1024,384]{1,0:T(8,128)S(1)} %get-tuple-element.65.slope_ref, ...), custom_call_target="tpu_custom_call" | custom-call | flops 100000000 | bytes 1048576 | tf_op jit(solution)/shard_map/backward_rest/pallas_call | solution.py:22
  53.2 0.8 weights.1
  54.0 1.8 %collective-permute-start.18 = (bf16[256,640]{1,0:T(8,128)(2,1)S(1)}, bf16[256,640]{1,0:T(8,128)(2,1)S(1)}, u32[]{:S(2)}, u32[]{:S(2)}) collective-permute-start(bf16[256,640]{1,0:T(8,128)(2,1)S(1)} %get-tuple-element.85), channel_id=1, source_target_pairs={{0,4},{4,0},{8,12},{12,8},{16,20},{20,16},{24,28},{28,24},{1,5},{5... | collective-permute-start | bytes 983048 | tf_op jit(solution)/shard_map/ppermute | solution.py:484
  55.8 1.0 collective-permute-done.14.far_ref
  56.8 3.1 %collective-permute-done.15.cross_ref = bf16[256,384]{1,0:T(8,128)(2,1)S(1)} collective-permute-done((bf16[256,384]{1,0:T(8,128)(2,1)S(1)}, bf16[256,384]{1,0:T(8,128)(2,1)S(1)}, u32[]{:S(2)}, u32[]{:S(2)}) %collective-permute-start.15) | collective-permute-done | bytes 196640 | tf_op jit(solution)/shard_map/ppermute | solution.py:469
  60.4 3.4 %collective-permute-done.18.came_ref = bf16[256,640]{1,0:T(8,128)(2,1)S(1)} collective-permute-done((bf16[256,640]{1,0:T(8,128)(2,1)S(1)}, bf16[256,640]{1,0:T(8,128)(2,1)S(1)}, u32[]{:S(2)}, u32[]{:S(2)}) %collective-permute-start.18) | collective-permute-done | bytes 327712 | tf_op jit(solution)/shard_map/ppermute | solution.py:484
  63.8 5.5 %collective-permute-start.19 = (bf16[64,640]{1,0:T(8,128)(2,1)S(1)}, bf16[64,640]{1,0:T(8,128)(2,1)S(1)}, u32[]{:S(2)}, u32[]{:S(2)}) collective-permute-start(bf16[64,640]{1,0:T(8,128)(2,1)S(1)} %get-tuple-element.87), channel_id=1, source_target_pairs={{0,8},{4,12},{8,0},{12,4},{16,24},{20,28},{24,16},{28,20},{1,9},{5... | collective-permute-start | bytes 245768 | tf_op jit(solution)/shard_map/ppermute | solution.py:484
  69.3 2.2 %collective-permute-start.20 = (bf16[64,640]{1,0:T(8,128)(2,1)S(1)}, bf16[64,640]{1,0:T(8,128)(2,1)S(1)}, u32[]{:S(2)}, u32[]{:S(2)}) collective-permute-start(bf16[64,640]{1,0:T(8,128)(2,1)S(1)} %get-tuple-element.88), channel_id=1, source_target_pairs={{0,16},{4,20},{8,24},{12,28},{16,0},{20,4},{24,8},{28,12},{1,17},{... | collective-permute-start | bytes 245768 | tf_op jit(solution)/shard_map/ppermute | solution.py:484
  71.5 1.4 %collective-permute-start.21 = (bf16[64,640]{1,0:T(8,128)(2,1)S(1)}, bf16[64,640]{1,0:T(8,128)(2,1)S(1)}, u32[]{:S(2)}, u32[]{:S(2)}) collective-permute-start(bf16[64,640]{1,0:T(8,128)(2,1)S(1)} %get-tuple-element.89), channel_id=1, source_target_pairs={{0,24},{4,28},{8,16},{12,20},{16,8},{20,12},{24,0},{28,4},{1,25},{... | collective-permute-start | bytes 245768 | tf_op jit(solution)/shard_map/ppermute | solution.py:484
  72.9 0.9 input_grad.1.refs_0_
  73.9 0.8 copy-done.2
  74.7 4.1 %collective-permute-done.20.refs_2_ = bf16[64,640]{1,0:T(8,128)(2,1)S(1)} collective-permute-done((bf16[64,640]{1,0:T(8,128)(2,1)S(1)}, bf16[64,640]{1,0:T(8,128)(2,1)S(1)}, u32[]{:S(2)}, u32[]{:S(2)}) %collective-permute-start.20) | collective-permute-done | bytes 81952 | tf_op jit(solution)/shard_map/ppermute | solution.py:484
  79.5 4.0 %all-to-all-start = ((bf16[8,64,512]{2,1,0:T(8,128)(2,1)}), bf16[8,64,512]{2,1,0:T(8,128)(2,1)S(1)}, u32[]{:S(2)}, u32[]{:S(2)}) async-start(bf16[8,64,512]{2,1,0:T(8,128)(2,1)} %bitcast.6), calls=%async_computation | async-start | bytes 1048576 | tf_op jit(solution)/shard_map/all_to_all | solution.py:488
  83.5 1.3 %collective-permute-start.23 = (bf16[64,640]{1,0:T(8,128)(2,1)}, bf16[64,640]{1,0:T(8,128)(2,1)S(1)}, u32[]{:S(2)}, u32[]{:S(2)}) collective-permute-start(bf16[64,640]{1,0:T(8,128)(2,1)} %copy-done.9), channel_id=1, source_target_pairs={{0,2},{1,3},{2,0},{3,1},{4,6},{5,7},{6,4},{7,5},{8,10},{9,11},{10,... | collective-permute-start | bytes 245768 | tf_op jit(solution)/shard_map/ppermute | solution.py:469
  85.3 3.7 %collective-permute-done.23.w2_ref = bf16[64,640]{1,0:T(8,128)(2,1)S(1)} collective-permute-done((bf16[64,640]{1,0:T(8,128)(2,1)}, bf16[64,640]{1,0:T(8,128)(2,1)S(1)}, u32[]{:S(2)}, u32[]{:S(2)}) %collective-permute-start.23) | collective-permute-done | bytes 81952 | tf_op jit(solution)/shard_map/ppermute | solution.py:469
  89.0 0.8 collective-permute-done.24.w3_ref
  89.8 0.9 copy-done.10
  90.7 0.9 finish.1
  91.6 6.1 %all-to-all-done = bf16[8,64,512]{2,1,0:T(8,128)(2,1)S(1)} async-done(((bf16[8,64,512]{2,1,0:T(8,128)(2,1)}), bf16[8,64,512]{2,1,0:T(8,128)(2,1)S(1)}, u32[]{:S(2)}, u32[]{:S(2)}) %all-to-all-start) | async-done | bytes 524320 | tf_op jit(solution)/shard_map/all_to_all | solution.py:488
  97.7 1.2 %give_back.1 = bf16[256,512]{1,0:T(8,128)(2,1)} custom-call(s32[1]{0:T(128)} %bitcast.1.mask_ref.dp_ref, s32[1,256]{1,0:T(1,128)S(1)} %get-tuple-element.63.owner_ref, bf16[512,512]{1,0:T(8,128)(2,1)S(1)} %bitcast.7), custom_call_target="tpu_custom_call" | custom-call | flops 100000000 | bytes 1048576 | tf_op jit(solution)/shard_map/give_back/pallas_call | solution.py:22
  (56 shorter events, 5.4 us)
Async XLA Ops:
  0.6 1.0 copy-start.13
  1.6 0.7 copy-start.14
  2.3 0.7 copy-start.15
  3.7 0.6 copy-start.11
  4.3 15.3 %collective-permute-start = (bf16[72,512]{1,0:T(8,128)(2,1)S(1)}, bf16[72,512]{1,0:T(8,128)(2,1)S(1)}, u32[]{:S(2)}, u32[]{:S(2)}) collective-permute-start(bf16[72,512]{1,0:T(8,128)(2,1)S(1)} %get-tuple-element.49), channel_id=1, source_target_pairs={{0,16},{4,20},{8,24},{12,28},{16,0},{20,4},{24,8},{28,12},{1,17},{... | collective-permute-start | bytes 221192 | tf_op jit(solution)/shard_map/ppermute | solution.py:484
  8.3 11.3 %collective-permute-start.1 = (bf16[72,512]{1,0:T(8,128)(2,1)S(1)}, bf16[72,512]{1,0:T(8,128)(2,1)S(1)}, u32[]{:S(2)}, u32[]{:S(2)}) collective-permute-start(bf16[72,512]{1,0:T(8,128)(2,1)S(1)} %get-tuple-element.50), channel_id=1, source_target_pairs={{0,20},{4,16},{8,28},{12,24},{16,4},{20,0},{24,12},{28,8},{1,21},{... | collective-permute-start | bytes 221192 | tf_op jit(solution)/shard_map/ppermute | solution.py:484
  9.6 11.8 %collective-permute-start.2 = (bf16[72,512]{1,0:T(8,128)(2,1)S(1)}, bf16[72,512]{1,0:T(8,128)(2,1)S(1)}, u32[]{:S(2)}, u32[]{:S(2)}) collective-permute-start(bf16[72,512]{1,0:T(8,128)(2,1)S(1)} %get-tuple-element.51), channel_id=1, source_target_pairs={{0,24},{4,28},{8,16},{12,20},{16,8},{20,12},{24,0},{28,4},{1,25},{... | collective-permute-start | bytes 221192 | tf_op jit(solution)/shard_map/ppermute | solution.py:484
  13.2 8.2 %collective-permute-start.3 = (bf16[72,512]{1,0:T(8,128)(2,1)S(1)}, bf16[72,512]{1,0:T(8,128)(2,1)S(1)}, u32[]{:S(2)}, u32[]{:S(2)}) collective-permute-start(bf16[72,512]{1,0:T(8,128)(2,1)S(1)} %get-tuple-element.52), channel_id=1, source_target_pairs={{0,28},{4,24},{8,20},{12,16},{16,12},{20,8},{24,4},{28,0},{1,29},{... | collective-permute-start | bytes 221192 | tf_op jit(solution)/shard_map/ppermute | solution.py:484
  13.2 8.2 %collective-permute-start.4 = (bf16[72,512]{1,0:T(8,128)(2,1)S(1)}, bf16[72,512]{1,0:T(8,128)(2,1)S(1)}, u32[]{:S(2)}, u32[]{:S(2)}) collective-permute-start(bf16[72,512]{1,0:T(8,128)(2,1)S(1)} %get-tuple-element.53), channel_id=1, source_target_pairs={{0,4},{4,0},{8,12},{12,8},{16,20},{20,16},{24,28},{28,24},{1,5},{5... | collective-permute-start | bytes 221192 | tf_op jit(solution)/shard_map/ppermute | solution.py:484
  14.9 1.6 %copy-start = (bf16[512,2048]{1,0:T(8,128)(2,1)S(1)}, bf16[512,2048]{1,0:T(8,128)(2,1)}, u32[]{:S(2)}) copy-start(bf16[512,2048]{1,0:T(8,128)(2,1)} %proj_ref.15) | copy-start | bytes 6291460
  16.5 0.9 copy-start.5
  17.4 1.0 %copy-start.7 = (bf16[512,512]{1,0:T(8,128)(2,1)S(1)}, bf16[512,512]{1,0:T(8,128)(2,1)}, u32[]{:S(2)}) copy-start(bf16[512,512]{1,0:T(8,128)(2,1)} %outw_ref.3) | copy-start | bytes 1572868
  18.5 8.9 %copy-start.1 = (bf16[512,2048]{1,0:T(8,128)(2,1)S(1)}, bf16[512,2048]{1,0:T(8,128)(2,1)}, u32[]{:S(2)}) copy-start(bf16[512,2048]{1,0:T(8,128)(2,1)} %proj_ref.15) | copy-start | bytes 6291460
  18.5 8.9 %copy-start.12 = (s32[1,3]{1,0:T(1,128)S(1)}, s32[1,3]{1,0:T(1,128)}, u32[]{:S(2)}) copy-start(s32[1,3]{1,0:T(1,128)} %lengths_ref.9) | copy-start | bytes 40
  18.8 0.8 copy-start.3
  19.6 4.6 %collective-permute-start.5 = (bf16[72,512]{1,0:T(8,128)(2,1)}, bf16[72,512]{1,0:T(8,128)(2,1)S(1)}, u32[]{:S(2)}, u32[]{:S(2)}) collective-permute-start(bf16[72,512]{1,0:T(8,128)(2,1)} %relay.2), channel_id=1, source_target_pairs={{0,8},{4,12},{8,0},{12,4},{16,24},{20,28},{24,16},{28,20},{1,9},{5... | collective-permute-start | bytes 221192 | tf_op jit(solution)/shard_map/ppermute | solution.py:484
  19.6 5.3 %collective-permute-start.6 = (bf16[72,512]{1,0:T(8,128)(2,1)S(1)}, bf16[72,512]{1,0:T(8,128)(2,1)S(1)}, u32[]{:S(2)}, u32[]{:S(2)}) collective-permute-start(bf16[72,512]{1,0:T(8,128)(2,1)S(1)} %get-tuple-element.55), channel_id=1, source_target_pairs={{0,12},{4,8},{8,4},{12,0},{16,28},{20,24},{24,20},{28,16},{1,13},{... | collective-permute-start | bytes 221192 | tf_op jit(solution)/shard_map/ppermute | solution.py:484
  25.8 6.4 %collective-permute-start.7 = (bf16[256,512]{1,0:T(8,128)(2,1)S(1)}, bf16[256,512]{1,0:T(8,128)(2,1)S(1)}, u32[]{:S(2)}, u32[]{:S(2)}) collective-permute-start(bf16[256,512]{1,0:T(8,128)(2,1)S(1)} %get-tuple-element.56.normed_ref.n0_ref.refs_0_), channel_id=1, source_target_pairs={{0,2},{1,3},{2,0},{3,1},{4,6},{5,7},{6,4},{7,5},{8,10},{9,11},{10,... | collective-permute-start | bytes 786440 | tf_op jit(solution)/shard_map/ppermute | solution.py:469
  27.4 4.9 %collective-permute-start.9 = (bf16[256,512]{1,0:T(8,128)(2,1)S(1)}, bf16[256,512]{1,0:T(8,128)(2,1)S(1)}, u32[]{:S(2)}, u32[]{:S(2)}) collective-permute-start(bf16[256,512]{1,0:T(8,128)(2,1)S(1)} %get-tuple-element.56.normed_ref.n0_ref.refs_0_), channel_id=1, source_target_pairs={{0,1},{1,0},{2,3},{3,2},{4,5},{5,4},{6,7},{7,6},{8,9},{9,8},{10,11... | collective-permute-start | bytes 786440 | tf_op jit(solution)/shard_map/ppermute | solution.py:469
  32.2 1.5 %collective-permute-start.8 = (bf16[256,512]{1,0:T(8,128)(2,1)S(1)}, bf16[256,512]{1,0:T(8,128)(2,1)S(1)}, u32[]{:S(2)}, u32[]{:S(2)}) collective-permute-start(bf16[256,512]{1,0:T(8,128)(2,1)S(1)} %collective-permute-done.7.far_ref.n2_ref.refs_2_), channel_id=1, source_target_pairs={{0,1},{1,0},{2,3},{3,2},{4,5},{5,4},{6,7},{7,6},{8,9},{9,8},{10,11... | collective-permute-start | bytes 786440 | tf_op jit(solution)/shard_map/ppermute | solution.py:469
  32.2 1.5 %copy-start.4 = (f32[256,512]{1,0:T(8,128)S(1)}, f32[256,512]{1,0:T(8,128)}, u32[]{:S(2)}) copy-start(f32[256,512]{1,0:T(8,128)} %copy-done.3) | copy-start | bytes 1572868
  32.3 1.5 %copy-start.8 = (bf16[512,512]{1,0:T(8,128)(2,1)S(1)}, bf16[512,512]{1,0:T(8,128)(2,1)}, u32[]{:S(2)}) copy-start(bf16[512,512]{1,0:T(8,128)(2,1)} %outw_ref.3) | copy-start | bytes 1572868
  33.8 2.0 %copy-start.6 = (bf16[256,512]{1,0:T(8,128)(2,1)S(1)}, bf16[256,512]{1,0:T(8,128)(2,1)}, u32[]{:S(2)}) copy-start(bf16[256,512]{1,0:T(8,128)(2,1)} %cot_ref.5) | copy-start | bytes 786436
  36.5 4.8 %collective-permute-start.16 = (bf16[512,512]{1,0:T(8,128)(2,1)S(1)}, bf16[512,512]{1,0:T(8,128)(2,1)S(1)}, u32[]{:S(2)}, u32[]{:S(2)}) collective-permute-start(bf16[512,512]{1,0:T(8,128)(2,1)S(1)} %get-tuple-element.81), channel_id=1, source_target_pairs={{0,1},{1,0},{2,3},{3,2},{4,5},{5,4},{6,7},{7,6},{8,9},{9,8},{10,11... | collective-permute-start | bytes 1572872 | tf_op jit(solution)/shard_map/ppermute | solution.py:469
  36.8 6.5 %collective-permute-start.10 = (bf16[256,128]{1,0:T(8,128)(2,1)S(1)}, bf16[256,128]{1,0:T(8,128)(2,1)S(1)}, u32[]{:S(2)}, u32[]{:S(2)}) collective-permute-start(bf16[256,128]{1,0:T(8,128)(2,1)S(1)} %get-tuple-element.67), channel_id=1, source_target_pairs={{0,1},{1,0},{2,3},{3,2},{4,5},{5,4},{6,7},{7,6},{8,9},{9,8},{10,11... | collective-permute-start | bytes 196616 | tf_op jit(solution)/shard_map/ppermute | solution.py:469
  37.1 6.2 %collective-permute-start.11 = (bf16[256,128]{1,0:T(8,128)(2,1)S(1)}, bf16[256,128]{1,0:T(8,128)(2,1)S(1)}, u32[]{:S(2)}, u32[]{:S(2)}) collective-permute-start(bf16[256,128]{1,0:T(8,128)(2,1)S(1)} %get-tuple-element.68), channel_id=1, source_target_pairs={{0,2},{1,3},{2,0},{3,1},{4,6},{5,7},{6,4},{7,5},{8,10},{9,11},{10,... | collective-permute-start | bytes 196616 | tf_op jit(solution)/shard_map/ppermute | solution.py:469
  40.5 4.1 %collective-permute-start.12 = (bf16[256,128]{1,0:T(8,128)(2,1)S(1)}, bf16[256,128]{1,0:T(8,128)(2,1)S(1)}, u32[]{:S(2)}, u32[]{:S(2)}) collective-permute-start(bf16[256,128]{1,0:T(8,128)(2,1)S(1)} %get-tuple-element.69), channel_id=1, source_target_pairs={{0,3},{1,2},{2,1},{3,0},{4,7},{5,6},{6,5},{7,4},{8,11},{9,10},{10,... | collective-permute-start | bytes 196616 | tf_op jit(solution)/shard_map/ppermute | solution.py:469
  41.5 11.7 %collective-permute-start.17 = (bf16[512,256]{1,0:T(8,128)(2,1)S(1)}, bf16[512,256]{1,0:T(8,128)(2,1)S(1)}, u32[]{:S(2)}, u32[]{:S(2)}) collective-permute-start(bf16[512,256]{1,0:T(8,128)(2,1)S(1)} %get-tuple-element.83), channel_id=1, source_target_pairs={{0,2},{1,3},{2,0},{3,1},{4,6},{5,7},{6,4},{7,5},{8,10},{9,11},{10,... | collective-permute-start | bytes 786440 | tf_op jit(solution)/shard_map/ppermute | solution.py:469
  49.0 7.8 %collective-permute-start.14 = (bf16[256,384]{1,0:T(8,128)(2,1)S(1)}, bf16[256,384]{1,0:T(8,128)(2,1)S(1)}, u32[]{:S(2)}, u32[]{:S(2)}) collective-permute-start(bf16[256,384]{1,0:T(8,128)(2,1)S(1)} %get-tuple-element.74.refs_6_), channel_id=1, source_target_pairs={{0,2},{1,3},{2,0},{3,1},{4,6},{5,7},{6,4},{7,5},{8,10},{9,11},{10,... | collective-permute-start | bytes 589832 | tf_op jit(solution)/shard_map/ppermute | solution.py:469
  49.6 10.2 %collective-permute-start.15 = (bf16[256,384]{1,0:T(8,128)(2,1)S(1)}, bf16[256,384]{1,0:T(8,128)(2,1)S(1)}, u32[]{:S(2)}, u32[]{:S(2)}) collective-permute-start(bf16[256,384]{1,0:T(8,128)(2,1)S(1)} %get-tuple-element.75.refs_7_), channel_id=1, source_target_pairs={{0,3},{1,2},{2,1},{3,0},{4,7},{5,6},{6,5},{7,4},{8,11},{9,10},{10,... | collective-permute-start | bytes 589832 | tf_op jit(solution)/shard_map/ppermute | solution.py:469
  52.6 20.3 %collective-permute-start.13 = (bf16[256,384]{1,0:T(8,128)(2,1)S(1)}, bf16[256,384]{1,0:T(8,128)(2,1)S(1)}, u32[]{:S(2)}, u32[]{:S(2)}) collective-permute-start(bf16[256,384]{1,0:T(8,128)(2,1)S(1)} %get-tuple-element.73.refs_5_), channel_id=1, source_target_pairs={{0,1},{1,0},{2,3},{3,2},{4,5},{5,4},{6,7},{7,6},{8,9},{9,8},{10,11... | collective-permute-start | bytes 589832 | tf_op jit(solution)/shard_map/ppermute | solution.py:469
  54.0 9.7 %collective-permute-start.18 = (bf16[256,640]{1,0:T(8,128)(2,1)S(1)}, bf16[256,640]{1,0:T(8,128)(2,1)S(1)}, u32[]{:S(2)}, u32[]{:S(2)}) collective-permute-start(bf16[256,640]{1,0:T(8,128)(2,1)S(1)} %get-tuple-element.85), channel_id=1, source_target_pairs={{0,4},{4,0},{8,12},{12,8},{16,20},{20,16},{24,28},{28,24},{1,5},{5... | collective-permute-start | bytes 983048 | tf_op jit(solution)/shard_map/ppermute | solution.py:484
  63.8 10.8 %collective-permute-start.19 = (bf16[64,640]{1,0:T(8,128)(2,1)S(1)}, bf16[64,640]{1,0:T(8,128)(2,1)S(1)}, u32[]{:S(2)}, u32[]{:S(2)}) collective-permute-start(bf16[64,640]{1,0:T(8,128)(2,1)S(1)} %get-tuple-element.87), channel_id=1, source_target_pairs={{0,8},{4,12},{8,0},{12,4},{16,24},{20,28},{24,16},{28,20},{1,9},{5... | collective-permute-start | bytes 245768 | tf_op jit(solution)/shard_map/ppermute | solution.py:484
  69.3 9.5 %collective-permute-start.20 = (bf16[64,640]{1,0:T(8,128)(2,1)S(1)}, bf16[64,640]{1,0:T(8,128)(2,1)S(1)}, u32[]{:S(2)}, u32[]{:S(2)}) collective-permute-start(bf16[64,640]{1,0:T(8,128)(2,1)S(1)} %get-tuple-element.88), channel_id=1, source_target_pairs={{0,16},{4,20},{8,24},{12,28},{16,0},{20,4},{24,8},{28,12},{1,17},{... | collective-permute-start | bytes 245768 | tf_op jit(solution)/shard_map/ppermute | solution.py:484
  71.5 7.3 %collective-permute-start.21 = (bf16[64,640]{1,0:T(8,128)(2,1)S(1)}, bf16[64,640]{1,0:T(8,128)(2,1)S(1)}, u32[]{:S(2)}, u32[]{:S(2)}) collective-permute-start(bf16[64,640]{1,0:T(8,128)(2,1)S(1)} %get-tuple-element.89), channel_id=1, source_target_pairs={{0,24},{4,28},{8,16},{12,20},{16,8},{20,12},{24,0},{28,4},{1,25},{... | collective-permute-start | bytes 245768 | tf_op jit(solution)/shard_map/ppermute | solution.py:484
  73.9 0.8 copy-start.2
  78.9 0.6 copy-start.9
  79.5 18.2 %all-to-all-start = ((bf16[8,64,512]{2,1,0:T(8,128)(2,1)}), bf16[8,64,512]{2,1,0:T(8,128)(2,1)S(1)}, u32[]{:S(2)}, u32[]{:S(2)}) async-start(bf16[8,64,512]{2,1,0:T(8,128)(2,1)} %bitcast.6), calls=%async_computation | async-start | bytes 1048576 | tf_op jit(solution)/shard_map/all_to_all | solution.py:488
  83.5 1.9 %collective-permute-start.22 = (bf16[64,640]{1,0:T(8,128)(2,1)}, bf16[64,640]{1,0:T(8,128)(2,1)S(1)}, u32[]{:S(2)}, u32[]{:S(2)}) collective-permute-start(bf16[64,640]{1,0:T(8,128)(2,1)} %copy-done.9), channel_id=1, source_target_pairs={{0,1},{1,0},{2,3},{3,2},{4,5},{5,4},{6,7},{7,6},{8,9},{9,8},{10,11... | collective-permute-start | bytes 245768 | tf_op jit(solution)/shard_map/ppermute | solution.py:469
  83.5 5.5 %collective-permute-start.23 = (bf16[64,640]{1,0:T(8,128)(2,1)}, bf16[64,640]{1,0:T(8,128)(2,1)S(1)}, u32[]{:S(2)}, u32[]{:S(2)}) collective-permute-start(bf16[64,640]{1,0:T(8,128)(2,1)} %copy-done.9), channel_id=1, source_target_pairs={{0,2},{1,3},{2,0},{3,1},{4,6},{5,7},{6,4},{7,5},{8,10},{9,11},{10,... | collective-permute-start | bytes 245768 | tf_op jit(solution)/shard_map/ppermute | solution.py:469
  84.8 5.1 %collective-permute-start.24 = (bf16[64,640]{1,0:T(8,128)(2,1)}, bf16[64,640]{1,0:T(8,128)(2,1)S(1)}, u32[]{:S(2)}, u32[]{:S(2)}) collective-permute-start(bf16[64,640]{1,0:T(8,128)(2,1)} %copy-done.9), channel_id=1, source_target_pairs={{0,3},{1,2},{2,1},{3,0},{4,7},{5,6},{6,5},{7,4},{8,11},{9,10},{10,... | collective-permute-start | bytes 245768 | tf_op jit(solution)/shard_map/ppermute | solution.py:469
  89.8 0.9 copy-start.10

commit v11 on v10

--- a/solution.py
+++ b/solution.py
@@ -107,30 +107,31 @@
     ).astype(BF16)
 
 
-def pack_body(capacity, stride, outs, mask_ref, owner_hbm, slot_hbm, tokens_hbm, *refs):
-    out_refs, (owner_ref, slot_ref, tokens_ref, sems) = refs[:outs], refs[outs:]
+def pack_blocks(steps, capacity, stride, owner, slot, tokens, out_refs):
+    rows, width = tokens.shape
+    rank_row, rank_col = rank_rows(owner)
+    place = iota((len(steps) * stride, rows), 0)
+    for i, (before, k) in enumerate(zip((-1, *steps), steps)):
+        if k != before + 1:
+            place = jnp.where(iota(place.shape, 0) >= i * stride, place + (k - before - 1) * stride, place)
+    chosen = hot(place == owner * stride + rank_row)
+    slots = jnp.where(place == owner * stride + capacity, slot + 1, 0)
+    by_rank = hot(rank_col == iota((rows, width), 1))
+    store_blocks(out_refs, mm(chosen, tokens) + mm(slots.astype(F32).astype(BF16), by_rank))
+
+
+def pack_body(steps, capacity, stride, mask_ref, owner_hbm, slot_hbm, tokens_hbm, *refs):
+    *out_refs, owner_ref, slot_ref, tokens_ref, sems = refs
     fetch((owner_hbm, slot_hbm, tokens_hbm), (owner_ref, slot_ref, tokens_ref), sems)
     owner = owner_ref[...] ^ mask_ref[0]
     owner_ref[...] = owner
-    rows = owner.shape[1]
-    rank_row, rank_col = rank_rows(owner)
-    total, width = outs * out_refs[0].shape[0], out_refs[0].shape[1]
-    place = iota((total, rows), 0)
-    chosen = hot(place == owner * stride + rank_row)
-    slots = jnp.where(place == owner * stride + capacity, slot_ref[...] + 1, 0)
-    by_rank = hot(rank_col == iota((rows, width), 1))
-    store_blocks(out_refs, mm(chosen, tokens_ref[...]) + mm(slots.astype(F32).astype(BF16), by_rank))
-
-
-def relay(value, after):
-    return pl.pallas_call(
-        lambda *refs: None,
-        name="relay",
-        out_shape=jax.ShapeDtypeStruct(value.shape, value.dtype),
-        in_specs=[ANYWHERE] * (1 + len(after)),
-        out_specs=ANYWHERE,
-        input_output_aliases={0: 0},
-    )(value, *after)
+    if len(steps) == 1:
+        steps = range(out_refs[0].shape[0] // stride)
+    pack_blocks(tuple(steps), capacity, stride, owner, slot_ref[...], tokens_ref[...], out_refs)
+
+
+def pack_rest_body(steps, capacity, stride, owner_ref, slot_ref, tokens_ref, _, *out_refs):
+    pack_blocks(steps, capacity, stride, owner_ref[...], slot_ref[...], tokens_ref[...], out_refs)
 
 
 def block_rem(owners, stride):
@@ -229,35 +230,34 @@
 
 
 def forward_body(
-    me_ref, lengths_ref, cross_ref, proj_ref, outw_ref, owned_ref,
-    gate_ref, slope_ref, query_ref, partial_ref, grad_ref,
-    out_ref, gated_ref, gate_grad_ref, *rest,
+    me_ref, lengths_ref, cross_ref, proj_ref, gate_ref, query_ref, partial_ref, grad_ref,
+    normed_ref, *rest,
 ):
     grads, acc_ref = rest[:-1], rest[-1]
-    rows, width = query_ref.shape
+    width = query_ref.shape[1]
     me = me_ref[0]
     acc_ref[...] = partial_ref[...]
     attend_other(3, me, lengths_ref, cross_ref, proj_ref, query_ref, acc_ref)
-    gate = gate_ref[...].astype(F32)
     normed, inv_dev = normalize(acc_ref[...])
-    gated = (normed * gate).astype(BF16)
-    gated_ref[...] = gated
-    grad_gated = grad_ref[...]
-    grad_attended = norm_back(grad_gated * gate, normed, inv_dev).astype(BF16)
-    acc_ref[...] = grad_attended.astype(F32)
+    normed_ref[...] = normed
+    acc_ref[...] = norm_back(grad_ref[...] * gate_ref[...].astype(F32), normed, inv_dev)
     piece = width // len(grads)
     for step, ref in enumerate(grads):
         ref[...] = acc_ref[:, pl.ds(pl.multiple_of((me ^ step) * piece, LANES), piece)].astype(BF16)
+
+
+def side_body(
+    me_ref, own_ref, normed_ref, gate_ref, slope_ref, grad_ref, cot_ref, proj_ref, outw_ref, owned_ref,
+    kept_ref, sent_ref, gate_in_ref, out_ref, part_ref,
+):
+    width = own_ref.shape[1]
+    me = me_ref[0]
+    normed = normed_ref[...]
+    gated = (normed * gate_ref[...].astype(F32)).astype(BF16)
+    gate_grad = (grad_ref[...] * normed * slope_ref[...]).astype(BF16)
     out_ref[...] = (mm(gated, outw_ref[...]) + owned_ref[...].astype(F32)).astype(BF16)
-    gate_grad_ref[...] = (grad_gated * normed * slope_ref[...]).astype(BF16)
-
-
-def side_body(me_ref, normed_ref, gated_ref, cot_ref, gate_grad_ref, proj_ref, kept_ref, sent_ref, gate_in_ref, part_ref):
-    width = gated_ref.shape[1]
-    me = me_ref[0]
-    gate_grad = gate_grad_ref[...]
-    part_ref[:, :width] = t_mm(normed_ref[...], gate_grad)
-    part_ref[:, width:] = t_mm(gated_ref[...], cot_ref[...])
+    part_ref[:, :width] = t_mm(own_ref[...], gate_grad)
+    part_ref[:, width:] = t_mm(gated, cot_ref[...])
     gate_in_ref[...] = mm_t(gate_grad, proj_ref[:, :width])
     for ref, steps in ((kept_ref, (0, 2)), (sent_ref, (1, 3))):
         place = 0
@@ -347,17 +347,16 @@
         ref[...] = (total_ref[at, :] * slope_ref[at, :]).astype(BF16)
 
 
-def backward_far_body(
-    me_ref, lengths_ref, g0_ref, g1_ref, g2_ref, g3_ref, part_ref, slope_ref, *rest
-):
-    o2_ref, o3_ref, total_ref, grad_ref = rest[-4:]
+def collect_body(me_ref, g0_ref, g1_ref, g2_ref, g3_ref, grad_ref):
     rows = g0_ref.shape[0]
-    me = me_ref[0]
     for step, ref in enumerate((g0_ref, g1_ref, g2_ref, g3_ref)):
-        grad_ref[block_at(me ^ step, rows), :] = ref[...]
+        grad_ref[block_at(me_ref[0] ^ step, rows), :] = ref[...]
+
+
+def backward_far_body(me_ref, lengths_ref, part_ref, slope_ref, grad_ref, o2_ref, o3_ref, total_ref):
     total_ref[...] = jnp.zeros_like(total_ref)
     backward_rows(
-        (2, 3), (), me, lengths_ref, part_ref, slope_ref, grad_ref, total_ref, (o2_ref, o3_ref)
+        (2, 3), (), me_ref[0], lengths_ref, part_ref, slope_ref, grad_ref, total_ref, (o2_ref, o3_ref)
     )
 
 
@@ -407,19 +406,18 @@
     out_ref[...] = total + mm_t(cross_ref[...], head_columns(me ^ 3, proj_ref))
 
 
-def input_body(
-    blocks, me_ref, mask_ref, own_ref, near_ref, partial_ref,
-    owned_ref, cot_ref, landing_ref, proj_ref, *rest,
-):
-    out_ref = rest[-1]
-    rows = owned_ref.shape[0]
+def input_body(me_ref, own_ref, near_ref, partial_ref, owned_ref, cot_ref, proj_ref, out_ref):
     me = me_ref[0]
     total = partial_ref[...] + mm_t(own_ref[...], head_columns(me, proj_ref))
     total += mm_t(near_ref[...], head_columns(me ^ 1, proj_ref))
     centred, inv_scale = normalize(owned_ref[...].astype(F32))
     grad = (norm_back(total, centred, inv_scale) + cot_ref[...].astype(F32)).astype(BF16)
-    select = hot(iota((rows, landing_ref.shape[1]), 0) + 1 == landing_ref[...])
-    value = t_mm(select, grad)
+    out_ref[...] = grad
+
+
+def spread_body(blocks, mask_ref, grad_ref, landing_ref, _, out_ref):
+    select = hot(iota((grad_ref.shape[0], landing_ref.shape[1]), 0) + 1 == landing_ref[...])
+    value = t_mm(select, grad_ref[...])
     size = value.shape[0] // blocks
     for k in range(blocks):
         at = pl.ds(pl.multiple_of((mask_ref[0] ^ k) * size, size), size)
@@ -496,20 +494,25 @@
         return [((owners * height // blocks, columns), dtype)] * blocks
 
     wide = ((rows, width), F32)
-    *outgoing, owner_here = call(
-        functools.partial(pack_body, capacity, stride, blocks),
-        "pack", block_shapes(stride, width, BF16) + [((1, rows), jnp.int32)],
-        [mask], [], far=[owner_row, slot_row, tokens],
-        scratch=[
-            pltpu.VMEM((1, rows), jnp.int32),
-            pltpu.VMEM((rows, width), BF16),
-            pltpu.SemaphoreType.DMA((3,)),
-        ],
+    steps = tuple(range(blocks))
+    later = steps[owners // 4 : owners // 2] if by_hops else ()
+    first = tuple(k for k in steps if k not in later)
+    *outgoing, owner_here, slot_here, tokens_here = call(
+        functools.partial(pack_body, first, capacity, stride),
+        "pack",
+        block_shapes(stride, width, BF16)[: len(first)] + [((1, rows), jnp.int32)] * 2 + [square],
+        [mask], [], far=[owner_row, slot_row, tokens], scratch=[pltpu.SemaphoreType.DMA((3,))],
     )
     (grad_gated,) = call(early_body, "early", [wide], [], [cotangent, out_weight, proj_weight])
-    if by_hops:
-        outgoing[owners // 4] = relay(outgoing[owners // 4], [grad_gated])
-    arrived = swap(outgoing)
+    outgoing = dict(zip(first, outgoing))
+    if later:
+        rest = call(
+            functools.partial(pack_rest_body, later, capacity, stride),
+            "pack_rest", block_shapes(stride, width, BF16)[: len(later)], [],
+            [owner_here, slot_here, tokens_here], far=[grad_gated],
+        )
+        outgoing.update(zip(later, rest))
+    arrived = swap([outgoing[k] for k in steps])
     owned, normed, landing = call(
         functools.partial(place_body, owners, capacity, stride),
         "place", [square, square, ((1, owners * capacity), jnp.int32)], [], arrived,
@@ -523,19 +526,17 @@
         middle_body, "middle", [wide], [me, lengths], [near, far, proj_weight, query, partial],
         flops=10**10, vmem=16,
     )
-    layer_out, gated, gate_grad, *grad_pieces = call(
-        forward_body, "forward",
-        [square, square, square] + [((rows, piece), BF16)] * cycle,
-        [me, lengths],
-        [cross, proj_weight, out_weight, owned, gate, slope, query, partial, grad_gated],
+    normed_out, *grad_pieces = call(
+        forward_body, "forward", [wide] + [((rows, piece), BF16)] * cycle,
+        [me, lengths], [cross, proj_weight, gate, query, partial, grad_gated],
         scratch=[pltpu.VMEM((rows, width), F32)], vmem=16,
     )
     r0, r2, r3, r1 = exchange(grad_pieces)
     side_half = ((width, 4 * piece), BF16)
     side_piece = ((width, 2 * piece), BF16)
-    side_kept, side_sent, gate_in = call(
-        side_body, "side", [side_half, side_half, wide],
-        [me], [normed, gated, cotangent, gate_grad, proj_weight],
+    side_kept, side_sent, gate_in, layer_out = call(
+        side_body, "side", [side_half, side_half, wide, square],
+        [me], [normed, normed_out, gate, slope, grad_gated, cotangent, proj_weight, out_weight, owned],
         scratch=[pltpu.VMEM((width, 2 * width), F32)], vmem=16,
     )
     side_came = hop(side_sent, 1)
@@ -551,9 +552,12 @@
     grad_block = ((rows, 3 * piece), BF16)
     sums = ((rows * cycle, 3 * piece), F32)
     grad_rows = ((rows * cycle, piece), BF16)
-    far_block, cross_block, totals, grad_all = call(
-        backward_far_body, "backward_far", [grad_block, grad_block, sums, grad_rows],
-        [me, lengths], [r0, r1, r2, r3, parts, slopes], flops=10**10, vmem=16,
+    (grad_all,) = call(
+        collect_body, "collect", [grad_rows], [me], [r0, r1, r2, r3], flops=6 * 10**9,
+    )
+    far_block, cross_block, totals = call(
+        backward_far_body, "backward_far", [grad_block, grad_block, sums],
+        [me, lengths], [parts, slopes, grad_all], flops=10**10, vmem=16,
     )
     p2, p3 = hop(far_block, 2), hop(cross_block, 3)
     own_block, near_block = call(
@@ -575,9 +579,9 @@
     (partial_in,) = call(
         input_far_body, "input_far", [wide], [me], [p2, p3, gate_in, proj_weight], flops=6 * 10**9,
     )
-    (back,) = call(
-        functools.partial(input_body, blocks), "input_grad", [((owners * capacity, width), BF16)], [me, mask],
-        [own_block, p1, partial_in, owned, cotangent, landing, proj_weight], vmem=16,
+    (grad_owned,) = call(
+        input_body, "input_grad", [square], [me],
+        [own_block, p1, partial_in, owned, cotangent, proj_weight], vmem=16,
     )
     if by_hops:
         kept, sent = weight_parts
@@ -589,7 +593,11 @@
     else:
         summed_parts = [swap_whole(weight_parts[0]).reshape(owners, share, columns)]
     (mine,) = call(sum_body, "sum", [((share, columns), BF16)], [], summed_parts)
-    returned = swap_whole(relay(back, [mine]))
+    (back,) = call(
+        functools.partial(spread_body, blocks), "spread", [((owners * capacity, width), BF16)],
+        [mask], [grad_owned, landing], far=[mine],
+    )
+    returned = swap_whole(back)
     w1, w2, w3 = (hop(mine, step) for step in range(1, cycle))
     (grad_tokens,) = call(
         functools.partial(return_body, capacity), "give_back", [square], [mask], [owner_here, returned]

time: 98.4 us -> 99.5 us (1.011); the launches traced: 98.9 us -> 98.1 us
  waiting for transfers between devices: 30.6 us -> 35.9 us
  local copies, waits for them, and re-layouts: 9.63 us -> 5.9 us
  starting transfers between devices: 38.8 us -> 35.2 us
  Pallas kernels: 19 us -> 20.3 us
    unnamed x32 -> x20, local copies, waits for them, and re-layouts: 9.63 us -> 5.9 us
    ppermute x14, waiting for transfers between devices: 13.5 us -> 16.2 us  [hop(): return lax.ppermute(value, 'ctx', [(i, i ^ step) for i in range(cycle)])]
    ppermute x11, starting transfers between devices: 23.3 us -> 20.6 us  [dp_hop(): return lax.ppermute(value, 'dp', [(i, i ^ step) for i in range(owners)])]
    ppermute x11, waiting for transfers between devices: 11 us -> 12.7 us  [dp_hop(): return lax.ppermute(value, 'dp', [(i, i ^ step) for i in range(owners)])]
    pallas_call x18 -> x21, Pallas kernels: 19 us -> 20.3 us  [call(): pl.pallas_call(body, name=name, out_shape=[jax.ShapeDtypeStruct(s, d) for...]
  transfers between devices with their start and end apart: 26 -> 26, of which waited for: 12 -> 13; matrix products, arithmetic and copies ran while one was open for 0% -> 0% of each run, Pallas kernels for 14% -> 16%
where the time goes in v11:
time: 99.5 us; the launch traced here: 98.1 us
  waiting for transfers between devices  35.9 us (36%)
  starting transfers between devices  35.2 us (35%)
  Pallas kernels  20.3 us (20%)
  local copies, waits for them, and re-layouts  5.9 us (6%)
    ppermute x11, starting transfers between devices, dp_hop(): return lax.ppermute(value, 'dp', [(i, i ^ step) for i in range(owners)])  20.6 us
    pallas_call x21, Pallas kernels, call(): pl.pallas_call(body, name=name, out_shape=[jax.ShapeDtypeStruct(s, d) for...  20.3 us
    ppermute x14, waiting for transfers between devices, hop(): return lax.ppermute(value, 'ctx', [(i, i ^ step) for i in range(cycle)])  16.2 us
    ppermute x11, waiting for transfers between devices, dp_hop(): return lax.ppermute(value, 'dp', [(i, i ^ step) for i in range(owners)])  12.7 us
    ppermute x14, starting transfers between devices, hop(): return lax.ppermute(value, 'ctx', [(i, i ^ step) for i in range(cycle)])  10.9 us
    all_to_all x1, waiting for transfers between devices, swap_whole(): lax.all_to_all(split, 'dp', split_axis=0, concat_axis=0, tiled=True)  6.92 us
    unnamed x20, local copies, waits for them, and re-layouts  5.9 us
    all_to_all x1, starting transfers between devices, swap_whole(): lax.all_to_all(split, 'dp', split_axis=0, concat_axis=0, tiled=True)  3.74 us
  transfers between devices with their start and end apart: 26, of which 13 were waited for; matrix products, arithmetic and copies ran while one was open for 0% of the time, Pallas kernels for 16%

profile of v11, /device:TPU:0, one launch (start us, length us, event | category | flops | bytes accessed | tf_op | source)
XLA Modules:
  0.0 98.1 jit_solution(6268218049042879511)
XLA Ops:
  0.6 0.9 copy-done.7
  1.6 0.7 copy-done.8
  2.3 0.7 copy-done.9
  3.6 4.1 %collective-permute-start = (bf16[72,512]{1,0:T(8,128)(2,1)S(1)}, bf16[72,512]{1,0:T(8,128)(2,1)S(1)}, u32[]{:S(2)}, u32[]{:S(2)}) collective-permute-start(bf16[72,512]{1,0:T(8,128)(2,1)S(1)} %get-tuple-element.49), channel_id=1, source_target_pairs={{0,16},{4,20},{8,24},{12,28},{16,0},{20,4},{24,8},{28,12},{1,17},{... | collective-permute-start | bytes 221192 | tf_op jit(solution)/shard_map/ppermute | solution.py:482
  7.7 1.3 %collective-permute-start.1 = (bf16[72,512]{1,0:T(8,128)(2,1)S(1)}, bf16[72,512]{1,0:T(8,128)(2,1)S(1)}, u32[]{:S(2)}, u32[]{:S(2)}) collective-permute-start(bf16[72,512]{1,0:T(8,128)(2,1)S(1)} %get-tuple-element.50), channel_id=1, source_target_pairs={{0,20},{4,16},{8,28},{12,24},{16,4},{20,0},{24,12},{28,8},{1,21},{... | collective-permute-start | bytes 221192 | tf_op jit(solution)/shard_map/ppermute | solution.py:482
  9.0 3.6 %collective-permute-start.2 = (bf16[72,512]{1,0:T(8,128)(2,1)S(1)}, bf16[72,512]{1,0:T(8,128)(2,1)S(1)}, u32[]{:S(2)}, u32[]{:S(2)}) collective-permute-start(bf16[72,512]{1,0:T(8,128)(2,1)S(1)} %get-tuple-element.51), channel_id=1, source_target_pairs={{0,24},{4,28},{8,16},{12,20},{16,8},{20,12},{24,0},{28,4},{1,25},{... | collective-permute-start | bytes 221192 | tf_op jit(solution)/shard_map/ppermute | solution.py:482
  12.6 1.7 %collective-permute-start.4 = (bf16[72,512]{1,0:T(8,128)(2,1)S(1)}, bf16[72,512]{1,0:T(8,128)(2,1)S(1)}, u32[]{:S(2)}, u32[]{:S(2)}) collective-permute-start(bf16[72,512]{1,0:T(8,128)(2,1)S(1)} %get-tuple-element.53), channel_id=1, source_target_pairs={{0,4},{4,0},{8,12},{12,8},{16,20},{20,16},{24,28},{28,24},{1,5},{5... | collective-permute-start | bytes 221192 | tf_op jit(solution)/shard_map/ppermute | solution.py:482
  14.3 1.6 %copy-done = bf16[512,2048]{1,0:T(8,128)(2,1)S(1)} copy-done((bf16[512,2048]{1,0:T(8,128)(2,1)S(1)}, bf16[512,2048]{1,0:T(8,128)(2,1)}, u32[]{:S(2)}) %copy-start) | copy-done | bytes 2097176
  15.9 0.9 copy-done.2
  16.8 1.0 %copy-done.4 = bf16[512,512]{1,0:T(8,128)(2,1)S(1)} copy-done((bf16[512,512]{1,0:T(8,128)(2,1)S(1)}, bf16[512,512]{1,0:T(8,128)(2,1)}, u32[]{:S(2)}) %copy-start.4) | copy-done | bytes 524312
  18.2 1.0 %pack_rest.1 = (bf16[72,512]{1,0:T(8,128)(2,1)}, bf16[72,512]{1,0:T(8,128)(2,1)S(1)}) custom-call(s32[1,256]{1,0:T(1,128)S(1)} %get-tuple-element.54.owner_ref, s32[1,256]{1,0:T(1,128)S(1)} %get-tuple-element.55.slot_ref, bf16[256,512]{1,0:T(8,128)(2,1)S(1)} %get-tuple-element.56.tokens_ref, f32[256,512]{1,0:T(8,128)S(1)} %early.1._.grad_ref), custom_call_target="tpu_custom_call" | custom-call | flops 100000000 | bytes 1048576 | tf_op jit(solution)/shard_map/pack_rest/pallas_call | solution.py:22
  19.2 1.8 %collective-permute-start.6 = (bf16[72,512]{1,0:T(8,128)(2,1)S(1)}, bf16[72,512]{1,0:T(8,128)(2,1)S(1)}, u32[]{:S(2)}, u32[]{:S(2)}) collective-permute-start(bf16[72,512]{1,0:T(8,128)(2,1)S(1)} %get-tuple-element.58), channel_id=1, source_target_pairs={{0,12},{4,8},{8,4},{12,0},{16,28},{20,24},{24,20},{28,16},{1,13},{... | collective-permute-start | bytes 221192 | tf_op jit(solution)/shard_map/ppermute | solution.py:482
  21.0 2.7 %collective-permute-done.5.refs_6_ = bf16[72,512]{1,0:T(8,128)(2,1)S(1)} collective-permute-done((bf16[72,512]{1,0:T(8,128)(2,1)}, bf16[72,512]{1,0:T(8,128)(2,1)S(1)}, u32[]{:S(2)}, u32[]{:S(2)}) %collective-permute-start.5) | collective-permute-done | bytes 73760 | tf_op jit(solution)/shard_map/ppermute | solution.py:482
  23.8 0.8 collective-permute-done.6.refs_7_
  24.5 0.8 place.1
  25.5 1.6 %collective-permute-start.7 = (bf16[256,512]{1,0:T(8,128)(2,1)S(1)}, bf16[256,512]{1,0:T(8,128)(2,1)S(1)}, u32[]{:S(2)}, u32[]{:S(2)}) collective-permute-start(bf16[256,512]{1,0:T(8,128)(2,1)S(1)} %get-tuple-element.59.normed_ref.own_ref.n0_ref.refs_0_), channel_id=1, source_target_pairs={{0,2},{1,3},{2,0},{3,1},{4,6},{5,7},{6,4},{7,5},{8,10},{9,11},{10,... | collective-permute-start | bytes 786440 | tf_op jit(solution)/shard_map/ppermute | solution.py:467
  27.0 2.2 %own_rows.1 = (bf16[256,512]{1,0:T(8,128)(2,1)S(1)}, f32[256,512]{1,0:T(8,128)S(1)}, bf16[256,512]{1,0:T(8,128)(2,1)S(1)}, f32[256,512]{1,0:T(8,128)S(1)}) custom-call(s32[1]{0:T(128)} %bitcast.me_ref, s32[1,3]{1,0:T(1,128)S(1)} %copy-done.6, bf16[256,512]{1,0:T(8,128)(2,1)S(1)} %get-tuple-element.59.normed_ref.own_ref.n0_ref.refs_0_, ...), custom_call_target="tpu_custom_call" | custom-call | flops 10000000000 | bytes 1048576 | tf_op jit(solution)/shard_map/own_rows/pallas_call | solution.py:22
  29.2 4.9 %collective-permute-done.7.far_ref.n2_ref.refs_2_ = bf16[256,512]{1,0:T(8,128)(2,1)S(1)} collective-permute-done((bf16[256,512]{1,0:T(8,128)(2,1)S(1)}, bf16[256,512]{1,0:T(8,128)(2,1)S(1)}, u32[]{:S(2)}, u32[]{:S(2)}) %collective-permute-start.7) | collective-permute-done | bytes 262176 | tf_op jit(solution)/shard_map/ppermute | solution.py:467
  34.8 0.9 collective-permute-done.8.cross_ref.n3_ref.refs_3_
  35.7 1.0 %forward.1 = (f32[256,512]{1,0:T(8,128)S(1)}, bf16[256,128]{1,0:T(8,128)(2,1)S(1)}, bf16[256,128]{1,0:T(8,128)(2,1)S(1)}, bf16[256,128]{1,0:T(8,128)(2,1)S(1)}, bf16[256,128]{1,0:T(8,128)(2,1)S(1)}) custom-call(s32[1]{0:T(128)} %bitcast.me_ref, s32[1,3]{1,0:T(1,128)S(1)} %copy-done.6, bf16[256,512]{1,0:T(8,128)(2,1)S(1)} %collective-permute-done.8.cross_ref.n3_ref.refs_3_, ...), custom_call_target="tpu_custom_call" | custom-call | flops 100000000 | bytes 1048576 | tf_op jit(solution)/shard_map/forward/pallas_call | solution.py:22
  36.7 1.0 %collective-permute-start.10 = (bf16[256,128]{1,0:T(8,128)(2,1)S(1)}, bf16[256,128]{1,0:T(8,128)(2,1)S(1)}, u32[]{:S(2)}, u32[]{:S(2)}) collective-permute-start(bf16[256,128]{1,0:T(8,128)(2,1)S(1)} %get-tuple-element.70), channel_id=1, source_target_pairs={{0,1},{1,0},{2,3},{3,2},{4,5},{5,4},{6,7},{7,6},{8,9},{9,8},{10,11... | collective-permute-start | bytes 196616 | tf_op jit(solution)/shard_map/ppermute | solution.py:467
  37.8 2.4 %collective-permute-start.11 = (bf16[256,128]{1,0:T(8,128)(2,1)S(1)}, bf16[256,128]{1,0:T(8,128)(2,1)S(1)}, u32[]{:S(2)}, u32[]{:S(2)}) collective-permute-start(bf16[256,128]{1,0:T(8,128)(2,1)S(1)} %get-tuple-element.71), channel_id=1, source_target_pairs={{0,2},{1,3},{2,0},{3,1},{4,6},{5,7},{6,4},{7,5},{8,10},{9,11},{10,... | collective-permute-start | bytes 196616 | tf_op jit(solution)/shard_map/ppermute | solution.py:467
  40.3 1.1 %side.1 = (bf16[512,512]{1,0:T(8,128)(2,1)S(1)}, bf16[512,512]{1,0:T(8,128)(2,1)S(1)}, f32[256,512]{1,0:T(8,128)S(1)}, bf16[256,512]{1,0:T(8,128)(2,1)}) custom-call(s32[1]{0:T(128)} %bitcast.me_ref, bf16[256,512]{1,0:T(8,128)(2,1)S(1)} %get-tuple-element.59.normed_ref.own_ref.n0_ref.refs_0_, f32[256,512]{1,0:T(8,128)S(1)} %get-tuple-element.63.normed_ref, ...), custom_call_target="tpu_custom_call" | custom-call | flops 100000000 | bytes 1048576 | tf_op jit(solution)/shard_map/side/pallas_call | solution.py:22
  41.5 0.8 heads.1
  42.9 1.4 %collective-permute-done.12.g3_ref = bf16[256,128]{1,0:T(8,128)(2,1)S(1)} collective-permute-done((bf16[256,128]{1,0:T(8,128)(2,1)S(1)}, bf16[256,128]{1,0:T(8,128)(2,1)S(1)}, u32[]{:S(2)}, u32[]{:S(2)}) %collective-permute-start.12) | collective-permute-done | bytes 65568 | tf_op jit(solution)/shard_map/ppermute | solution.py:467
  44.4 1.4 %collective-permute-start.17 = (bf16[512,256]{1,0:T(8,128)(2,1)S(1)}, bf16[512,256]{1,0:T(8,128)(2,1)S(1)}, u32[]{:S(2)}, u32[]{:S(2)}) collective-permute-start(bf16[512,256]{1,0:T(8,128)(2,1)S(1)} %get-tuple-element.83), channel_id=1, source_target_pairs={{0,2},{1,3},{2,0},{3,1},{4,6},{5,7},{6,4},{7,5},{8,10},{9,11},{10,... | collective-permute-start | bytes 786440 | tf_op jit(solution)/shard_map/ppermute | solution.py:467
  45.8 3.7 %backward_far.1 = (bf16[256,384]{1,0:T(8,128)(2,1)S(1)}, bf16[256,384]{1,0:T(8,128)(2,1)S(1)}, f32[1024,384]{1,0:T(8,128)S(1)}) custom-call(s32[1]{0:T(128)} %bitcast.me_ref, s32[1,3]{1,0:T(1,128)S(1)} %copy-done.6, bf16[1024,384]{1,0:T(8,128)(2,1)S(1)} %get-tuple-element.67.part_ref, f32[1024,384]{1,0:T(8,128)S(1)} %get-tuple-element.68.slope_ref, ...), custom_call_target="tpu_custom_call" | custom-call | flops 10000000000 | bytes 1048576 | tf_op jit(solution)/shard_map/backward_far/pallas_call | solution.py:22
  49.5 1.4 %collective-permute-start.14 = (bf16[256,384]{1,0:T(8,128)(2,1)S(1)}, bf16[256,384]{1,0:T(8,128)(2,1)S(1)}, u32[]{:S(2)}, u32[]{:S(2)}) collective-permute-start(bf16[256,384]{1,0:T(8,128)(2,1)S(1)} %get-tuple-element.76.refs_6_), channel_id=1, source_target_pairs={{0,2},{1,3},{2,0},{3,1},{4,6},{5,7},{6,4},{7,5},{8,10},{9,11},{10,... | collective-permute-start | bytes 589832 | tf_op jit(solution)/shard_map/ppermute | solution.py:467
  51.0 2.6 %backward_rest.1 = (bf16[256,384]{1,0:T(8,128)(2,1)S(1)}, bf16[256,384]{1,0:T(8,128)(2,1)S(1)}) custom-call(s32[1]{0:T(128)} %bitcast.me_ref, s32[1,3]{1,0:T(1,128)S(1)} %copy-done.6, bf16[1024,384]{1,0:T(8,128)(2,1)S(1)} %get-tuple-element.67.part_ref, f32[1024,384]{1,0:T(8,128)S(1)} %get-tuple-element.68.slope_ref, bf16[1024,128]{1,0:T(8,128)(2,1)S(1)} %collect.1.grad_ref, ...), custom_call_target="tpu_custom_call" | custom-call | flops 100000000 | bytes 1048576 | tf_op jit(solution)/shard_map/backward_rest/pallas_call | solution.py:22
  53.6 0.8 collective-permute-start.13
  54.4 0.8 weights.1
  55.2 1.6 %collective-permute-start.18 = (bf16[256,640]{1,0:T(8,128)(2,1)S(1)}, bf16[256,640]{1,0:T(8,128)(2,1)S(1)}, u32[]{:S(2)}, u32[]{:S(2)}) collective-permute-start(bf16[256,640]{1,0:T(8,128)(2,1)S(1)} %get-tuple-element.85), channel_id=1, source_target_pairs={{0,4},{4,0},{8,12},{12,8},{16,20},{20,16},{24,28},{28,24},{1,5},{5... | collective-permute-start | bytes 983048 | tf_op jit(solution)/shard_map/ppermute | solution.py:482
  56.8 0.9 collective-permute-done.14.far_ref
  57.7 3.0 %collective-permute-done.15.cross_ref = bf16[256,384]{1,0:T(8,128)(2,1)S(1)} collective-permute-done((bf16[256,384]{1,0:T(8,128)(2,1)S(1)}, bf16[256,384]{1,0:T(8,128)(2,1)S(1)}, u32[]{:S(2)}, u32[]{:S(2)}) %collective-permute-start.15) | collective-permute-done | bytes 196640 | tf_op jit(solution)/shard_map/ppermute | solution.py:467
  61.2 3.8 %collective-permute-done.18.came_ref = bf16[256,640]{1,0:T(8,128)(2,1)S(1)} collective-permute-done((bf16[256,640]{1,0:T(8,128)(2,1)S(1)}, bf16[256,640]{1,0:T(8,128)(2,1)S(1)}, u32[]{:S(2)}, u32[]{:S(2)}) %collective-permute-start.18) | collective-permute-done | bytes 327712 | tf_op jit(solution)/shard_map/ppermute | solution.py:482
  65.0 4.1 %collective-permute-start.19 = (bf16[64,640]{1,0:T(8,128)(2,1)S(1)}, bf16[64,640]{1,0:T(8,128)(2,1)S(1)}, u32[]{:S(2)}, u32[]{:S(2)}) collective-permute-start(bf16[64,640]{1,0:T(8,128)(2,1)S(1)} %get-tuple-element.87), channel_id=1, source_target_pairs={{0,8},{4,12},{8,0},{12,4},{16,24},{20,28},{24,16},{28,20},{1,9},{5... | collective-permute-start | bytes 245768 | tf_op jit(solution)/shard_map/ppermute | solution.py:482
  69.3 2.3 %collective-permute-start.21 = (bf16[64,640]{1,0:T(8,128)(2,1)S(1)}, bf16[64,640]{1,0:T(8,128)(2,1)S(1)}, u32[]{:S(2)}, u32[]{:S(2)}) collective-permute-start(bf16[64,640]{1,0:T(8,128)(2,1)S(1)} %get-tuple-element.89), channel_id=1, source_target_pairs={{0,24},{4,28},{8,16},{12,20},{16,8},{20,12},{24,0},{28,4},{1,25},{... | collective-permute-start | bytes 245768 | tf_op jit(solution)/shard_map/ppermute | solution.py:482
  71.5 0.7 input_grad.1.grad_ref
  72.2 5.4 %collective-permute-done.20.refs_2_ = bf16[64,640]{1,0:T(8,128)(2,1)S(1)} collective-permute-done((bf16[64,640]{1,0:T(8,128)(2,1)S(1)}, bf16[64,640]{1,0:T(8,128)(2,1)S(1)}, u32[]{:S(2)}, u32[]{:S(2)}) %collective-permute-start.20) | collective-permute-done | bytes 81952 | tf_op jit(solution)/shard_map/ppermute | solution.py:482
  77.7 1.1 %spread.1 = bf16[512,512]{1,0:T(8,128)(2,1)} custom-call(s32[1]{0:T(128)} %bitcast.1.mask_ref.dp_ref, bf16[256,512]{1,0:T(8,128)(2,1)S(1)} %input_grad.1.grad_ref, s32[1,512]{1,0:T(1,128)S(1)} %get-tuple-element.79.landing_ref, bf16[64,640]{1,0:T(8,128)(2,1)S(1)} %sum.1._.w0_ref), custom_call_target="tpu_custom_call" | custom-call | flops 100000000 | bytes 1048576 | tf_op jit(solution)/shard_map/spread/pallas_call | solution.py:22
  78.8 3.7 %all-to-all-start = ((bf16[8,64,512]{2,1,0:T(8,128)(2,1)}), bf16[8,64,512]{2,1,0:T(8,128)(2,1)S(1)}, u32[]{:S(2)}, u32[]{:S(2)}) async-start(bf16[8,64,512]{2,1,0:T(8,128)(2,1)} %bitcast.4), calls=%async_computation | async-start | bytes 1048576 | tf_op jit(solution)/shard_map/all_to_all | solution.py:486
  82.6 0.7 collective-permute-start.24
  83.3 1.0 collective-permute-start.23
  84.5 2.7 %collective-permute-done.24.w3_ref = bf16[64,640]{1,0:T(8,128)(2,1)S(1)} collective-permute-done((bf16[64,640]{1,0:T(8,128)(2,1)S(1)}, bf16[64,640]{1,0:T(8,128)(2,1)S(1)}, u32[]{:S(2)}, u32[]{:S(2)}) %collective-permute-start.24) | collective-permute-done | bytes 81952 | tf_op jit(solution)/shard_map/ppermute | solution.py:467
  87.1 2.0 %collective-permute-done.23.w2_ref = bf16[64,640]{1,0:T(8,128)(2,1)S(1)} collective-permute-done((bf16[64,640]{1,0:T(8,128)(2,1)S(1)}, bf16[64,640]{1,0:T(8,128)(2,1)S(1)}, u32[]{:S(2)}, u32[]{:S(2)}) %collective-permute-start.23) | collective-permute-done | bytes 81952 | tf_op jit(solution)/shard_map/ppermute | solution.py:467
  89.1 0.9 finish.1
  90.0 6.9 %all-to-all-done = bf16[8,64,512]{2,1,0:T(8,128)(2,1)S(1)} async-done(((bf16[8,64,512]{2,1,0:T(8,128)(2,1)}), bf16[8,64,512]{2,1,0:T(8,128)(2,1)S(1)}, u32[]{:S(2)}, u32[]{:S(2)}) %all-to-all-start) | async-done | bytes 524320 | tf_op jit(solution)/shard_map/all_to_all | solution.py:486
  96.9 1.2 %give_back.1 = bf16[256,512]{1,0:T(8,128)(2,1)} custom-call(s32[1]{0:T(128)} %bitcast.1.mask_ref.dp_ref, s32[1,256]{1,0:T(1,128)S(1)} %get-tuple-element.54.owner_ref, bf16[512,512]{1,0:T(8,128)(2,1)S(1)} %bitcast.6), custom_call_target="tpu_custom_call" | custom-call | flops 100000000 | bytes 1048576 | tf_op jit(solution)/shard_map/give_back/pallas_call | solution.py:22
  (45 shorter events, 3.5 us)
Async XLA Ops:
  0.6 1.0 copy-start.7
  1.6 0.7 copy-start.8
  2.3 0.7 copy-start.9
  3.6 15.6 %collective-permute-start = (bf16[72,512]{1,0:T(8,128)(2,1)S(1)}, bf16[72,512]{1,0:T(8,128)(2,1)S(1)}, u32[]{:S(2)}, u32[]{:S(2)}) collective-permute-start(bf16[72,512]{1,0:T(8,128)(2,1)S(1)} %get-tuple-element.49), channel_id=1, source_target_pairs={{0,16},{4,20},{8,24},{12,28},{16,0},{20,4},{24,8},{28,12},{1,17},{... | collective-permute-start | bytes 221192 | tf_op jit(solution)/shard_map/ppermute | solution.py:482
  7.7 11.5 %collective-permute-start.1 = (bf16[72,512]{1,0:T(8,128)(2,1)S(1)}, bf16[72,512]{1,0:T(8,128)(2,1)S(1)}, u32[]{:S(2)}, u32[]{:S(2)}) collective-permute-start(bf16[72,512]{1,0:T(8,128)(2,1)S(1)} %get-tuple-element.50), channel_id=1, source_target_pairs={{0,20},{4,16},{8,28},{12,24},{16,4},{20,0},{24,12},{28,8},{1,21},{... | collective-permute-start | bytes 221192 | tf_op jit(solution)/shard_map/ppermute | solution.py:482
  9.0 12.1 %collective-permute-start.2 = (bf16[72,512]{1,0:T(8,128)(2,1)S(1)}, bf16[72,512]{1,0:T(8,128)(2,1)S(1)}, u32[]{:S(2)}, u32[]{:S(2)}) collective-permute-start(bf16[72,512]{1,0:T(8,128)(2,1)S(1)} %get-tuple-element.51), channel_id=1, source_target_pairs={{0,24},{4,28},{8,16},{12,20},{16,8},{20,12},{24,0},{28,4},{1,25},{... | collective-permute-start | bytes 221192 | tf_op jit(solution)/shard_map/ppermute | solution.py:482
  12.6 8.5 %collective-permute-start.3 = (bf16[72,512]{1,0:T(8,128)(2,1)S(1)}, bf16[72,512]{1,0:T(8,128)(2,1)S(1)}, u32[]{:S(2)}, u32[]{:S(2)}) collective-permute-start(bf16[72,512]{1,0:T(8,128)(2,1)S(1)} %get-tuple-element.52), channel_id=1, source_target_pairs={{0,28},{4,24},{8,20},{12,16},{16,12},{20,8},{24,4},{28,0},{1,29},{... | collective-permute-start | bytes 221192 | tf_op jit(solution)/shard_map/ppermute | solution.py:482
  12.6 8.5 %collective-permute-start.4 = (bf16[72,512]{1,0:T(8,128)(2,1)S(1)}, bf16[72,512]{1,0:T(8,128)(2,1)S(1)}, u32[]{:S(2)}, u32[]{:S(2)}) collective-permute-start(bf16[72,512]{1,0:T(8,128)(2,1)S(1)} %get-tuple-element.53), channel_id=1, source_target_pairs={{0,4},{4,0},{8,12},{12,8},{16,20},{20,16},{24,28},{28,24},{1,5},{5... | collective-permute-start | bytes 221192 | tf_op jit(solution)/shard_map/ppermute | solution.py:482
  14.3 1.6 %copy-start = (bf16[512,2048]{1,0:T(8,128)(2,1)S(1)}, bf16[512,2048]{1,0:T(8,128)(2,1)}, u32[]{:S(2)}) copy-start(bf16[512,2048]{1,0:T(8,128)(2,1)} %proj_ref.15) | copy-start | bytes 6291460
  15.8 0.9 copy-start.2
  16.8 1.0 %copy-start.4 = (bf16[512,512]{1,0:T(8,128)(2,1)S(1)}, bf16[512,512]{1,0:T(8,128)(2,1)}, u32[]{:S(2)}) copy-start(bf16[512,512]{1,0:T(8,128)(2,1)} %outw_ref.3) | copy-start | bytes 1572868
  17.8 9.2 %copy-start.1 = (bf16[512,2048]{1,0:T(8,128)(2,1)S(1)}, bf16[512,2048]{1,0:T(8,128)(2,1)}, u32[]{:S(2)}) copy-start(bf16[512,2048]{1,0:T(8,128)(2,1)} %proj_ref.15) | copy-start | bytes 6291460
  17.8 9.2 %copy-start.6 = (s32[1,3]{1,0:T(1,128)S(1)}, s32[1,3]{1,0:T(1,128)}, u32[]{:S(2)}) copy-start(s32[1,3]{1,0:T(1,128)} %lengths_ref.9) | copy-start | bytes 40
  19.2 4.6 %collective-permute-start.5 = (bf16[72,512]{1,0:T(8,128)(2,1)}, bf16[72,512]{1,0:T(8,128)(2,1)S(1)}, u32[]{:S(2)}, u32[]{:S(2)}) collective-permute-start(bf16[72,512]{1,0:T(8,128)(2,1)} %get-tuple-element.57), channel_id=1, source_target_pairs={{0,8},{4,12},{8,0},{12,4},{16,24},{20,28},{24,16},{28,20},{1,9},{5... | collective-permute-start | bytes 221192 | tf_op jit(solution)/shard_map/ppermute | solution.py:482
  19.2 5.3 %collective-permute-start.6 = (bf16[72,512]{1,0:T(8,128)(2,1)S(1)}, bf16[72,512]{1,0:T(8,128)(2,1)S(1)}, u32[]{:S(2)}, u32[]{:S(2)}) collective-permute-start(bf16[72,512]{1,0:T(8,128)(2,1)S(1)} %get-tuple-element.58), channel_id=1, source_target_pairs={{0,12},{4,8},{8,4},{12,0},{16,28},{20,24},{24,20},{28,16},{1,13},{... | collective-permute-start | bytes 221192 | tf_op jit(solution)/shard_map/ppermute | solution.py:482
  25.4 8.8 %collective-permute-start.9 = (bf16[256,512]{1,0:T(8,128)(2,1)S(1)}, bf16[256,512]{1,0:T(8,128)(2,1)S(1)}, u32[]{:S(2)}, u32[]{:S(2)}) collective-permute-start(bf16[256,512]{1,0:T(8,128)(2,1)S(1)} %get-tuple-element.59.normed_ref.own_ref.n0_ref.refs_0_), channel_id=1, source_target_pairs={{0,1},{1,0},{2,3},{3,2},{4,5},{5,4},{6,7},{7,6},{8,9},{9,8},{10,11... | collective-permute-start | bytes 786440 | tf_op jit(solution)/shard_map/ppermute | solution.py:467
  25.5 8.7 %collective-permute-start.7 = (bf16[256,512]{1,0:T(8,128)(2,1)S(1)}, bf16[256,512]{1,0:T(8,128)(2,1)S(1)}, u32[]{:S(2)}, u32[]{:S(2)}) collective-permute-start(bf16[256,512]{1,0:T(8,128)(2,1)S(1)} %get-tuple-element.59.normed_ref.own_ref.n0_ref.refs_0_), channel_id=1, source_target_pairs={{0,2},{1,3},{2,0},{3,1},{4,6},{5,7},{6,4},{7,5},{8,10},{9,11},{10,... | collective-permute-start | bytes 786440 | tf_op jit(solution)/shard_map/ppermute | solution.py:467
  34.2 1.5 %collective-permute-start.8 = (bf16[256,512]{1,0:T(8,128)(2,1)S(1)}, bf16[256,512]{1,0:T(8,128)(2,1)S(1)}, u32[]{:S(2)}, u32[]{:S(2)}) collective-permute-start(bf16[256,512]{1,0:T(8,128)(2,1)S(1)} %collective-permute-done.7.far_ref.n2_ref.refs_2_), channel_id=1, source_target_pairs={{0,1},{1,0},{2,3},{3,2},{4,5},{5,4},{6,7},{7,6},{8,9},{9,8},{10,11... | collective-permute-start | bytes 786440 | tf_op jit(solution)/shard_map/ppermute | solution.py:467
  35.7 4.5 %copy-start.3 = (bf16[256,512]{1,0:T(8,128)(2,1)S(1)}, bf16[256,512]{1,0:T(8,128)(2,1)}, u32[]{:S(2)}) copy-start(bf16[256,512]{1,0:T(8,128)(2,1)} %cot_ref.5) | copy-start | bytes 786436
  35.7 4.5 %copy-start.5 = (bf16[512,512]{1,0:T(8,128)(2,1)S(1)}, bf16[512,512]{1,0:T(8,128)(2,1)}, u32[]{:S(2)}) copy-start(bf16[512,512]{1,0:T(8,128)(2,1)} %outw_ref.3) | copy-start | bytes 1572868
  36.7 5.6 %collective-permute-start.10 = (bf16[256,128]{1,0:T(8,128)(2,1)S(1)}, bf16[256,128]{1,0:T(8,128)(2,1)S(1)}, u32[]{:S(2)}, u32[]{:S(2)}) collective-permute-start(bf16[256,128]{1,0:T(8,128)(2,1)S(1)} %get-tuple-element.70), channel_id=1, source_target_pairs={{0,1},{1,0},{2,3},{3,2},{4,5},{5,4},{6,7},{7,6},{8,9},{9,8},{10,11... | collective-permute-start | bytes 196616 | tf_op jit(solution)/shard_map/ppermute | solution.py:467
  37.8 5.1 %collective-permute-start.11 = (bf16[256,128]{1,0:T(8,128)(2,1)S(1)}, bf16[256,128]{1,0:T(8,128)(2,1)S(1)}, u32[]{:S(2)}, u32[]{:S(2)}) collective-permute-start(bf16[256,128]{1,0:T(8,128)(2,1)S(1)} %get-tuple-element.71), channel_id=1, source_target_pairs={{0,2},{1,3},{2,0},{3,1},{4,6},{5,7},{6,4},{7,5},{8,10},{9,11},{10,... | collective-permute-start | bytes 196616 | tf_op jit(solution)/shard_map/ppermute | solution.py:467
  40.2 4.0 %collective-permute-start.12 = (bf16[256,128]{1,0:T(8,128)(2,1)S(1)}, bf16[256,128]{1,0:T(8,128)(2,1)S(1)}, u32[]{:S(2)}, u32[]{:S(2)}) collective-permute-start(bf16[256,128]{1,0:T(8,128)(2,1)S(1)} %get-tuple-element.72), channel_id=1, source_target_pairs={{0,3},{1,2},{2,1},{3,0},{4,7},{5,6},{6,5},{7,4},{8,11},{9,10},{10,... | collective-permute-start | bytes 196616 | tf_op jit(solution)/shard_map/ppermute | solution.py:467
  41.4 2.9 %collective-permute-start.16 = (bf16[512,512]{1,0:T(8,128)(2,1)S(1)}, bf16[512,512]{1,0:T(8,128)(2,1)S(1)}, u32[]{:S(2)}, u32[]{:S(2)}) collective-permute-start(bf16[512,512]{1,0:T(8,128)(2,1)S(1)} %get-tuple-element.81), channel_id=1, source_target_pairs={{0,1},{1,0},{2,3},{3,2},{4,5},{5,4},{6,7},{7,6},{8,9},{9,8},{10,11... | collective-permute-start | bytes 1572872 | tf_op jit(solution)/shard_map/ppermute | solution.py:467
  44.4 10.0 %collective-permute-start.17 = (bf16[512,256]{1,0:T(8,128)(2,1)S(1)}, bf16[512,256]{1,0:T(8,128)(2,1)S(1)}, u32[]{:S(2)}, u32[]{:S(2)}) collective-permute-start(bf16[512,256]{1,0:T(8,128)(2,1)S(1)} %get-tuple-element.83), channel_id=1, source_target_pairs={{0,2},{1,3},{2,0},{3,1},{4,6},{5,7},{6,4},{7,5},{8,10},{9,11},{10,... | collective-permute-start | bytes 786440 | tf_op jit(solution)/shard_map/ppermute | solution.py:467
  49.5 8.2 %collective-permute-start.14 = (bf16[256,384]{1,0:T(8,128)(2,1)S(1)}, bf16[256,384]{1,0:T(8,128)(2,1)S(1)}, u32[]{:S(2)}, u32[]{:S(2)}) collective-permute-start(bf16[256,384]{1,0:T(8,128)(2,1)S(1)} %get-tuple-element.76.refs_6_), channel_id=1, source_target_pairs={{0,2},{1,3},{2,0},{3,1},{4,6},{5,7},{6,4},{7,5},{8,10},{9,11},{10,... | collective-permute-start | bytes 589832 | tf_op jit(solution)/shard_map/ppermute | solution.py:467
  51.0 9.7 %collective-permute-start.15 = (bf16[256,384]{1,0:T(8,128)(2,1)S(1)}, bf16[256,384]{1,0:T(8,128)(2,1)S(1)}, u32[]{:S(2)}, u32[]{:S(2)}) collective-permute-start(bf16[256,384]{1,0:T(8,128)(2,1)S(1)} %get-tuple-element.77.refs_7_), channel_id=1, source_target_pairs={{0,3},{1,2},{2,1},{3,0},{4,7},{5,6},{6,5},{7,4},{8,11},{9,10},{10,... | collective-permute-start | bytes 589832 | tf_op jit(solution)/shard_map/ppermute | solution.py:467
  53.6 18.0 %collective-permute-start.13 = (bf16[256,384]{1,0:T(8,128)(2,1)S(1)}, bf16[256,384]{1,0:T(8,128)(2,1)S(1)}, u32[]{:S(2)}, u32[]{:S(2)}) collective-permute-start(bf16[256,384]{1,0:T(8,128)(2,1)S(1)} %get-tuple-element.75.refs_5_), channel_id=1, source_target_pairs={{0,1},{1,0},{2,3},{3,2},{4,5},{5,4},{6,7},{7,6},{8,9},{9,8},{10,11... | collective-permute-start | bytes 589832 | tf_op jit(solution)/shard_map/ppermute | solution.py:467
  55.2 9.7 %collective-permute-start.18 = (bf16[256,640]{1,0:T(8,128)(2,1)S(1)}, bf16[256,640]{1,0:T(8,128)(2,1)S(1)}, u32[]{:S(2)}, u32[]{:S(2)}) collective-permute-start(bf16[256,640]{1,0:T(8,128)(2,1)S(1)} %get-tuple-element.85), channel_id=1, source_target_pairs={{0,4},{4,0},{8,12},{12,8},{16,20},{20,16},{24,28},{28,24},{1,5},{5... | collective-permute-start | bytes 983048 | tf_op jit(solution)/shard_map/ppermute | solution.py:482
  65.0 7.2 %collective-permute-start.19 = (bf16[64,640]{1,0:T(8,128)(2,1)S(1)}, bf16[64,640]{1,0:T(8,128)(2,1)S(1)}, u32[]{:S(2)}, u32[]{:S(2)}) collective-permute-start(bf16[64,640]{1,0:T(8,128)(2,1)S(1)} %get-tuple-element.87), channel_id=1, source_target_pairs={{0,8},{4,12},{8,0},{12,4},{16,24},{20,28},{24,16},{28,20},{1,9},{5... | collective-permute-start | bytes 245768 | tf_op jit(solution)/shard_map/ppermute | solution.py:482
  69.1 8.5 %collective-permute-start.20 = (bf16[64,640]{1,0:T(8,128)(2,1)S(1)}, bf16[64,640]{1,0:T(8,128)(2,1)S(1)}, u32[]{:S(2)}, u32[]{:S(2)}) collective-permute-start(bf16[64,640]{1,0:T(8,128)(2,1)S(1)} %get-tuple-element.88), channel_id=1, source_target_pairs={{0,16},{4,20},{8,24},{12,28},{16,0},{20,4},{24,8},{28,12},{1,17},{... | collective-permute-start | bytes 245768 | tf_op jit(solution)/shard_map/ppermute | solution.py:482
  69.3 8.4 %collective-permute-start.21 = (bf16[64,640]{1,0:T(8,128)(2,1)S(1)}, bf16[64,640]{1,0:T(8,128)(2,1)S(1)}, u32[]{:S(2)}, u32[]{:S(2)}) collective-permute-start(bf16[64,640]{1,0:T(8,128)(2,1)S(1)} %get-tuple-element.89), channel_id=1, source_target_pairs={{0,24},{4,28},{8,16},{12,20},{16,8},{20,12},{24,0},{28,4},{1,25},{... | collective-permute-start | bytes 245768 | tf_op jit(solution)/shard_map/ppermute | solution.py:482
  78.8 18.1 %all-to-all-start = ((bf16[8,64,512]{2,1,0:T(8,128)(2,1)}), bf16[8,64,512]{2,1,0:T(8,128)(2,1)S(1)}, u32[]{:S(2)}, u32[]{:S(2)}) async-start(bf16[8,64,512]{2,1,0:T(8,128)(2,1)} %bitcast.4), calls=%async_computation | async-start | bytes 1048576 | tf_op jit(solution)/shard_map/all_to_all | solution.py:486
  82.6 4.5 %collective-permute-start.24 = (bf16[64,640]{1,0:T(8,128)(2,1)S(1)}, bf16[64,640]{1,0:T(8,128)(2,1)S(1)}, u32[]{:S(2)}, u32[]{:S(2)}) collective-permute-start(bf16[64,640]{1,0:T(8,128)(2,1)S(1)} %sum.1._.w0_ref), channel_id=1, source_target_pairs={{0,3},{1,2},{2,1},{3,0},{4,7},{5,6},{6,5},{7,4},{8,11},{9,10},{10,... | collective-permute-start | bytes 245768 | tf_op jit(solution)/shard_map/ppermute | solution.py:467
  83.3 5.8 %collective-permute-start.23 = (bf16[64,640]{1,0:T(8,128)(2,1)S(1)}, bf16[64,640]{1,0:T(8,128)(2,1)S(1)}, u32[]{:S(2)}, u32[]{:S(2)}) collective-permute-start(bf16[64,640]{1,0:T(8,128)(2,1)S(1)} %sum.1._.w0_ref), channel_id=1, source_target_pairs={{0,2},{1,3},{2,0},{3,1},{4,6},{5,7},{6,4},{7,5},{8,10},{9,11},{10,... | collective-permute-start | bytes 245768 | tf_op jit(solution)/shard_map/ppermute | solution.py:467
  84.3 4.8 %collective-permute-start.22 = (bf16[64,640]{1,0:T(8,128)(2,1)S(1)}, bf16[64,640]{1,0:T(8,128)(2,1)S(1)}, u32[]{:S(2)}, u32[]{:S(2)}) collective-permute-start(bf16[64,640]{1,0:T(8,128)(2,1)S(1)} %sum.1._.w0_ref), channel_id=1, source_target_pairs={{0,1},{1,0},{2,3},{3,2},{4,5},{5,4},{6,7},{7,6},{8,9},{9,8},{10,11... | collective-permute-start | bytes 245768 | tf_op jit(solution)/shard_map/ppermute | solution.py:467

commit v12 on v11

--- a/solution.py
+++ b/solution.py
@@ -208,8 +208,11 @@
         attend(query_ref, key, value, shared_factor(block, me, rows, lengths_ref), acc_ref)
 
 
-def own_body(me_ref, lengths_ref, normed_ref, proj_ref, gate_ref, slope_ref, query_ref, acc_ref):
+def own_body(
+    me_ref, lengths_ref, normed_ref, proj_ref, gate_ref, slope_ref, query_ref, acc_ref, copy_ref
+):
     rows, width = normed_ref.shape
+    copy_ref[...] = normed_ref[...]
     me = me_ref[0]
     preact = mm(normed_ref[...], proj_ref[...])
     gate, slope = silu_both(preact[:, :width])
@@ -466,10 +469,6 @@
     def hop(value, step):
         return lax.ppermute(value, "ctx", [(i, i ^ step) for i in range(cycle)])
 
-    def gather(value):
-        near, far = hop(value, 1), hop(value, 2)
-        return near, far, hop(far, 1)
-
     def exchange(values):
         return [values[0]] + [hop(values[step], step) for step in (2, 3, 1)]
 
@@ -517,11 +516,13 @@
         functools.partial(place_body, owners, capacity, stride),
         "place", [square, square, ((1, owners * capacity), jnp.int32)], [], arrived,
     )
-    near, far, cross = gather(normed)
-    gate, slope, query, partial = call(
-        own_body, "own_rows", [square, wide, square, wide],
+    far = hop(normed, 2)
+    cross = hop(far, 1)
+    gate, slope, query, partial, normed_copy = call(
+        own_body, "own_rows", [square, wide, square, wide, square],
         [me, lengths], [normed, proj_weight], flops=10**10, vmem=16,
     )
+    near = hop(normed_copy, 1)
     (partial,) = call(
         middle_body, "middle", [wide], [me, lengths], [near, far, proj_weight, query, partial],
         flops=10**10, vmem=16,
@@ -591,11 +592,12 @@
         )
         summed_parts = [halves[0]] + [dp_hop(halves[j], 2 * j) for j in range(1, pairs)]
     else:
+        halves = weight_parts
         summed_parts = [swap_whole(weight_parts[0]).reshape(owners, share, columns)]
-    (mine,) = call(sum_body, "sum", [((share, columns), BF16)], [], summed_parts)
+    (mine,) = call(sum_body, "sum", [((share, columns), BF16)], [], summed_parts, flops=10**11)
     (back,) = call(
         functools.partial(spread_body, blocks), "spread", [((owners * capacity, width), BF16)],
-        [mask], [grad_owned, landing], far=[mine],
+        [mask], [grad_owned, landing], far=halves[:1],
     )
     returned = swap_whole(back)
     w1, w2, w3 = (hop(mine, step) for step in range(1, cycle))

time: 99.5 us -> 92.6 us (0.931); the launches traced: 98.1 us -> 92.2 us
  waiting for transfers between devices: 35.9 us -> 26.8 us
  starting transfers between devices: 35.2 us -> 38.3 us
    ppermute x11, waiting for transfers between devices: 12.7 us -> 6.34 us  [dp_hop(): return lax.ppermute(value, 'dp', [(i, i ^ step) for i in range(owners)])]
    all_to_all x1, starting transfers between devices: 3.74 us -> 6.27 us  [swap_whole(): lax.all_to_all(split, 'dp', split_axis=0, concat_axis=0, tiled=True)]
    all_to_all x1, waiting for transfers between devices: 6.92 us -> 5.42 us  [swap_whole(): lax.all_to_all(split, 'dp', split_axis=0, concat_axis=0, tiled=True)]
    ppermute x14, waiting for transfers between devices: 16.2 us -> 15 us  [hop(): return lax.ppermute(value, 'ctx', [(i, i ^ step) for i in range(cycle)])]
    ppermute x11, starting transfers between devices: 20.6 us -> 21.7 us  [dp_hop(): return lax.ppermute(value, 'dp', [(i, i ^ step) for i in range(owners)])]
    unnamed x20 -> x24, local copies, waits for them, and re-layouts: 5.9 us -> 5.91 us
  transfers between devices with their start and end apart: 26 -> 26, of which waited for: 13 -> 12; matrix products, arithmetic and copies ran while one was open for 0% -> 0% of each run, Pallas kernels for 16% -> 18%
where the time goes in v12:
time: 92.6 us; the launch traced here: 92.2 us
  starting transfers between devices  38.3 us (41%)
  waiting for transfers between devices  26.8 us (29%)
  Pallas kernels  20.3 us (22%)
  local copies, waits for them, and re-layouts  5.91 us (6%)
    ppermute x11, starting transfers between devices, dp_hop(): return lax.ppermute(value, 'dp', [(i, i ^ step) for i in range(owners)])  21.7 us
    pallas_call x21, Pallas kernels, call(): pl.pallas_call(body, name=name, out_shape=[jax.ShapeDtypeStruct(s, d) for...  20.3 us
    ppermute x14, waiting for transfers between devices, hop(): return lax.ppermute(value, 'ctx', [(i, i ^ step) for i in range(cycle)])  15 us
    ppermute x14, starting transfers between devices, hop(): return lax.ppermute(value, 'ctx', [(i, i ^ step) for i in range(cycle)])  10.3 us
    ppermute x11, waiting for transfers between devices, dp_hop(): return lax.ppermute(value, 'dp', [(i, i ^ step) for i in range(owners)])  6.34 us
    all_to_all x1, starting transfers between devices, swap_whole(): lax.all_to_all(split, 'dp', split_axis=0, concat_axis=0, tiled=True)  6.27 us
    unnamed x24, local copies, waits for them, and re-layouts  5.91 us
    all_to_all x1, waiting for transfers between devices, swap_whole(): lax.all_to_all(split, 'dp', split_axis=0, concat_axis=0, tiled=True)  5.42 us
  transfers between devices with their start and end apart: 26, of which 12 were waited for; matrix products, arithmetic and copies ran while one was open for 0% of the time, Pallas kernels for 18%

profile of v12, /device:TPU:0, one launch (start us, length us, event | category | flops | bytes accessed | tf_op | source)
XLA Modules:
  0.0 92.2 jit_solution(15828836905106033301)
XLA Ops:
  0.6 0.9 %copy-done.9 = bf16[256,512]{1,0:T(8,128)(2,1)S(1)} copy-done((bf16[256,512]{1,0:T(8,128)(2,1)S(1)}, bf16[256,512]{1,0:T(8,128)(2,1)}, u32[]{:S(2)}) %copy-start.9) | copy-done | bytes 262168
  1.6 0.7 copy-done.10
  2.3 0.7 copy-done.11
  2.9 0.6 pack.1
  3.6 4.1 %collective-permute-start = (bf16[72,512]{1,0:T(8,128)(2,1)S(1)}, bf16[72,512]{1,0:T(8,128)(2,1)S(1)}, u32[]{:S(2)}, u32[]{:S(2)}) collective-permute-start(bf16[72,512]{1,0:T(8,128)(2,1)S(1)} %get-tuple-element.50), channel_id=1, source_target_pairs={{0,16},{4,20},{8,24},{12,28},{16,0},{20,4},{24,8},{28,12},{1,17},{... | collective-permute-start | bytes 221192 | tf_op jit(solution)/shard_map/ppermute | solution.py:481
  7.7 1.3 %collective-permute-start.1 = (bf16[72,512]{1,0:T(8,128)(2,1)S(1)}, bf16[72,512]{1,0:T(8,128)(2,1)S(1)}, u32[]{:S(2)}, u32[]{:S(2)}) collective-permute-start(bf16[72,512]{1,0:T(8,128)(2,1)S(1)} %get-tuple-element.51), channel_id=1, source_target_pairs={{0,20},{4,16},{8,28},{12,24},{16,4},{20,0},{24,12},{28,8},{1,21},{... | collective-permute-start | bytes 221192 | tf_op jit(solution)/shard_map/ppermute | solution.py:481
  9.0 3.6 %collective-permute-start.2 = (bf16[72,512]{1,0:T(8,128)(2,1)S(1)}, bf16[72,512]{1,0:T(8,128)(2,1)S(1)}, u32[]{:S(2)}, u32[]{:S(2)}) collective-permute-start(bf16[72,512]{1,0:T(8,128)(2,1)S(1)} %get-tuple-element.52), channel_id=1, source_target_pairs={{0,24},{4,28},{8,16},{12,20},{16,8},{20,12},{24,0},{28,4},{1,25},{... | collective-permute-start | bytes 221192 | tf_op jit(solution)/shard_map/ppermute | solution.py:481
  12.6 1.7 %collective-permute-start.4 = (bf16[72,512]{1,0:T(8,128)(2,1)S(1)}, bf16[72,512]{1,0:T(8,128)(2,1)S(1)}, u32[]{:S(2)}, u32[]{:S(2)}) collective-permute-start(bf16[72,512]{1,0:T(8,128)(2,1)S(1)} %get-tuple-element.54), channel_id=1, source_target_pairs={{0,4},{4,0},{8,12},{12,8},{16,20},{20,16},{24,28},{28,24},{1,5},{5... | collective-permute-start | bytes 221192 | tf_op jit(solution)/shard_map/ppermute | solution.py:481
  14.3 1.6 %copy-done = bf16[512,2048]{1,0:T(8,128)(2,1)S(1)} copy-done((bf16[512,2048]{1,0:T(8,128)(2,1)S(1)}, bf16[512,2048]{1,0:T(8,128)(2,1)}, u32[]{:S(2)}) %copy-start) | copy-done | bytes 2097176
  15.9 0.9 %copy-done.2 = bf16[256,512]{1,0:T(8,128)(2,1)S(1)} copy-done((bf16[256,512]{1,0:T(8,128)(2,1)S(1)}, bf16[256,512]{1,0:T(8,128)(2,1)}, u32[]{:S(2)}) %copy-start.2) | copy-done | bytes 262168
  16.8 1.0 %copy-done.4 = bf16[512,512]{1,0:T(8,128)(2,1)S(1)} copy-done((bf16[512,512]{1,0:T(8,128)(2,1)S(1)}, bf16[512,512]{1,0:T(8,128)(2,1)}, u32[]{:S(2)}) %copy-start.4) | copy-done | bytes 524312
  18.2 1.0 %pack_rest.1 = (bf16[72,512]{1,0:T(8,128)(2,1)}, bf16[72,512]{1,0:T(8,128)(2,1)S(1)}) custom-call(s32[1,256]{1,0:T(1,128)S(1)} %get-tuple-element.55.owner_ref, s32[1,256]{1,0:T(1,128)S(1)} %get-tuple-element.56.slot_ref, bf16[256,512]{1,0:T(8,128)(2,1)S(1)} %get-tuple-element.57.tokens_ref, f32[256,512]{1,0:T(8,128)S(1)} %early.1._.grad_ref), custom_call_target="tpu_custom_call" | custom-call | flops 100000000 | bytes 1048576 | tf_op jit(solution)/shard_map/pack_rest/pallas_call | solution.py:22
  19.2 1.8 %collective-permute-start.6 = (bf16[72,512]{1,0:T(8,128)(2,1)S(1)}, bf16[72,512]{1,0:T(8,128)(2,1)S(1)}, u32[]{:S(2)}, u32[]{:S(2)}) collective-permute-start(bf16[72,512]{1,0:T(8,128)(2,1)S(1)} %get-tuple-element.59), channel_id=1, source_target_pairs={{0,12},{4,8},{8,4},{12,0},{16,28},{20,24},{24,20},{28,16},{1,13},{... | collective-permute-start | bytes 221192 | tf_op jit(solution)/shard_map/ppermute | solution.py:481
  21.1 2.7 %collective-permute-done.5.refs_6_ = bf16[72,512]{1,0:T(8,128)(2,1)S(1)} collective-permute-done((bf16[72,512]{1,0:T(8,128)(2,1)}, bf16[72,512]{1,0:T(8,128)(2,1)S(1)}, u32[]{:S(2)}, u32[]{:S(2)}) %collective-permute-start.5) | collective-permute-done | bytes 73760 | tf_op jit(solution)/shard_map/ppermute | solution.py:481
  23.8 0.8 collective-permute-done.6.refs_7_
  24.6 0.8 place.1
  25.4 1.6 %collective-permute-start.7 = (bf16[256,512]{1,0:T(8,128)(2,1)S(1)}, bf16[256,512]{1,0:T(8,128)(2,1)S(1)}, u32[]{:S(2)}, u32[]{:S(2)}) collective-permute-start(bf16[256,512]{1,0:T(8,128)(2,1)S(1)} %get-tuple-element.60.normed_ref.own_ref.n0_ref.refs_0_), channel_id=1, source_target_pairs={{0,2},{1,3},{2,0},{3,1},{4,6},{5,7},{6,4},{7,5},{8,10},{9,11},{10,... | collective-permute-start | bytes 786440 | tf_op jit(solution)/shard_map/ppermute | solution.py:470
  27.0 2.2 %own_rows.1 = (bf16[256,512]{1,0:T(8,128)(2,1)S(1)}, f32[256,512]{1,0:T(8,128)S(1)}, bf16[256,512]{1,0:T(8,128)(2,1)S(1)}, f32[256,512]{1,0:T(8,128)S(1)}, bf16[256,512]{1,0:T(8,128)(2,1)S(1)}) custom-call(s32[1]{0:T(128)} %bitcast.me_ref, s32[1,3]{1,0:T(1,128)S(1)} %copy-done.8, bf16[256,512]{1,0:T(8,128)(2,1)S(1)} %get-tuple-element.60.normed_ref.own_ref.n0_ref.refs_0_, ...), custom_call_target="tpu_custom_call" | custom-call | flops 10000000000 | bytes 1048576 | tf_op jit(solution)/shard_map/own_rows/pallas_call | solution.py:22
  29.3 2.6 %collective-permute-done.7.far_ref.n2_ref.refs_2_ = bf16[256,512]{1,0:T(8,128)(2,1)S(1)} collective-permute-done((bf16[256,512]{1,0:T(8,128)(2,1)S(1)}, bf16[256,512]{1,0:T(8,128)(2,1)S(1)}, u32[]{:S(2)}, u32[]{:S(2)}) %collective-permute-start.7) | collective-permute-done | bytes 262176 | tf_op jit(solution)/shard_map/ppermute | solution.py:470
  31.9 0.6 middle.1.partial_ref
  32.4 0.9 %collective-permute-done.8.cross_ref.n3_ref.refs_3_ = bf16[256,512]{1,0:T(8,128)(2,1)S(1)} collective-permute-done((bf16[256,512]{1,0:T(8,128)(2,1)S(1)}, bf16[256,512]{1,0:T(8,128)(2,1)S(1)}, u32[]{:S(2)}, u32[]{:S(2)}) %collective-permute-start.8) | collective-permute-done | bytes 262176 | tf_op jit(solution)/shard_map/ppermute | solution.py:470
  33.4 1.0 %forward.1 = (f32[256,512]{1,0:T(8,128)S(1)}, bf16[256,128]{1,0:T(8,128)(2,1)S(1)}, bf16[256,128]{1,0:T(8,128)(2,1)S(1)}, bf16[256,128]{1,0:T(8,128)(2,1)S(1)}, bf16[256,128]{1,0:T(8,128)(2,1)S(1)}) custom-call(s32[1]{0:T(128)} %bitcast.me_ref, s32[1,3]{1,0:T(1,128)S(1)} %copy-done.8, bf16[256,512]{1,0:T(8,128)(2,1)S(1)} %collective-permute-done.8.cross_ref.n3_ref.refs_3_, ...), custom_call_target="tpu_custom_call" | custom-call | flops 100000000 | bytes 1048576 | tf_op jit(solution)/shard_map/forward/pallas_call | solution.py:22
  34.6 3.7 %collective-permute-start.11 = (bf16[256,128]{1,0:T(8,128)(2,1)S(1)}, bf16[256,128]{1,0:T(8,128)(2,1)S(1)}, u32[]{:S(2)}, u32[]{:S(2)}) collective-permute-start(bf16[256,128]{1,0:T(8,128)(2,1)S(1)} %get-tuple-element.73), channel_id=1, source_target_pairs={{0,2},{1,3},{2,0},{3,1},{4,6},{5,7},{6,4},{7,5},{8,10},{9,11},{10,... | collective-permute-start | bytes 196616 | tf_op jit(solution)/shard_map/ppermute | solution.py:470
  38.3 1.1 %side.1 = (bf16[512,512]{1,0:T(8,128)(2,1)S(1)}, bf16[512,512]{1,0:T(8,128)(2,1)S(1)}, f32[256,512]{1,0:T(8,128)S(1)}, bf16[256,512]{1,0:T(8,128)(2,1)}) custom-call(s32[1]{0:T(128)} %bitcast.me_ref, bf16[256,512]{1,0:T(8,128)(2,1)S(1)} %get-tuple-element.60.normed_ref.own_ref.n0_ref.refs_0_, f32[256,512]{1,0:T(8,128)S(1)} %get-tuple-element.65.normed_ref, ...), custom_call_target="tpu_custom_call" | custom-call | flops 100000000 | bytes 1048576 | tf_op jit(solution)/shard_map/side/pallas_call | solution.py:22
  39.5 0.8 heads.1
  40.6 2.0 %collective-permute-done.12.g3_ref = bf16[256,128]{1,0:T(8,128)(2,1)S(1)} collective-permute-done((bf16[256,128]{1,0:T(8,128)(2,1)S(1)}, bf16[256,128]{1,0:T(8,128)(2,1)S(1)}, u32[]{:S(2)}, u32[]{:S(2)}) %collective-permute-start.12) | collective-permute-done | bytes 65568 | tf_op jit(solution)/shard_map/ppermute | solution.py:470
  43.3 4.4 %backward_far.1 = (bf16[256,384]{1,0:T(8,128)(2,1)S(1)}, bf16[256,384]{1,0:T(8,128)(2,1)S(1)}, f32[1024,384]{1,0:T(8,128)S(1)}) custom-call(s32[1]{0:T(128)} %bitcast.me_ref, s32[1,3]{1,0:T(1,128)S(1)} %copy-done.8, bf16[1024,384]{1,0:T(8,128)(2,1)S(1)} %get-tuple-element.69.part_ref, f32[1024,384]{1,0:T(8,128)S(1)} %get-tuple-element.70.slope_ref, ...), custom_call_target="tpu_custom_call" | custom-call | flops 10000000000 | bytes 1048576 | tf_op jit(solution)/shard_map/backward_far/pallas_call | solution.py:22
  47.7 1.0 %collective-permute-start.14 = (bf16[256,384]{1,0:T(8,128)(2,1)S(1)}, bf16[256,384]{1,0:T(8,128)(2,1)S(1)}, u32[]{:S(2)}, u32[]{:S(2)}) collective-permute-start(bf16[256,384]{1,0:T(8,128)(2,1)S(1)} %get-tuple-element.78.refs_6_), channel_id=1, source_target_pairs={{0,2},{1,3},{2,0},{3,1},{4,6},{5,7},{6,4},{7,5},{8,10},{9,11},{10,... | collective-permute-start | bytes 589832 | tf_op jit(solution)/shard_map/ppermute | solution.py:470
  48.6 0.7 collective-permute-start.15
  49.3 1.9 %backward_rest.1 = (bf16[256,384]{1,0:T(8,128)(2,1)S(1)}, bf16[256,384]{1,0:T(8,128)(2,1)S(1)}) custom-call(s32[1]{0:T(128)} %bitcast.me_ref, s32[1,3]{1,0:T(1,128)S(1)} %copy-done.8, bf16[1024,384]{1,0:T(8,128)(2,1)S(1)} %get-tuple-element.69.part_ref, f32[1024,384]{1,0:T(8,128)S(1)} %get-tuple-element.70.slope_ref, bf16[1024,128]{1,0:T(8,128)(2,1)S(1)} %collect.1.grad_ref, ...), custom_call_target="tpu_custom_call" | custom-call | flops 100000000 | bytes 1048576 | tf_op jit(solution)/shard_map/backward_rest/pallas_call | solution.py:22
  51.2 0.6 collective-permute-start.13
  51.9 0.8 weights.1
  52.7 1.8 %collective-permute-start.18 = (bf16[256,640]{1,0:T(8,128)(2,1)S(1)}, bf16[256,640]{1,0:T(8,128)(2,1)S(1)}, u32[]{:S(2)}, u32[]{:S(2)}) collective-permute-start(bf16[256,640]{1,0:T(8,128)(2,1)S(1)} %get-tuple-element.87), channel_id=1, source_target_pairs={{0,4},{4,0},{8,12},{12,8},{16,20},{20,16},{24,28},{28,24},{1,5},{5... | collective-permute-start | bytes 983048 | tf_op jit(solution)/shard_map/ppermute | solution.py:481
  54.5 1.4 %collective-permute-done.14.far_ref = bf16[256,384]{1,0:T(8,128)(2,1)S(1)} collective-permute-done((bf16[256,384]{1,0:T(8,128)(2,1)S(1)}, bf16[256,384]{1,0:T(8,128)(2,1)S(1)}, u32[]{:S(2)}, u32[]{:S(2)}) %collective-permute-start.14) | collective-permute-done | bytes 196640 | tf_op jit(solution)/shard_map/ppermute | solution.py:470
  55.9 3.2 %collective-permute-done.15.cross_ref = bf16[256,384]{1,0:T(8,128)(2,1)S(1)} collective-permute-done((bf16[256,384]{1,0:T(8,128)(2,1)S(1)}, bf16[256,384]{1,0:T(8,128)(2,1)S(1)}, u32[]{:S(2)}, u32[]{:S(2)}) %collective-permute-start.15) | collective-permute-done | bytes 196640 | tf_op jit(solution)/shard_map/ppermute | solution.py:470
  59.1 0.5 input_far.1.partial_ref._
  59.6 2.8 %collective-permute-done.18.came_ref = bf16[256,640]{1,0:T(8,128)(2,1)S(1)} collective-permute-done((bf16[256,640]{1,0:T(8,128)(2,1)S(1)}, bf16[256,640]{1,0:T(8,128)(2,1)S(1)}, u32[]{:S(2)}, u32[]{:S(2)}) %collective-permute-start.18) | collective-permute-done | bytes 327712 | tf_op jit(solution)/shard_map/ppermute | solution.py:481
  62.5 2.2 %collective-permute-start.19 = (bf16[64,640]{1,0:T(8,128)(2,1)S(1)}, bf16[64,640]{1,0:T(8,128)(2,1)S(1)}, u32[]{:S(2)}, u32[]{:S(2)}) collective-permute-start(bf16[64,640]{1,0:T(8,128)(2,1)S(1)} %get-tuple-element.89), channel_id=1, source_target_pairs={{0,8},{4,12},{8,0},{12,4},{16,24},{20,28},{24,16},{28,20},{1,9},{5... | collective-permute-start | bytes 245768 | tf_op jit(solution)/shard_map/ppermute | solution.py:481
  64.7 5.2 %collective-permute-start.20 = (bf16[64,640]{1,0:T(8,128)(2,1)S(1)}, bf16[64,640]{1,0:T(8,128)(2,1)S(1)}, u32[]{:S(2)}, u32[]{:S(2)}) collective-permute-start(bf16[64,640]{1,0:T(8,128)(2,1)S(1)} %get-tuple-element.90), channel_id=1, source_target_pairs={{0,16},{4,20},{8,24},{12,28},{16,0},{20,4},{24,8},{28,12},{1,17},{... | collective-permute-start | bytes 245768 | tf_op jit(solution)/shard_map/ppermute | solution.py:481
  70.0 0.7 input_grad.1.grad_ref
  70.6 1.1 %spread.1 = bf16[512,512]{1,0:T(8,128)(2,1)} custom-call(s32[1]{0:T(128)} %bitcast.1.mask_ref.dp_ref, bf16[256,512]{1,0:T(8,128)(2,1)S(1)} %input_grad.1.grad_ref, s32[1,512]{1,0:T(1,128)S(1)} %get-tuple-element.81.landing_ref, bf16[64,640]{1,0:T(8,128)(2,1)S(1)} %get-tuple-element.88._.refs_0_), custom_call_target="tpu_custom_call" | custom-call | flops 100000000 | bytes 1048576 | tf_op jit(solution)/shard_map/spread/pallas_call | solution.py:22
  71.8 6.3 %all-to-all-start = ((bf16[8,64,512]{2,1,0:T(8,128)(2,1)}), bf16[8,64,512]{2,1,0:T(8,128)(2,1)S(1)}, u32[]{:S(2)}, u32[]{:S(2)}) async-start(bf16[8,64,512]{2,1,0:T(8,128)(2,1)} %bitcast.4), calls=%async_computation | async-start | bytes 1048576 | tf_op jit(solution)/shard_map/all_to_all | solution.py:485
  78.2 1.7 %collective-permute-start.23 = (bf16[64,640]{1,0:T(8,128)(2,1)S(1)}, bf16[64,640]{1,0:T(8,128)(2,1)S(1)}, u32[]{:S(2)}, u32[]{:S(2)}) collective-permute-start(bf16[64,640]{1,0:T(8,128)(2,1)S(1)} %sum.1.w0_ref), channel_id=1, source_target_pairs={{0,2},{1,3},{2,0},{3,1},{4,6},{5,7},{6,4},{7,5},{8,10},{9,11},{10,... | collective-permute-start | bytes 245768 | tf_op jit(solution)/shard_map/ppermute | solution.py:470
  80.1 2.7 %collective-permute-done.24.w3_ref = bf16[64,640]{1,0:T(8,128)(2,1)S(1)} collective-permute-done((bf16[64,640]{1,0:T(8,128)(2,1)S(1)}, bf16[64,640]{1,0:T(8,128)(2,1)S(1)}, u32[]{:S(2)}, u32[]{:S(2)}) %collective-permute-start.24) | collective-permute-done | bytes 81952 | tf_op jit(solution)/shard_map/ppermute | solution.py:470
  82.7 1.9 %collective-permute-done.23.w2_ref = bf16[64,640]{1,0:T(8,128)(2,1)S(1)} collective-permute-done((bf16[64,640]{1,0:T(8,128)(2,1)S(1)}, bf16[64,640]{1,0:T(8,128)(2,1)S(1)}, u32[]{:S(2)}, u32[]{:S(2)}) %collective-permute-start.23) | collective-permute-done | bytes 81952 | tf_op jit(solution)/shard_map/ppermute | solution.py:470
  84.7 0.9 finish.1
  85.6 5.4 %all-to-all-done = bf16[8,64,512]{2,1,0:T(8,128)(2,1)S(1)} async-done(((bf16[8,64,512]{2,1,0:T(8,128)(2,1)}), bf16[8,64,512]{2,1,0:T(8,128)(2,1)S(1)}, u32[]{:S(2)}, u32[]{:S(2)}) %all-to-all-start) | async-done | bytes 524320 | tf_op jit(solution)/shard_map/all_to_all | solution.py:485
  91.0 1.2 %give_back.1 = bf16[256,512]{1,0:T(8,128)(2,1)} custom-call(s32[1]{0:T(128)} %bitcast.1.mask_ref.dp_ref, s32[1,256]{1,0:T(1,128)S(1)} %copy-done.7, bf16[512,512]{1,0:T(8,128)(2,1)S(1)} %bitcast.6), custom_call_target="tpu_custom_call" | custom-call | flops 100000000 | bytes 1048576 | tf_op jit(solution)/shard_map/give_back/pallas_call | solution.py:22
  (49 shorter events, 2.0 us)
Async XLA Ops:
  0.6 1.0 %copy-start.9 = (bf16[256,512]{1,0:T(8,128)(2,1)S(1)}, bf16[256,512]{1,0:T(8,128)(2,1)}, u32[]{:S(2)}) copy-start(bf16[256,512]{1,0:T(8,128)(2,1)} %tokens_hbm.1) | copy-start | bytes 786436
  1.6 0.7 copy-start.10
  2.3 0.7 copy-start.11
  3.6 14.6 %copy-start.6 = (s32[1,256]{1,0:T(1,128)}, s32[1,256]{1,0:T(1,128)S(1)}, u32[]{:S(2)}) copy-start(s32[1,256]{1,0:T(1,128)S(1)} %get-tuple-element.55.owner_ref) | copy-start | bytes 3076
  3.6 15.6 %collective-permute-start = (bf16[72,512]{1,0:T(8,128)(2,1)S(1)}, bf16[72,512]{1,0:T(8,128)(2,1)S(1)}, u32[]{:S(2)}, u32[]{:S(2)}) collective-permute-start(bf16[72,512]{1,0:T(8,128)(2,1)S(1)} %get-tuple-element.50), channel_id=1, source_target_pairs={{0,16},{4,20},{8,24},{12,28},{16,0},{20,4},{24,8},{28,12},{1,17},{... | collective-permute-start | bytes 221192 | tf_op jit(solution)/shard_map/ppermute | solution.py:481
  7.7 11.6 %collective-permute-start.1 = (bf16[72,512]{1,0:T(8,128)(2,1)S(1)}, bf16[72,512]{1,0:T(8,128)(2,1)S(1)}, u32[]{:S(2)}, u32[]{:S(2)}) collective-permute-start(bf16[72,512]{1,0:T(8,128)(2,1)S(1)} %get-tuple-element.51), channel_id=1, source_target_pairs={{0,20},{4,16},{8,28},{12,24},{16,4},{20,0},{24,12},{28,8},{1,21},{... | collective-permute-start | bytes 221192 | tf_op jit(solution)/shard_map/ppermute | solution.py:481
  9.0 12.1 %collective-permute-start.2 = (bf16[72,512]{1,0:T(8,128)(2,1)S(1)}, bf16[72,512]{1,0:T(8,128)(2,1)S(1)}, u32[]{:S(2)}, u32[]{:S(2)}) collective-permute-start(bf16[72,512]{1,0:T(8,128)(2,1)S(1)} %get-tuple-element.52), channel_id=1, source_target_pairs={{0,24},{4,28},{8,16},{12,20},{16,8},{20,12},{24,0},{28,4},{1,25},{... | collective-permute-start | bytes 221192 | tf_op jit(solution)/shard_map/ppermute | solution.py:481
  12.6 8.5 %collective-permute-start.3 = (bf16[72,512]{1,0:T(8,128)(2,1)S(1)}, bf16[72,512]{1,0:T(8,128)(2,1)S(1)}, u32[]{:S(2)}, u32[]{:S(2)}) collective-permute-start(bf16[72,512]{1,0:T(8,128)(2,1)S(1)} %get-tuple-element.53), channel_id=1, source_target_pairs={{0,28},{4,24},{8,20},{12,16},{16,12},{20,8},{24,4},{28,0},{1,29},{... | collective-permute-start | bytes 221192 | tf_op jit(solution)/shard_map/ppermute | solution.py:481
  12.6 8.5 %collective-permute-start.4 = (bf16[72,512]{1,0:T(8,128)(2,1)S(1)}, bf16[72,512]{1,0:T(8,128)(2,1)S(1)}, u32[]{:S(2)}, u32[]{:S(2)}) collective-permute-start(bf16[72,512]{1,0:T(8,128)(2,1)S(1)} %get-tuple-element.54), channel_id=1, source_target_pairs={{0,4},{4,0},{8,12},{12,8},{16,20},{20,16},{24,28},{28,24},{1,5},{5... | collective-permute-start | bytes 221192 | tf_op jit(solution)/shard_map/ppermute | solution.py:481
  14.3 1.6 %copy-start = (bf16[512,2048]{1,0:T(8,128)(2,1)S(1)}, bf16[512,2048]{1,0:T(8,128)(2,1)}, u32[]{:S(2)}) copy-start(bf16[512,2048]{1,0:T(8,128)(2,1)} %proj_ref.15) | copy-start | bytes 6291460
  15.9 0.9 %copy-start.2 = (bf16[256,512]{1,0:T(8,128)(2,1)S(1)}, bf16[256,512]{1,0:T(8,128)(2,1)}, u32[]{:S(2)}) copy-start(bf16[256,512]{1,0:T(8,128)(2,1)} %cot_ref.5) | copy-start | bytes 786436
  16.8 1.0 %copy-start.4 = (bf16[512,512]{1,0:T(8,128)(2,1)S(1)}, bf16[512,512]{1,0:T(8,128)(2,1)}, u32[]{:S(2)}) copy-start(bf16[512,512]{1,0:T(8,128)(2,1)} %outw_ref.3) | copy-start | bytes 1572868
  17.9 9.1 %copy-start.1 = (bf16[512,2048]{1,0:T(8,128)(2,1)S(1)}, bf16[512,2048]{1,0:T(8,128)(2,1)}, u32[]{:S(2)}) copy-start(bf16[512,2048]{1,0:T(8,128)(2,1)} %proj_ref.15) | copy-start | bytes 6291460
  17.9 9.1 %copy-start.8 = (s32[1,3]{1,0:T(1,128)S(1)}, s32[1,3]{1,0:T(1,128)}, u32[]{:S(2)}) copy-start(s32[1,3]{1,0:T(1,128)} %lengths_ref.9) | copy-start | bytes 40
  19.2 4.6 %collective-permute-start.5 = (bf16[72,512]{1,0:T(8,128)(2,1)}, bf16[72,512]{1,0:T(8,128)(2,1)S(1)}, u32[]{:S(2)}, u32[]{:S(2)}) collective-permute-start(bf16[72,512]{1,0:T(8,128)(2,1)} %get-tuple-element.58), channel_id=1, source_target_pairs={{0,8},{4,12},{8,0},{12,4},{16,24},{20,28},{24,16},{28,20},{1,9},{5... | collective-permute-start | bytes 221192 | tf_op jit(solution)/shard_map/ppermute | solution.py:481
  19.2 5.3 %collective-permute-start.6 = (bf16[72,512]{1,0:T(8,128)(2,1)S(1)}, bf16[72,512]{1,0:T(8,128)(2,1)S(1)}, u32[]{:S(2)}, u32[]{:S(2)}) collective-permute-start(bf16[72,512]{1,0:T(8,128)(2,1)S(1)} %get-tuple-element.59), channel_id=1, source_target_pairs={{0,12},{4,8},{8,4},{12,0},{16,28},{20,24},{24,20},{28,16},{1,13},{... | collective-permute-start | bytes 221192 | tf_op jit(solution)/shard_map/ppermute | solution.py:481
  25.4 6.4 %collective-permute-start.7 = (bf16[256,512]{1,0:T(8,128)(2,1)S(1)}, bf16[256,512]{1,0:T(8,128)(2,1)S(1)}, u32[]{:S(2)}, u32[]{:S(2)}) collective-permute-start(bf16[256,512]{1,0:T(8,128)(2,1)S(1)} %get-tuple-element.60.normed_ref.own_ref.n0_ref.refs_0_), channel_id=1, source_target_pairs={{0,2},{1,3},{2,0},{3,1},{4,6},{5,7},{6,4},{7,5},{8,10},{9,11},{10,... | collective-permute-start | bytes 786440 | tf_op jit(solution)/shard_map/ppermute | solution.py:470
  29.2 2.7 %collective-permute-start.9 = (bf16[256,512]{1,0:T(8,128)(2,1)S(1)}, bf16[256,512]{1,0:T(8,128)(2,1)S(1)}, u32[]{:S(2)}, u32[]{:S(2)}) collective-permute-start(bf16[256,512]{1,0:T(8,128)(2,1)S(1)} %get-tuple-element.63), channel_id=1, source_target_pairs={{0,1},{1,0},{2,3},{3,2},{4,5},{5,4},{6,7},{7,6},{8,9},{9,8},{10,11... | collective-permute-start | bytes 786440 | tf_op jit(solution)/shard_map/ppermute | solution.py:470
  31.8 1.5 %collective-permute-start.8 = (bf16[256,512]{1,0:T(8,128)(2,1)S(1)}, bf16[256,512]{1,0:T(8,128)(2,1)S(1)}, u32[]{:S(2)}, u32[]{:S(2)}) collective-permute-start(bf16[256,512]{1,0:T(8,128)(2,1)S(1)} %collective-permute-done.7.far_ref.n2_ref.refs_2_), channel_id=1, source_target_pairs={{0,1},{1,0},{2,3},{3,2},{4,5},{5,4},{6,7},{7,6},{8,9},{9,8},{10,11... | collective-permute-start | bytes 786440 | tf_op jit(solution)/shard_map/ppermute | solution.py:470
  33.4 4.9 %copy-start.3 = (bf16[256,512]{1,0:T(8,128)(2,1)S(1)}, bf16[256,512]{1,0:T(8,128)(2,1)}, u32[]{:S(2)}) copy-start(bf16[256,512]{1,0:T(8,128)(2,1)} %cot_ref.5) | copy-start | bytes 786436
  33.4 4.9 %copy-start.5 = (bf16[512,512]{1,0:T(8,128)(2,1)S(1)}, bf16[512,512]{1,0:T(8,128)(2,1)}, u32[]{:S(2)}) copy-start(bf16[512,512]{1,0:T(8,128)(2,1)} %outw_ref.3) | copy-start | bytes 1572868
  34.4 6.0 %collective-permute-start.10 = (bf16[256,128]{1,0:T(8,128)(2,1)S(1)}, bf16[256,128]{1,0:T(8,128)(2,1)S(1)}, u32[]{:S(2)}, u32[]{:S(2)}) collective-permute-start(bf16[256,128]{1,0:T(8,128)(2,1)S(1)} %get-tuple-element.72), channel_id=1, source_target_pairs={{0,1},{1,0},{2,3},{3,2},{4,5},{5,4},{6,7},{7,6},{8,9},{9,8},{10,11... | collective-permute-start | bytes 196616 | tf_op jit(solution)/shard_map/ppermute | solution.py:470
  34.6 6.0 %collective-permute-start.11 = (bf16[256,128]{1,0:T(8,128)(2,1)S(1)}, bf16[256,128]{1,0:T(8,128)(2,1)S(1)}, u32[]{:S(2)}, u32[]{:S(2)}) collective-permute-start(bf16[256,128]{1,0:T(8,128)(2,1)S(1)} %get-tuple-element.73), channel_id=1, source_target_pairs={{0,2},{1,3},{2,0},{3,1},{4,6},{5,7},{6,4},{7,5},{8,10},{9,11},{10,... | collective-permute-start | bytes 196616 | tf_op jit(solution)/shard_map/ppermute | solution.py:470
  38.3 4.4 %collective-permute-start.12 = (bf16[256,128]{1,0:T(8,128)(2,1)S(1)}, bf16[256,128]{1,0:T(8,128)(2,1)S(1)}, u32[]{:S(2)}, u32[]{:S(2)}) collective-permute-start(bf16[256,128]{1,0:T(8,128)(2,1)S(1)} %get-tuple-element.74), channel_id=1, source_target_pairs={{0,3},{1,2},{2,1},{3,0},{4,7},{5,6},{6,5},{7,4},{8,11},{9,10},{10,... | collective-permute-start | bytes 196616 | tf_op jit(solution)/shard_map/ppermute | solution.py:470
  39.4 3.3 %collective-permute-start.16 = (bf16[512,512]{1,0:T(8,128)(2,1)S(1)}, bf16[512,512]{1,0:T(8,128)(2,1)S(1)}, u32[]{:S(2)}, u32[]{:S(2)}) collective-permute-start(bf16[512,512]{1,0:T(8,128)(2,1)S(1)} %get-tuple-element.83), channel_id=1, source_target_pairs={{0,1},{1,0},{2,3},{3,2},{4,5},{5,4},{6,7},{7,6},{8,9},{9,8},{10,11... | collective-permute-start | bytes 1572872 | tf_op jit(solution)/shard_map/ppermute | solution.py:470
  42.8 9.1 %collective-permute-start.17 = (bf16[512,256]{1,0:T(8,128)(2,1)S(1)}, bf16[512,256]{1,0:T(8,128)(2,1)S(1)}, u32[]{:S(2)}, u32[]{:S(2)}) collective-permute-start(bf16[512,256]{1,0:T(8,128)(2,1)S(1)} %get-tuple-element.85), channel_id=1, source_target_pairs={{0,2},{1,3},{2,0},{3,1},{4,6},{5,7},{6,4},{7,5},{8,10},{9,11},{10,... | collective-permute-start | bytes 786440 | tf_op jit(solution)/shard_map/ppermute | solution.py:470
  47.7 8.2 %collective-permute-start.14 = (bf16[256,384]{1,0:T(8,128)(2,1)S(1)}, bf16[256,384]{1,0:T(8,128)(2,1)S(1)}, u32[]{:S(2)}, u32[]{:S(2)}) collective-permute-start(bf16[256,384]{1,0:T(8,128)(2,1)S(1)} %get-tuple-element.78.refs_6_), channel_id=1, source_target_pairs={{0,2},{1,3},{2,0},{3,1},{4,6},{5,7},{6,4},{7,5},{8,10},{9,11},{10,... | collective-permute-start | bytes 589832 | tf_op jit(solution)/shard_map/ppermute | solution.py:470
  48.6 10.4 %collective-permute-start.15 = (bf16[256,384]{1,0:T(8,128)(2,1)S(1)}, bf16[256,384]{1,0:T(8,128)(2,1)S(1)}, u32[]{:S(2)}, u32[]{:S(2)}) collective-permute-start(bf16[256,384]{1,0:T(8,128)(2,1)S(1)} %get-tuple-element.79.refs_7_), channel_id=1, source_target_pairs={{0,3},{1,2},{2,1},{3,0},{4,7},{5,6},{6,5},{7,4},{8,11},{9,10},{10,... | collective-permute-start | bytes 589832 | tf_op jit(solution)/shard_map/ppermute | solution.py:470
  51.2 18.7 %collective-permute-start.13 = (bf16[256,384]{1,0:T(8,128)(2,1)S(1)}, bf16[256,384]{1,0:T(8,128)(2,1)S(1)}, u32[]{:S(2)}, u32[]{:S(2)}) collective-permute-start(bf16[256,384]{1,0:T(8,128)(2,1)S(1)} %get-tuple-element.77.refs_5_), channel_id=1, source_target_pairs={{0,1},{1,0},{2,3},{3,2},{4,5},{5,4},{6,7},{7,6},{8,9},{9,8},{10,11... | collective-permute-start | bytes 589832 | tf_op jit(solution)/shard_map/ppermute | solution.py:470
  52.7 9.7 %collective-permute-start.18 = (bf16[256,640]{1,0:T(8,128)(2,1)S(1)}, bf16[256,640]{1,0:T(8,128)(2,1)S(1)}, u32[]{:S(2)}, u32[]{:S(2)}) collective-permute-start(bf16[256,640]{1,0:T(8,128)(2,1)S(1)} %get-tuple-element.87), channel_id=1, source_target_pairs={{0,4},{4,0},{8,12},{12,8},{16,20},{20,16},{24,28},{28,24},{1,5},{5... | collective-permute-start | bytes 983048 | tf_op jit(solution)/shard_map/ppermute | solution.py:481
  62.5 15.6 %collective-permute-start.19 = (bf16[64,640]{1,0:T(8,128)(2,1)S(1)}, bf16[64,640]{1,0:T(8,128)(2,1)S(1)}, u32[]{:S(2)}, u32[]{:S(2)}) collective-permute-start(bf16[64,640]{1,0:T(8,128)(2,1)S(1)} %get-tuple-element.89), channel_id=1, source_target_pairs={{0,8},{4,12},{8,0},{12,4},{16,24},{20,28},{24,16},{28,20},{1,9},{5... | collective-permute-start | bytes 245768 | tf_op jit(solution)/shard_map/ppermute | solution.py:481
  64.7 13.3 %collective-permute-start.20 = (bf16[64,640]{1,0:T(8,128)(2,1)S(1)}, bf16[64,640]{1,0:T(8,128)(2,1)S(1)}, u32[]{:S(2)}, u32[]{:S(2)}) collective-permute-start(bf16[64,640]{1,0:T(8,128)(2,1)S(1)} %get-tuple-element.90), channel_id=1, source_target_pairs={{0,16},{4,20},{8,24},{12,28},{16,0},{20,4},{24,8},{28,12},{1,17},{... | collective-permute-start | bytes 245768 | tf_op jit(solution)/shard_map/ppermute | solution.py:481
  70.0 8.1 %collective-permute-start.21 = (bf16[64,640]{1,0:T(8,128)(2,1)S(1)}, bf16[64,640]{1,0:T(8,128)(2,1)S(1)}, u32[]{:S(2)}, u32[]{:S(2)}) collective-permute-start(bf16[64,640]{1,0:T(8,128)(2,1)S(1)} %get-tuple-element.91), channel_id=1, source_target_pairs={{0,24},{4,28},{8,16},{12,20},{16,8},{20,12},{24,0},{28,4},{1,25},{... | collective-permute-start | bytes 245768 | tf_op jit(solution)/shard_map/ppermute | solution.py:481
  71.8 19.3 %all-to-all-start = ((bf16[8,64,512]{2,1,0:T(8,128)(2,1)}), bf16[8,64,512]{2,1,0:T(8,128)(2,1)S(1)}, u32[]{:S(2)}, u32[]{:S(2)}) async-start(bf16[8,64,512]{2,1,0:T(8,128)(2,1)} %bitcast.4), calls=%async_computation | async-start | bytes 1048576 | tf_op jit(solution)/shard_map/all_to_all | solution.py:485
  78.0 13.0 %copy-start.7 = (s32[1,256]{1,0:T(1,128)S(1)}, s32[1,256]{1,0:T(1,128)}, u32[]{:S(2)}) copy-start(s32[1,256]{1,0:T(1,128)} %copy-done.6) | copy-start | bytes 3076
  78.1 4.6 %collective-permute-start.24 = (bf16[64,640]{1,0:T(8,128)(2,1)S(1)}, bf16[64,640]{1,0:T(8,128)(2,1)S(1)}, u32[]{:S(2)}, u32[]{:S(2)}) collective-permute-start(bf16[64,640]{1,0:T(8,128)(2,1)S(1)} %sum.1.w0_ref), channel_id=1, source_target_pairs={{0,3},{1,2},{2,1},{3,0},{4,7},{5,6},{6,5},{7,4},{8,11},{9,10},{10,... | collective-permute-start | bytes 245768 | tf_op jit(solution)/shard_map/ppermute | solution.py:470
  78.2 6.5 %collective-permute-start.23 = (bf16[64,640]{1,0:T(8,128)(2,1)S(1)}, bf16[64,640]{1,0:T(8,128)(2,1)S(1)}, u32[]{:S(2)}, u32[]{:S(2)}) collective-permute-start(bf16[64,640]{1,0:T(8,128)(2,1)S(1)} %sum.1.w0_ref), channel_id=1, source_target_pairs={{0,2},{1,3},{2,0},{3,1},{4,6},{5,7},{6,4},{7,5},{8,10},{9,11},{10,... | collective-permute-start | bytes 245768 | tf_op jit(solution)/shard_map/ppermute | solution.py:470
  79.9 4.8 %collective-permute-start.22 = (bf16[64,640]{1,0:T(8,128)(2,1)S(1)}, bf16[64,640]{1,0:T(8,128)(2,1)S(1)}, u32[]{:S(2)}, u32[]{:S(2)}) collective-permute-start(bf16[64,640]{1,0:T(8,128)(2,1)S(1)} %sum.1.w0_ref), channel_id=1, source_target_pairs={{0,1},{1,0},{2,3},{3,2},{4,5},{5,4},{6,7},{7,6},{8,9},{9,8},{10,11... | collective-permute-start | bytes 245768 | tf_op jit(solution)/shard_map/ppermute | solution.py:470

commit v13 on v12

--- a/solution.py
+++ b/solution.py
@@ -418,7 +418,7 @@
     out_ref[...] = grad
 
 
-def spread_body(blocks, mask_ref, grad_ref, landing_ref, _, out_ref):
+def spread_body(blocks, mask_ref, grad_ref, landing_ref, out_ref):
     select = hot(iota((grad_ref.shape[0], landing_ref.shape[1]), 0) + 1 == landing_ref[...])
     value = t_mm(select, grad_ref[...])
     size = value.shape[0] // blocks
@@ -500,7 +500,7 @@
         functools.partial(pack_body, first, capacity, stride),
         "pack",
         block_shapes(stride, width, BF16)[: len(first)] + [((1, rows), jnp.int32)] * 2 + [square],
-        [mask], [], far=[owner_row, slot_row, tokens], scratch=[pltpu.SemaphoreType.DMA((3,))],
+        [mask], [], far=[owner_row, slot_row, tokens], scratch=[pltpu.SemaphoreType.DMA((3,))], vmem=60,
     )
     (grad_gated,) = call(early_body, "early", [wide], [], [cotangent, out_weight, proj_weight])
     outgoing = dict(zip(first, outgoing))
@@ -584,21 +584,20 @@
         input_body, "input_grad", [square], [me],
         [own_block, p1, partial_in, owned, cotangent, proj_weight], vmem=16,
     )
+    (back,) = call(
+        functools.partial(spread_body, blocks), "spread", [((owners * capacity, width), BF16)],
+        [mask], [grad_owned, landing],
+    )
     if by_hops:
         kept, sent = weight_parts
         halves = call(
             pair_body, "pair_sum", [((share, columns), BF16)] * pairs, [], [kept, dp_hop(sent, 1)],
-            far=[partial_in],
+            far=[back],
         )
         summed_parts = [halves[0]] + [dp_hop(halves[j], 2 * j) for j in range(1, pairs)]
     else:
-        halves = weight_parts
         summed_parts = [swap_whole(weight_parts[0]).reshape(owners, share, columns)]
     (mine,) = call(sum_body, "sum", [((share, columns), BF16)], [], summed_parts, flops=10**11)
-    (back,) = call(
-        functools.partial(spread_body, blocks), "spread", [((owners * capacity, width), BF16)],
-        [mask], [grad_owned, landing], far=halves[:1],
-    )
     returned = swap_whole(back)
     w1, w2, w3 = (hop(mine, step) for step in range(1, cycle))
     (grad_tokens,) = call(

time: 92.6 us -> 89.9 us (0.971)
  starting transfers between devices: 38.3 us -> 36.2 us
  local copies, waits for them, and re-layouts: 5.91 us -> 4.2 us
  Pallas kernels: 20.3 us -> 21.3 us
    ppermute x14, waiting for transfers between devices: 15 us -> 6.03 us  [hop(): return lax.ppermute(value, 'ctx', [(i, i ^ step) for i in range(cycle)])]
    all_to_all x1, waiting for transfers between devices: 5.42 us -> 10.2 us  [swap_whole(): lax.all_to_all(split, 'dp', split_axis=0, concat_axis=0, tiled=True)]
    ppermute x11, waiting for transfers between devices: 6.34 us -> 9.88 us  [dp_hop(): return lax.ppermute(value, 'dp', [(i, i ^ step) for i in range(owners)])]
    all_to_all x1, starting transfers between devices: 6.27 us -> 3.49 us  [swap_whole(): lax.all_to_all(split, 'dp', split_axis=0, concat_axis=0, tiled=True)]
    unnamed x24, local copies, waits for them, and re-layouts: 5.91 us -> 4.2 us
    pallas_call x21, Pallas kernels: 20.3 us -> 21.3 us  [call(): pl.pallas_call(body, name=name, out_shape=[jax.ShapeDtypeStruct(s, d) for...]
  transfers between devices with their start and end apart: 26 -> 26, of which waited for: 12 -> 10; matrix products, arithmetic and copies ran while one was open for 0% -> 0% of each run, Pallas kernels for 18% -> 18%
where the time goes in v13:
time: 89.9 us; the launch traced here: 88.7 us
  starting transfers between devices  36.2 us (40%)
  waiting for transfers between devices  26.1 us (29%)
  Pallas kernels  21.3 us (24%)
  local copies, waits for them, and re-layouts  4.2 us (5%)
    ppermute x11, starting transfers between devices, dp_hop(): return lax.ppermute(value, 'dp', [(i, i ^ step) for i in range(owners)])  21.8 us
    pallas_call x21, Pallas kernels, call(): pl.pallas_call(body, name=name, out_shape=[jax.ShapeDtypeStruct(s, d) for...  21.3 us
    ppermute x14, starting transfers between devices, hop(): return lax.ppermute(value, 'ctx', [(i, i ^ step) for i in range(cycle)])  10.9 us
    all_to_all x1, waiting for transfers between devices, swap_whole(): lax.all_to_all(split, 'dp', split_axis=0, concat_axis=0, tiled=True)  10.2 us
    ppermute x11, waiting for transfers between devices, dp_hop(): return lax.ppermute(value, 'dp', [(i, i ^ step) for i in range(owners)])  9.88 us
    ppermute x14, waiting for transfers between devices, hop(): return lax.ppermute(value, 'ctx', [(i, i ^ step) for i in range(cycle)])  6.03 us
    unnamed x24, local copies, waits for them, and re-layouts  4.2 us
    all_to_all x1, starting transfers between devices, swap_whole(): lax.all_to_all(split, 'dp', split_axis=0, concat_axis=0, tiled=True)  3.49 us
  transfers between devices with their start and end apart: 26, of which 10 were waited for; matrix products, arithmetic and copies ran while one was open for 0% of the time, Pallas kernels for 18%

profile of v13, /device:TPU:0, one launch (start us, length us, event | category | flops | bytes accessed | tf_op | source)
XLA Modules:
  0.0 88.7 jit_solution(17350555717737727202)
XLA Ops:
  0.6 2.2 %pack.1 = (bf16[72,512]{1,0:T(8,128)(2,1)}, bf16[72,512]{1,0:T(8,128)(2,1)}, bf16[72,512]{1,0:T(8,128)(2,1)}, bf16[72,512]{1,0:T(8,128)(2,1)}, bf16[72,512]{1,0:...) custom-call(s32[1]{0:T(128)} %bitcast.1.mask_ref.dp_ref, ...), custom_call_target="tpu_custom_call" | custom-call | flops 100000000 | bytes 1048576 | tf_op jit(solution)/shard_map/pack/pallas_call | solution.py:22
  2.9 4.1 %collective-permute-start = (bf16[72,512]{1,0:T(8,128)(2,1)}, bf16[72,512]{1,0:T(8,128)(2,1)S(1)}, u32[]{:S(2)}, u32[]{:S(2)}) collective-permute-start(bf16[72,512]{1,0:T(8,128)(2,1)} %get-tuple-element.50), channel_id=1, source_target_pairs={{0,16},{4,20},{8,24},{12,28},{16,0},{20,4},{24,8},{28,12},{1,17},{... | collective-permute-start | bytes 221192 | tf_op jit(solution)/shard_map/ppermute | solution.py:481
  7.0 1.3 %collective-permute-start.1 = (bf16[72,512]{1,0:T(8,128)(2,1)}, bf16[72,512]{1,0:T(8,128)(2,1)S(1)}, u32[]{:S(2)}, u32[]{:S(2)}) collective-permute-start(bf16[72,512]{1,0:T(8,128)(2,1)} %get-tuple-element.51), channel_id=1, source_target_pairs={{0,20},{4,16},{8,28},{12,24},{16,4},{20,0},{24,12},{28,8},{1,21},{... | collective-permute-start | bytes 221192 | tf_op jit(solution)/shard_map/ppermute | solution.py:481
  8.3 3.6 %collective-permute-start.2 = (bf16[72,512]{1,0:T(8,128)(2,1)}, bf16[72,512]{1,0:T(8,128)(2,1)S(1)}, u32[]{:S(2)}, u32[]{:S(2)}) collective-permute-start(bf16[72,512]{1,0:T(8,128)(2,1)} %get-tuple-element.52), channel_id=1, source_target_pairs={{0,24},{4,28},{8,16},{12,20},{16,8},{20,12},{24,0},{28,4},{1,25},{... | collective-permute-start | bytes 221192 | tf_op jit(solution)/shard_map/ppermute | solution.py:481
  11.9 1.7 %collective-permute-start.4 = (bf16[72,512]{1,0:T(8,128)(2,1)}, bf16[72,512]{1,0:T(8,128)(2,1)S(1)}, u32[]{:S(2)}, u32[]{:S(2)}) collective-permute-start(bf16[72,512]{1,0:T(8,128)(2,1)} %get-tuple-element.54), channel_id=1, source_target_pairs={{0,4},{4,0},{8,12},{12,8},{16,20},{20,16},{24,28},{28,24},{1,5},{5... | collective-permute-start | bytes 221192 | tf_op jit(solution)/shard_map/ppermute | solution.py:481
  13.6 1.6 %copy-done = bf16[512,2048]{1,0:T(8,128)(2,1)S(1)} copy-done((bf16[512,2048]{1,0:T(8,128)(2,1)S(1)}, bf16[512,2048]{1,0:T(8,128)(2,1)}, u32[]{:S(2)}) %copy-start) | copy-done | bytes 2097176
  15.2 0.9 %copy-done.2 = bf16[256,512]{1,0:T(8,128)(2,1)S(1)} copy-done((bf16[256,512]{1,0:T(8,128)(2,1)S(1)}, bf16[256,512]{1,0:T(8,128)(2,1)}, u32[]{:S(2)}) %copy-start.2) | copy-done | bytes 262168
  16.1 1.0 %copy-done.4 = bf16[512,512]{1,0:T(8,128)(2,1)S(1)} copy-done((bf16[512,512]{1,0:T(8,128)(2,1)S(1)}, bf16[512,512]{1,0:T(8,128)(2,1)}, u32[]{:S(2)}) %copy-start.4) | copy-done | bytes 524312
  17.2 0.3 early.1._.grad_ref
  17.5 0.6 copy-done.6
  18.1 0.4 pack_rest.1
  18.6 1.8 %collective-permute-start.6 = (bf16[72,512]{1,0:T(8,128)(2,1)S(1)}, bf16[72,512]{1,0:T(8,128)(2,1)S(1)}, u32[]{:S(2)}, u32[]{:S(2)}) collective-permute-start(bf16[72,512]{1,0:T(8,128)(2,1)S(1)} %get-tuple-element.59), channel_id=1, source_target_pairs={{0,12},{4,8},{8,4},{12,0},{16,28},{20,24},{24,20},{28,16},{1,13},{... | collective-permute-start | bytes 221192 | tf_op jit(solution)/shard_map/ppermute | solution.py:481
  20.4 2.5 %collective-permute-done.5.refs_6_ = bf16[72,512]{1,0:T(8,128)(2,1)S(1)} collective-permute-done((bf16[72,512]{1,0:T(8,128)(2,1)S(1)}, bf16[72,512]{1,0:T(8,128)(2,1)S(1)}, u32[]{:S(2)}, u32[]{:S(2)}) %collective-permute-start.5) | collective-permute-done | bytes 73760 | tf_op jit(solution)/shard_map/ppermute | solution.py:481
  23.0 1.0 %collective-permute-done.6.refs_7_ = bf16[72,512]{1,0:T(8,128)(2,1)S(1)} collective-permute-done((bf16[72,512]{1,0:T(8,128)(2,1)S(1)}, bf16[72,512]{1,0:T(8,128)(2,1)S(1)}, u32[]{:S(2)}, u32[]{:S(2)}) %collective-permute-start.6) | collective-permute-done | bytes 73760 | tf_op jit(solution)/shard_map/ppermute | solution.py:481
  23.9 0.8 place.1
  24.8 1.6 %collective-permute-start.7 = (bf16[256,512]{1,0:T(8,128)(2,1)S(1)}, bf16[256,512]{1,0:T(8,128)(2,1)S(1)}, u32[]{:S(2)}, u32[]{:S(2)}) collective-permute-start(bf16[256,512]{1,0:T(8,128)(2,1)S(1)} %get-tuple-element.60.normed_ref.own_ref.n0_ref.refs_0_), channel_id=1, source_target_pairs={{0,2},{1,3},{2,0},{3,1},{4,6},{5,7},{6,4},{7,5},{8,10},{9,11},{10,... | collective-permute-start | bytes 786440 | tf_op jit(solution)/shard_map/ppermute | solution.py:470
  26.4 2.2 %own_rows.1 = (bf16[256,512]{1,0:T(8,128)(2,1)S(1)}, f32[256,512]{1,0:T(8,128)S(1)}, bf16[256,512]{1,0:T(8,128)(2,1)S(1)}, f32[256,512]{1,0:T(8,128)S(1)}, bf16[256,512]{1,0:T(8,128)(2,1)S(1)}) custom-call(s32[1]{0:T(128)} %bitcast.me_ref, s32[1,3]{1,0:T(1,128)S(1)} %copy-done.10, bf16[256,512]{1,0:T(8,128)(2,1)S(1)} %get-tuple-element.60.normed_ref.own_ref.n0_ref.refs_0_, ...), custom_call_target="tpu_custom_call" | custom-call | flops 10000000000 | bytes 1048576 | tf_op jit(solution)/shard_map/own_rows/pallas_call | solution.py:22
  28.6 2.6 %collective-permute-done.7.far_ref.n2_ref.refs_2_ = bf16[256,512]{1,0:T(8,128)(2,1)S(1)} collective-permute-done((bf16[256,512]{1,0:T(8,128)(2,1)S(1)}, bf16[256,512]{1,0:T(8,128)(2,1)S(1)}, u32[]{:S(2)}, u32[]{:S(2)}) %collective-permute-start.7) | collective-permute-done | bytes 262176 | tf_op jit(solution)/shard_map/ppermute | solution.py:470
  31.2 0.6 middle.1.partial_ref
  31.8 0.9 %collective-permute-done.8.cross_ref.n3_ref.refs_3_ = bf16[256,512]{1,0:T(8,128)(2,1)S(1)} collective-permute-done((bf16[256,512]{1,0:T(8,128)(2,1)S(1)}, bf16[256,512]{1,0:T(8,128)(2,1)S(1)}, u32[]{:S(2)}, u32[]{:S(2)}) %collective-permute-start.8) | collective-permute-done | bytes 262176 | tf_op jit(solution)/shard_map/ppermute | solution.py:470
  32.8 1.0 %forward.1 = (f32[256,512]{1,0:T(8,128)S(1)}, bf16[256,128]{1,0:T(8,128)(2,1)S(1)}, bf16[256,128]{1,0:T(8,128)(2,1)S(1)}, bf16[256,128]{1,0:T(8,128)(2,1)S(1)}, bf16[256,128]{1,0:T(8,128)(2,1)S(1)}) custom-call(s32[1]{0:T(128)} %bitcast.me_ref, s32[1,3]{1,0:T(1,128)S(1)} %copy-done.10, bf16[256,512]{1,0:T(8,128)(2,1)S(1)} %collective-permute-done.8.cross_ref.n3_ref.refs_3_, ...), custom_call_target="tpu_custom_call" | custom-call | flops 100000000 | bytes 1048576 | tf_op jit(solution)/shard_map/forward/pallas_call | solution.py:22
  33.8 1.0 %collective-permute-start.10 = (bf16[256,128]{1,0:T(8,128)(2,1)S(1)}, bf16[256,128]{1,0:T(8,128)(2,1)S(1)}, u32[]{:S(2)}, u32[]{:S(2)}) collective-permute-start(bf16[256,128]{1,0:T(8,128)(2,1)S(1)} %get-tuple-element.72), channel_id=1, source_target_pairs={{0,1},{1,0},{2,3},{3,2},{4,5},{5,4},{6,7},{7,6},{8,9},{9,8},{10,11... | collective-permute-start | bytes 196616 | tf_op jit(solution)/shard_map/ppermute | solution.py:470
  34.8 2.4 %collective-permute-start.11 = (bf16[256,128]{1,0:T(8,128)(2,1)S(1)}, bf16[256,128]{1,0:T(8,128)(2,1)S(1)}, u32[]{:S(2)}, u32[]{:S(2)}) collective-permute-start(bf16[256,128]{1,0:T(8,128)(2,1)S(1)} %get-tuple-element.73), channel_id=1, source_target_pairs={{0,2},{1,3},{2,0},{3,1},{4,6},{5,7},{6,4},{7,5},{8,10},{9,11},{10,... | collective-permute-start | bytes 196616 | tf_op jit(solution)/shard_map/ppermute | solution.py:470
  37.3 1.1 %side.1 = (bf16[512,512]{1,0:T(8,128)(2,1)S(1)}, bf16[512,512]{1,0:T(8,128)(2,1)S(1)}, f32[256,512]{1,0:T(8,128)S(1)}, bf16[256,512]{1,0:T(8,128)(2,1)}) custom-call(s32[1]{0:T(128)} %bitcast.me_ref, bf16[256,512]{1,0:T(8,128)(2,1)S(1)} %get-tuple-element.60.normed_ref.own_ref.n0_ref.refs_0_, f32[256,512]{1,0:T(8,128)S(1)} %get-tuple-element.65.normed_ref, ...), custom_call_target="tpu_custom_call" | custom-call | flops 100000000 | bytes 1048576 | tf_op jit(solution)/shard_map/side/pallas_call | solution.py:22
  38.5 0.8 heads.1
  39.4 0.5 collective-permute-done.11.g2_ref
  39.9 1.4 %collective-permute-done.12.g3_ref = bf16[256,128]{1,0:T(8,128)(2,1)S(1)} collective-permute-done((bf16[256,128]{1,0:T(8,128)(2,1)S(1)}, bf16[256,128]{1,0:T(8,128)(2,1)S(1)}, u32[]{:S(2)}, u32[]{:S(2)}) %collective-permute-start.12) | collective-permute-done | bytes 65568 | tf_op jit(solution)/shard_map/ppermute | solution.py:470
  41.4 1.4 %collective-permute-start.17 = (bf16[512,256]{1,0:T(8,128)(2,1)S(1)}, bf16[512,256]{1,0:T(8,128)(2,1)S(1)}, u32[]{:S(2)}, u32[]{:S(2)}) collective-permute-start(bf16[512,256]{1,0:T(8,128)(2,1)S(1)} %get-tuple-element.85), channel_id=1, source_target_pairs={{0,2},{1,3},{2,0},{3,1},{4,6},{5,7},{6,4},{7,5},{8,10},{9,11},{10,... | collective-permute-start | bytes 786440 | tf_op jit(solution)/shard_map/ppermute | solution.py:470
  42.9 3.7 %backward_far.1 = (bf16[256,384]{1,0:T(8,128)(2,1)S(1)}, bf16[256,384]{1,0:T(8,128)(2,1)S(1)}, f32[1024,384]{1,0:T(8,128)S(1)}) custom-call(s32[1]{0:T(128)} %bitcast.me_ref, s32[1,3]{1,0:T(1,128)S(1)} %copy-done.10, bf16[1024,384]{1,0:T(8,128)(2,1)S(1)} %get-tuple-element.69.part_ref, f32[1024,384]{1,0:T(8,128)S(1)} %get-tuple-element.70.slope_ref, ...), custom_call_target="tpu_custom_call" | custom-call | flops 10000000000 | bytes 1048576 | tf_op jit(solution)/shard_map/backward_far/pallas_call | solution.py:22
  46.5 1.5 %collective-permute-start.14 = (bf16[256,384]{1,0:T(8,128)(2,1)S(1)}, bf16[256,384]{1,0:T(8,128)(2,1)S(1)}, u32[]{:S(2)}, u32[]{:S(2)}) collective-permute-start(bf16[256,384]{1,0:T(8,128)(2,1)S(1)} %get-tuple-element.78.refs_6_), channel_id=1, source_target_pairs={{0,2},{1,3},{2,0},{3,1},{4,6},{5,7},{6,4},{7,5},{8,10},{9,11},{10,... | collective-permute-start | bytes 589832 | tf_op jit(solution)/shard_map/ppermute | solution.py:470
  48.0 2.6 %backward_rest.1 = (bf16[256,384]{1,0:T(8,128)(2,1)S(1)}, bf16[256,384]{1,0:T(8,128)(2,1)S(1)}) custom-call(s32[1]{0:T(128)} %bitcast.me_ref, s32[1,3]{1,0:T(1,128)S(1)} %copy-done.10, bf16[1024,384]{1,0:T(8,128)(2,1)S(1)} %get-tuple-element.69.part_ref, f32[1024,384]{1,0:T(8,128)S(1)} %get-tuple-element.70.slope_ref, ...), custom_call_target="tpu_custom_call" | custom-call | flops 100000000 | bytes 1048576 | tf_op jit(solution)/shard_map/backward_rest/pallas_call | solution.py:22
  50.6 0.8 collective-permute-start.13
  51.4 0.8 weights.1
  52.3 4.8 %collective-permute-start.18 = (bf16[256,640]{1,0:T(8,128)(2,1)S(1)}, bf16[256,640]{1,0:T(8,128)(2,1)S(1)}, u32[]{:S(2)}, u32[]{:S(2)}) collective-permute-start(bf16[256,640]{1,0:T(8,128)(2,1)S(1)} %get-tuple-element.87), channel_id=1, source_target_pairs={{0,4},{4,0},{8,12},{12,8},{16,20},{20,16},{24,28},{28,24},{1,5},{5... | collective-permute-start | bytes 983048 | tf_op jit(solution)/shard_map/ppermute | solution.py:481
  57.1 0.6 collective-permute-done.15.cross_ref
  57.7 0.5 input_far.1.partial_ref
  58.2 0.7 input_grad.1.grad_ref
  58.9 1.1 %spread.1._ = bf16[512,512]{1,0:T(8,128)(2,1)} custom-call(s32[1]{0:T(128)} %bitcast.1.mask_ref.dp_ref, bf16[256,512]{1,0:T(8,128)(2,1)S(1)} %input_grad.1.grad_ref, s32[1,512]{1,0:T(1,128)S(1)} %get-tuple-element.81.landing_ref), custom_call_target="tpu_custom_call" | custom-call | flops 100000000 | bytes 1048576 | tf_op jit(solution)/shard_map/spread/pallas_call | solution.py:22
  60.0 5.0 %collective-permute-done.18.came_ref = bf16[256,640]{1,0:T(8,128)(2,1)S(1)} collective-permute-done((bf16[256,640]{1,0:T(8,128)(2,1)S(1)}, bf16[256,640]{1,0:T(8,128)(2,1)S(1)}, u32[]{:S(2)}, u32[]{:S(2)}) %collective-permute-start.18) | collective-permute-done | bytes 327712 | tf_op jit(solution)/shard_map/ppermute | solution.py:481
  65.1 1.9 %collective-permute-start.20 = (bf16[64,640]{1,0:T(8,128)(2,1)S(1)}, bf16[64,640]{1,0:T(8,128)(2,1)S(1)}, u32[]{:S(2)}, u32[]{:S(2)}) collective-permute-start(bf16[64,640]{1,0:T(8,128)(2,1)S(1)} %get-tuple-element.90), channel_id=1, source_target_pairs={{0,16},{4,20},{8,24},{12,28},{16,0},{20,4},{24,8},{28,12},{1,17},{... | collective-permute-start | bytes 245768 | tf_op jit(solution)/shard_map/ppermute | solution.py:481
  67.0 2.5 %collective-permute-start.21 = (bf16[64,640]{1,0:T(8,128)(2,1)S(1)}, bf16[64,640]{1,0:T(8,128)(2,1)S(1)}, u32[]{:S(2)}, u32[]{:S(2)}) collective-permute-start(bf16[64,640]{1,0:T(8,128)(2,1)S(1)} %get-tuple-element.91), channel_id=1, source_target_pairs={{0,24},{4,28},{8,16},{12,20},{16,8},{20,12},{24,0},{28,4},{1,25},{... | collective-permute-start | bytes 245768 | tf_op jit(solution)/shard_map/ppermute | solution.py:481
  69.5 3.5 %all-to-all-start = ((bf16[8,64,512]{2,1,0:T(8,128)(2,1)}), bf16[8,64,512]{2,1,0:T(8,128)(2,1)S(1)}, u32[]{:S(2)}, u32[]{:S(2)}) async-start(bf16[8,64,512]{2,1,0:T(8,128)(2,1)} %bitcast.4), calls=%async_computation | async-start | bytes 1048576 | tf_op jit(solution)/shard_map/all_to_all | solution.py:485
  73.0 1.4 %collective-permute-done.20.refs_2_ = bf16[64,640]{1,0:T(8,128)(2,1)S(1)} collective-permute-done((bf16[64,640]{1,0:T(8,128)(2,1)S(1)}, bf16[64,640]{1,0:T(8,128)(2,1)S(1)}, u32[]{:S(2)}, u32[]{:S(2)}) %collective-permute-start.20) | collective-permute-done | bytes 81952 | tf_op jit(solution)/shard_map/ppermute | solution.py:481
  74.5 1.6 %collective-permute-start.23 = (bf16[64,640]{1,0:T(8,128)(2,1)S(1)}, bf16[64,640]{1,0:T(8,128)(2,1)S(1)}, u32[]{:S(2)}, u32[]{:S(2)}) collective-permute-start(bf16[64,640]{1,0:T(8,128)(2,1)S(1)} %sum.1.w0_ref), channel_id=1, source_target_pairs={{0,2},{1,3},{2,0},{3,1},{4,6},{5,7},{6,4},{7,5},{8,10},{9,11},{10,... | collective-permute-start | bytes 245768 | tf_op jit(solution)/shard_map/ppermute | solution.py:470
  76.2 0.2 collective-permute-start.22
  76.4 10.2 %all-to-all-done = bf16[8,64,512]{2,1,0:T(8,128)(2,1)S(1)} async-done(((bf16[8,64,512]{2,1,0:T(8,128)(2,1)}), bf16[8,64,512]{2,1,0:T(8,128)(2,1)S(1)}, u32[]{:S(2)}, u32[]{:S(2)}) %all-to-all-start) | async-done | bytes 524320 | tf_op jit(solution)/shard_map/all_to_all | solution.py:485
  86.6 1.2 %give_back.1 = bf16[256,512]{1,0:T(8,128)(2,1)} custom-call(s32[1]{0:T(128)} %bitcast.1.mask_ref.dp_ref, s32[1,256]{1,0:T(1,128)S(1)} %copy-done.9, bf16[512,512]{1,0:T(8,128)(2,1)S(1)} %bitcast.6), custom_call_target="tpu_custom_call" | custom-call | flops 100000000 | bytes 1048576 | tf_op jit(solution)/shard_map/give_back/pallas_call | solution.py:22
  87.8 0.9 %finish.1 = (f32[64,2048]{1,0:T(8,128)}, f32[64,512]{1,0:T(8,128)}) custom-call(s32[1]{0:T(128)} %bitcast.me_ref, bf16[64,640]{1,0:T(8,128)(2,1)S(1)} %sum.1.w0_ref, bf16[64,640]{1,0:T(8,128)(2,1)S(1)} %collective-permute-done.22.w1_ref, bf16[64,640]{1,0:T(8,128)(2,1)S(1)} %collective-permute-done.23.w2_ref, bf16[64,640]{1,0:T(8,128)(2,1)S(1)} %collective-permute-done.24.w3_ref), custom_call_target="tpu_custom_call" | custom-call | flops 100000000 | bytes 1048576 | tf_op jit(solution)/shard_map/finish/pallas_call | solution.py:22
  (49 shorter events, 0.8 us)
Async XLA Ops:
  2.9 15.6 %collective-permute-start = (bf16[72,512]{1,0:T(8,128)(2,1)}, bf16[72,512]{1,0:T(8,128)(2,1)S(1)}, u32[]{:S(2)}, u32[]{:S(2)}) collective-permute-start(bf16[72,512]{1,0:T(8,128)(2,1)} %get-tuple-element.50), channel_id=1, source_target_pairs={{0,16},{4,20},{8,24},{12,28},{16,0},{20,4},{24,8},{28,12},{1,17},{... | collective-permute-start | bytes 221192 | tf_op jit(solution)/shard_map/ppermute | solution.py:481
  7.0 11.6 %collective-permute-start.1 = (bf16[72,512]{1,0:T(8,128)(2,1)}, bf16[72,512]{1,0:T(8,128)(2,1)S(1)}, u32[]{:S(2)}, u32[]{:S(2)}) collective-permute-start(bf16[72,512]{1,0:T(8,128)(2,1)} %get-tuple-element.51), channel_id=1, source_target_pairs={{0,20},{4,16},{8,28},{12,24},{16,4},{20,0},{24,12},{28,8},{1,21},{... | collective-permute-start | bytes 221192 | tf_op jit(solution)/shard_map/ppermute | solution.py:481
  8.3 12.1 %collective-permute-start.2 = (bf16[72,512]{1,0:T(8,128)(2,1)}, bf16[72,512]{1,0:T(8,128)(2,1)S(1)}, u32[]{:S(2)}, u32[]{:S(2)}) collective-permute-start(bf16[72,512]{1,0:T(8,128)(2,1)} %get-tuple-element.52), channel_id=1, source_target_pairs={{0,24},{4,28},{8,16},{12,20},{16,8},{20,12},{24,0},{28,4},{1,25},{... | collective-permute-start | bytes 221192 | tf_op jit(solution)/shard_map/ppermute | solution.py:481
  11.9 8.5 %collective-permute-start.3 = (bf16[72,512]{1,0:T(8,128)(2,1)}, bf16[72,512]{1,0:T(8,128)(2,1)S(1)}, u32[]{:S(2)}, u32[]{:S(2)}) collective-permute-start(bf16[72,512]{1,0:T(8,128)(2,1)} %get-tuple-element.53), channel_id=1, source_target_pairs={{0,28},{4,24},{8,20},{12,16},{16,12},{20,8},{24,4},{28,0},{1,29},{... | collective-permute-start | bytes 221192 | tf_op jit(solution)/shard_map/ppermute | solution.py:481
  11.9 8.5 %collective-permute-start.4 = (bf16[72,512]{1,0:T(8,128)(2,1)}, bf16[72,512]{1,0:T(8,128)(2,1)S(1)}, u32[]{:S(2)}, u32[]{:S(2)}) collective-permute-start(bf16[72,512]{1,0:T(8,128)(2,1)} %get-tuple-element.54), channel_id=1, source_target_pairs={{0,4},{4,0},{8,12},{12,8},{16,20},{20,16},{24,28},{28,24},{1,5},{5... | collective-permute-start | bytes 221192 | tf_op jit(solution)/shard_map/ppermute | solution.py:481
  13.6 1.6 %copy-start = (bf16[512,2048]{1,0:T(8,128)(2,1)S(1)}, bf16[512,2048]{1,0:T(8,128)(2,1)}, u32[]{:S(2)}) copy-start(bf16[512,2048]{1,0:T(8,128)(2,1)} %proj_ref.15) | copy-start | bytes 6291460
  15.2 0.9 %copy-start.2 = (bf16[256,512]{1,0:T(8,128)(2,1)S(1)}, bf16[256,512]{1,0:T(8,128)(2,1)}, u32[]{:S(2)}) copy-start(bf16[256,512]{1,0:T(8,128)(2,1)} %cot_ref.5) | copy-start | bytes 786436
  16.1 1.0 %copy-start.4 = (bf16[512,512]{1,0:T(8,128)(2,1)S(1)}, bf16[512,512]{1,0:T(8,128)(2,1)}, u32[]{:S(2)}) copy-start(bf16[512,512]{1,0:T(8,128)(2,1)} %outw_ref.3) | copy-start | bytes 1572868
  17.2 0.9 %copy-start.6 = (bf16[256,512]{1,0:T(8,128)(2,1)S(1)}, bf16[256,512]{1,0:T(8,128)(2,1)}, u32[]{:S(2)}) copy-start(bf16[256,512]{1,0:T(8,128)(2,1)} %get-tuple-element.57.tokens_ref) | copy-start | bytes 786436
  17.2 1.0 %copy-start.8 = (s32[1,256]{1,0:T(1,128)S(1)}, s32[1,256]{1,0:T(1,128)}, u32[]{:S(2)}) copy-start(s32[1,256]{1,0:T(1,128)} %get-tuple-element.55.owner_ref) | copy-start | bytes 3076
  17.2 1.0 %copy-start.11 = (s32[1,256]{1,0:T(1,128)S(1)}, s32[1,256]{1,0:T(1,128)}, u32[]{:S(2)}) copy-start(s32[1,256]{1,0:T(1,128)} %get-tuple-element.56.slot_ref) | copy-start | bytes 3076
  17.2 6.8 %copy-start.7 = (bf16[72,512]{1,0:T(8,128)(2,1)S(1)}, bf16[72,512]{1,0:T(8,128)(2,1)}, u32[]{:S(2)}) copy-start(bf16[72,512]{1,0:T(8,128)(2,1)} %get-tuple-element.49.refs_0_) | copy-start | bytes 221188
  17.2 9.2 %copy-start.1 = (bf16[512,2048]{1,0:T(8,128)(2,1)S(1)}, bf16[512,2048]{1,0:T(8,128)(2,1)}, u32[]{:S(2)}) copy-start(bf16[512,2048]{1,0:T(8,128)(2,1)} %proj_ref.15) | copy-start | bytes 6291460
  17.2 9.2 %copy-start.10 = (s32[1,3]{1,0:T(1,128)S(1)}, s32[1,3]{1,0:T(1,128)}, u32[]{:S(2)}) copy-start(s32[1,3]{1,0:T(1,128)} %lengths_ref.9) | copy-start | bytes 40
  18.5 4.4 %collective-permute-start.5 = (bf16[72,512]{1,0:T(8,128)(2,1)S(1)}, bf16[72,512]{1,0:T(8,128)(2,1)S(1)}, u32[]{:S(2)}, u32[]{:S(2)}) collective-permute-start(bf16[72,512]{1,0:T(8,128)(2,1)S(1)} %get-tuple-element.58), channel_id=1, source_target_pairs={{0,8},{4,12},{8,0},{12,4},{16,24},{20,28},{24,16},{28,20},{1,9},{5... | collective-permute-start | bytes 221192 | tf_op jit(solution)/shard_map/ppermute | solution.py:481
  18.6 5.3 %collective-permute-start.6 = (bf16[72,512]{1,0:T(8,128)(2,1)S(1)}, bf16[72,512]{1,0:T(8,128)(2,1)S(1)}, u32[]{:S(2)}, u32[]{:S(2)}) collective-permute-start(bf16[72,512]{1,0:T(8,128)(2,1)S(1)} %get-tuple-element.59), channel_id=1, source_target_pairs={{0,12},{4,8},{8,4},{12,0},{16,28},{20,24},{24,20},{28,16},{1,13},{... | collective-permute-start | bytes 221192 | tf_op jit(solution)/shard_map/ppermute | solution.py:481
  24.8 6.4 %collective-permute-start.7 = (bf16[256,512]{1,0:T(8,128)(2,1)S(1)}, bf16[256,512]{1,0:T(8,128)(2,1)S(1)}, u32[]{:S(2)}, u32[]{:S(2)}) collective-permute-start(bf16[256,512]{1,0:T(8,128)(2,1)S(1)} %get-tuple-element.60.normed_ref.own_ref.n0_ref.refs_0_), channel_id=1, source_target_pairs={{0,2},{1,3},{2,0},{3,1},{4,6},{5,7},{6,4},{7,5},{8,10},{9,11},{10,... | collective-permute-start | bytes 786440 | tf_op jit(solution)/shard_map/ppermute | solution.py:470
  28.6 2.7 %collective-permute-start.9 = (bf16[256,512]{1,0:T(8,128)(2,1)S(1)}, bf16[256,512]{1,0:T(8,128)(2,1)S(1)}, u32[]{:S(2)}, u32[]{:S(2)}) collective-permute-start(bf16[256,512]{1,0:T(8,128)(2,1)S(1)} %get-tuple-element.63), channel_id=1, source_target_pairs={{0,1},{1,0},{2,3},{3,2},{4,5},{5,4},{6,7},{7,6},{8,9},{9,8},{10,11... | collective-permute-start | bytes 786440 | tf_op jit(solution)/shard_map/ppermute | solution.py:470
  31.2 1.5 %collective-permute-start.8 = (bf16[256,512]{1,0:T(8,128)(2,1)S(1)}, bf16[256,512]{1,0:T(8,128)(2,1)S(1)}, u32[]{:S(2)}, u32[]{:S(2)}) collective-permute-start(bf16[256,512]{1,0:T(8,128)(2,1)S(1)} %collective-permute-done.7.far_ref.n2_ref.refs_2_), channel_id=1, source_target_pairs={{0,1},{1,0},{2,3},{3,2},{4,5},{5,4},{6,7},{7,6},{8,9},{9,8},{10,11... | collective-permute-start | bytes 786440 | tf_op jit(solution)/shard_map/ppermute | solution.py:470
  32.8 4.5 %copy-start.3 = (bf16[256,512]{1,0:T(8,128)(2,1)S(1)}, bf16[256,512]{1,0:T(8,128)(2,1)}, u32[]{:S(2)}) copy-start(bf16[256,512]{1,0:T(8,128)(2,1)} %cot_ref.5) | copy-start | bytes 786436
  32.8 4.5 %copy-start.5 = (bf16[512,512]{1,0:T(8,128)(2,1)S(1)}, bf16[512,512]{1,0:T(8,128)(2,1)}, u32[]{:S(2)}) copy-start(bf16[512,512]{1,0:T(8,128)(2,1)} %outw_ref.3) | copy-start | bytes 1572868
  33.8 5.6 %collective-permute-start.10 = (bf16[256,128]{1,0:T(8,128)(2,1)S(1)}, bf16[256,128]{1,0:T(8,128)(2,1)S(1)}, u32[]{:S(2)}, u32[]{:S(2)}) collective-permute-start(bf16[256,128]{1,0:T(8,128)(2,1)S(1)} %get-tuple-element.72), channel_id=1, source_target_pairs={{0,1},{1,0},{2,3},{3,2},{4,5},{5,4},{6,7},{7,6},{8,9},{9,8},{10,11... | collective-permute-start | bytes 196616 | tf_op jit(solution)/shard_map/ppermute | solution.py:470
  34.8 5.1 %collective-permute-start.11 = (bf16[256,128]{1,0:T(8,128)(2,1)S(1)}, bf16[256,128]{1,0:T(8,128)(2,1)S(1)}, u32[]{:S(2)}, u32[]{:S(2)}) collective-permute-start(bf16[256,128]{1,0:T(8,128)(2,1)S(1)} %get-tuple-element.73), channel_id=1, source_target_pairs={{0,2},{1,3},{2,0},{3,1},{4,6},{5,7},{6,4},{7,5},{8,10},{9,11},{10,... | collective-permute-start | bytes 196616 | tf_op jit(solution)/shard_map/ppermute | solution.py:470
  37.2 4.0 %collective-permute-start.12 = (bf16[256,128]{1,0:T(8,128)(2,1)S(1)}, bf16[256,128]{1,0:T(8,128)(2,1)S(1)}, u32[]{:S(2)}, u32[]{:S(2)}) collective-permute-start(bf16[256,128]{1,0:T(8,128)(2,1)S(1)} %get-tuple-element.74), channel_id=1, source_target_pairs={{0,3},{1,2},{2,1},{3,0},{4,7},{5,6},{6,5},{7,4},{8,11},{9,10},{10,... | collective-permute-start | bytes 196616 | tf_op jit(solution)/shard_map/ppermute | solution.py:470
  38.4 2.9 %collective-permute-start.16 = (bf16[512,512]{1,0:T(8,128)(2,1)S(1)}, bf16[512,512]{1,0:T(8,128)(2,1)S(1)}, u32[]{:S(2)}, u32[]{:S(2)}) collective-permute-start(bf16[512,512]{1,0:T(8,128)(2,1)S(1)} %get-tuple-element.83), channel_id=1, source_target_pairs={{0,1},{1,0},{2,3},{3,2},{4,5},{5,4},{6,7},{7,6},{8,9},{9,8},{10,11... | collective-permute-start | bytes 1572872 | tf_op jit(solution)/shard_map/ppermute | solution.py:470
  41.4 10.0 %collective-permute-start.17 = (bf16[512,256]{1,0:T(8,128)(2,1)S(1)}, bf16[512,256]{1,0:T(8,128)(2,1)S(1)}, u32[]{:S(2)}, u32[]{:S(2)}) collective-permute-start(bf16[512,256]{1,0:T(8,128)(2,1)S(1)} %get-tuple-element.85), channel_id=1, source_target_pairs={{0,2},{1,3},{2,0},{3,1},{4,6},{5,7},{6,4},{7,5},{8,10},{9,11},{10,... | collective-permute-start | bytes 786440 | tf_op jit(solution)/shard_map/ppermute | solution.py:470
  46.5 10.5 %collective-permute-start.14 = (bf16[256,384]{1,0:T(8,128)(2,1)S(1)}, bf16[256,384]{1,0:T(8,128)(2,1)S(1)}, u32[]{:S(2)}, u32[]{:S(2)}) collective-permute-start(bf16[256,384]{1,0:T(8,128)(2,1)S(1)} %get-tuple-element.78.refs_6_), channel_id=1, source_target_pairs={{0,2},{1,3},{2,0},{3,1},{4,6},{5,7},{6,4},{7,5},{8,10},{9,11},{10,... | collective-permute-start | bytes 589832 | tf_op jit(solution)/shard_map/ppermute | solution.py:470
  48.0 9.7 %collective-permute-start.15 = (bf16[256,384]{1,0:T(8,128)(2,1)S(1)}, bf16[256,384]{1,0:T(8,128)(2,1)S(1)}, u32[]{:S(2)}, u32[]{:S(2)}) collective-permute-start(bf16[256,384]{1,0:T(8,128)(2,1)S(1)} %get-tuple-element.79.refs_7_), channel_id=1, source_target_pairs={{0,3},{1,2},{2,1},{3,0},{4,7},{5,6},{6,5},{7,4},{8,11},{9,10},{10,... | collective-permute-start | bytes 589832 | tf_op jit(solution)/shard_map/ppermute | solution.py:470
  50.6 7.6 %collective-permute-start.13 = (bf16[256,384]{1,0:T(8,128)(2,1)S(1)}, bf16[256,384]{1,0:T(8,128)(2,1)S(1)}, u32[]{:S(2)}, u32[]{:S(2)}) collective-permute-start(bf16[256,384]{1,0:T(8,128)(2,1)S(1)} %get-tuple-element.77.refs_5_), channel_id=1, source_target_pairs={{0,1},{1,0},{2,3},{3,2},{4,5},{5,4},{6,7},{7,6},{8,9},{9,8},{10,11... | collective-permute-start | bytes 589832 | tf_op jit(solution)/shard_map/ppermute | solution.py:470
  52.3 12.7 %collective-permute-start.18 = (bf16[256,640]{1,0:T(8,128)(2,1)S(1)}, bf16[256,640]{1,0:T(8,128)(2,1)S(1)}, u32[]{:S(2)}, u32[]{:S(2)}) collective-permute-start(bf16[256,640]{1,0:T(8,128)(2,1)S(1)} %get-tuple-element.87), channel_id=1, source_target_pairs={{0,4},{4,0},{8,12},{12,8},{16,20},{20,16},{24,28},{28,24},{1,5},{5... | collective-permute-start | bytes 983048 | tf_op jit(solution)/shard_map/ppermute | solution.py:481
  65.1 8.0 %collective-permute-start.19 = (bf16[64,640]{1,0:T(8,128)(2,1)S(1)}, bf16[64,640]{1,0:T(8,128)(2,1)S(1)}, u32[]{:S(2)}, u32[]{:S(2)}) collective-permute-start(bf16[64,640]{1,0:T(8,128)(2,1)S(1)} %get-tuple-element.89), channel_id=1, source_target_pairs={{0,8},{4,12},{8,0},{12,4},{16,24},{20,28},{24,16},{28,20},{1,9},{5... | collective-permute-start | bytes 245768 | tf_op jit(solution)/shard_map/ppermute | solution.py:481
  65.1 9.3 %collective-permute-start.20 = (bf16[64,640]{1,0:T(8,128)(2,1)S(1)}, bf16[64,640]{1,0:T(8,128)(2,1)S(1)}, u32[]{:S(2)}, u32[]{:S(2)}) collective-permute-start(bf16[64,640]{1,0:T(8,128)(2,1)S(1)} %get-tuple-element.90), channel_id=1, source_target_pairs={{0,16},{4,20},{8,24},{12,28},{16,0},{20,4},{24,8},{28,12},{1,17},{... | collective-permute-start | bytes 245768 | tf_op jit(solution)/shard_map/ppermute | solution.py:481
  67.0 7.4 %collective-permute-start.21 = (bf16[64,640]{1,0:T(8,128)(2,1)S(1)}, bf16[64,640]{1,0:T(8,128)(2,1)S(1)}, u32[]{:S(2)}, u32[]{:S(2)}) collective-permute-start(bf16[64,640]{1,0:T(8,128)(2,1)S(1)} %get-tuple-element.91), channel_id=1, source_target_pairs={{0,24},{4,28},{8,16},{12,20},{16,8},{20,12},{24,0},{28,4},{1,25},{... | collective-permute-start | bytes 245768 | tf_op jit(solution)/shard_map/ppermute | solution.py:481
  69.5 17.1 %all-to-all-start = ((bf16[8,64,512]{2,1,0:T(8,128)(2,1)}), bf16[8,64,512]{2,1,0:T(8,128)(2,1)S(1)}, u32[]{:S(2)}, u32[]{:S(2)}) async-start(bf16[8,64,512]{2,1,0:T(8,128)(2,1)} %bitcast.4), calls=%async_computation | async-start | bytes 1048576 | tf_op jit(solution)/shard_map/all_to_all | solution.py:485
  74.4 12.2 %copy-start.9 = (s32[1,256]{1,0:T(1,128)S(1)}, s32[1,256]{1,0:T(1,128)}, u32[]{:S(2)}) copy-start(s32[1,256]{1,0:T(1,128)} %get-tuple-element.55.owner_ref) | copy-start | bytes 3076
  74.5 13.3 %collective-permute-start.24 = (bf16[64,640]{1,0:T(8,128)(2,1)S(1)}, bf16[64,640]{1,0:T(8,128)(2,1)S(1)}, u32[]{:S(2)}, u32[]{:S(2)}) collective-permute-start(bf16[64,640]{1,0:T(8,128)(2,1)S(1)} %sum.1.w0_ref), channel_id=1, source_target_pairs={{0,3},{1,2},{2,1},{3,0},{4,7},{5,6},{6,5},{7,4},{8,11},{9,10},{10,... | collective-permute-start | bytes 245768 | tf_op jit(solution)/shard_map/ppermute | solution.py:470
  74.5 13.2 %collective-permute-start.23 = (bf16[64,640]{1,0:T(8,128)(2,1)S(1)}, bf16[64,640]{1,0:T(8,128)(2,1)S(1)}, u32[]{:S(2)}, u32[]{:S(2)}) collective-permute-start(bf16[64,640]{1,0:T(8,128)(2,1)S(1)} %sum.1.w0_ref), channel_id=1, source_target_pairs={{0,2},{1,3},{2,0},{3,1},{4,6},{5,7},{6,4},{7,5},{8,10},{9,11},{10,... | collective-permute-start | bytes 245768 | tf_op jit(solution)/shard_map/ppermute | solution.py:470
  76.2 11.6 %collective-permute-start.22 = (bf16[64,640]{1,0:T(8,128)(2,1)S(1)}, bf16[64,640]{1,0:T(8,128)(2,1)S(1)}, u32[]{:S(2)}, u32[]{:S(2)}) collective-permute-start(bf16[64,640]{1,0:T(8,128)(2,1)S(1)} %sum.1.w0_ref), channel_id=1, source_target_pairs={{0,1},{1,0},{2,3},{3,2},{4,5},{5,4},{6,7},{7,6},{8,9},{9,8},{10,11... | collective-permute-start | bytes 245768 | tf_op jit(solution)/shard_map/ppermute | solution.py:470

commit v14 on v13

--- a/solution.py
+++ b/solution.py
@@ -372,9 +372,15 @@
     )
 
 
-def weight_body(sources, pairs, dp_ref, kept_side_ref, came_side_ref, *refs):
+def weight_body(sources, pairs, blocks, dp_ref, mask_ref, kept_side_ref, came_side_ref, landing_ref, *refs):
     normed, grads = refs[:sources], refs[sources : 2 * sources]
-    outs, total_ref = refs[2 * sources : -1], refs[-1]
+    outs, (select_ref, total_ref) = refs[2 * sources : -2], refs[-2:]
+    select = jnp.where(iota((select_ref.shape[1], landing_ref.shape[1]), 0) + 1 == landing_ref[...], 1.0, 0.0)
+    select = jnp.transpose(select)
+    size = select.shape[0] // blocks
+    for k in range(blocks):
+        at = pl.ds(pl.multiple_of((mask_ref[0] ^ k) * size, size), size)
+        select_ref[at, :] = select[k * size : (k + 1) * size].astype(BF16)
     side = kept_side_ref.shape[1]
     total = 0.0
     for n_ref, g_ref in zip(normed, grads):
@@ -418,20 +424,12 @@
     out_ref[...] = grad
 
 
-def spread_body(blocks, mask_ref, grad_ref, landing_ref, out_ref):
-    select = hot(iota((grad_ref.shape[0], landing_ref.shape[1]), 0) + 1 == landing_ref[...])
-    value = t_mm(select, grad_ref[...])
-    size = value.shape[0] // blocks
-    for k in range(blocks):
-        at = pl.ds(pl.multiple_of((mask_ref[0] ^ k) * size, size), size)
-        out_ref[at, :] = value[k * size : (k + 1) * size].astype(BF16)
-
-
-def return_body(capacity, mask_ref, owner_ref, back_ref, out_ref):
-    owner = owner_ref[...] ^ mask_ref[0]
-    rank_row, _ = rank_rows(owner)
-    chosen = hot(iota((back_ref.shape[0], owner.shape[1]), 0) == owner * capacity + rank_row)
-    out_ref[...] = t_mm(chosen, back_ref[...]).astype(BF16)
+def spread_body(select_ref, grad_ref, out_ref):
+    out_ref[...] = mm(select_ref[...], grad_ref[...]).astype(BF16)
+
+
+def return_body(chosen_ref, back_ref, out_ref):
+    out_ref[...] = mm(chosen_ref[...], back_ref[...]).astype(BF16)
 
 
 def sum_body(*refs):
@@ -442,7 +440,15 @@
     refs[-1][...] = total.astype(BF16)
 
 
-def finish_body(me_ref, w0_ref, w1_ref, w2_ref, w3_ref, proj_ref, outw_ref):
+def finish_body(
+    capacity, me_ref, mask_ref, w0_ref, w1_ref, w2_ref, w3_ref, owner_ref, proj_ref, outw_ref, chosen_ref
+):
+    owner = owner_ref[...] ^ mask_ref[0]
+    rank_row, _ = rank_rows(owner)
+    chosen = jnp.where(
+        iota(chosen_ref.shape[::-1], 0) == owner * capacity + rank_row, 1.0, 0.0
+    )
+    chosen_ref[...] = jnp.transpose(chosen).astype(BF16)
     me = me_ref[0]
     width = outw_ref.shape[1]
     for step, ref in enumerate((w0_ref, w1_ref, w2_ref, w3_ref)):
@@ -571,10 +577,12 @@
     share = width // owners
     pairs = owners // 2
     columns = 5 * piece
-    weight_parts = call(
-        functools.partial(weight_body, cycle, pairs), "weights",
-        [((pairs * share, columns), BF16)] * 2 if by_hops else [((width, columns), BF16)], [dp],
-        [side_keep, side_last, normed, near, far, cross, *grads], vmem=16,
+    *weight_parts, select = call(
+        functools.partial(weight_body, cycle, pairs, blocks), "weights",
+        ([((pairs * share, columns), BF16)] * 2 if by_hops else [((width, columns), BF16)])
+        + [((owners * capacity, rows), BF16)],
+        [dp, mask],
+        [side_keep, side_last, landing, normed, near, far, cross, *grads], vmem=16,
         scratch=[pltpu.VMEM((width, columns), F32)],
     )
     (partial_in,) = call(
@@ -585,8 +593,7 @@
         [own_block, p1, partial_in, owned, cotangent, proj_weight], vmem=16,
     )
     (back,) = call(
-        functools.partial(spread_body, blocks), "spread", [((owners * capacity, width), BF16)],
-        [mask], [grad_owned, landing],
+        spread_body, "spread", [((owners * capacity, width), BF16)], [], [select, grad_owned],
     )
     if by_hops:
         kept, sent = weight_parts
@@ -600,13 +607,12 @@
     (mine,) = call(sum_body, "sum", [((share, columns), BF16)], [], summed_parts, flops=10**11)
     returned = swap_whole(back)
     w1, w2, w3 = (hop(mine, step) for step in range(1, cycle))
-    (grad_tokens,) = call(
-        functools.partial(return_body, capacity), "give_back", [square], [mask], [owner_here, returned]
-    )
-    grad_proj, grad_outw = call(
-        finish_body, "finish", [((share, 4 * width), F32), ((share, width), F32)],
-        [me], [mine, w1, w2, w3],
-    )
+    grad_proj, grad_outw, chosen = call(
+        functools.partial(finish_body, capacity), "finish",
+        [((share, 4 * width), F32), ((share, width), F32), ((rows, owners * capacity), BF16)],
+        [me, mask], [mine, w1, w2, w3, owner_here],
+    )
+    (grad_tokens,) = call(return_body, "give_back", [square], [], [chosen, returned])
     return layer_out, grad_tokens, grad_proj, grad_outw
 
 

time: 89.9 us -> 88.8 us (0.988)
  starting transfers between devices: 36.2 us -> 32.3 us
  Pallas kernels: 21.3 us -> 23.4 us
  waiting for transfers between devices: 26.1 us -> 27.4 us
    ppermute x14, waiting for transfers between devices: 6.03 us -> 15.3 us  [hop(): return lax.ppermute(value, 'ctx', [(i, i ^ step) for i in range(cycle)])]
    all_to_all x1, waiting for transfers between devices: 10.2 us -> 4.29 us  [swap_whole(): lax.all_to_all(split, 'dp', split_axis=0, concat_axis=0, tiled=True)]
    ppermute x11, starting transfers between devices: 21.8 us -> 17.1 us  [dp_hop(): return lax.ppermute(value, 'dp', [(i, i ^ step) for i in range(owners)])]
    pallas_call x21, Pallas kernels: 21.3 us -> 23.4 us  [call(): pl.pallas_call(body, name=name, out_shape=[jax.ShapeDtypeStruct(s, d) for...]
    ppermute x11, waiting for transfers between devices: 9.88 us -> 7.81 us  [dp_hop(): return lax.ppermute(value, 'dp', [(i, i ^ step) for i in range(owners)])]
  transfers between devices with their start and end apart: 26 -> 26, of which waited for: 10 -> 13; matrix products, arithmetic and copies ran while one was open for 0% -> 0% of each run, Pallas kernels for 18% -> 21%
where the time goes in v14:
time: 88.8 us; the launch traced here: 88.1 us
  starting transfers between devices  32.3 us (36%)
  waiting for transfers between devices  27.4 us (31%)
  Pallas kernels  23.4 us (26%)
  local copies, waits for them, and re-layouts  4.2 us (5%)
  between operations  0.89 us (1%)
    pallas_call x21, Pallas kernels, call(): pl.pallas_call(body, name=name, out_shape=[jax.ShapeDtypeStruct(s, d) for...  23.4 us
    ppermute x11, starting transfers between devices, dp_hop(): return lax.ppermute(value, 'dp', [(i, i ^ step) for i in range(owners)])  17.1 us
    ppermute x14, waiting for transfers between devices, hop(): return lax.ppermute(value, 'ctx', [(i, i ^ step) for i in range(cycle)])  15.3 us
    ppermute x14, starting transfers between devices, hop(): return lax.ppermute(value, 'ctx', [(i, i ^ step) for i in range(cycle)])  11.7 us
    ppermute x11, waiting for transfers between devices, dp_hop(): return lax.ppermute(value, 'dp', [(i, i ^ step) for i in range(owners)])  7.81 us
    all_to_all x1, waiting for transfers between devices, swap_whole(): lax.all_to_all(split, 'dp', split_axis=0, concat_axis=0, tiled=True)  4.29 us
    unnamed x24, local copies, waits for them, and re-layouts  4.2 us
    all_to_all x1, starting transfers between devices, swap_whole(): lax.all_to_all(split, 'dp', split_axis=0, concat_axis=0, tiled=True)  3.49 us
  transfers between devices with their start and end apart: 26, of which 13 were waited for; matrix products, arithmetic and copies ran while one was open for 0% of the time, Pallas kernels for 21%

profile of v14, /device:TPU:0, one launch (start us, length us, event | category | flops | bytes accessed | tf_op | source)
XLA Modules:
  0.0 88.1 jit_solution(6657513547008279208)
XLA Ops:
  0.6 2.2 %pack.1 = (bf16[72,512]{1,0:T(8,128)(2,1)}, bf16[72,512]{1,0:T(8,128)(2,1)}, bf16[72,512]{1,0:T(8,128)(2,1)}, bf16[72,512]{1,0:T(8,128)(2,1)}, bf16[72,512]{1,0:...) custom-call(s32[1]{0:T(128)} %bitcast.1.mask_ref.dp_ref, ...), custom_call_target="tpu_custom_call" | custom-call | flops 100000000 | bytes 1048576 | tf_op jit(solution)/shard_map/pack/pallas_call | solution.py:22
  2.9 4.1 %collective-permute-start = (bf16[72,512]{1,0:T(8,128)(2,1)}, bf16[72,512]{1,0:T(8,128)(2,1)S(1)}, u32[]{:S(2)}, u32[]{:S(2)}) collective-permute-start(bf16[72,512]{1,0:T(8,128)(2,1)} %get-tuple-element.52), channel_id=1, source_target_pairs={{0,16},{4,20},{8,24},{12,28},{16,0},{20,4},{24,8},{28,12},{1,17},{... | collective-permute-start | bytes 221192 | tf_op jit(solution)/shard_map/ppermute | solution.py:487
  7.0 1.3 %collective-permute-start.1 = (bf16[72,512]{1,0:T(8,128)(2,1)}, bf16[72,512]{1,0:T(8,128)(2,1)S(1)}, u32[]{:S(2)}, u32[]{:S(2)}) collective-permute-start(bf16[72,512]{1,0:T(8,128)(2,1)} %get-tuple-element.53), channel_id=1, source_target_pairs={{0,20},{4,16},{8,28},{12,24},{16,4},{20,0},{24,12},{28,8},{1,21},{... | collective-permute-start | bytes 221192 | tf_op jit(solution)/shard_map/ppermute | solution.py:487
  8.3 3.6 %collective-permute-start.2 = (bf16[72,512]{1,0:T(8,128)(2,1)}, bf16[72,512]{1,0:T(8,128)(2,1)S(1)}, u32[]{:S(2)}, u32[]{:S(2)}) collective-permute-start(bf16[72,512]{1,0:T(8,128)(2,1)} %get-tuple-element.54), channel_id=1, source_target_pairs={{0,24},{4,28},{8,16},{12,20},{16,8},{20,12},{24,0},{28,4},{1,25},{... | collective-permute-start | bytes 221192 | tf_op jit(solution)/shard_map/ppermute | solution.py:487
  11.9 1.7 %collective-permute-start.4 = (bf16[72,512]{1,0:T(8,128)(2,1)}, bf16[72,512]{1,0:T(8,128)(2,1)S(1)}, u32[]{:S(2)}, u32[]{:S(2)}) collective-permute-start(bf16[72,512]{1,0:T(8,128)(2,1)} %get-tuple-element.56), channel_id=1, source_target_pairs={{0,4},{4,0},{8,12},{12,8},{16,20},{20,16},{24,28},{28,24},{1,5},{5... | collective-permute-start | bytes 221192 | tf_op jit(solution)/shard_map/ppermute | solution.py:487
  13.6 1.6 %copy-done = bf16[512,2048]{1,0:T(8,128)(2,1)S(1)} copy-done((bf16[512,2048]{1,0:T(8,128)(2,1)S(1)}, bf16[512,2048]{1,0:T(8,128)(2,1)}, u32[]{:S(2)}) %copy-start) | copy-done | bytes 2097176
  15.2 0.9 %copy-done.2 = bf16[256,512]{1,0:T(8,128)(2,1)S(1)} copy-done((bf16[256,512]{1,0:T(8,128)(2,1)S(1)}, bf16[256,512]{1,0:T(8,128)(2,1)}, u32[]{:S(2)}) %copy-start.2) | copy-done | bytes 262168
  16.1 1.0 %copy-done.4 = bf16[512,512]{1,0:T(8,128)(2,1)S(1)} copy-done((bf16[512,512]{1,0:T(8,128)(2,1)S(1)}, bf16[512,512]{1,0:T(8,128)(2,1)}, u32[]{:S(2)}) %copy-start.4) | copy-done | bytes 524312
  17.5 0.6 copy-done.6
  18.1 0.4 pack_rest.1
  18.6 1.8 %collective-permute-start.6 = (bf16[72,512]{1,0:T(8,128)(2,1)S(1)}, bf16[72,512]{1,0:T(8,128)(2,1)S(1)}, u32[]{:S(2)}, u32[]{:S(2)}) collective-permute-start(bf16[72,512]{1,0:T(8,128)(2,1)S(1)} %get-tuple-element.61), channel_id=1, source_target_pairs={{0,12},{4,8},{8,4},{12,0},{16,28},{20,24},{24,20},{28,16},{1,13},{... | collective-permute-start | bytes 221192 | tf_op jit(solution)/shard_map/ppermute | solution.py:487
  20.4 2.5 %collective-permute-done.5.refs_6_ = bf16[72,512]{1,0:T(8,128)(2,1)S(1)} collective-permute-done((bf16[72,512]{1,0:T(8,128)(2,1)S(1)}, bf16[72,512]{1,0:T(8,128)(2,1)S(1)}, u32[]{:S(2)}, u32[]{:S(2)}) %collective-permute-start.5) | collective-permute-done | bytes 73760 | tf_op jit(solution)/shard_map/ppermute | solution.py:487
  22.9 1.0 %collective-permute-done.6.refs_7_ = bf16[72,512]{1,0:T(8,128)(2,1)S(1)} collective-permute-done((bf16[72,512]{1,0:T(8,128)(2,1)S(1)}, bf16[72,512]{1,0:T(8,128)(2,1)S(1)}, u32[]{:S(2)}, u32[]{:S(2)}) %collective-permute-start.6) | collective-permute-done | bytes 73760 | tf_op jit(solution)/shard_map/ppermute | solution.py:487
  23.9 0.8 place.1
  24.8 1.6 %collective-permute-start.7 = (bf16[256,512]{1,0:T(8,128)(2,1)S(1)}, bf16[256,512]{1,0:T(8,128)(2,1)S(1)}, u32[]{:S(2)}, u32[]{:S(2)}) collective-permute-start(bf16[256,512]{1,0:T(8,128)(2,1)S(1)} %get-tuple-element.62.normed_ref.own_ref.n0_ref.refs_0_), channel_id=1, source_target_pairs={{0,2},{1,3},{2,0},{3,1},{4,6},{5,7},{6,4},{7,5},{8,10},{9,11},{10,... | collective-permute-start | bytes 786440 | tf_op jit(solution)/shard_map/ppermute | solution.py:476
  26.3 2.2 %own_rows.1 = (bf16[256,512]{1,0:T(8,128)(2,1)S(1)}, f32[256,512]{1,0:T(8,128)S(1)}, bf16[256,512]{1,0:T(8,128)(2,1)S(1)}, f32[256,512]{1,0:T(8,128)S(1)}, bf16[256,512]{1,0:T(8,128)(2,1)S(1)}) custom-call(s32[1]{0:T(128)} %bitcast.me_ref, s32[1,3]{1,0:T(1,128)S(1)} %copy-done.8, bf16[256,512]{1,0:T(8,128)(2,1)S(1)} %get-tuple-element.62.normed_ref.own_ref.n0_ref.refs_0_, ...), custom_call_target="tpu_custom_call" | custom-call | flops 10000000000 | bytes 1048576 | tf_op jit(solution)/shard_map/own_rows/pallas_call | solution.py:22
  28.6 2.6 %collective-permute-done.7.far_ref.n2_ref.refs_2_ = bf16[256,512]{1,0:T(8,128)(2,1)S(1)} collective-permute-done((bf16[256,512]{1,0:T(8,128)(2,1)S(1)}, bf16[256,512]{1,0:T(8,128)(2,1)S(1)}, u32[]{:S(2)}, u32[]{:S(2)}) %collective-permute-start.7) | collective-permute-done | bytes 262176 | tf_op jit(solution)/shard_map/ppermute | solution.py:476
  31.2 0.6 middle.1.partial_ref
  31.8 0.9 %collective-permute-done.8.cross_ref.n3_ref.refs_3_ = bf16[256,512]{1,0:T(8,128)(2,1)S(1)} collective-permute-done((bf16[256,512]{1,0:T(8,128)(2,1)S(1)}, bf16[256,512]{1,0:T(8,128)(2,1)S(1)}, u32[]{:S(2)}, u32[]{:S(2)}) %collective-permute-start.8) | collective-permute-done | bytes 262176 | tf_op jit(solution)/shard_map/ppermute | solution.py:476
  32.8 1.0 %forward.1 = (f32[256,512]{1,0:T(8,128)S(1)}, bf16[256,128]{1,0:T(8,128)(2,1)S(1)}, bf16[256,128]{1,0:T(8,128)(2,1)S(1)}, bf16[256,128]{1,0:T(8,128)(2,1)S(1)}, bf16[256,128]{1,0:T(8,128)(2,1)S(1)}) custom-call(s32[1]{0:T(128)} %bitcast.me_ref, s32[1,3]{1,0:T(1,128)S(1)} %copy-done.8, bf16[256,512]{1,0:T(8,128)(2,1)S(1)} %collective-permute-done.8.cross_ref.n3_ref.refs_3_, ...), custom_call_target="tpu_custom_call" | custom-call | flops 100000000 | bytes 1048576 | tf_op jit(solution)/shard_map/forward/pallas_call | solution.py:22
  33.7 1.0 %collective-permute-start.12 = (bf16[256,128]{1,0:T(8,128)(2,1)S(1)}, bf16[256,128]{1,0:T(8,128)(2,1)S(1)}, u32[]{:S(2)}, u32[]{:S(2)}) collective-permute-start(bf16[256,128]{1,0:T(8,128)(2,1)S(1)} %get-tuple-element.79), channel_id=1, source_target_pairs={{0,1},{1,0},{2,3},{3,2},{4,5},{5,4},{6,7},{7,6},{8,9},{9,8},{10,11... | collective-permute-start | bytes 196616 | tf_op jit(solution)/shard_map/ppermute | solution.py:476
  34.8 4.2 %collective-permute-start.13 = (bf16[256,128]{1,0:T(8,128)(2,1)S(1)}, bf16[256,128]{1,0:T(8,128)(2,1)S(1)}, u32[]{:S(2)}, u32[]{:S(2)}) collective-permute-start(bf16[256,128]{1,0:T(8,128)(2,1)S(1)} %get-tuple-element.80), channel_id=1, source_target_pairs={{0,2},{1,3},{2,0},{3,1},{4,6},{5,7},{6,4},{7,5},{8,10},{9,11},{10,... | collective-permute-start | bytes 196616 | tf_op jit(solution)/shard_map/ppermute | solution.py:476
  39.0 1.1 %side.1 = (bf16[512,512]{1,0:T(8,128)(2,1)S(1)}, bf16[512,512]{1,0:T(8,128)(2,1)S(1)}, f32[256,512]{1,0:T(8,128)S(1)}, bf16[256,512]{1,0:T(8,128)(2,1)}) custom-call(s32[1]{0:T(128)} %bitcast.me_ref, bf16[256,512]{1,0:T(8,128)(2,1)S(1)} %get-tuple-element.62.normed_ref.own_ref.n0_ref.refs_0_, f32[256,512]{1,0:T(8,128)S(1)} %get-tuple-element.67.normed_ref, ...), custom_call_target="tpu_custom_call" | custom-call | flops 100000000 | bytes 1048576 | tf_op jit(solution)/shard_map/side/pallas_call | solution.py:22
  40.3 0.8 heads.1
  41.3 2.0 %collective-permute-done.14.g3_ref = bf16[256,128]{1,0:T(8,128)(2,1)S(1)} collective-permute-done((bf16[256,128]{1,0:T(8,128)(2,1)S(1)}, bf16[256,128]{1,0:T(8,128)(2,1)S(1)}, u32[]{:S(2)}, u32[]{:S(2)}) %collective-permute-start.14) | collective-permute-done | bytes 65568 | tf_op jit(solution)/shard_map/ppermute | solution.py:476
  43.5 0.5 collective-permute-start.11
  44.0 5.8 %backward_far.1 = (bf16[256,384]{1,0:T(8,128)(2,1)S(1)}, bf16[256,384]{1,0:T(8,128)(2,1)S(1)}, f32[1024,384]{1,0:T(8,128)S(1)}) custom-call(s32[1]{0:T(128)} %bitcast.me_ref, s32[1,3]{1,0:T(1,128)S(1)} %copy-done.8, bf16[1024,384]{1,0:T(8,128)(2,1)S(1)} %get-tuple-element.76.part_ref, f32[1024,384]{1,0:T(8,128)S(1)} %get-tuple-element.77.slope_ref, ...), custom_call_target="tpu_custom_call" | custom-call | flops 10000000000 | bytes 1048576 | tf_op jit(solution)/shard_map/backward_far/pallas_call | solution.py:22
  49.8 1.7 %collective-permute-start.17 = (bf16[256,384]{1,0:T(8,128)(2,1)S(1)}, bf16[256,384]{1,0:T(8,128)(2,1)S(1)}, u32[]{:S(2)}, u32[]{:S(2)}) collective-permute-start(bf16[256,384]{1,0:T(8,128)(2,1)S(1)} %get-tuple-element.85.refs_6_), channel_id=1, source_target_pairs={{0,2},{1,3},{2,0},{3,1},{4,6},{5,7},{6,4},{7,5},{8,10},{9,11},{10,... | collective-permute-start | bytes 589832 | tf_op jit(solution)/shard_map/ppermute | solution.py:476
  51.5 2.6 %backward_rest.1 = (bf16[256,384]{1,0:T(8,128)(2,1)S(1)}, bf16[256,384]{1,0:T(8,128)(2,1)S(1)}) custom-call(s32[1]{0:T(128)} %bitcast.me_ref, s32[1,3]{1,0:T(1,128)S(1)} %copy-done.8, bf16[1024,384]{1,0:T(8,128)(2,1)S(1)} %get-tuple-element.76.part_ref, f32[1024,384]{1,0:T(8,128)S(1)} %get-tuple-element.77.slope_ref, bf16[1024,128]{1,0:T(8,128)(2,1)S(1)} %collect.1.grad_ref, ...), custom_call_target="tpu_custom_call" | custom-call | flops 100000000 | bytes 1048576 | tf_op jit(solution)/shard_map/backward_rest/pallas_call | solution.py:22
  54.1 0.6 collective-permute-start.16
  54.7 0.8 weights.1
  55.6 2.0 %collective-permute-done.17.far_ref = bf16[256,384]{1,0:T(8,128)(2,1)S(1)} collective-permute-done((bf16[256,384]{1,0:T(8,128)(2,1)S(1)}, bf16[256,384]{1,0:T(8,128)(2,1)S(1)}, u32[]{:S(2)}, u32[]{:S(2)}) %collective-permute-start.17) | collective-permute-done | bytes 196640 | tf_op jit(solution)/shard_map/ppermute | solution.py:476
  57.6 2.8 %collective-permute-done.18.cross_ref = bf16[256,384]{1,0:T(8,128)(2,1)S(1)} collective-permute-done((bf16[256,384]{1,0:T(8,128)(2,1)S(1)}, bf16[256,384]{1,0:T(8,128)(2,1)S(1)}, u32[]{:S(2)}, u32[]{:S(2)}) %collective-permute-start.18) | collective-permute-done | bytes 196640 | tf_op jit(solution)/shard_map/ppermute | solution.py:476
  60.5 0.5 input_far.1.partial_ref
  61.0 0.7 input_grad.1.grad_ref
  61.7 1.1 %spread.1._ = bf16[512,512]{1,0:T(8,128)(2,1)} custom-call(bf16[512,256]{1,0:T(8,128)(2,1)S(1)} %get-tuple-element.89.select_ref, bf16[256,512]{1,0:T(8,128)(2,1)S(1)} %input_grad.1.grad_ref), custom_call_target="tpu_custom_call" | custom-call | flops 100000000 | bytes 1048576 | tf_op jit(solution)/shard_map/spread/pallas_call | solution.py:22
  62.8 2.5 %collective-permute-done.15.came_ref = bf16[256,640]{1,0:T(8,128)(2,1)S(1)} collective-permute-done((bf16[256,640]{1,0:T(8,128)(2,1)S(1)}, bf16[256,640]{1,0:T(8,128)(2,1)S(1)}, u32[]{:S(2)}, u32[]{:S(2)}) %collective-permute-start.15) | collective-permute-done | bytes 327712 | tf_op jit(solution)/shard_map/ppermute | solution.py:487
  65.3 0.8 collective-permute-start.19
  66.1 0.7 collective-permute-start.20
  66.8 3.0 %collective-permute-start.21 = (bf16[64,640]{1,0:T(8,128)(2,1)S(1)}, bf16[64,640]{1,0:T(8,128)(2,1)S(1)}, u32[]{:S(2)}, u32[]{:S(2)}) collective-permute-start(bf16[64,640]{1,0:T(8,128)(2,1)S(1)} %get-tuple-element.94), channel_id=1, source_target_pairs={{0,24},{4,28},{8,16},{12,20},{16,8},{20,12},{24,0},{28,4},{1,25},{... | collective-permute-start | bytes 245768 | tf_op jit(solution)/shard_map/ppermute | solution.py:487
  69.8 3.5 %all-to-all-start = ((bf16[8,64,512]{2,1,0:T(8,128)(2,1)}), bf16[8,64,512]{2,1,0:T(8,128)(2,1)S(1)}, u32[]{:S(2)}, u32[]{:S(2)}) async-start(bf16[8,64,512]{2,1,0:T(8,128)(2,1)} %bitcast.4), calls=%async_computation | async-start | bytes 1048576 | tf_op jit(solution)/shard_map/all_to_all | solution.py:491
  73.3 1.8 %collective-permute-done.20.refs_2_ = bf16[64,640]{1,0:T(8,128)(2,1)S(1)} collective-permute-done((bf16[64,640]{1,0:T(8,128)(2,1)S(1)}, bf16[64,640]{1,0:T(8,128)(2,1)S(1)}, u32[]{:S(2)}, u32[]{:S(2)}) %collective-permute-start.20) | collective-permute-done | bytes 81952 | tf_op jit(solution)/shard_map/ppermute | solution.py:487
  75.2 1.7 %collective-permute-start.23 = (bf16[64,640]{1,0:T(8,128)(2,1)S(1)}, bf16[64,640]{1,0:T(8,128)(2,1)S(1)}, u32[]{:S(2)}, u32[]{:S(2)}) collective-permute-start(bf16[64,640]{1,0:T(8,128)(2,1)S(1)} %sum.1.w0_ref), channel_id=1, source_target_pairs={{0,2},{1,3},{2,0},{3,1},{4,6},{5,7},{6,4},{7,5},{8,10},{9,11},{10,... | collective-permute-start | bytes 245768 | tf_op jit(solution)/shard_map/ppermute | solution.py:476
  77.1 2.7 %collective-permute-done.24.w3_ref = bf16[64,640]{1,0:T(8,128)(2,1)S(1)} collective-permute-done((bf16[64,640]{1,0:T(8,128)(2,1)S(1)}, bf16[64,640]{1,0:T(8,128)(2,1)S(1)}, u32[]{:S(2)}, u32[]{:S(2)}) %collective-permute-start.24) | collective-permute-done | bytes 81952 | tf_op jit(solution)/shard_map/ppermute | solution.py:476
  79.8 1.9 %collective-permute-done.23.w2_ref = bf16[64,640]{1,0:T(8,128)(2,1)S(1)} collective-permute-done((bf16[64,640]{1,0:T(8,128)(2,1)S(1)}, bf16[64,640]{1,0:T(8,128)(2,1)S(1)}, u32[]{:S(2)}, u32[]{:S(2)}) %collective-permute-start.23) | collective-permute-done | bytes 81952 | tf_op jit(solution)/shard_map/ppermute | solution.py:476
  81.7 1.1 %finish.1 = (f32[64,2048]{1,0:T(8,128)}, f32[64,512]{1,0:T(8,128)}, bf16[256,512]{1,0:T(8,128)(2,1)S(1)}) custom-call(s32[1]{0:T(128)} %bitcast.me_ref, s32[1]{0:T(128)} %bitcast.1.mask_ref.dp_ref, bf16[64,640]{1,0:T(8,128)(2,1)S(1)} %sum.1.w0_ref, bf16[64,640]{1,0:T(8,128)(2,1)S(1)} %collective-permute-done.22.w1_ref, ...), custom_call_target="tpu_custom_call" | custom-call | flops 100000000 | bytes 1048576 | tf_op jit(solution)/shard_map/finish/pallas_call | solution.py:22
  82.8 4.3 %all-to-all-done = bf16[8,64,512]{2,1,0:T(8,128)(2,1)S(1)} async-done(((bf16[8,64,512]{2,1,0:T(8,128)(2,1)}), bf16[8,64,512]{2,1,0:T(8,128)(2,1)S(1)}, u32[]{:S(2)}, u32[]{:S(2)}) %all-to-all-start) | async-done | bytes 524320 | tf_op jit(solution)/shard_map/all_to_all | solution.py:491
  87.1 1.0 %give_back.1 = bf16[256,512]{1,0:T(8,128)(2,1)} custom-call(bf16[256,512]{1,0:T(8,128)(2,1)S(1)} %get-tuple-element.95.chosen_ref, bf16[512,512]{1,0:T(8,128)(2,1)S(1)} %bitcast.6), custom_call_target="tpu_custom_call" | custom-call | flops 100000000 | bytes 1048576 | tf_op jit(solution)/shard_map/give_back/pallas_call | solution.py:22
  (49 shorter events, 1.5 us)
Async XLA Ops:
  2.9 15.6 %collective-permute-start = (bf16[72,512]{1,0:T(8,128)(2,1)}, bf16[72,512]{1,0:T(8,128)(2,1)S(1)}, u32[]{:S(2)}, u32[]{:S(2)}) collective-permute-start(bf16[72,512]{1,0:T(8,128)(2,1)} %get-tuple-element.52), channel_id=1, source_target_pairs={{0,16},{4,20},{8,24},{12,28},{16,0},{20,4},{24,8},{28,12},{1,17},{... | collective-permute-start | bytes 221192 | tf_op jit(solution)/shard_map/ppermute | solution.py:487
  7.0 11.6 %collective-permute-start.1 = (bf16[72,512]{1,0:T(8,128)(2,1)}, bf16[72,512]{1,0:T(8,128)(2,1)S(1)}, u32[]{:S(2)}, u32[]{:S(2)}) collective-permute-start(bf16[72,512]{1,0:T(8,128)(2,1)} %get-tuple-element.53), channel_id=1, source_target_pairs={{0,20},{4,16},{8,28},{12,24},{16,4},{20,0},{24,12},{28,8},{1,21},{... | collective-permute-start | bytes 221192 | tf_op jit(solution)/shard_map/ppermute | solution.py:487
  8.3 12.1 %collective-permute-start.2 = (bf16[72,512]{1,0:T(8,128)(2,1)}, bf16[72,512]{1,0:T(8,128)(2,1)S(1)}, u32[]{:S(2)}, u32[]{:S(2)}) collective-permute-start(bf16[72,512]{1,0:T(8,128)(2,1)} %get-tuple-element.54), channel_id=1, source_target_pairs={{0,24},{4,28},{8,16},{12,20},{16,8},{20,12},{24,0},{28,4},{1,25},{... | collective-permute-start | bytes 221192 | tf_op jit(solution)/shard_map/ppermute | solution.py:487
  11.9 8.5 %collective-permute-start.3 = (bf16[72,512]{1,0:T(8,128)(2,1)}, bf16[72,512]{1,0:T(8,128)(2,1)S(1)}, u32[]{:S(2)}, u32[]{:S(2)}) collective-permute-start(bf16[72,512]{1,0:T(8,128)(2,1)} %get-tuple-element.55), channel_id=1, source_target_pairs={{0,28},{4,24},{8,20},{12,16},{16,12},{20,8},{24,4},{28,0},{1,29},{... | collective-permute-start | bytes 221192 | tf_op jit(solution)/shard_map/ppermute | solution.py:487
  11.9 8.5 %collective-permute-start.4 = (bf16[72,512]{1,0:T(8,128)(2,1)}, bf16[72,512]{1,0:T(8,128)(2,1)S(1)}, u32[]{:S(2)}, u32[]{:S(2)}) collective-permute-start(bf16[72,512]{1,0:T(8,128)(2,1)} %get-tuple-element.56), channel_id=1, source_target_pairs={{0,4},{4,0},{8,12},{12,8},{16,20},{20,16},{24,28},{28,24},{1,5},{5... | collective-permute-start | bytes 221192 | tf_op jit(solution)/shard_map/ppermute | solution.py:487
  13.6 1.6 %copy-start = (bf16[512,2048]{1,0:T(8,128)(2,1)S(1)}, bf16[512,2048]{1,0:T(8,128)(2,1)}, u32[]{:S(2)}) copy-start(bf16[512,2048]{1,0:T(8,128)(2,1)} %proj_ref.15) | copy-start | bytes 6291460
  15.1 0.9 %copy-start.2 = (bf16[256,512]{1,0:T(8,128)(2,1)S(1)}, bf16[256,512]{1,0:T(8,128)(2,1)}, u32[]{:S(2)}) copy-start(bf16[256,512]{1,0:T(8,128)(2,1)} %cot_ref.5) | copy-start | bytes 786436
  16.1 1.0 %copy-start.4 = (bf16[512,512]{1,0:T(8,128)(2,1)S(1)}, bf16[512,512]{1,0:T(8,128)(2,1)}, u32[]{:S(2)}) copy-start(bf16[512,512]{1,0:T(8,128)(2,1)} %outw_ref.3) | copy-start | bytes 1572868
  17.1 0.9 %copy-start.6 = (bf16[256,512]{1,0:T(8,128)(2,1)S(1)}, bf16[256,512]{1,0:T(8,128)(2,1)}, u32[]{:S(2)}) copy-start(bf16[256,512]{1,0:T(8,128)(2,1)} %get-tuple-element.59.tokens_ref) | copy-start | bytes 786436
  17.1 1.0 %copy-start.9 = (s32[1,256]{1,0:T(1,128)S(1)}, s32[1,256]{1,0:T(1,128)}, u32[]{:S(2)}) copy-start(s32[1,256]{1,0:T(1,128)} %get-tuple-element.57.owner_ref) | copy-start | bytes 3076
  17.1 1.0 %copy-start.11 = (s32[1,256]{1,0:T(1,128)S(1)}, s32[1,256]{1,0:T(1,128)}, u32[]{:S(2)}) copy-start(s32[1,256]{1,0:T(1,128)} %get-tuple-element.58.slot_ref) | copy-start | bytes 3076
  17.1 6.8 %copy-start.7 = (bf16[72,512]{1,0:T(8,128)(2,1)S(1)}, bf16[72,512]{1,0:T(8,128)(2,1)}, u32[]{:S(2)}) copy-start(bf16[72,512]{1,0:T(8,128)(2,1)} %get-tuple-element.51.refs_0_) | copy-start | bytes 221188
  17.2 9.2 %copy-start.1 = (bf16[512,2048]{1,0:T(8,128)(2,1)S(1)}, bf16[512,2048]{1,0:T(8,128)(2,1)}, u32[]{:S(2)}) copy-start(bf16[512,2048]{1,0:T(8,128)(2,1)} %proj_ref.15) | copy-start | bytes 6291460
  17.2 9.2 %copy-start.8 = (s32[1,3]{1,0:T(1,128)S(1)}, s32[1,3]{1,0:T(1,128)}, u32[]{:S(2)}) copy-start(s32[1,3]{1,0:T(1,128)} %lengths_ref.9) | copy-start | bytes 40
  18.5 4.4 %collective-permute-start.5 = (bf16[72,512]{1,0:T(8,128)(2,1)S(1)}, bf16[72,512]{1,0:T(8,128)(2,1)S(1)}, u32[]{:S(2)}, u32[]{:S(2)}) collective-permute-start(bf16[72,512]{1,0:T(8,128)(2,1)S(1)} %get-tuple-element.60), channel_id=1, source_target_pairs={{0,8},{4,12},{8,0},{12,4},{16,24},{20,28},{24,16},{28,20},{1,9},{5... | collective-permute-start | bytes 221192 | tf_op jit(solution)/shard_map/ppermute | solution.py:487
  18.6 5.3 %collective-permute-start.6 = (bf16[72,512]{1,0:T(8,128)(2,1)S(1)}, bf16[72,512]{1,0:T(8,128)(2,1)S(1)}, u32[]{:S(2)}, u32[]{:S(2)}) collective-permute-start(bf16[72,512]{1,0:T(8,128)(2,1)S(1)} %get-tuple-element.61), channel_id=1, source_target_pairs={{0,12},{4,8},{8,4},{12,0},{16,28},{20,24},{24,20},{28,16},{1,13},{... | collective-permute-start | bytes 221192 | tf_op jit(solution)/shard_map/ppermute | solution.py:487
  24.8 6.4 %collective-permute-start.7 = (bf16[256,512]{1,0:T(8,128)(2,1)S(1)}, bf16[256,512]{1,0:T(8,128)(2,1)S(1)}, u32[]{:S(2)}, u32[]{:S(2)}) collective-permute-start(bf16[256,512]{1,0:T(8,128)(2,1)S(1)} %get-tuple-element.62.normed_ref.own_ref.n0_ref.refs_0_), channel_id=1, source_target_pairs={{0,2},{1,3},{2,0},{3,1},{4,6},{5,7},{6,4},{7,5},{8,10},{9,11},{10,... | collective-permute-start | bytes 786440 | tf_op jit(solution)/shard_map/ppermute | solution.py:476
  28.6 2.7 %collective-permute-start.9 = (bf16[256,512]{1,0:T(8,128)(2,1)S(1)}, bf16[256,512]{1,0:T(8,128)(2,1)S(1)}, u32[]{:S(2)}, u32[]{:S(2)}) collective-permute-start(bf16[256,512]{1,0:T(8,128)(2,1)S(1)} %get-tuple-element.65), channel_id=1, source_target_pairs={{0,1},{1,0},{2,3},{3,2},{4,5},{5,4},{6,7},{7,6},{8,9},{9,8},{10,11... | collective-permute-start | bytes 786440 | tf_op jit(solution)/shard_map/ppermute | solution.py:476
  31.2 1.5 %collective-permute-start.8 = (bf16[256,512]{1,0:T(8,128)(2,1)S(1)}, bf16[256,512]{1,0:T(8,128)(2,1)S(1)}, u32[]{:S(2)}, u32[]{:S(2)}) collective-permute-start(bf16[256,512]{1,0:T(8,128)(2,1)S(1)} %collective-permute-done.7.far_ref.n2_ref.refs_2_), channel_id=1, source_target_pairs={{0,1},{1,0},{2,3},{3,2},{4,5},{5,4},{6,7},{7,6},{8,9},{9,8},{10,11... | collective-permute-start | bytes 786440 | tf_op jit(solution)/shard_map/ppermute | solution.py:476
  32.8 6.3 %copy-start.3 = (bf16[256,512]{1,0:T(8,128)(2,1)S(1)}, bf16[256,512]{1,0:T(8,128)(2,1)}, u32[]{:S(2)}) copy-start(bf16[256,512]{1,0:T(8,128)(2,1)} %cot_ref.5) | copy-start | bytes 786436
  32.8 6.3 %copy-start.5 = (bf16[512,512]{1,0:T(8,128)(2,1)S(1)}, bf16[512,512]{1,0:T(8,128)(2,1)}, u32[]{:S(2)}) copy-start(bf16[512,512]{1,0:T(8,128)(2,1)} %outw_ref.3) | copy-start | bytes 1572868
  33.7 7.4 %collective-permute-start.12 = (bf16[256,128]{1,0:T(8,128)(2,1)S(1)}, bf16[256,128]{1,0:T(8,128)(2,1)S(1)}, u32[]{:S(2)}, u32[]{:S(2)}) collective-permute-start(bf16[256,128]{1,0:T(8,128)(2,1)S(1)} %get-tuple-element.79), channel_id=1, source_target_pairs={{0,1},{1,0},{2,3},{3,2},{4,5},{5,4},{6,7},{7,6},{8,9},{9,8},{10,11... | collective-permute-start | bytes 196616 | tf_op jit(solution)/shard_map/ppermute | solution.py:476
  34.8 6.6 %collective-permute-start.13 = (bf16[256,128]{1,0:T(8,128)(2,1)S(1)}, bf16[256,128]{1,0:T(8,128)(2,1)S(1)}, u32[]{:S(2)}, u32[]{:S(2)}) collective-permute-start(bf16[256,128]{1,0:T(8,128)(2,1)S(1)} %get-tuple-element.80), channel_id=1, source_target_pairs={{0,2},{1,3},{2,0},{3,1},{4,6},{5,7},{6,4},{7,5},{8,10},{9,11},{10,... | collective-permute-start | bytes 196616 | tf_op jit(solution)/shard_map/ppermute | solution.py:476
  39.0 4.4 %collective-permute-start.14 = (bf16[256,128]{1,0:T(8,128)(2,1)S(1)}, bf16[256,128]{1,0:T(8,128)(2,1)S(1)}, u32[]{:S(2)}, u32[]{:S(2)}) collective-permute-start(bf16[256,128]{1,0:T(8,128)(2,1)S(1)} %get-tuple-element.81), channel_id=1, source_target_pairs={{0,3},{1,2},{2,1},{3,0},{4,7},{5,6},{6,5},{7,4},{8,11},{9,10},{10,... | collective-permute-start | bytes 196616 | tf_op jit(solution)/shard_map/ppermute | solution.py:476
  40.1 3.3 %collective-permute-start.10 = (bf16[512,512]{1,0:T(8,128)(2,1)S(1)}, bf16[512,512]{1,0:T(8,128)(2,1)S(1)}, u32[]{:S(2)}, u32[]{:S(2)}) collective-permute-start(bf16[512,512]{1,0:T(8,128)(2,1)S(1)} %get-tuple-element.72), channel_id=1, source_target_pairs={{0,1},{1,0},{2,3},{3,2},{4,5},{5,4},{6,7},{7,6},{8,9},{9,8},{10,11... | collective-permute-start | bytes 1572872 | tf_op jit(solution)/shard_map/ppermute | solution.py:476
  43.5 11.2 %collective-permute-start.11 = (bf16[512,256]{1,0:T(8,128)(2,1)S(1)}, bf16[512,256]{1,0:T(8,128)(2,1)S(1)}, u32[]{:S(2)}, u32[]{:S(2)}) collective-permute-start(bf16[512,256]{1,0:T(8,128)(2,1)S(1)} %get-tuple-element.74), channel_id=1, source_target_pairs={{0,2},{1,3},{2,0},{3,1},{4,6},{5,7},{6,4},{7,5},{8,10},{9,11},{10,... | collective-permute-start | bytes 786440 | tf_op jit(solution)/shard_map/ppermute | solution.py:476
  49.8 7.8 %collective-permute-start.17 = (bf16[256,384]{1,0:T(8,128)(2,1)S(1)}, bf16[256,384]{1,0:T(8,128)(2,1)S(1)}, u32[]{:S(2)}, u32[]{:S(2)}) collective-permute-start(bf16[256,384]{1,0:T(8,128)(2,1)S(1)} %get-tuple-element.85.refs_6_), channel_id=1, source_target_pairs={{0,2},{1,3},{2,0},{3,1},{4,6},{5,7},{6,4},{7,5},{8,10},{9,11},{10,... | collective-permute-start | bytes 589832 | tf_op jit(solution)/shard_map/ppermute | solution.py:476
  51.5 8.9 %collective-permute-start.18 = (bf16[256,384]{1,0:T(8,128)(2,1)S(1)}, bf16[256,384]{1,0:T(8,128)(2,1)S(1)}, u32[]{:S(2)}, u32[]{:S(2)}) collective-permute-start(bf16[256,384]{1,0:T(8,128)(2,1)S(1)} %get-tuple-element.86.refs_7_), channel_id=1, source_target_pairs={{0,3},{1,2},{2,1},{3,0},{4,7},{5,6},{6,5},{7,4},{8,11},{9,10},{10,... | collective-permute-start | bytes 589832 | tf_op jit(solution)/shard_map/ppermute | solution.py:476
  54.1 6.8 %collective-permute-start.16 = (bf16[256,384]{1,0:T(8,128)(2,1)S(1)}, bf16[256,384]{1,0:T(8,128)(2,1)S(1)}, u32[]{:S(2)}, u32[]{:S(2)}) collective-permute-start(bf16[256,384]{1,0:T(8,128)(2,1)S(1)} %get-tuple-element.84.refs_5_), channel_id=1, source_target_pairs={{0,1},{1,0},{2,3},{3,2},{4,5},{5,4},{6,7},{7,6},{8,9},{9,8},{10,11... | collective-permute-start | bytes 589832 | tf_op jit(solution)/shard_map/ppermute | solution.py:476
  55.5 9.7 %collective-permute-start.15 = (bf16[256,640]{1,0:T(8,128)(2,1)S(1)}, bf16[256,640]{1,0:T(8,128)(2,1)S(1)}, u32[]{:S(2)}, u32[]{:S(2)}) collective-permute-start(bf16[256,640]{1,0:T(8,128)(2,1)S(1)} %get-tuple-element.88), channel_id=1, source_target_pairs={{0,4},{4,0},{8,12},{12,8},{16,20},{20,16},{24,28},{28,24},{1,5},{5... | collective-permute-start | bytes 983048 | tf_op jit(solution)/shard_map/ppermute | solution.py:487
  65.3 8.0 %collective-permute-start.19 = (bf16[64,640]{1,0:T(8,128)(2,1)S(1)}, bf16[64,640]{1,0:T(8,128)(2,1)S(1)}, u32[]{:S(2)}, u32[]{:S(2)}) collective-permute-start(bf16[64,640]{1,0:T(8,128)(2,1)S(1)} %get-tuple-element.92), channel_id=1, source_target_pairs={{0,8},{4,12},{8,0},{12,4},{16,24},{20,28},{24,16},{28,20},{1,9},{5... | collective-permute-start | bytes 245768 | tf_op jit(solution)/shard_map/ppermute | solution.py:487
  66.1 9.0 %collective-permute-start.20 = (bf16[64,640]{1,0:T(8,128)(2,1)S(1)}, bf16[64,640]{1,0:T(8,128)(2,1)S(1)}, u32[]{:S(2)}, u32[]{:S(2)}) collective-permute-start(bf16[64,640]{1,0:T(8,128)(2,1)S(1)} %get-tuple-element.93), channel_id=1, source_target_pairs={{0,16},{4,20},{8,24},{12,28},{16,0},{20,4},{24,8},{28,12},{1,17},{... | collective-permute-start | bytes 245768 | tf_op jit(solution)/shard_map/ppermute | solution.py:487
  66.8 8.3 %collective-permute-start.21 = (bf16[64,640]{1,0:T(8,128)(2,1)S(1)}, bf16[64,640]{1,0:T(8,128)(2,1)S(1)}, u32[]{:S(2)}, u32[]{:S(2)}) collective-permute-start(bf16[64,640]{1,0:T(8,128)(2,1)S(1)} %get-tuple-element.94), channel_id=1, source_target_pairs={{0,24},{4,28},{8,16},{12,20},{16,8},{20,12},{24,0},{28,4},{1,25},{... | collective-permute-start | bytes 245768 | tf_op jit(solution)/shard_map/ppermute | solution.py:487
  69.8 17.3 %all-to-all-start = ((bf16[8,64,512]{2,1,0:T(8,128)(2,1)}), bf16[8,64,512]{2,1,0:T(8,128)(2,1)S(1)}, u32[]{:S(2)}, u32[]{:S(2)}) async-start(bf16[8,64,512]{2,1,0:T(8,128)(2,1)} %bitcast.4), calls=%async_computation | async-start | bytes 1048576 | tf_op jit(solution)/shard_map/all_to_all | solution.py:491
  75.1 6.6 %copy-start.10 = (s32[1,256]{1,0:T(1,128)S(1)}, s32[1,256]{1,0:T(1,128)}, u32[]{:S(2)}) copy-start(s32[1,256]{1,0:T(1,128)} %get-tuple-element.57.owner_ref) | copy-start | bytes 3076
  75.1 4.6 %collective-permute-start.24 = (bf16[64,640]{1,0:T(8,128)(2,1)S(1)}, bf16[64,640]{1,0:T(8,128)(2,1)S(1)}, u32[]{:S(2)}, u32[]{:S(2)}) collective-permute-start(bf16[64,640]{1,0:T(8,128)(2,1)S(1)} %sum.1.w0_ref), channel_id=1, source_target_pairs={{0,3},{1,2},{2,1},{3,0},{4,7},{5,6},{6,5},{7,4},{8,11},{9,10},{10,... | collective-permute-start | bytes 245768 | tf_op jit(solution)/shard_map/ppermute | solution.py:476
  75.2 6.5 %collective-permute-start.23 = (bf16[64,640]{1,0:T(8,128)(2,1)S(1)}, bf16[64,640]{1,0:T(8,128)(2,1)S(1)}, u32[]{:S(2)}, u32[]{:S(2)}) collective-permute-start(bf16[64,640]{1,0:T(8,128)(2,1)S(1)} %sum.1.w0_ref), channel_id=1, source_target_pairs={{0,2},{1,3},{2,0},{3,1},{4,6},{5,7},{6,4},{7,5},{8,10},{9,11},{10,... | collective-permute-start | bytes 245768 | tf_op jit(solution)/shard_map/ppermute | solution.py:476
  76.9 4.8 %collective-permute-start.22 = (bf16[64,640]{1,0:T(8,128)(2,1)S(1)}, bf16[64,640]{1,0:T(8,128)(2,1)S(1)}, u32[]{:S(2)}, u32[]{:S(2)}) collective-permute-start(bf16[64,640]{1,0:T(8,128)(2,1)S(1)} %sum.1.w0_ref), channel_id=1, source_target_pairs={{0,1},{1,0},{2,3},{3,2},{4,5},{5,4},{6,7},{7,6},{8,9},{9,8},{10,11... | collective-permute-start | bytes 245768 | tf_op jit(solution)/shard_map/ppermute | solution.py:476

commit v15 on v14

--- a/solution.py
+++ b/solution.py
@@ -601,7 +601,8 @@
             pair_body, "pair_sum", [((share, columns), BF16)] * pairs, [], [kept, dp_hop(sent, 1)],
             far=[back],
         )
-        summed_parts = [halves[0]] + [dp_hop(halves[j], 2 * j) for j in range(1, pairs)]
+        order = sorted(range(1, pairs), key=lambda j: (j < pairs // 2, j))
+        summed_parts = [halves[0]] + [dp_hop(halves[j], 2 * j) for j in order]
     else:
         summed_parts = [swap_whole(weight_parts[0]).reshape(owners, share, columns)]
     (mine,) = call(sum_body, "sum", [((share, columns), BF16)], [], summed_parts, flops=10**11)

time: 88.8 us -> 89.5 us (level)
  starting transfers between devices: 32.3 us -> 38 us
  waiting for transfers between devices: 27.4 us -> 24.9 us
  Pallas kernels: 23.4 us -> 21.2 us
    ppermute x11, starting transfers between devices: 17.1 us -> 22.6 us  [dp_hop(): return lax.ppermute(value, 'dp', [(i, i ^ step) for i in range(owners)])]
    ppermute x14, waiting for transfers between devices: 15.3 us -> 11.8 us  [hop(): return lax.ppermute(value, 'ctx', [(i, i ^ step) for i in range(cycle)])]
    pallas_call x21, Pallas kernels: 23.4 us -> 21.2 us  [call(): pl.pallas_call(body, name=name, out_shape=[jax.ShapeDtypeStruct(s, d) for...]
    all_to_all x1, starting transfers between devices: 3.49 us -> 5.02 us  [swap_whole(): lax.all_to_all(split, 'dp', split_axis=0, concat_axis=0, tiled=True)]
    ppermute x14, starting transfers between devices: 11.7 us -> 10.3 us  [hop(): return lax.ppermute(value, 'ctx', [(i, i ^ step) for i in range(cycle)])]
  transfers between devices with their start and end apart: 26 -> 26, of which waited for: 13 -> 12; matrix products, arithmetic and copies ran while one was open for 0% -> 0% of each run, Pallas kernels for 21% -> 18%
where the time goes in v15:
time: 89.5 us; the launch traced here: 89.2 us
  starting transfers between devices  38 us (42%)
  waiting for transfers between devices  24.9 us (28%)
  Pallas kernels  21.2 us (24%)
  local copies, waits for them, and re-layouts  4.2 us (5%)
    ppermute x11, starting transfers between devices, dp_hop(): return lax.ppermute(value, 'dp', [(i, i ^ step) for i in range(owners)])  22.6 us
    pallas_call x21, Pallas kernels, call(): pl.pallas_call(body, name=name, out_shape=[jax.ShapeDtypeStruct(s, d) for...  21.2 us
    ppermute x14, waiting for transfers between devices, hop(): return lax.ppermute(value, 'ctx', [(i, i ^ step) for i in range(cycle)])  11.8 us
    ppermute x14, starting transfers between devices, hop(): return lax.ppermute(value, 'ctx', [(i, i ^ step) for i in range(cycle)])  10.3 us
    ppermute x11, waiting for transfers between devices, dp_hop(): return lax.ppermute(value, 'dp', [(i, i ^ step) for i in range(owners)])  8.57 us
    all_to_all x1, starting transfers between devices, swap_whole(): lax.all_to_all(split, 'dp', split_axis=0, concat_axis=0, tiled=True)  5.02 us
    all_to_all x1, waiting for transfers between devices, swap_whole(): lax.all_to_all(split, 'dp', split_axis=0, concat_axis=0, tiled=True)  4.5 us
    unnamed x24, local copies, waits for them, and re-layouts  4.2 us
  transfers between devices with their start and end apart: 26, of which 12 were waited for; matrix products, arithmetic and copies ran while one was open for 0% of the time, Pallas kernels for 18%

profile of v15, /device:TPU:0, one launch (start us, length us, event | category | flops | bytes accessed | tf_op | source)
XLA Modules:
  0.0 89.2 jit_solution(15509981409755584608)
XLA Ops:
  0.6 2.2 %pack.1 = (bf16[72,512]{1,0:T(8,128)(2,1)}, bf16[72,512]{1,0:T(8,128)(2,1)}, bf16[72,512]{1,0:T(8,128)(2,1)}, bf16[72,512]{1,0:T(8,128)(2,1)}, bf16[72,512]{1,0:...) custom-call(s32[1]{0:T(128)} %bitcast.1.mask_ref.dp_ref, ...), custom_call_target="tpu_custom_call" | custom-call | flops 100000000 | bytes 1048576 | tf_op jit(solution)/shard_map/pack/pallas_call | solution.py:22
  2.9 4.1 %collective-permute-start = (bf16[72,512]{1,0:T(8,128)(2,1)}, bf16[72,512]{1,0:T(8,128)(2,1)S(1)}, u32[]{:S(2)}, u32[]{:S(2)}) collective-permute-start(bf16[72,512]{1,0:T(8,128)(2,1)} %get-tuple-element.52), channel_id=1, source_target_pairs={{0,16},{4,20},{8,24},{12,28},{16,0},{20,4},{24,8},{28,12},{1,17},{... | collective-permute-start | bytes 221192 | tf_op jit(solution)/shard_map/ppermute | solution.py:487
  7.0 1.3 %collective-permute-start.1 = (bf16[72,512]{1,0:T(8,128)(2,1)}, bf16[72,512]{1,0:T(8,128)(2,1)S(1)}, u32[]{:S(2)}, u32[]{:S(2)}) collective-permute-start(bf16[72,512]{1,0:T(8,128)(2,1)} %get-tuple-element.53), channel_id=1, source_target_pairs={{0,20},{4,16},{8,28},{12,24},{16,4},{20,0},{24,12},{28,8},{1,21},{... | collective-permute-start | bytes 221192 | tf_op jit(solution)/shard_map/ppermute | solution.py:487
  8.3 3.6 %collective-permute-start.2 = (bf16[72,512]{1,0:T(8,128)(2,1)}, bf16[72,512]{1,0:T(8,128)(2,1)S(1)}, u32[]{:S(2)}, u32[]{:S(2)}) collective-permute-start(bf16[72,512]{1,0:T(8,128)(2,1)} %get-tuple-element.54), channel_id=1, source_target_pairs={{0,24},{4,28},{8,16},{12,20},{16,8},{20,12},{24,0},{28,4},{1,25},{... | collective-permute-start | bytes 221192 | tf_op jit(solution)/shard_map/ppermute | solution.py:487
  11.9 1.7 %collective-permute-start.4 = (bf16[72,512]{1,0:T(8,128)(2,1)}, bf16[72,512]{1,0:T(8,128)(2,1)S(1)}, u32[]{:S(2)}, u32[]{:S(2)}) collective-permute-start(bf16[72,512]{1,0:T(8,128)(2,1)} %get-tuple-element.56), channel_id=1, source_target_pairs={{0,4},{4,0},{8,12},{12,8},{16,20},{20,16},{24,28},{28,24},{1,5},{5... | collective-permute-start | bytes 221192 | tf_op jit(solution)/shard_map/ppermute | solution.py:487
  13.6 1.6 %copy-done = bf16[512,2048]{1,0:T(8,128)(2,1)S(1)} copy-done((bf16[512,2048]{1,0:T(8,128)(2,1)S(1)}, bf16[512,2048]{1,0:T(8,128)(2,1)}, u32[]{:S(2)}) %copy-start) | copy-done | bytes 2097176
  15.2 0.9 %copy-done.2 = bf16[256,512]{1,0:T(8,128)(2,1)S(1)} copy-done((bf16[256,512]{1,0:T(8,128)(2,1)S(1)}, bf16[256,512]{1,0:T(8,128)(2,1)}, u32[]{:S(2)}) %copy-start.2) | copy-done | bytes 262168
  16.1 1.0 %copy-done.4 = bf16[512,512]{1,0:T(8,128)(2,1)S(1)} copy-done((bf16[512,512]{1,0:T(8,128)(2,1)S(1)}, bf16[512,512]{1,0:T(8,128)(2,1)}, u32[]{:S(2)}) %copy-start.4) | copy-done | bytes 524312
  17.2 0.3 early.1._.grad_ref
  17.5 0.6 copy-done.6
  18.1 0.4 pack_rest.1
  18.6 1.8 %collective-permute-start.6 = (bf16[72,512]{1,0:T(8,128)(2,1)S(1)}, bf16[72,512]{1,0:T(8,128)(2,1)S(1)}, u32[]{:S(2)}, u32[]{:S(2)}) collective-permute-start(bf16[72,512]{1,0:T(8,128)(2,1)S(1)} %get-tuple-element.61), channel_id=1, source_target_pairs={{0,12},{4,8},{8,4},{12,0},{16,28},{20,24},{24,20},{28,16},{1,13},{... | collective-permute-start | bytes 221192 | tf_op jit(solution)/shard_map/ppermute | solution.py:487
  20.4 2.5 %collective-permute-done.5.refs_6_ = bf16[72,512]{1,0:T(8,128)(2,1)S(1)} collective-permute-done((bf16[72,512]{1,0:T(8,128)(2,1)S(1)}, bf16[72,512]{1,0:T(8,128)(2,1)S(1)}, u32[]{:S(2)}, u32[]{:S(2)}) %collective-permute-start.5) | collective-permute-done | bytes 73760 | tf_op jit(solution)/shard_map/ppermute | solution.py:487
  22.9 1.0 %collective-permute-done.6.refs_7_ = bf16[72,512]{1,0:T(8,128)(2,1)S(1)} collective-permute-done((bf16[72,512]{1,0:T(8,128)(2,1)S(1)}, bf16[72,512]{1,0:T(8,128)(2,1)S(1)}, u32[]{:S(2)}, u32[]{:S(2)}) %collective-permute-start.6) | collective-permute-done | bytes 73760 | tf_op jit(solution)/shard_map/ppermute | solution.py:487
  23.9 0.8 place.1
  24.8 1.6 %collective-permute-start.7 = (bf16[256,512]{1,0:T(8,128)(2,1)S(1)}, bf16[256,512]{1,0:T(8,128)(2,1)S(1)}, u32[]{:S(2)}, u32[]{:S(2)}) collective-permute-start(bf16[256,512]{1,0:T(8,128)(2,1)S(1)} %get-tuple-element.62.normed_ref.own_ref.n0_ref.refs_0_), channel_id=1, source_target_pairs={{0,2},{1,3},{2,0},{3,1},{4,6},{5,7},{6,4},{7,5},{8,10},{9,11},{10,... | collective-permute-start | bytes 786440 | tf_op jit(solution)/shard_map/ppermute | solution.py:476
  26.3 2.2 %own_rows.1 = (bf16[256,512]{1,0:T(8,128)(2,1)S(1)}, f32[256,512]{1,0:T(8,128)S(1)}, bf16[256,512]{1,0:T(8,128)(2,1)S(1)}, f32[256,512]{1,0:T(8,128)S(1)}, bf16[256,512]{1,0:T(8,128)(2,1)S(1)}) custom-call(s32[1]{0:T(128)} %bitcast.me_ref, s32[1,3]{1,0:T(1,128)S(1)} %copy-done.8, bf16[256,512]{1,0:T(8,128)(2,1)S(1)} %get-tuple-element.62.normed_ref.own_ref.n0_ref.refs_0_, ...), custom_call_target="tpu_custom_call" | custom-call | flops 10000000000 | bytes 1048576 | tf_op jit(solution)/shard_map/own_rows/pallas_call | solution.py:22
  28.6 2.6 %collective-permute-done.7.far_ref.n2_ref.refs_2_ = bf16[256,512]{1,0:T(8,128)(2,1)S(1)} collective-permute-done((bf16[256,512]{1,0:T(8,128)(2,1)S(1)}, bf16[256,512]{1,0:T(8,128)(2,1)S(1)}, u32[]{:S(2)}, u32[]{:S(2)}) %collective-permute-start.7) | collective-permute-done | bytes 262176 | tf_op jit(solution)/shard_map/ppermute | solution.py:476
  31.2 0.6 middle.1.partial_ref
  31.8 0.9 %collective-permute-done.8.cross_ref.n3_ref.refs_3_ = bf16[256,512]{1,0:T(8,128)(2,1)S(1)} collective-permute-done((bf16[256,512]{1,0:T(8,128)(2,1)S(1)}, bf16[256,512]{1,0:T(8,128)(2,1)S(1)}, u32[]{:S(2)}, u32[]{:S(2)}) %collective-permute-start.8) | collective-permute-done | bytes 262176 | tf_op jit(solution)/shard_map/ppermute | solution.py:476
  32.8 1.0 %forward.1 = (f32[256,512]{1,0:T(8,128)S(1)}, bf16[256,128]{1,0:T(8,128)(2,1)S(1)}, bf16[256,128]{1,0:T(8,128)(2,1)S(1)}, bf16[256,128]{1,0:T(8,128)(2,1)S(1)}, bf16[256,128]{1,0:T(8,128)(2,1)S(1)}) custom-call(s32[1]{0:T(128)} %bitcast.me_ref, s32[1,3]{1,0:T(1,128)S(1)} %copy-done.8, bf16[256,512]{1,0:T(8,128)(2,1)S(1)} %collective-permute-done.8.cross_ref.n3_ref.refs_3_, ...), custom_call_target="tpu_custom_call" | custom-call | flops 100000000 | bytes 1048576 | tf_op jit(solution)/shard_map/forward/pallas_call | solution.py:22
  33.9 3.7 %collective-permute-start.13 = (bf16[256,128]{1,0:T(8,128)(2,1)S(1)}, bf16[256,128]{1,0:T(8,128)(2,1)S(1)}, u32[]{:S(2)}, u32[]{:S(2)}) collective-permute-start(bf16[256,128]{1,0:T(8,128)(2,1)S(1)} %get-tuple-element.80), channel_id=1, source_target_pairs={{0,2},{1,3},{2,0},{3,1},{4,6},{5,7},{6,4},{7,5},{8,10},{9,11},{10,... | collective-permute-start | bytes 196616 | tf_op jit(solution)/shard_map/ppermute | solution.py:476
  37.6 1.1 %side.1 = (bf16[512,512]{1,0:T(8,128)(2,1)S(1)}, bf16[512,512]{1,0:T(8,128)(2,1)S(1)}, f32[256,512]{1,0:T(8,128)S(1)}, bf16[256,512]{1,0:T(8,128)(2,1)}) custom-call(s32[1]{0:T(128)} %bitcast.me_ref, bf16[256,512]{1,0:T(8,128)(2,1)S(1)} %get-tuple-element.62.normed_ref.own_ref.n0_ref.refs_0_, f32[256,512]{1,0:T(8,128)S(1)} %get-tuple-element.67.normed_ref, ...), custom_call_target="tpu_custom_call" | custom-call | flops 100000000 | bytes 1048576 | tf_op jit(solution)/shard_map/side/pallas_call | solution.py:22
  38.9 0.8 heads.1
  40.0 2.0 %collective-permute-done.14.g3_ref = bf16[256,128]{1,0:T(8,128)(2,1)S(1)} collective-permute-done((bf16[256,128]{1,0:T(8,128)(2,1)S(1)}, bf16[256,128]{1,0:T(8,128)(2,1)S(1)}, u32[]{:S(2)}, u32[]{:S(2)}) %collective-permute-start.14) | collective-permute-done | bytes 65568 | tf_op jit(solution)/shard_map/ppermute | solution.py:476
  42.2 0.5 collective-permute-start.11
  42.6 4.4 %backward_far.1 = (bf16[256,384]{1,0:T(8,128)(2,1)S(1)}, bf16[256,384]{1,0:T(8,128)(2,1)S(1)}, f32[1024,384]{1,0:T(8,128)S(1)}) custom-call(s32[1]{0:T(128)} %bitcast.me_ref, s32[1,3]{1,0:T(1,128)S(1)} %copy-done.8, bf16[1024,384]{1,0:T(8,128)(2,1)S(1)} %get-tuple-element.76.part_ref, f32[1024,384]{1,0:T(8,128)S(1)} %get-tuple-element.77.slope_ref, ...), custom_call_target="tpu_custom_call" | custom-call | flops 10000000000 | bytes 1048576 | tf_op jit(solution)/shard_map/backward_far/pallas_call | solution.py:22
  47.0 1.0 %collective-permute-start.17 = (bf16[256,384]{1,0:T(8,128)(2,1)S(1)}, bf16[256,384]{1,0:T(8,128)(2,1)S(1)}, u32[]{:S(2)}, u32[]{:S(2)}) collective-permute-start(bf16[256,384]{1,0:T(8,128)(2,1)S(1)} %get-tuple-element.85.refs_6_), channel_id=1, source_target_pairs={{0,2},{1,3},{2,0},{3,1},{4,6},{5,7},{6,4},{7,5},{8,10},{9,11},{10,... | collective-permute-start | bytes 589832 | tf_op jit(solution)/shard_map/ppermute | solution.py:476
  48.0 0.7 collective-permute-start.18
  48.7 1.9 %backward_rest.1 = (bf16[256,384]{1,0:T(8,128)(2,1)S(1)}, bf16[256,384]{1,0:T(8,128)(2,1)S(1)}) custom-call(s32[1]{0:T(128)} %bitcast.me_ref, s32[1,3]{1,0:T(1,128)S(1)} %copy-done.8, bf16[1024,384]{1,0:T(8,128)(2,1)S(1)} %get-tuple-element.76.part_ref, f32[1024,384]{1,0:T(8,128)S(1)} %get-tuple-element.77.slope_ref, bf16[1024,128]{1,0:T(8,128)(2,1)S(1)} %collect.1.grad_ref, ...), custom_call_target="tpu_custom_call" | custom-call | flops 100000000 | bytes 1048576 | tf_op jit(solution)/shard_map/backward_rest/pallas_call | solution.py:22
  50.6 0.6 collective-permute-start.16
  51.2 0.8 weights.1
  52.1 5.0 %collective-permute-start.15 = (bf16[256,640]{1,0:T(8,128)(2,1)S(1)}, bf16[256,640]{1,0:T(8,128)(2,1)S(1)}, u32[]{:S(2)}, u32[]{:S(2)}) collective-permute-start(bf16[256,640]{1,0:T(8,128)(2,1)S(1)} %get-tuple-element.88), channel_id=1, source_target_pairs={{0,4},{4,0},{8,12},{12,8},{16,20},{20,16},{24,28},{28,24},{1,5},{5... | collective-permute-start | bytes 983048 | tf_op jit(solution)/shard_map/ppermute | solution.py:487
  57.1 1.4 %collective-permute-done.18.cross_ref = bf16[256,384]{1,0:T(8,128)(2,1)S(1)} collective-permute-done((bf16[256,384]{1,0:T(8,128)(2,1)S(1)}, bf16[256,384]{1,0:T(8,128)(2,1)S(1)}, u32[]{:S(2)}, u32[]{:S(2)}) %collective-permute-start.18) | collective-permute-done | bytes 196640 | tf_op jit(solution)/shard_map/ppermute | solution.py:476
  58.4 0.5 input_far.1.partial_ref
  59.0 0.7 input_grad.1.grad_ref
  59.6 1.1 %spread.1._ = bf16[512,512]{1,0:T(8,128)(2,1)} custom-call(bf16[512,256]{1,0:T(8,128)(2,1)S(1)} %get-tuple-element.89.select_ref, bf16[256,512]{1,0:T(8,128)(2,1)S(1)} %input_grad.1.grad_ref), custom_call_target="tpu_custom_call" | custom-call | flops 100000000 | bytes 1048576 | tf_op jit(solution)/shard_map/spread/pallas_call | solution.py:22
  60.7 4.3 %collective-permute-done.15.came_ref = bf16[256,640]{1,0:T(8,128)(2,1)S(1)} collective-permute-done((bf16[256,640]{1,0:T(8,128)(2,1)S(1)}, bf16[256,640]{1,0:T(8,128)(2,1)S(1)}, u32[]{:S(2)}, u32[]{:S(2)}) %collective-permute-start.15) | collective-permute-done | bytes 327712 | tf_op jit(solution)/shard_map/ppermute | solution.py:487
  65.1 4.4 %collective-permute-start.19 = (bf16[64,640]{1,0:T(8,128)(2,1)S(1)}, bf16[64,640]{1,0:T(8,128)(2,1)S(1)}, u32[]{:S(2)}, u32[]{:S(2)}) collective-permute-start(bf16[64,640]{1,0:T(8,128)(2,1)S(1)} %get-tuple-element.92), channel_id=1, source_target_pairs={{0,16},{4,20},{8,24},{12,28},{16,0},{20,4},{24,8},{28,12},{1,17},{... | collective-permute-start | bytes 245768 | tf_op jit(solution)/shard_map/ppermute | solution.py:487
  69.7 0.4 collective-permute-start.21
  70.1 5.0 %all-to-all-start = ((bf16[8,64,512]{2,1,0:T(8,128)(2,1)}), bf16[8,64,512]{2,1,0:T(8,128)(2,1)S(1)}, u32[]{:S(2)}, u32[]{:S(2)}) async-start(bf16[8,64,512]{2,1,0:T(8,128)(2,1)} %bitcast.4), calls=%async_computation | async-start | bytes 1048576 | tf_op jit(solution)/shard_map/all_to_all | solution.py:491
  75.2 0.7 collective-permute-done.20.refs_2_
  76.1 1.7 %collective-permute-start.23 = (bf16[64,640]{1,0:T(8,128)(2,1)S(1)}, bf16[64,640]{1,0:T(8,128)(2,1)S(1)}, u32[]{:S(2)}, u32[]{:S(2)}) collective-permute-start(bf16[64,640]{1,0:T(8,128)(2,1)S(1)} %sum.1.w0_ref), channel_id=1, source_target_pairs={{0,2},{1,3},{2,0},{3,1},{4,6},{5,7},{6,4},{7,5},{8,10},{9,11},{10,... | collective-permute-start | bytes 245768 | tf_op jit(solution)/shard_map/ppermute | solution.py:476
  77.9 2.7 %collective-permute-done.24.w3_ref = bf16[64,640]{1,0:T(8,128)(2,1)S(1)} collective-permute-done((bf16[64,640]{1,0:T(8,128)(2,1)S(1)}, bf16[64,640]{1,0:T(8,128)(2,1)S(1)}, u32[]{:S(2)}, u32[]{:S(2)}) %collective-permute-start.24) | collective-permute-done | bytes 81952 | tf_op jit(solution)/shard_map/ppermute | solution.py:476
  80.6 2.0 %collective-permute-done.23.w2_ref = bf16[64,640]{1,0:T(8,128)(2,1)S(1)} collective-permute-done((bf16[64,640]{1,0:T(8,128)(2,1)S(1)}, bf16[64,640]{1,0:T(8,128)(2,1)S(1)}, u32[]{:S(2)}, u32[]{:S(2)}) %collective-permute-start.23) | collective-permute-done | bytes 81952 | tf_op jit(solution)/shard_map/ppermute | solution.py:476
  82.6 1.1 %finish.1 = (f32[64,2048]{1,0:T(8,128)}, f32[64,512]{1,0:T(8,128)}, bf16[256,512]{1,0:T(8,128)(2,1)S(1)}) custom-call(s32[1]{0:T(128)} %bitcast.me_ref, s32[1]{0:T(128)} %bitcast.1.mask_ref.dp_ref, bf16[64,640]{1,0:T(8,128)(2,1)S(1)} %sum.1.w0_ref, bf16[64,640]{1,0:T(8,128)(2,1)S(1)} %collective-permute-done.22.w1_ref, ...), custom_call_target="tpu_custom_call" | custom-call | flops 100000000 | bytes 1048576 | tf_op jit(solution)/shard_map/finish/pallas_call | solution.py:22
  83.7 4.5 %all-to-all-done = bf16[8,64,512]{2,1,0:T(8,128)(2,1)S(1)} async-done(((bf16[8,64,512]{2,1,0:T(8,128)(2,1)}), bf16[8,64,512]{2,1,0:T(8,128)(2,1)S(1)}, u32[]{:S(2)}, u32[]{:S(2)}) %all-to-all-start) | async-done | bytes 524320 | tf_op jit(solution)/shard_map/all_to_all | solution.py:491
  88.1 1.0 %give_back.1 = bf16[256,512]{1,0:T(8,128)(2,1)} custom-call(bf16[256,512]{1,0:T(8,128)(2,1)S(1)} %get-tuple-element.95.chosen_ref, bf16[512,512]{1,0:T(8,128)(2,1)S(1)} %bitcast.6), custom_call_target="tpu_custom_call" | custom-call | flops 100000000 | bytes 1048576 | tf_op jit(solution)/shard_map/give_back/pallas_call | solution.py:22
  (49 shorter events, 1.6 us)
Async XLA Ops:
  2.9 15.6 %collective-permute-start = (bf16[72,512]{1,0:T(8,128)(2,1)}, bf16[72,512]{1,0:T(8,128)(2,1)S(1)}, u32[]{:S(2)}, u32[]{:S(2)}) collective-permute-start(bf16[72,512]{1,0:T(8,128)(2,1)} %get-tuple-element.52), channel_id=1, source_target_pairs={{0,16},{4,20},{8,24},{12,28},{16,0},{20,4},{24,8},{28,12},{1,17},{... | collective-permute-start | bytes 221192 | tf_op jit(solution)/shard_map/ppermute | solution.py:487
  7.0 11.6 %collective-permute-start.1 = (bf16[72,512]{1,0:T(8,128)(2,1)}, bf16[72,512]{1,0:T(8,128)(2,1)S(1)}, u32[]{:S(2)}, u32[]{:S(2)}) collective-permute-start(bf16[72,512]{1,0:T(8,128)(2,1)} %get-tuple-element.53), channel_id=1, source_target_pairs={{0,20},{4,16},{8,28},{12,24},{16,4},{20,0},{24,12},{28,8},{1,21},{... | collective-permute-start | bytes 221192 | tf_op jit(solution)/shard_map/ppermute | solution.py:487
  8.3 12.1 %collective-permute-start.2 = (bf16[72,512]{1,0:T(8,128)(2,1)}, bf16[72,512]{1,0:T(8,128)(2,1)S(1)}, u32[]{:S(2)}, u32[]{:S(2)}) collective-permute-start(bf16[72,512]{1,0:T(8,128)(2,1)} %get-tuple-element.54), channel_id=1, source_target_pairs={{0,24},{4,28},{8,16},{12,20},{16,8},{20,12},{24,0},{28,4},{1,25},{... | collective-permute-start | bytes 221192 | tf_op jit(solution)/shard_map/ppermute | solution.py:487
  11.9 8.5 %collective-permute-start.3 = (bf16[72,512]{1,0:T(8,128)(2,1)}, bf16[72,512]{1,0:T(8,128)(2,1)S(1)}, u32[]{:S(2)}, u32[]{:S(2)}) collective-permute-start(bf16[72,512]{1,0:T(8,128)(2,1)} %get-tuple-element.55), channel_id=1, source_target_pairs={{0,28},{4,24},{8,20},{12,16},{16,12},{20,8},{24,4},{28,0},{1,29},{... | collective-permute-start | bytes 221192 | tf_op jit(solution)/shard_map/ppermute | solution.py:487
  11.9 8.5 %collective-permute-start.4 = (bf16[72,512]{1,0:T(8,128)(2,1)}, bf16[72,512]{1,0:T(8,128)(2,1)S(1)}, u32[]{:S(2)}, u32[]{:S(2)}) collective-permute-start(bf16[72,512]{1,0:T(8,128)(2,1)} %get-tuple-element.56), channel_id=1, source_target_pairs={{0,4},{4,0},{8,12},{12,8},{16,20},{20,16},{24,28},{28,24},{1,5},{5... | collective-permute-start | bytes 221192 | tf_op jit(solution)/shard_map/ppermute | solution.py:487
  13.6 1.6 %copy-start = (bf16[512,2048]{1,0:T(8,128)(2,1)S(1)}, bf16[512,2048]{1,0:T(8,128)(2,1)}, u32[]{:S(2)}) copy-start(bf16[512,2048]{1,0:T(8,128)(2,1)} %proj_ref.15) | copy-start | bytes 6291460
  15.1 0.9 %copy-start.2 = (bf16[256,512]{1,0:T(8,128)(2,1)S(1)}, bf16[256,512]{1,0:T(8,128)(2,1)}, u32[]{:S(2)}) copy-start(bf16[256,512]{1,0:T(8,128)(2,1)} %cot_ref.5) | copy-start | bytes 786436
  16.1 1.0 %copy-start.4 = (bf16[512,512]{1,0:T(8,128)(2,1)S(1)}, bf16[512,512]{1,0:T(8,128)(2,1)}, u32[]{:S(2)}) copy-start(bf16[512,512]{1,0:T(8,128)(2,1)} %outw_ref.3) | copy-start | bytes 1572868
  17.1 0.9 %copy-start.6 = (bf16[256,512]{1,0:T(8,128)(2,1)S(1)}, bf16[256,512]{1,0:T(8,128)(2,1)}, u32[]{:S(2)}) copy-start(bf16[256,512]{1,0:T(8,128)(2,1)} %get-tuple-element.59.tokens_ref) | copy-start | bytes 786436
  17.1 1.0 %copy-start.9 = (s32[1,256]{1,0:T(1,128)S(1)}, s32[1,256]{1,0:T(1,128)}, u32[]{:S(2)}) copy-start(s32[1,256]{1,0:T(1,128)} %get-tuple-element.57.owner_ref) | copy-start | bytes 3076
  17.1 1.0 %copy-start.11 = (s32[1,256]{1,0:T(1,128)S(1)}, s32[1,256]{1,0:T(1,128)}, u32[]{:S(2)}) copy-start(s32[1,256]{1,0:T(1,128)} %get-tuple-element.58.slot_ref) | copy-start | bytes 3076
  17.1 6.8 %copy-start.7 = (bf16[72,512]{1,0:T(8,128)(2,1)S(1)}, bf16[72,512]{1,0:T(8,128)(2,1)}, u32[]{:S(2)}) copy-start(bf16[72,512]{1,0:T(8,128)(2,1)} %get-tuple-element.51.refs_0_) | copy-start | bytes 221188
  17.2 9.2 %copy-start.1 = (bf16[512,2048]{1,0:T(8,128)(2,1)S(1)}, bf16[512,2048]{1,0:T(8,128)(2,1)}, u32[]{:S(2)}) copy-start(bf16[512,2048]{1,0:T(8,128)(2,1)} %proj_ref.15) | copy-start | bytes 6291460
  17.2 9.2 %copy-start.8 = (s32[1,3]{1,0:T(1,128)S(1)}, s32[1,3]{1,0:T(1,128)}, u32[]{:S(2)}) copy-start(s32[1,3]{1,0:T(1,128)} %lengths_ref.9) | copy-start | bytes 40
  18.5 4.4 %collective-permute-start.5 = (bf16[72,512]{1,0:T(8,128)(2,1)S(1)}, bf16[72,512]{1,0:T(8,128)(2,1)S(1)}, u32[]{:S(2)}, u32[]{:S(2)}) collective-permute-start(bf16[72,512]{1,0:T(8,128)(2,1)S(1)} %get-tuple-element.60), channel_id=1, source_target_pairs={{0,8},{4,12},{8,0},{12,4},{16,24},{20,28},{24,16},{28,20},{1,9},{5... | collective-permute-start | bytes 221192 | tf_op jit(solution)/shard_map/ppermute | solution.py:487
  18.6 5.3 %collective-permute-start.6 = (bf16[72,512]{1,0:T(8,128)(2,1)S(1)}, bf16[72,512]{1,0:T(8,128)(2,1)S(1)}, u32[]{:S(2)}, u32[]{:S(2)}) collective-permute-start(bf16[72,512]{1,0:T(8,128)(2,1)S(1)} %get-tuple-element.61), channel_id=1, source_target_pairs={{0,12},{4,8},{8,4},{12,0},{16,28},{20,24},{24,20},{28,16},{1,13},{... | collective-permute-start | bytes 221192 | tf_op jit(solution)/shard_map/ppermute | solution.py:487
  24.8 6.4 %collective-permute-start.7 = (bf16[256,512]{1,0:T(8,128)(2,1)S(1)}, bf16[256,512]{1,0:T(8,128)(2,1)S(1)}, u32[]{:S(2)}, u32[]{:S(2)}) collective-permute-start(bf16[256,512]{1,0:T(8,128)(2,1)S(1)} %get-tuple-element.62.normed_ref.own_ref.n0_ref.refs_0_), channel_id=1, source_target_pairs={{0,2},{1,3},{2,0},{3,1},{4,6},{5,7},{6,4},{7,5},{8,10},{9,11},{10,... | collective-permute-start | bytes 786440 | tf_op jit(solution)/shard_map/ppermute | solution.py:476
  28.6 2.7 %collective-permute-start.9 = (bf16[256,512]{1,0:T(8,128)(2,1)S(1)}, bf16[256,512]{1,0:T(8,128)(2,1)S(1)}, u32[]{:S(2)}, u32[]{:S(2)}) collective-permute-start(bf16[256,512]{1,0:T(8,128)(2,1)S(1)} %get-tuple-element.65), channel_id=1, source_target_pairs={{0,1},{1,0},{2,3},{3,2},{4,5},{5,4},{6,7},{7,6},{8,9},{9,8},{10,11... | collective-permute-start | bytes 786440 | tf_op jit(solution)/shard_map/ppermute | solution.py:476
  31.2 1.5 %collective-permute-start.8 = (bf16[256,512]{1,0:T(8,128)(2,1)S(1)}, bf16[256,512]{1,0:T(8,128)(2,1)S(1)}, u32[]{:S(2)}, u32[]{:S(2)}) collective-permute-start(bf16[256,512]{1,0:T(8,128)(2,1)S(1)} %collective-permute-done.7.far_ref.n2_ref.refs_2_), channel_id=1, source_target_pairs={{0,1},{1,0},{2,3},{3,2},{4,5},{5,4},{6,7},{7,6},{8,9},{9,8},{10,11... | collective-permute-start | bytes 786440 | tf_op jit(solution)/shard_map/ppermute | solution.py:476
  32.8 4.9 %copy-start.3 = (bf16[256,512]{1,0:T(8,128)(2,1)S(1)}, bf16[256,512]{1,0:T(8,128)(2,1)}, u32[]{:S(2)}) copy-start(bf16[256,512]{1,0:T(8,128)(2,1)} %cot_ref.5) | copy-start | bytes 786436
  32.8 4.9 %copy-start.5 = (bf16[512,512]{1,0:T(8,128)(2,1)S(1)}, bf16[512,512]{1,0:T(8,128)(2,1)}, u32[]{:S(2)}) copy-start(bf16[512,512]{1,0:T(8,128)(2,1)} %outw_ref.3) | copy-start | bytes 1572868
  33.7 6.0 %collective-permute-start.12 = (bf16[256,128]{1,0:T(8,128)(2,1)S(1)}, bf16[256,128]{1,0:T(8,128)(2,1)S(1)}, u32[]{:S(2)}, u32[]{:S(2)}) collective-permute-start(bf16[256,128]{1,0:T(8,128)(2,1)S(1)} %get-tuple-element.79), channel_id=1, source_target_pairs={{0,1},{1,0},{2,3},{3,2},{4,5},{5,4},{6,7},{7,6},{8,9},{9,8},{10,11... | collective-permute-start | bytes 196616 | tf_op jit(solution)/shard_map/ppermute | solution.py:476
  33.9 6.0 %collective-permute-start.13 = (bf16[256,128]{1,0:T(8,128)(2,1)S(1)}, bf16[256,128]{1,0:T(8,128)(2,1)S(1)}, u32[]{:S(2)}, u32[]{:S(2)}) collective-permute-start(bf16[256,128]{1,0:T(8,128)(2,1)S(1)} %get-tuple-element.80), channel_id=1, source_target_pairs={{0,2},{1,3},{2,0},{3,1},{4,6},{5,7},{6,4},{7,5},{8,10},{9,11},{10,... | collective-permute-start | bytes 196616 | tf_op jit(solution)/shard_map/ppermute | solution.py:476
  37.6 4.4 %collective-permute-start.14 = (bf16[256,128]{1,0:T(8,128)(2,1)S(1)}, bf16[256,128]{1,0:T(8,128)(2,1)S(1)}, u32[]{:S(2)}, u32[]{:S(2)}) collective-permute-start(bf16[256,128]{1,0:T(8,128)(2,1)S(1)} %get-tuple-element.81), channel_id=1, source_target_pairs={{0,3},{1,2},{2,1},{3,0},{4,7},{5,6},{6,5},{7,4},{8,11},{9,10},{10,... | collective-permute-start | bytes 196616 | tf_op jit(solution)/shard_map/ppermute | solution.py:476
  38.7 3.3 %collective-permute-start.10 = (bf16[512,512]{1,0:T(8,128)(2,1)S(1)}, bf16[512,512]{1,0:T(8,128)(2,1)S(1)}, u32[]{:S(2)}, u32[]{:S(2)}) collective-permute-start(bf16[512,512]{1,0:T(8,128)(2,1)S(1)} %get-tuple-element.72), channel_id=1, source_target_pairs={{0,1},{1,0},{2,3},{3,2},{4,5},{5,4},{6,7},{7,6},{8,9},{9,8},{10,11... | collective-permute-start | bytes 1572872 | tf_op jit(solution)/shard_map/ppermute | solution.py:476
  42.2 9.1 %collective-permute-start.11 = (bf16[512,256]{1,0:T(8,128)(2,1)S(1)}, bf16[512,256]{1,0:T(8,128)(2,1)S(1)}, u32[]{:S(2)}, u32[]{:S(2)}) collective-permute-start(bf16[512,256]{1,0:T(8,128)(2,1)S(1)} %get-tuple-element.74), channel_id=1, source_target_pairs={{0,2},{1,3},{2,0},{3,1},{4,6},{5,7},{6,4},{7,5},{8,10},{9,11},{10,... | collective-permute-start | bytes 786440 | tf_op jit(solution)/shard_map/ppermute | solution.py:476
  47.0 10.0 %collective-permute-start.17 = (bf16[256,384]{1,0:T(8,128)(2,1)S(1)}, bf16[256,384]{1,0:T(8,128)(2,1)S(1)}, u32[]{:S(2)}, u32[]{:S(2)}) collective-permute-start(bf16[256,384]{1,0:T(8,128)(2,1)S(1)} %get-tuple-element.85.refs_6_), channel_id=1, source_target_pairs={{0,2},{1,3},{2,0},{3,1},{4,6},{5,7},{6,4},{7,5},{8,10},{9,11},{10,... | collective-permute-start | bytes 589832 | tf_op jit(solution)/shard_map/ppermute | solution.py:476
  48.0 10.4 %collective-permute-start.18 = (bf16[256,384]{1,0:T(8,128)(2,1)S(1)}, bf16[256,384]{1,0:T(8,128)(2,1)S(1)}, u32[]{:S(2)}, u32[]{:S(2)}) collective-permute-start(bf16[256,384]{1,0:T(8,128)(2,1)S(1)} %get-tuple-element.86.refs_7_), channel_id=1, source_target_pairs={{0,3},{1,2},{2,1},{3,0},{4,7},{5,6},{6,5},{7,4},{8,11},{9,10},{10,... | collective-permute-start | bytes 589832 | tf_op jit(solution)/shard_map/ppermute | solution.py:476
  50.6 8.3 %collective-permute-start.16 = (bf16[256,384]{1,0:T(8,128)(2,1)S(1)}, bf16[256,384]{1,0:T(8,128)(2,1)S(1)}, u32[]{:S(2)}, u32[]{:S(2)}) collective-permute-start(bf16[256,384]{1,0:T(8,128)(2,1)S(1)} %get-tuple-element.84.refs_5_), channel_id=1, source_target_pairs={{0,1},{1,0},{2,3},{3,2},{4,5},{5,4},{6,7},{7,6},{8,9},{9,8},{10,11... | collective-permute-start | bytes 589832 | tf_op jit(solution)/shard_map/ppermute | solution.py:476
  52.1 12.9 %collective-permute-start.15 = (bf16[256,640]{1,0:T(8,128)(2,1)S(1)}, bf16[256,640]{1,0:T(8,128)(2,1)S(1)}, u32[]{:S(2)}, u32[]{:S(2)}) collective-permute-start(bf16[256,640]{1,0:T(8,128)(2,1)S(1)} %get-tuple-element.88), channel_id=1, source_target_pairs={{0,4},{4,0},{8,12},{12,8},{16,20},{20,16},{24,28},{28,24},{1,5},{5... | collective-permute-start | bytes 983048 | tf_op jit(solution)/shard_map/ppermute | solution.py:487
  65.1 10.1 %collective-permute-start.19 = (bf16[64,640]{1,0:T(8,128)(2,1)S(1)}, bf16[64,640]{1,0:T(8,128)(2,1)S(1)}, u32[]{:S(2)}, u32[]{:S(2)}) collective-permute-start(bf16[64,640]{1,0:T(8,128)(2,1)S(1)} %get-tuple-element.92), channel_id=1, source_target_pairs={{0,16},{4,20},{8,24},{12,28},{16,0},{20,4},{24,8},{28,12},{1,17},{... | collective-permute-start | bytes 245768 | tf_op jit(solution)/shard_map/ppermute | solution.py:487
  69.5 6.4 %collective-permute-start.20 = (bf16[64,640]{1,0:T(8,128)(2,1)S(1)}, bf16[64,640]{1,0:T(8,128)(2,1)S(1)}, u32[]{:S(2)}, u32[]{:S(2)}) collective-permute-start(bf16[64,640]{1,0:T(8,128)(2,1)S(1)} %get-tuple-element.93), channel_id=1, source_target_pairs={{0,24},{4,28},{8,16},{12,20},{16,8},{20,12},{24,0},{28,4},{1,25},{... | collective-permute-start | bytes 245768 | tf_op jit(solution)/shard_map/ppermute | solution.py:487
  69.7 6.2 %collective-permute-start.21 = (bf16[64,640]{1,0:T(8,128)(2,1)S(1)}, bf16[64,640]{1,0:T(8,128)(2,1)S(1)}, u32[]{:S(2)}, u32[]{:S(2)}) collective-permute-start(bf16[64,640]{1,0:T(8,128)(2,1)S(1)} %get-tuple-element.94), channel_id=1, source_target_pairs={{0,8},{4,12},{8,0},{12,4},{16,24},{20,28},{24,16},{28,20},{1,9},{5... | collective-permute-start | bytes 245768 | tf_op jit(solution)/shard_map/ppermute | solution.py:487
  70.1 18.0 %all-to-all-start = ((bf16[8,64,512]{2,1,0:T(8,128)(2,1)}), bf16[8,64,512]{2,1,0:T(8,128)(2,1)S(1)}, u32[]{:S(2)}, u32[]{:S(2)}) async-start(bf16[8,64,512]{2,1,0:T(8,128)(2,1)} %bitcast.4), calls=%async_computation | async-start | bytes 1048576 | tf_op jit(solution)/shard_map/all_to_all | solution.py:491
  75.9 6.6 %copy-start.10 = (s32[1,256]{1,0:T(1,128)S(1)}, s32[1,256]{1,0:T(1,128)}, u32[]{:S(2)}) copy-start(s32[1,256]{1,0:T(1,128)} %get-tuple-element.57.owner_ref) | copy-start | bytes 3076
  76.0 4.6 %collective-permute-start.24 = (bf16[64,640]{1,0:T(8,128)(2,1)S(1)}, bf16[64,640]{1,0:T(8,128)(2,1)S(1)}, u32[]{:S(2)}, u32[]{:S(2)}) collective-permute-start(bf16[64,640]{1,0:T(8,128)(2,1)S(1)} %sum.1.w0_ref), channel_id=1, source_target_pairs={{0,3},{1,2},{2,1},{3,0},{4,7},{5,6},{6,5},{7,4},{8,11},{9,10},{10,... | collective-permute-start | bytes 245768 | tf_op jit(solution)/shard_map/ppermute | solution.py:476
  76.1 6.5 %collective-permute-start.23 = (bf16[64,640]{1,0:T(8,128)(2,1)S(1)}, bf16[64,640]{1,0:T(8,128)(2,1)S(1)}, u32[]{:S(2)}, u32[]{:S(2)}) collective-permute-start(bf16[64,640]{1,0:T(8,128)(2,1)S(1)} %sum.1.w0_ref), channel_id=1, source_target_pairs={{0,2},{1,3},{2,0},{3,1},{4,6},{5,7},{6,4},{7,5},{8,10},{9,11},{10,... | collective-permute-start | bytes 245768 | tf_op jit(solution)/shard_map/ppermute | solution.py:476
  77.8 4.8 %collective-permute-start.22 = (bf16[64,640]{1,0:T(8,128)(2,1)S(1)}, bf16[64,640]{1,0:T(8,128)(2,1)S(1)}, u32[]{:S(2)}, u32[]{:S(2)}) collective-permute-start(bf16[64,640]{1,0:T(8,128)(2,1)S(1)} %sum.1.w0_ref), channel_id=1, source_target_pairs={{0,1},{1,0},{2,3},{3,2},{4,5},{5,4},{6,7},{7,6},{8,9},{9,8},{10,11... | collective-permute-start | bytes 245768 | tf_op jit(solution)/shard_map/ppermute | solution.py:476
